TPU v7x, 32 devices: a whole 2x2x4 slice. The times are simulated.
32 devices in a mesh: group: 2 (over x), dom: 8 (over z, y), feat: 2 (over core).
Axes of the slice: x: 2, y: 2, z: 4, core: 2. Of those that a mesh axis runs over, the one named last changes fastest.
Arguments:
- grid: bfloat16 [65536, 512], P(('group', 'dom', 'feat')), parts along dimension 0, may hold values from -6 to 6
- mesh_feat: bfloat16 [8192, 512], P(('group', 'dom', 'feat')), parts along dimension 0, may hold values from -6 to 6
- owner: int32 [65536, 1], P(('group', 'dom', 'feat')), parts along dimension 0, may hold values from 0 to 15, as said below
- node: int32 [65536], P(('group', 'dom', 'feat')), parts along dimension 0, may hold values from 0 to 255
- halo_index: int32 [2048], P(('group', 'dom', 'feat')), parts along dimension 0, may hold values from 0 to 255
- edge_src: int32 [8192, 6], P(('group', 'dom', 'feat')), parts along dimension 0, may hold values from 0 to 383
- w_enc1: bfloat16 [512, 512], replicated, may hold values from -0.25 to 0.25
- enc_bias: float32 [512], replicated, may hold values from -4 to 4
- w_enc2: bfloat16 [512, 512], replicated, may hold values from -0.25 to 0.25
- proc_src: bfloat16 [2, 512, 512], replicated, may hold values from -0.25 to 0.25
- proc_dst: bfloat16 [2, 512, 512], replicated, may hold values from -0.25 to 0.25
- proc_bias: float32 [2, 512], replicated, may hold values from -4 to 4
- proc_out: bfloat16 [2, 512, 512], replicated, may hold values from -0.046875 to 0.046875
- dec_grid: bfloat16 [512, 512], replicated, may hold values from -0.25 to 0.25
- dec_mesh: bfloat16 [512, 512], replicated, may hold values from -0.0625 to 0.0625
- dec_out: bfloat16 [512, 512], replicated, may hold values from -0.25 to 0.25
Outputs:
- new_grid: bfloat16 [65536, 512], P(('group', 'dom', 'feat')), parts along dimension 0
There are 2 independent parts, one for each index of `group`. A program takes and returns all parts, laid end to end along the dimension named above; an argument that names none is the same for every part. Nothing has to cross between parts.
Inputs may be any that keep to these rules, and one draw needn't show every extreme that they name: `owner`: the 2048 rows of device p (an aligned block) name partition p or one of the four partitions p-2, p-1, p+1, p+2 (mod 16); each of those four is named at most 256 times by one device's rows, and in every draw some device names one of them exactly 256 times; at least half of a device's rows name p itself.
All inputs are finite; a program needn't handle non-finite values.
Results may differ from a plain program's by a relative error of at most 0.014.
Values may be sent and summed in bfloat16 or wider, within the bound.
No kernel may reach another device: no remote copies, remote signals or barrier semaphores. Data moves between devices by JAX's collectives and lax.ppermute only.
A program may use at most 64 MiB of HBM per device.

v0:
```python
import jax
import jax.numpy as jnp
from jax import lax
from jax.sharding import PartitionSpec as P

L = 2


def from_behind(value, axis, steps):
    count = lax.axis_size(axis)
    pairs = [(source, (source + steps) % count) for source in range(count)]
    return lax.ppermute(value, axis, pairs)


def extended_2(value, sides, width):
    for axis, dim in sides:
        size, length = (lax.axis_size(axis), value.shape[dim])
        up = [(i, (i + 1) % size) for i in range(size)]
        down = [(j, i) for i, j in up]
        last = lax.slice_in_dim(value, length - width, length, axis=dim)
        initial = lax.slice_in_dim(value, 0, width, axis=dim)
        before = lax.ppermute(last, axis, up)
        after = lax.ppermute(initial, axis, down)
        value = jnp.concatenate([before, value, after], axis=dim)
    return value


def send_rows(payload, indices):
    received = []
    for place, step in enumerate((1, 2, -1, -2)):
        received.append(from_behind((payload[place], indices[place]), ("dom", "feat"), step))
    rows = jnp.stack([item[0] for item in received])
    marks = jnp.stack([item[1] for item in received])
    return (rows, marks)


def return_rows(outgoing):
    backs = []
    for place, step in enumerate((1, 2, -1, -2)):
        backs.append(from_behind(outgoing[place], ("dom", "feat"), -step))
    return jnp.stack(backs)


def body(
    grid,
    mesh_feat,
    owner,
    node,
    halo_index,
    edge_src,
    w_enc1,
    enc_bias,
    w_enc2,
    proc_src,
    proc_dst,
    proc_bias,
    proc_out,
    dec_grid,
    dec_mesh,
    dec_out,
):
    parts = lax.axis_size(("dom", "feat"))
    myself = lax.axis_index(("dom", "feat"))
    grid_rows, width = grid.shape
    mesh_rows = mesh_feat.shape[0]
    border = halo_index.shape[0]
    capacity = grid_rows // 8
    hidden_enc = jax.nn.silu(
        jnp.dot(grid, w_enc1, preferred_element_type=jnp.float32) + enc_bias
    ).astype(jnp.bfloat16)
    message = jnp.dot(hidden_enc, w_enc2, preferred_element_type=jnp.float32).astype(jnp.bfloat16)
    distance = (owner[:, 0] - myself + parts) % parts
    steps_table = jnp.array([1, 2, parts - 1, parts - 2], jnp.int32)
    member = (distance[:, None] == steps_table[None, :]).astype(jnp.int32)
    remote = jnp.sum(member, axis=1)
    label = jnp.sum(member * jnp.arange(4, dtype=jnp.int32)[None, :], axis=1)
    ranks = jnp.sum((jnp.cumsum(member, axis=0) - 1) * member, axis=1)
    dump = 4 * capacity
    slots = jnp.where(remote > 0, label * capacity + ranks, dump)
    payload = jnp.zeros((dump + 1, width), jnp.bfloat16).at[slots].set(message)[:dump]
    indices = jnp.full((dump + 1,), mesh_rows, jnp.int32).at[slots].set(node)[:dump]
    arrived, arrived_ids = send_rows(
        payload.reshape(4, capacity, width), indices.reshape(4, capacity)
    )
    own_ids = jnp.where(remote > 0, mesh_rows, node)
    all_rows = jnp.concatenate([message, arrived.reshape(dump, width)], axis=0)
    all_ids = jnp.concatenate([own_ids, arrived_ids.reshape(dump)], axis=0)
    onehot = (all_ids[:, None] == jnp.arange(mesh_rows, dtype=jnp.int32)[None, :]).astype(
        jnp.bfloat16
    )
    summed = lax.dot_general(
        onehot, all_rows, (((0,), (0,)), ((), ())), preferred_element_type=jnp.float32
    )
    latent = (mesh_feat.astype(jnp.float32) + summed).astype(jnp.bfloat16)
    for layer in range(L):
        boundary_rows = latent[halo_index]
        widened = extended_2(boundary_rows, ((("dom", "feat"), 0),), border)
        extended = jnp.concatenate([latent, widened[:border], widened[2 * border :]], axis=0)
        source_proj = jnp.dot(extended, proc_src[layer], preferred_element_type=jnp.float32)
        node_proj = (
            jnp.dot(latent, proc_dst[layer], preferred_element_type=jnp.float32) + proc_bias[layer]
        )
        edge_msg = jax.nn.silu(source_proj[edge_src] + node_proj[:, None, :]).astype(jnp.bfloat16)
        edge_sum = jnp.sum(edge_msg.astype(jnp.float32), axis=1).astype(jnp.bfloat16)
        latent = (
            latent.astype(jnp.float32)
            + jnp.dot(edge_sum, proc_out[layer], preferred_element_type=jnp.float32)
        ).astype(jnp.bfloat16)
    outgoing = latent[jnp.minimum(arrived_ids, mesh_rows - 1)]
    returned = return_rows(outgoing).reshape(dump, width)
    returned = jnp.concatenate([returned, jnp.zeros((1, width), jnp.bfloat16)], axis=0)
    fetched = jnp.where((remote > 0)[:, None], returned[slots], latent[node])
    hidden_dec = jax.nn.silu(
        jnp.dot(grid, dec_grid, preferred_element_type=jnp.float32)
        + jnp.dot(fetched, dec_mesh, preferred_element_type=jnp.float32)
    ).astype(jnp.bfloat16)
    return jnp.dot(hidden_dec, dec_out, preferred_element_type=jnp.float32).astype(jnp.bfloat16)


def solution(mesh):
    return jax.shard_map(
        body,
        mesh=mesh,
        in_specs=(
            P(("group", "dom", "feat"), None),
            P(("group", "dom", "feat"), None),
            P(("group", "dom", "feat"), None),
            P(("group", "dom", "feat")),
            P(("group", "dom", "feat")),
            P(("group", "dom", "feat"), None),
            P(),
            P(),
            P(),
            P(),
            P(),
            P(),
            P(),
            P(),
            P(),
            P(),
        ),
        out_specs=P(("group", "dom", "feat"), None),
        check_vma=False,
    )
```

profile of v0, /device:TPU:0, one launch (start us, length us, event | category | flops | bytes accessed | tf_op | source)
XLA Modules:
  0.0 147.8 jit_solution(16097345908841852526)
XLA Ops:
  1.6 1.1 reduce-window.6
  4.8 8.2 %scatter_custom_fusion = s32[1025]{0:T(1024)S(1)} fusion(s32[2048]{0:T(1024)S(1)} %bitcast.82, s32[2048]{0:T(1024)} %param.20, s32[]{:T(128)} %constant.33.clone.1), kind=kCustom, calls=%fused_computation.87 | custom fusion | bytes 4612 | tf_op jit(solution)/shard_map/scatter | solution.py:81
  13.5 5.6 %collective-permute-start.3 = (s32[256]{0:T(256)S(1)}, s32[256]{0:T(256)S(1)}, u32[]{:S(2)}, u32[]{:S(2)}) collective-permute-start(s32[256]{0:T(256)S(1)} %get-tuple-element.20), channel_id=1, source_target_pairs={{0,14},{1,15},{2,0},{3,1},{4,2},{5,3},{6,4},{7,5},{8,6},{9,7},{10,... | collective-permute-start | bytes 3080 | tf_op jit(solution)/shard_map/ppermute | solution.py:12
  19.1 1.4 collective-permute-start.2
  20.5 5.3 %convolution_convert_fusion.1 = bf16[2048,512]{1,0:T(8,128)(2,1)} fusion(bf16[512,512]{1,0:T(8,128)(2,1)} %param.25, bf16[2048,512]{1,0:T(8,128)(2,1)S(1)} %copy-done, bf16[512,512]{1,0:T(8,128)(2,1)} %param.23, f32[512]{0:T(512)} %param.24), kind=kOutput, calls=%fused_computation.19 | convolution fusion | flops 2154823680 | bytes 5244928 | tf_op jit(solution)/shard_map/dot_general | solution.py:71
  25.9 10.1 %scatter_custom_fusion.1 = bf16[1025,512]{1,0:T(8,128)(2,1)S(1)} fusion(s32[2048]{0:T(1024)S(1)} %bitcast.83, bf16[2048,512]{1,0:T(8,128)(2,1)} %convolution_convert_fusion.1, bf16[]{:T(256)} %constant.65.clone.1), kind=kCustom, calls=%fused_computation.35 | custom fusion | bytes 1050112 | tf_op jit(solution)/shard_map/scatter | solution.py:80
  37.3 4.8 %collective-permute-start.7 = (bf16[256,512]{1,0:T(8,128)(2,1)}, bf16[256,512]{1,0:T(8,128)(2,1)S(1)}, u32[]{:S(2)}, u32[]{:S(2)}) collective-permute-start(bf16[256,512]{1,0:T(8,128)(2,1)} %get-tuple-element.11), channel_id=1, source_target_pairs={{0,14},{1,15},{2,0},{3,1},{4,2},{5,3},{6,4},{7,5},{8,6},{9,7},{10,... | collective-permute-start | bytes 786440 | tf_op jit(solution)/shard_map/ppermute | solution.py:12
  42.1 1.5 collective-permute-start.6
  43.6 2.1 %collective-permute-done.4 = bf16[256,512]{1,0:T(8,128)(2,1)S(1)} collective-permute-done((bf16[256,512]{1,0:T(8,128)(2,1)}, bf16[256,512]{1,0:T(8,128)(2,1)S(1)}, u32[]{:S(2)}, u32[]{:S(2)}) %collective-permute-start.4) | collective-permute-done | bytes 262176 | tf_op jit(solution)/shard_map/ppermute | solution.py:12
  45.7 8.5 %collective-permute-done.7 = bf16[256,512]{1,0:T(8,128)(2,1)S(1)} collective-permute-done((bf16[256,512]{1,0:T(8,128)(2,1)}, bf16[256,512]{1,0:T(8,128)(2,1)S(1)}, u32[]{:S(2)}, u32[]{:S(2)}) %collective-permute-start.7) | collective-permute-done | bytes 262176 | tf_op jit(solution)/shard_map/ppermute | solution.py:12
  54.3 3.1 %fusion.14 = bf16[256,512]{1,0:T(8,128)(2,1)S(1)} fusion(bf16[1024,512]{1,0:T(8,128)(2,1)S(1)} %bitcast.71, bf16[2048,512]{1,0:T(8,128)(2,1)} %convolution_convert_fusion.1, s32[3072]{0:T(1024)S(1)} %pad_add_fusion, bf16[256,512]{1,0:T(8,128)(2,1)} %param.18), kind=kOutput, calls=%fused_computation.30 | convolution fusion | flops 812777472 | bytes 3682304 | tf_op jit(solution)/shard_map/dot_general | solution.py:91
  58.2 2.7 %collective-permute-start.8 = (bf16[64,512]{1,0:T(8,128)(2,1)S(1)}, bf16[64,512]{1,0:T(8,128)(2,1)S(1)}, u32[]{:S(2)}, u32[]{:S(2)}) collective-permute-start(bf16[64,512]{1,0:T(8,128)(2,1)S(1)} %gather_fusion), channel_id=1, source_target_pairs={{0,1},{1,2},{2,3},{3,4},{4,5},{5,6},{6,7},{7,8},{8,9},{9,10},{10,1... | collective-permute-start | bytes 196616 | tf_op jit(solution)/shard_map/ppermute | solution.py:22
  60.8 4.7 %collective-permute-start.9 = (bf16[64,512]{1,0:T(8,128)(2,1)S(1)}, bf16[64,512]{1,0:T(8,128)(2,1)S(1)}, u32[]{:S(2)}, u32[]{:S(2)}) collective-permute-start(bf16[64,512]{1,0:T(8,128)(2,1)S(1)} %gather_fusion), channel_id=1, source_target_pairs={{1,0},{2,1},{3,2},{4,3},{5,4},{6,5},{7,6},{8,7},{9,8},{10,9},{11,1... | collective-permute-start | bytes 196616 | tf_op jit(solution)/shard_map/ppermute | solution.py:23
  65.5 2.1 %convolution_add_fusion.3 = f32[256,512]{1,0:T(8,128)} fusion(bf16[256,512]{1,0:T(8,128)(2,1)S(1)} %fusion.14, bf16[2,512,512]{2,1,0:T(8,128)(2,1)} %param.27, f32[512]{0:T(512)S(1)} %bitcast.89), kind=kOutput, calls=%fused_computation.28 | convolution fusion | flops 134348800 | bytes 1312768 | tf_op jit(solution)/shard_map/dot_general | solution.py:101
  67.7 1.4 fusion.27
  69.1 5.0 %gather_fusion.1 = f32[1536,512]{1,0:T(8,128)} fusion(f32[384,512]{1,0:T(8,128)S(1)} %fusion.27, s32[2048]{0:T(1024)S(1)} %pad_clamp_fusion), kind=kCustom, calls=%fused_computation.1 | custom fusion | bytes 6297600 | tf_op jit(solution)/shard_map/gather | solution.py:103
  74.1 4.6 %reshape.174 = f32[256,6,512]{2,1,0:T(8,128)} reshape(f32[1536,512]{1,0:T(8,128)} %gather_fusion.1) | data formatting | bytes 6291456 | tf_op jit(solution)/shard_map/gather | solution.py:103
  78.7 4.6 %fusion.6 = bf16[256,512]{1,0:T(8,128)(2,1)S(1)} fusion(f32[256,6,512]{2,1,0:T(8,128)} %reshape.174, f32[256,512]{1,0:T(8,128)S(1)} %copy-done.2), kind=kLoop, calls=%fused_computation.22 | loop fusion | flops 5373952 | bytes 3932160 | tf_op jit(solution)/shard_map/reduce_sum | solution.py:104
  84.4 4.4 %collective-permute-start.11 = (bf16[64,512]{1,0:T(8,128)(2,1)S(1)}, bf16[64,512]{1,0:T(8,128)(2,1)S(1)}, u32[]{:S(2)}, u32[]{:S(2)}) collective-permute-start(bf16[64,512]{1,0:T(8,128)(2,1)S(1)} %gather_fusion.2), channel_id=1, source_target_pairs={{1,0},{2,1},{3,2},{4,3},{5,4},{6,5},{7,6},{8,7},{9,8},{10,9},{11,1... | collective-permute-start | bytes 196616 | tf_op jit(solution)/shard_map/ppermute | solution.py:23
  88.8 2.1 %convolution_add_fusion.1 = f32[256,512]{1,0:T(8,128)} fusion(bf16[256,512]{1,0:T(8,128)(2,1)S(1)} %fusion.17, bf16[2,512,512]{2,1,0:T(8,128)(2,1)} %param.27, f32[512]{0:T(512)S(1)} %bitcast.88), kind=kOutput, calls=%fused_computation.26 | convolution fusion | flops 134348800 | bytes 1312768 | tf_op jit(solution)/shard_map/dot_general | solution.py:101
  91.0 1.4 fusion.23
  92.4 5.0 %gather_fusion.3 = f32[1536,512]{1,0:T(8,128)} fusion(f32[384,512]{1,0:T(8,128)S(1)} %fusion.23, s32[2048]{0:T(1024)S(1)} %pad_clamp_fusion), kind=kCustom, calls=%fused_computation.3 | custom fusion | bytes 6297600 | tf_op jit(solution)/shard_map/gather | solution.py:103
  97.3 4.6 %reshape.190 = f32[256,6,512]{2,1,0:T(8,128)} reshape(f32[1536,512]{1,0:T(8,128)} %gather_fusion.3) | data formatting | bytes 6291456 | tf_op jit(solution)/shard_map/gather | solution.py:103
  102.0 4.6 %fusion.7 = bf16[256,512]{1,0:T(8,128)(2,1)S(1)} fusion(f32[256,6,512]{2,1,0:T(8,128)} %reshape.190, f32[256,512]{1,0:T(8,128)S(1)} %copy-done.1), kind=kLoop, calls=%fused_computation.23 | loop fusion | flops 5373952 | bytes 3932160 | tf_op jit(solution)/shard_map/reduce_sum | solution.py:104
  106.9 4.0 %gather_fusion.4 = bf16[1024,512]{1,0:T(8,128)(2,1)S(1)} fusion(bf16[256,512]{1,0:T(8,128)(2,1)S(1)} %fusion.18, s32[1024]{0:T(1024)S(1)} %broadcast_clamp_fusion.1), kind=kCustom, calls=%fused_computation.4 | custom fusion | bytes 2101248 | tf_op jit(solution)/shard_map/gather | solution.py:109
  110.9 1.0 fusion.58
  111.9 4.2 %collective-permute-start.12 = (bf16[256,512]{1,0:T(8,128)(2,1)}, bf16[256,512]{1,0:T(8,128)(2,1)S(1)}, u32[]{:S(2)}, u32[]{:S(2)}) collective-permute-start(bf16[256,512]{1,0:T(8,128)(2,1)} %get-tuple-element.14), channel_id=1, source_target_pairs={{0,15},{1,0},{2,1},{3,2},{4,3},{5,4},{6,5},{7,6},{8,7},{9,8},{10,9... | collective-permute-start | bytes 786440 | tf_op jit(solution)/shard_map/ppermute | solution.py:12
  116.5 1.6 %collective-permute-start.15 = (bf16[256,512]{1,0:T(8,128)(2,1)}, bf16[256,512]{1,0:T(8,128)(2,1)S(1)}, u32[]{:S(2)}, u32[]{:S(2)}) collective-permute-start(bf16[256,512]{1,0:T(8,128)(2,1)} %get-tuple-element.17), channel_id=1, source_target_pairs={{0,2},{1,3},{2,4},{3,5},{4,6},{5,7},{6,8},{7,9},{8,10},{9,11},{10,... | collective-permute-start | bytes 786440 | tf_op jit(solution)/shard_map/ppermute | solution.py:12
  118.2 4.2 %fusion.61 = f32[2048,512]{1,0:T(8,128)} fusion(bf16[2048,512]{1,0:T(8,128)(2,1)S(1)} %copy-done, bf16[512,512]{1,0:T(8,128)(2,1)} %param.30), kind=kOutput, calls=%fused_computation.102 | convolution fusion | flops 1073741824 | bytes 6815744 | tf_op jit(solution)/shard_map/dot_general | solution.py:114
  122.4 9.2 %gather_fusion.6 = bf16[2048,512]{1,0:T(8,128)(2,1)} fusion(bf16[256,512]{1,0:T(8,128)(2,1)S(1)} %fusion.18, s32[2048]{0:T(1024)S(1)} %get-tuple-element.18), kind=kCustom, calls=%fused_computation.6 | custom fusion | bytes 4202496 | tf_op jit(solution)/shard_map/gather | solution.py:112
  131.8 9.2 %gather_fusion.5 = bf16[2048,512]{1,0:T(8,128)(2,1)} fusion(bf16[1025,512]{1,0:T(8,128)(2,1)S(1)} %concatenate.26, s32[2048]{0:T(1024)S(1)} %broadcast_clamp_fusion), kind=kCustom, calls=%fused_computation.5 | custom fusion | bytes 4202496 | tf_op jit(solution)/shard_map/gather | solution.py:112
  141.1 6.7 %convolution_convert_fusion = bf16[2048,512]{1,0:T(8,128)(2,1)} fusion(bf16[512,512]{1,0:T(8,128)(2,1)} %param.32, f32[2048,512]{1,0:T(8,128)} %fusion.61, bf16[512,512]{1,0:T(8,128)(2,1)} %param.31, bf16[2048,512]{1,0:T(8,128)(2,1)} %gather_fusion.5, bf16[2048,512]{1,0:T(8,128)(2,1)} %gather_fusion.6, pred[2048]{0:T(1024)(128)(4,1)S(1)} %get-tuple-element.9), kind=kOutput, calls=%fused_computation.18 | convolution fusion | flops 2155872256 | bytes 11536384 | tf_op jit(solution)/shard_map/dot_general | solution.py:117
  (68 shorter events, 8.3 us)
Async XLA Ops:
  0.0 20.5 %copy-start = (bf16[2048,512]{1,0:T(8,128)(2,1)S(1)}, bf16[2048,512]{1,0:T(8,128)(2,1)}, u32[]{:S(2)}) copy-start(bf16[2048,512]{1,0:T(8,128)(2,1)} %param.17) | copy-start | bytes 6291460
  13.0 24.3 %collective-permute-start = (s32[256]{0:T(256)S(1)}, s32[256]{0:T(256)S(1)}, u32[]{:S(2)}, u32[]{:S(2)}) collective-permute-start(s32[256]{0:T(256)S(1)} %get-tuple-element.19), channel_id=1, source_target_pairs={{0,1},{1,2},{2,3},{3,4},{4,5},{5,6},{6,7},{7,8},{8,9},{9,10},{10,1... | collective-permute-start | bytes 3080 | tf_op jit(solution)/shard_map/ppermute | solution.py:12
  13.5 28.6 %collective-permute-start.3 = (s32[256]{0:T(256)S(1)}, s32[256]{0:T(256)S(1)}, u32[]{:S(2)}, u32[]{:S(2)}) collective-permute-start(s32[256]{0:T(256)S(1)} %get-tuple-element.20), channel_id=1, source_target_pairs={{0,14},{1,15},{2,0},{3,1},{4,2},{5,3},{6,4},{7,5},{8,6},{9,7},{10,... | collective-permute-start | bytes 3080 | tf_op jit(solution)/shard_map/ppermute | solution.py:12
  19.1 24.4 %collective-permute-start.2 = (s32[256]{0:T(256)S(1)}, s32[256]{0:T(256)S(1)}, u32[]{:S(2)}, u32[]{:S(2)}) collective-permute-start(s32[256]{0:T(256)S(1)} %get-tuple-element.21), channel_id=1, source_target_pairs={{0,15},{1,0},{2,1},{3,2},{4,3},{5,4},{6,5},{7,6},{8,7},{9,8},{10,9... | collective-permute-start | bytes 3080 | tf_op jit(solution)/shard_map/ppermute | solution.py:12
  20.5 23.0 %collective-permute-start.1 = (s32[256]{0:T(256)S(1)}, s32[256]{0:T(256)S(1)}, u32[]{:S(2)}, u32[]{:S(2)}) collective-permute-start(s32[256]{0:T(256)S(1)} %get-tuple-element.22), channel_id=1, source_target_pairs={{0,2},{1,3},{2,4},{3,5},{4,6},{5,7},{6,8},{7,9},{8,10},{9,11},{10,... | collective-permute-start | bytes 3080 | tf_op jit(solution)/shard_map/ppermute | solution.py:12
  25.8 11.1 %copy-start.7 = (s32[64]{0:T(128)S(1)}, s32[64]{0:T(128)}, u32[]{:S(2)}) copy-start(s32[64]{0:T(128)} %param.21) | copy-start | bytes 772
  25.9 11.1 %copy-start.4 = (f32[2,512]{1,0:T(2,128)S(1)}, f32[2,512]{1,0:T(2,128)}, u32[]{:S(2)}) copy-start(f32[2,512]{1,0:T(2,128)} %param.28) | copy-start | bytes 12292
  25.9 11.1 %copy-start.3 = (s32[256,6]{0,1:T(8,128)S(1)}, s32[256,6]{0,1:T(8,128)}, u32[]{:S(2)}) copy-start(s32[256,6]{0,1:T(8,128)} %param.22) | copy-start | bytes 18436
  36.9 8.8 %collective-permute-start.4 = (bf16[256,512]{1,0:T(8,128)(2,1)}, bf16[256,512]{1,0:T(8,128)(2,1)S(1)}, u32[]{:S(2)}, u32[]{:S(2)}) collective-permute-start(bf16[256,512]{1,0:T(8,128)(2,1)} %get-tuple-element.10), channel_id=1, source_target_pairs={{0,1},{1,2},{2,3},{3,4},{4,5},{5,6},{6,7},{7,8},{8,9},{9,10},{10,1... | collective-permute-start | bytes 786440 | tf_op jit(solution)/shard_map/ppermute | solution.py:12
  37.3 16.9 %collective-permute-start.7 = (bf16[256,512]{1,0:T(8,128)(2,1)}, bf16[256,512]{1,0:T(8,128)(2,1)S(1)}, u32[]{:S(2)}, u32[]{:S(2)}) collective-permute-start(bf16[256,512]{1,0:T(8,128)(2,1)} %get-tuple-element.11), channel_id=1, source_target_pairs={{0,14},{1,15},{2,0},{3,1},{4,2},{5,3},{6,4},{7,5},{8,6},{9,7},{10,... | collective-permute-start | bytes 786440 | tf_op jit(solution)/shard_map/ppermute | solution.py:12
  42.1 12.1 %collective-permute-start.6 = (bf16[256,512]{1,0:T(8,128)(2,1)}, bf16[256,512]{1,0:T(8,128)(2,1)S(1)}, u32[]{:S(2)}, u32[]{:S(2)}) collective-permute-start(bf16[256,512]{1,0:T(8,128)(2,1)} %get-tuple-element.12), channel_id=1, source_target_pairs={{0,15},{1,0},{2,1},{3,2},{4,3},{5,4},{6,5},{7,6},{8,7},{9,8},{10,9... | collective-permute-start | bytes 786440 | tf_op jit(solution)/shard_map/ppermute | solution.py:12
  43.5 10.7 %collective-permute-start.5 = (bf16[256,512]{1,0:T(8,128)(2,1)S(1)}, bf16[256,512]{1,0:T(8,128)(2,1)S(1)}, u32[]{:S(2)}, u32[]{:S(2)}) collective-permute-start(bf16[256,512]{1,0:T(8,128)(2,1)S(1)} %get-tuple-element.13), channel_id=1, source_target_pairs={{0,2},{1,3},{2,4},{3,5},{4,6},{5,7},{6,8},{7,9},{8,10},{9,11},{10,... | collective-permute-start | bytes 786440 | tf_op jit(solution)/shard_map/ppermute | solution.py:12
  58.2 9.5 %collective-permute-start.8 = (bf16[64,512]{1,0:T(8,128)(2,1)S(1)}, bf16[64,512]{1,0:T(8,128)(2,1)S(1)}, u32[]{:S(2)}, u32[]{:S(2)}) collective-permute-start(bf16[64,512]{1,0:T(8,128)(2,1)S(1)} %gather_fusion), channel_id=1, source_target_pairs={{0,1},{1,2},{2,3},{3,4},{4,5},{5,6},{6,7},{7,8},{8,9},{9,10},{10,1... | collective-permute-start | bytes 196616 | tf_op jit(solution)/shard_map/ppermute | solution.py:22
  60.8 6.8 %collective-permute-start.9 = (bf16[64,512]{1,0:T(8,128)(2,1)S(1)}, bf16[64,512]{1,0:T(8,128)(2,1)S(1)}, u32[]{:S(2)}, u32[]{:S(2)}) collective-permute-start(bf16[64,512]{1,0:T(8,128)(2,1)S(1)} %gather_fusion), channel_id=1, source_target_pairs={{1,0},{2,1},{3,2},{4,3},{5,4},{6,5},{7,6},{8,7},{9,8},{10,9},{11,1... | collective-permute-start | bytes 196616 | tf_op jit(solution)/shard_map/ppermute | solution.py:23
  74.0 4.6 %copy-start.2 = (f32[256,512]{1,0:T(8,128)S(1)}, f32[256,512]{1,0:T(8,128)}, u32[]{:S(2)}) copy-start(f32[256,512]{1,0:T(8,128)} %convolution_add_fusion.3) | copy-start | bytes 1572868
  78.7 4.7 %copy-start.5 = (bf16[2,512,512]{2,1,0:T(8,128)(2,1)S(1)}, bf16[2,512,512]{2,1,0:T(8,128)(2,1)}, u32[]{:S(2)}) copy-start(bf16[2,512,512]{2,1,0:T(8,128)(2,1)} %param.29) | copy-start | bytes 3145732
  84.3 6.6 %collective-permute-start.10 = (bf16[64,512]{1,0:T(8,128)(2,1)S(1)}, bf16[64,512]{1,0:T(8,128)(2,1)S(1)}, u32[]{:S(2)}, u32[]{:S(2)}) collective-permute-start(bf16[64,512]{1,0:T(8,128)(2,1)S(1)} %gather_fusion.2), channel_id=1, source_target_pairs={{0,1},{1,2},{2,3},{3,4},{4,5},{5,6},{6,7},{7,8},{8,9},{9,10},{10,1... | collective-permute-start | bytes 196616 | tf_op jit(solution)/shard_map/ppermute | solution.py:22
  84.4 6.6 %collective-permute-start.11 = (bf16[64,512]{1,0:T(8,128)(2,1)S(1)}, bf16[64,512]{1,0:T(8,128)(2,1)S(1)}, u32[]{:S(2)}, u32[]{:S(2)}) collective-permute-start(bf16[64,512]{1,0:T(8,128)(2,1)S(1)} %gather_fusion.2), channel_id=1, source_target_pairs={{1,0},{2,1},{3,2},{4,3},{5,4},{6,5},{7,6},{8,7},{9,8},{10,9},{11,1... | collective-permute-start | bytes 196616 | tf_op jit(solution)/shard_map/ppermute | solution.py:23
  97.3 4.6 %copy-start.1 = (f32[256,512]{1,0:T(8,128)S(1)}, f32[256,512]{1,0:T(8,128)}, u32[]{:S(2)}) copy-start(f32[256,512]{1,0:T(8,128)} %convolution_add_fusion.1) | copy-start | bytes 1572868
  102.0 4.7 %copy-start.6 = (bf16[2,512,512]{2,1,0:T(8,128)(2,1)S(1)}, bf16[2,512,512]{2,1,0:T(8,128)(2,1)}, u32[]{:S(2)}) copy-start(bf16[2,512,512]{2,1,0:T(8,128)(2,1)} %param.29) | copy-start | bytes 3145732
  111.9 19.7 %collective-permute-start.12 = (bf16[256,512]{1,0:T(8,128)(2,1)}, bf16[256,512]{1,0:T(8,128)(2,1)S(1)}, u32[]{:S(2)}, u32[]{:S(2)}) collective-permute-start(bf16[256,512]{1,0:T(8,128)(2,1)} %get-tuple-element.14), channel_id=1, source_target_pairs={{0,15},{1,0},{2,1},{3,2},{4,3},{5,4},{6,5},{7,6},{8,7},{9,8},{10,9... | collective-permute-start | bytes 786440 | tf_op jit(solution)/shard_map/ppermute | solution.py:12
  116.1 15.5 %collective-permute-start.14 = (bf16[256,512]{1,0:T(8,128)(2,1)}, bf16[256,512]{1,0:T(8,128)(2,1)S(1)}, u32[]{:S(2)}, u32[]{:S(2)}) collective-permute-start(bf16[256,512]{1,0:T(8,128)(2,1)} %get-tuple-element.15), channel_id=1, source_target_pairs={{0,1},{1,2},{2,3},{3,4},{4,5},{5,6},{6,7},{7,8},{8,9},{9,10},{10,1... | collective-permute-start | bytes 786440 | tf_op jit(solution)/shard_map/ppermute | solution.py:12
  116.1 15.5 %collective-permute-start.13 = (bf16[256,512]{1,0:T(8,128)(2,1)}, bf16[256,512]{1,0:T(8,128)(2,1)S(1)}, u32[]{:S(2)}, u32[]{:S(2)}) collective-permute-start(bf16[256,512]{1,0:T(8,128)(2,1)} %get-tuple-element.16), channel_id=1, source_target_pairs={{0,14},{1,15},{2,0},{3,1},{4,2},{5,3},{6,4},{7,5},{8,6},{9,7},{10,... | collective-permute-start | bytes 786440 | tf_op jit(solution)/shard_map/ppermute | solution.py:12
  116.5 15.1 %collective-permute-start.15 = (bf16[256,512]{1,0:T(8,128)(2,1)}, bf16[256,512]{1,0:T(8,128)(2,1)S(1)}, u32[]{:S(2)}, u32[]{:S(2)}) collective-permute-start(bf16[256,512]{1,0:T(8,128)(2,1)} %get-tuple-element.17), channel_id=1, source_target_pairs={{0,2},{1,3},{2,4},{3,5},{4,6},{5,7},{6,8},{7,9},{8,10},{9,11},{10,... | collective-permute-start | bytes 786440 | tf_op jit(solution)/shard_map/ppermute | solution.py:12
where the time goes:
time: 151 us; the launch traced here: 148 us
  local copies, waits for them, and re-layouts  63.8 us (42%)
  starting transfers between devices  31.9 us (21%)
  matrix products  27 us (18%)
  other arithmetic  14.1 us (9%)
  waiting for transfers between devices  10.6 us (7%)
    ppermute x12, starting transfers between devices, from_behind(): return lax.ppermute(value, axis, pairs)  20 us
    gather x4, local copies, waits for them, and re-layouts, body(): source_proj[edge_src] + node_proj[:, None, :]  19.1 us
    gather x2, local copies, waits for them, and re-layouts, body(): fetched = jnp.where((remote > 0)[:, None], returned[slots], latent[node])  18.4 us
    ppermute x12, waiting for transfers between devices, from_behind(): return lax.ppermute(value, axis, pairs)  10.6 us
    scatter x1, local copies, waits for them, and re-layouts, body(): jnp.zeros((dump + 1, width), jnp.bfloat16).at[slots].set(message)[:dump]  10.1 us
    reduce_sum x2, other arithmetic, body(): jnp.sum(edge_msg.astype(jnp.float32), axis=1).astype(jnp.bfloat16)  9.29 us
    ppermute x2, starting transfers between devices, extended_2(): after = lax.ppermute(initial, axis, down)  9.13 us
    scatter x1, local copies, waits for them, and re-layouts, body(): jnp.full((dump + 1,), mesh_rows, jnp.int32).at[slots].set(node)[:dump]  8.21 us
  transfers between devices with their start and end apart: 16, of which 2 were waited for; matrix products, arithmetic and copies ran while one was open for 23% of the time, Pallas kernels for 0%

commit v1 on v0

v1 whole, which is shorter than its diff:
```python
import functools

import jax
import jax.numpy as jnp
from jax import lax
from jax.experimental import pallas as pl
from jax.experimental.pallas import tpu as pltpu
from jax.sharding import PartitionSpec as P

L = 2
AXES = ("dom", "feat")
F32, BF16 = jnp.float32, jnp.bfloat16
MIB = 1 << 20


def silu(x):
    half = 0.5 * x
    return half + half * jnp.tanh(half)


def dot(a, b):
    return jnp.dot(a, b, preferred_element_type=F32)


def slot_codes(owner, node, parts, mesh_rows):
    core = lax.axis_index("feat")
    me = lax.axis_index("dom") * 2 + core
    slot = (owner - me) * (1 - 2 * core) + 2
    slot = jnp.where(slot < 0, slot + parts, slot)
    slot = jnp.where(slot >= parts, slot - parts, slot)
    return slot * mesh_rows + node


def one_hot_down(code, first, rows):
    n = code.shape[1]
    at = lax.broadcasted_iota(jnp.int32, (rows, n), 0)
    return jnp.where(at == code - first, 1.0, 0.0).astype(BF16)


def columns(row):
    n = row.shape[1]
    row = row.astype(F32)
    parts = [
        jnp.broadcast_to(row[:, i : i + 128], (128, 128)).T for i in range(0, n, 128)
    ]
    return jnp.concatenate(parts, axis=0)


def one_hot_across(cols, first, width):
    at = lax.broadcasted_iota(jnp.int32, cols.shape, 1).astype(F32)
    blocks = [
        jnp.where(cols == at + float(first + i), 1.0, 0.0).astype(BF16)
        for i in range(0, width, 128)
    ]
    return jnp.concatenate(blocks, axis=1)


def encode_kernel(parts, mesh_rows, owner, node, grid, w1, bias, hidden, near, cross, acc):
    step = pl.program_id(0)
    code = slot_codes(owner[...], node[...], parts, mesh_rows)
    h = silu(dot(grid[...], w1[...]) + bias[...]).astype(BF16)
    hidden[...] = h
    sums = dot(one_hot_down(code, 0, 2 * mesh_rows), h)

    @pl.when(step == 0)
    def _():
        acc[...] = sums

    @pl.when(step > 0)
    def _():
        acc[...] += sums

    @pl.when(step == pl.num_programs(0) - 1)
    def _():
        near[...] = acc[:mesh_rows].astype(BF16)
        cross[...] = acc[mesh_rows:].astype(BF16)


def far_kernel(parts, mesh_rows, owner, node, hidden, crossed, far, acc):
    step = pl.program_id(0)
    code = slot_codes(owner[...], node[...], parts, mesh_rows)
    sums = dot(one_hot_down(code, 4 * mesh_rows, mesh_rows), hidden[...])

    @pl.when(step == 0)
    def _():
        acc[...] = sums + crossed[...].astype(F32)

    @pl.when(step > 0)
    def _():
        acc[...] += sums

    @pl.when(step == pl.num_programs(0) - 1)
    def _():
        far[...] = acc[...].astype(BF16)


def chip_kernel(parts, mesh_rows, owner, node, hidden, own, sibling, acc):
    step = pl.program_id(0)
    code = slot_codes(owner[...], node[...], parts, mesh_rows)
    sums = dot(one_hot_down(code, 2 * mesh_rows, 2 * mesh_rows), hidden[...])

    @pl.when(step == 0)
    def _():
        acc[...] = sums

    @pl.when(step > 0)
    def _():
        acc[...] += sums

    @pl.when(step == pl.num_programs(0) - 1)
    def _():
        own[...] = acc[:mesh_rows]
        sibling[...] = acc[mesh_rows:].astype(BF16)


def pick(index, table):
    one_hot = one_hot_down(index, 0, table.shape[0])
    out = lax.dot_general(one_hot, table, (((0,), (0,)), ((), ())), preferred_element_type=F32)
    return out.astype(BF16)


def latent_kernel(mesh, own, sibling, near, far, w2, halo_index, latent, halo):
    sums = own[...] + sibling[...].astype(F32) + near[...].astype(F32) + far[...].astype(F32)
    rows = (mesh[...].astype(F32) + dot(sums.astype(BF16), w2[...])).astype(BF16)
    latent[...] = rows
    halo[...] = pick(halo_index[...], rows)


def project_kernel(latent, w_src, w_dst, bias, source, target):
    source[...] = dot(latent[...], w_src[0]).astype(BF16)
    target[...] = dot(latent[...], w_dst[0]) + bias[0]


def layer_kernel(last, latent, source, target, across, beside, edges, w_src, w_out, w_next, *outs):
    core = lax.axis_index("feat")
    halo_across = dot(across[...], w_src[0]).astype(BF16)
    halo_beside = dot(beside[...], w_src[0]).astype(BF16)
    first = core == 0
    before = jnp.where(first, halo_across, halo_beside)
    after = jnp.where(first, halo_beside, halo_across)
    table = jnp.concatenate([source[...], before, after], axis=0)
    total = None
    for k in range(edges.shape[0]):
        one_hot = one_hot_across(columns(edges[k : k + 1, :]), 0, table.shape[0])
        message = silu(dot(one_hot, table) + target[...]).astype(BF16).astype(F32)
        total = message if total is None else total + message
    rows = latent[...].astype(F32) + dot(total.astype(BF16), w_out[0])
    rows = rows.astype(BF16)
    if last:
        outs[0][...] = dot(rows, w_next[...]).astype(BF16)
    else:
        outs[0][...] = rows
        outs[1][...] = pick(w_next[...], rows)


def base_kernel(parts, mesh_rows, owner, node, grid, w_grid, own, sibling, base):
    cols = columns(slot_codes(owner[...], node[...], parts, mesh_rows))
    out = dot(grid[...], w_grid[...])
    out += dot(one_hot_across(cols, 2 * mesh_rows, mesh_rows), own[...])
    out += dot(one_hot_across(cols, 3 * mesh_rows, mesh_rows), sibling[...])
    base[...] = out.astype(BF16)


def decode_kernel(parts, mesh_rows, owner, node, base, near, cross, far, w_out, out):
    cols = columns(slot_codes(owner[...], node[...], parts, mesh_rows))
    pre = base[...].astype(F32)
    pre += dot(one_hot_across(cols, 0, mesh_rows), near[...])
    pre += dot(one_hot_across(cols, mesh_rows, mesh_rows), cross[...])
    pre += dot(one_hot_across(cols, 4 * mesh_rows, mesh_rows), far[...])
    out[...] = dot(silu(pre).astype(BF16), w_out[...]).astype(BF16)


def whole(shape):
    return pl.BlockSpec(shape, lambda *_: (0,) * len(shape))


def call(kernel, grid, ins, outs, flops, scratch=(), vmem=24):
    moved = sum(a.size * a.dtype.itemsize for a, _ in ins)
    return pl.pallas_call(
        kernel,
        grid=grid,
        in_specs=[spec for _, spec in ins],
        out_specs=[spec for _, _, spec in outs],
        out_shape=[jax.ShapeDtypeStruct(shape, dtype) for shape, dtype, _ in outs],
        scratch_shapes=list(scratch),
        compiler_params=pltpu.CompilerParams(vmem_limit_bytes=vmem * MIB),
        cost_estimate=pl.CostEstimate(flops=flops, bytes_accessed=moved, transcendentals=0),
    )(*[a for a, _ in ins])


def body(
    grid,
    mesh_feat,
    owner,
    node,
    halo_index,
    edge_src,
    w_enc1,
    enc_bias,
    w_enc2,
    proc_src,
    proc_dst,
    proc_bias,
    proc_out,
    dec_grid,
    dec_mesh,
    dec_out,
):
    parts = lax.axis_size(AXES)
    rows, width = grid.shape
    mesh_rows = mesh_feat.shape[0]
    border = halo_index.shape[0]
    degree = edge_src.shape[1]
    block = 512
    steps = (rows // block,)

    def sided(step):
        return [(i, (i + step) % parts if i % 2 == 0 else (i - step) % parts) for i in range(parts)]

    def swap(value):
        return lax.ppermute(value, AXES, sided(1))

    def across(value):
        return lax.ppermute(value, AXES, sided(-1))

    def to_near(value):
        return lax.ppermute(value, AXES, sided(-2))

    def to_far(value):
        return lax.ppermute(value, AXES, sided(2))

    owner = owner.reshape(1, rows)
    node = node.reshape(1, rows)
    halo_index = halo_index.reshape(1, border)
    edges = edge_src.T
    enc_bias = enc_bias.reshape(1, width)
    proc_bias = proc_bias.reshape(L, 1, width)

    by_lane = pl.BlockSpec((1, block), lambda i: (0, i))
    by_row = pl.BlockSpec((block, width), lambda i: (i, 0))
    square = whole((width, width))
    table = whole((mesh_rows, width))
    part = functools.partial

    unit = 2 * rows * width
    hidden, near, cross = call(
        part(encode_kernel, parts, mesh_rows),
        steps,
        [(owner, by_lane), (node, by_lane), (grid, by_row), (w_enc1, square), (enc_bias, whole((1, width)))],
        [((rows, width), BF16, by_row), ((mesh_rows, width), BF16, table), ((mesh_rows, width), BF16, table)],
        unit * (width + 2 * mesh_rows),
        [pltpu.VMEM((2 * mesh_rows, width), F32)],
    )
    crossed = swap(cross)
    near = to_near(near)
    (far,) = call(
        part(far_kernel, parts, mesh_rows),
        steps,
        [(owner, by_lane), (node, by_lane), (hidden, by_row), (crossed, table)],
        [((mesh_rows, width), BF16, table)],
        unit * mesh_rows,
        [pltpu.VMEM((mesh_rows, width), F32)],
    )
    far = to_far(far)
    own, sibling = call(
        part(chip_kernel, parts, mesh_rows),
        steps,
        [(owner, by_lane), (node, by_lane), (hidden, by_row)],
        [((mesh_rows, width), F32, table), ((mesh_rows, width), BF16, table)],
        unit * 2 * mesh_rows,
        [pltpu.VMEM((2 * mesh_rows, width), F32)],
    )
    sibling = swap(sibling)
    halo_rows = whole((border, width))
    latent, halo = call(
        latent_kernel,
        (1,),
        [(mesh_feat, table), (own, table), (sibling, table), (near, table), (far, table), (w_enc2, square), (halo_index, whole((1, border)))],
        [((mesh_rows, width), BF16, table), ((border, width), BF16, halo_rows)],
        2 * mesh_rows * width * width,
    )
    for layer in range(L):
        last = layer == L - 1
        halo_across = across(halo)
        halo_beside = swap(halo)
        weights = pl.BlockSpec((1, width, width), lambda i, layer=layer: (layer, 0, 0))
        source, target = call(
            project_kernel,
            (1,),
            [(latent, table), (proc_src, weights), (proc_dst, weights), (proc_bias, pl.BlockSpec((1, 1, width), lambda i, layer=layer: (layer, 0, 0)))],
            [((mesh_rows, width), BF16, table), ((mesh_rows, width), F32, table)],
            4 * mesh_rows * width * width,
        )
        following = (dec_mesh, square) if last else (halo_index, whole((1, border)))
        outs = [((mesh_rows, width), BF16, table)]
        if not last:
            outs.append(((border, width), BF16, halo_rows))
        made = call(
            part(layer_kernel, last),
            (1,),
            [
                (latent, table),
                (source, table),
                (target, table),
                (halo_across, halo_rows),
                (halo_beside, halo_rows),
                (edges, whole((degree, mesh_rows))),
                (proc_src, weights),
                (proc_out, weights),
                following,
            ],
            outs,
            2 * mesh_rows * width * (degree * 2 * mesh_rows + 2 * width),
        )
        if last:
            (projected,) = made
        else:
            latent, halo = made
    sibling = swap(projected)
    far = to_near(projected)
    near = to_far(projected)
    cross = swap(far)
    (base,) = call(
        part(base_kernel, parts, mesh_rows),
        steps,
        [(owner, by_lane), (node, by_lane), (grid, by_row), (dec_grid, square), (projected, table), (sibling, table)],
        [((rows, width), BF16, by_row)],
        unit * (width + 2 * mesh_rows),
    )
    (out,) = call(
        part(decode_kernel, parts, mesh_rows),
        steps,
        [(owner, by_lane), (node, by_lane), (base, by_row), (near, table), (cross, table), (far, table), (dec_out, square)],
        [((rows, width), BF16, by_row)],
        unit * (width + 3 * mesh_rows),
    )
    return out


def solution(mesh):
    rows = P(("group", "dom", "feat"), None)
    flat = P(("group", "dom", "feat"))
    return jax.shard_map(
        body,
        mesh=mesh,
        in_specs=(rows, rows, rows, flat, flat, rows) + (P(),) * 10,
        out_specs=rows,
        check_vma=False,
    )
```

time: 151 us -> 68.7 us (0.45); the launches traced: 148 us -> 68.4 us
  local copies, waits for them, and re-layouts: 63.8 us -> 4.8 us
  matrix products: 27 us -> 0 us
  Pallas kernels: 0 us -> 21.5 us
  starting transfers between devices: 31.9 us -> 12.1 us
  waiting for transfers between devices: 10.6 us -> 29.6 us
  other arithmetic: 14.1 us -> 0 us
    gather x9 -> x0, local copies, waits for them, and re-layouts: 42.9 us -> none  [the longest x4 19.1 us: body(): source_proj[edge_src] + node_proj[:, None, :]]
    dot_general x10 -> x0, matrix products: 27 us -> none  [the longest x1 6.72 us: body(): jnp.dot(hidden_dec, dec_out, preferred_element_type=jnp.float32)]
    pallas_call x0 -> x10, Pallas kernels: none -> 21.5 us  [call(): pl.pallas_call(kernel, grid=grid, in_specs=[spec for _, spec in ins], out...]
    ppermute x16 -> x12, starting transfers between devices: 31.9 us -> 12.1 us  [the longest x2 5.68 us: to_near(): return lax.ppermute(value, AXES, sided(-2))]
    ppermute x16 -> x12, waiting for transfers between devices: 10.6 us -> 29.6 us  [the longest x2 12.2 us: to_near(): return lax.ppermute(value, AXES, sided(-2))]
    scatter x2 -> x0, local copies, waits for them, and re-layouts: 18.4 us -> none  [the longest x1 10.1 us: body(): jnp.zeros((dump + 1, width), jnp.bfloat16).at[slots].set(message)[:dump]]
    reduce_sum x3 -> x0, other arithmetic: 10.1 us -> none  [the longest x2 9.29 us: body(): jnp.sum(edge_msg.astype(jnp.float32), axis=1).astype(jnp.bfloat16)]
    unnamed x17 -> x38, local copies, waits for them, and re-layouts: 0.03 us -> 4.79 us
  transfers between devices with their start and end apart: 16 -> 12, of which waited for: 2 -> 4; matrix products, arithmetic and copies ran while one was open for 23% -> 0% of each run, Pallas kernels for 0% -> 11%
where the time goes in v1:
time: 68.7 us; the launch traced here: 68.4 us
  waiting for transfers between devices  29.6 us (43%)
  Pallas kernels  21.5 us (31%)
  starting transfers between devices  12.1 us (18%)
  local copies, waits for them, and re-layouts  4.8 us (7%)
    pallas_call x10, Pallas kernels, call(): pl.pallas_call(kernel, grid=grid, in_specs=[spec for _, spec in ins], out...  21.5 us
    ppermute x2, waiting for transfers between devices, to_near(): return lax.ppermute(value, AXES, sided(-2))  12.2 us
    ppermute x2, waiting for transfers between devices, to_far(): return lax.ppermute(value, AXES, sided(2))  9.04 us
    ppermute x2, waiting for transfers between devices, across(): return lax.ppermute(value, AXES, sided(-1))  8.29 us
    ppermute x2, starting transfers between devices, to_near(): return lax.ppermute(value, AXES, sided(-2))  5.68 us
    unnamed x38, local copies, waits for them, and re-layouts  4.79 us
    ppermute x2, starting transfers between devices, across(): return lax.ppermute(value, AXES, sided(-1))  3.64 us
    ppermute x2, starting transfers between devices, to_far(): return lax.ppermute(value, AXES, sided(2))  2 us
  transfers between devices with their start and end apart: 12, of which 4 were waited for; matrix products, arithmetic and copies ran while one was open for 0% of the time, Pallas kernels for 11%

profile of v1, /device:TPU:0, one launch (start us, length us, event | category | flops | bytes accessed | tf_op | source)
XLA Modules:
  0.0 68.4 jit_solution(4821338690332850967)
XLA Ops:
  0.0 0.7 %copy-done.7 = s32[2048,1]{0,1:T(1,128)S(1)} copy-done((s32[2048,1]{0,1:T(1,128)S(1)}, s32[2048,1]{0,1:T(1,128)}, u32[]{:S(2)}) %copy-start.7) | copy-done | bytes 8216
  0.7 0.7 %copy-done.9 = s32[2048]{0:T(1024)S(1)} copy-done((s32[2048]{0:T(1024)S(1)}, s32[2048]{0:T(1024)}, u32[]{:S(2)}) %copy-start.9) | copy-done | bytes 8216
  1.4 1.6 %copy-done.12 = bf16[2048,512]{1,0:T(8,128)(2,1)S(1)} copy-done((bf16[2048,512]{1,0:T(8,128)(2,1)S(1)}, bf16[2048,512]{1,0:T(8,128)(2,1)}, u32[]{:S(2)}) %copy-start.12) | copy-done | bytes 2097176
  3.0 1.0 %copy-done.14 = bf16[512,512]{1,0:T(8,128)(2,1)S(1)} copy-done((bf16[512,512]{1,0:T(8,128)(2,1)S(1)}, bf16[512,512]{1,0:T(8,128)(2,1)}, u32[]{:S(2)}) %copy-start.14) | copy-done | bytes 524312
  4.0 0.7 copy-done.17
  4.7 4.1 %shard_map.154 = (bf16[2048,512]{1,0:T(8,128)(2,1)S(1)}, bf16[256,512]{1,0:T(8,128)(2,1)S(1)}, bf16[256,512]{1,0:T(8,128)(2,1)S(1)}) custom-call(s32[1,2048]{1,0:T(1,128)S(1)} %bitcast.7, s32[1,2048]{1,0:T(1,128)S(1)} %bitcast.12, bf16[2048,512]{1,0:T(8,128)(2,1)S(1)} %copy-done.12, bf16[512,512]{1,0:T(8,128)(2,1)S(1)} %copy-done.14, f32[1,512]{1,0:T(1,128)S(1)} %bitcast.19), custom_call_target="tpu_custom_call" | custom-call | flops 2147483648 | bytes 2639872 | tf_op jit(solution)/shard_map/pallas_call | solution.py:179
  8.8 0.5 collective-permute-start.2
  9.3 5.6 %collective-permute-start.1 = (bf16[256,512]{1,0:T(8,128)(2,1)S(1)}, bf16[256,512]{1,0:T(8,128)(2,1)S(1)}, u32[]{:S(2)}, u32[]{:S(2)}) collective-permute-start(bf16[256,512]{1,0:T(8,128)(2,1)S(1)} %get-tuple-element.21), channel_id=1, source_target_pairs={{0,14},{1,3},{2,0},{3,5},{4,2},{5,7},{6,4},{7,9},{8,6},{9,11},{10,... | collective-permute-start | bytes 786440 | tf_op jit(solution)/shard_map/ppermute | solution.py:227
  14.9 2.2 %shard_map.155 = (f32[256,512]{1,0:T(8,128)S(1)}, bf16[256,512]{1,0:T(8,128)(2,1)S(1)}) custom-call(s32[1,2048]{1,0:T(1,128)S(1)} %bitcast.8, s32[1,2048]{1,0:T(1,128)S(1)} %bitcast.13, bf16[2048,512]{1,0:T(8,128)(2,1)S(1)} %get-tuple-element.18.hidden), custom_call_target="tpu_custom_call" | custom-call | flops 1073741824 | bytes 2113536 | tf_op jit(solution)/shard_map/pallas_call | solution.py:179
  17.1 0.0 copy-start.3
  17.1 0.0 copy-start.5
  17.2 0.1 collective-permute-start
  17.3 1.5 %shard_map.156 = bf16[256,512]{1,0:T(8,128)(2,1)S(1)} custom-call(s32[1,2048]{1,0:T(1,128)S(1)} %bitcast.9, s32[1,2048]{1,0:T(1,128)S(1)} %bitcast.14, bf16[2048,512]{1,0:T(8,128)(2,1)S(1)} %get-tuple-element.18.hidden, bf16[256,512]{1,0:T(8,128)(2,1)S(1)} %collective-permute-done.2.crossed), custom_call_target="tpu_custom_call" | custom-call | flops 536870912 | bytes 2375680 | tf_op jit(solution)/shard_map/pallas_call | solution.py:179
  18.8 0.1 collective-permute-start.3
  18.9 9.0 %collective-permute-done.3.far = bf16[256,512]{1,0:T(8,128)(2,1)S(1)} collective-permute-done((bf16[256,512]{1,0:T(8,128)(2,1)S(1)}, bf16[256,512]{1,0:T(8,128)(2,1)S(1)}, u32[]{:S(2)}, u32[]{:S(2)}) %collective-permute-start.3) | collective-permute-done | bytes 262176 | tf_op jit(solution)/shard_map/ppermute | solution.py:230
  27.9 0.4 shard_map.157
  28.4 0.1 collective-permute-start.5
  28.5 1.8 %collective-permute-start.4 = (bf16[64,512]{1,0:T(8,128)(2,1)S(1)}, bf16[64,512]{1,0:T(8,128)(2,1)S(1)}, u32[]{:S(2)}, u32[]{:S(2)}) collective-permute-start(bf16[64,512]{1,0:T(8,128)(2,1)S(1)} %get-tuple-element.26), channel_id=1, source_target_pairs={{0,15},{1,2},{2,1},{3,4},{4,3},{5,6},{6,5},{7,8},{8,7},{9,10},{10,... | collective-permute-start | bytes 196616 | tf_op jit(solution)/shard_map/ppermute | solution.py:224
  30.3 0.4 shard_map.158
  30.8 4.2 %collective-permute-done.4.across = bf16[64,512]{1,0:T(8,128)(2,1)S(1)} collective-permute-done((bf16[64,512]{1,0:T(8,128)(2,1)S(1)}, bf16[64,512]{1,0:T(8,128)(2,1)S(1)}, u32[]{:S(2)}, u32[]{:S(2)}) %collective-permute-start.4) | collective-permute-done | bytes 65568 | tf_op jit(solution)/shard_map/ppermute | solution.py:224
  34.9 2.1 %shard_map.159 = (bf16[256,512]{1,0:T(8,128)(2,1)S(1)}, bf16[64,512]{1,0:T(8,128)(2,1)S(1)}) custom-call(bf16[256,512]{1,0:T(8,128)(2,1)S(1)} %get-tuple-element.23.latent, bf16[256,512]{1,0:T(8,128)(2,1)S(1)} %get-tuple-element.24.source, f32[256,512]{1,0:T(8,128)S(1)} %get-tuple-element.25.target, bf16[64,512]{1,0:T(8,128)(2,1)S(1)} %collective-permute-done.4.across, ...), custom_call_target="tpu_custom_call" | custom-call | flops 1073741824 | bytes 3283200 | tf_op jit(solution)/shard_map/pallas_call | solution.py:179
  37.1 0.1 collective-permute-start.7
  37.2 1.8 %collective-permute-start.6 = (bf16[64,512]{1,0:T(8,128)(2,1)S(1)}, bf16[64,512]{1,0:T(8,128)(2,1)S(1)}, u32[]{:S(2)}, u32[]{:S(2)}) collective-permute-start(bf16[64,512]{1,0:T(8,128)(2,1)S(1)} %get-tuple-element.30), channel_id=1, source_target_pairs={{0,15},{1,2},{2,1},{3,4},{4,3},{5,6},{6,5},{7,8},{8,7},{9,10},{10,... | collective-permute-start | bytes 196616 | tf_op jit(solution)/shard_map/ppermute | solution.py:224
  39.0 0.4 shard_map.160
  39.5 4.1 %collective-permute-done.6.across = bf16[64,512]{1,0:T(8,128)(2,1)S(1)} collective-permute-done((bf16[64,512]{1,0:T(8,128)(2,1)S(1)}, bf16[64,512]{1,0:T(8,128)(2,1)S(1)}, u32[]{:S(2)}, u32[]{:S(2)}) %collective-permute-start.6) | collective-permute-done | bytes 65568 | tf_op jit(solution)/shard_map/ppermute | solution.py:224
  43.6 2.2 %shard_map.161.own = bf16[256,512]{1,0:T(8,128)(2,1)S(1)} custom-call(bf16[256,512]{1,0:T(8,128)(2,1)S(1)} %get-tuple-element.27.latent, bf16[256,512]{1,0:T(8,128)(2,1)S(1)} %get-tuple-element.28.source, f32[256,512]{1,0:T(8,128)S(1)} %get-tuple-element.29.target, bf16[64,512]{1,0:T(8,128)(2,1)S(1)} %collective-permute-done.6.across, ...), custom_call_target="tpu_custom_call" | custom-call | flops 1073741824 | bytes 3807232 | tf_op jit(solution)/shard_map/pallas_call | solution.py:179
  45.8 0.1 collective-permute-start.10
  45.9 0.1 collective-permute-start.8
  45.9 1.9 %collective-permute-start.9 = (bf16[256,512]{1,0:T(8,128)(2,1)S(1)}, bf16[256,512]{1,0:T(8,128)(2,1)S(1)}, u32[]{:S(2)}, u32[]{:S(2)}) collective-permute-start(bf16[256,512]{1,0:T(8,128)(2,1)S(1)} %shard_map.161.own), channel_id=1, source_target_pairs={{0,2},{1,15},{2,4},{3,1},{4,6},{5,3},{6,8},{7,5},{8,10},{9,7},{10,... | collective-permute-start | bytes 786440 | tf_op jit(solution)/shard_map/ppermute | solution.py:230
  47.9 12.2 %collective-permute-done.10.far = bf16[256,512]{1,0:T(8,128)(2,1)S(1)} collective-permute-done((bf16[256,512]{1,0:T(8,128)(2,1)S(1)}, bf16[256,512]{1,0:T(8,128)(2,1)S(1)}, u32[]{:S(2)}, u32[]{:S(2)}) %collective-permute-start.10) | collective-permute-done | bytes 262176 | tf_op jit(solution)/shard_map/ppermute | solution.py:227
  60.2 3.1 %shard_map.162.base = bf16[2048,512]{1,0:T(8,128)(2,1)S(1)} custom-call(s32[1,2048]{1,0:T(1,128)S(1)} %bitcast.10, s32[1,2048]{1,0:T(1,128)S(1)} %bitcast.15, bf16[2048,512]{1,0:T(8,128)(2,1)S(1)} %copy-done.13, bf16[512,512]{1,0:T(8,128)(2,1)S(1)} %copy-done.15, bf16[256,512]{1,0:T(8,128)(2,1)S(1)} %shard_map.161.own, ...), custom_call_target="tpu_custom_call" | custom-call | flops 2147483648 | bytes 3162112 | tf_op jit(solution)/shard_map/pallas_call | solution.py:179
  63.3 5.0 %shard_map.163 = bf16[2048,512]{1,0:T(8,128)(2,1)} custom-call(s32[1,2048]{1,0:T(1,128)S(1)} %bitcast.11, s32[1,2048]{1,0:T(1,128)S(1)} %bitcast.16, bf16[2048,512]{1,0:T(8,128)(2,1)S(1)} %shard_map.162.base, bf16[256,512]{1,0:T(8,128)(2,1)S(1)} %collective-permute-done.9.near, bf16[256,512]{1,0:T(8,128)(2,1)S(1)} %collective-permute-done.11.cross, ...), custom_call_target="tpu_custom_call" | custom-call | flops 2684354560 | bytes 3424256 | tf_op jit(solution)/shard_map/pallas_call | solution.py:179
  (41 shorter events, 0.1 us)
Async XLA Ops:
  0.0 0.7 %copy-start.7 = (s32[2048,1]{0,1:T(1,128)S(1)}, s32[2048,1]{0,1:T(1,128)}, u32[]{:S(2)}) copy-start(s32[2048,1]{0,1:T(1,128)} %param.18) | copy-start | bytes 24580
  0.7 0.7 %copy-start.9 = (s32[2048]{0:T(1024)S(1)}, s32[2048]{0:T(1024)}, u32[]{:S(2)}) copy-start(s32[2048]{0:T(1024)} %param.19) | copy-start | bytes 24580
  1.4 1.6 %copy-start.12 = (bf16[2048,512]{1,0:T(8,128)(2,1)S(1)}, bf16[2048,512]{1,0:T(8,128)(2,1)}, u32[]{:S(2)}) copy-start(bf16[2048,512]{1,0:T(8,128)(2,1)} %grid.3) | copy-start | bytes 6291460
  3.0 1.0 %copy-start.14 = (bf16[512,512]{1,0:T(8,128)(2,1)S(1)}, bf16[512,512]{1,0:T(8,128)(2,1)}, u32[]{:S(2)}) copy-start(bf16[512,512]{1,0:T(8,128)(2,1)} %w1.1) | copy-start | bytes 1572868
  4.0 0.7 copy-start.17
  8.8 8.5 %collective-permute-start.2 = (bf16[256,512]{1,0:T(8,128)(2,1)S(1)}, bf16[256,512]{1,0:T(8,128)(2,1)S(1)}, u32[]{:S(2)}, u32[]{:S(2)}) collective-permute-start(bf16[256,512]{1,0:T(8,128)(2,1)S(1)} %get-tuple-element.22), channel_id=1, source_target_pairs={{0,1},{1,0},{2,3},{3,2},{4,5},{5,4},{6,7},{7,6},{8,9},{9,8},{10,11... | collective-permute-start | bytes 786440 | tf_op jit(solution)/shard_map/ppermute | solution.py:221
  9.3 9.6 %collective-permute-start.1 = (bf16[256,512]{1,0:T(8,128)(2,1)S(1)}, bf16[256,512]{1,0:T(8,128)(2,1)S(1)}, u32[]{:S(2)}, u32[]{:S(2)}) collective-permute-start(bf16[256,512]{1,0:T(8,128)(2,1)S(1)} %get-tuple-element.21), channel_id=1, source_target_pairs={{0,14},{1,3},{2,0},{3,5},{4,2},{5,7},{6,4},{7,9},{8,6},{9,11},{10,... | collective-permute-start | bytes 786440 | tf_op jit(solution)/shard_map/ppermute | solution.py:227
  17.1 10.8 %copy-start.3 = (bf16[512,512]{1,0:T(8,128)(2,1)S(1)}, bf16[512,512]{1,0:T(8,128)(2,1)}, u32[]{:S(2)}) copy-start(bf16[512,512]{1,0:T(8,128)(2,1)} %w2.1) | copy-start | bytes 1572868
  17.1 10.8 %copy-start.5 = (bf16[256,512]{1,0:T(8,128)(2,1)S(1)}, bf16[256,512]{1,0:T(8,128)(2,1)}, u32[]{:S(2)}) copy-start(bf16[256,512]{1,0:T(8,128)(2,1)} %mesh.1) | copy-start | bytes 786436
  17.1 10.8 %copy-start.11 = (s32[64]{0:T(128)S(1)}, s32[64]{0:T(128)}, u32[]{:S(2)}) copy-start(s32[64]{0:T(128)} %param.20) | copy-start | bytes 772
  17.2 13.1 %copy-start.18 = (f32[2,512]{1,0:T(2,128)S(1)}, f32[2,512]{1,0:T(2,128)}, u32[]{:S(2)}) copy-start(f32[2,512]{1,0:T(2,128)} %param.27) | copy-start | bytes 12292
  17.2 13.1 %copy-start = (bf16[2,512,512]{2,1,0:T(8,128)(2,1)S(1)}, bf16[2,512,512]{2,1,0:T(8,128)(2,1)}, u32[]{:S(2)}) copy-start(bf16[2,512,512]{2,1,0:T(8,128)(2,1)} %w_src.7) | copy-start | bytes 3145732
  17.2 13.1 %copy-start.1 = (bf16[2,512,512]{2,1,0:T(8,128)(2,1)S(1)}, bf16[2,512,512]{2,1,0:T(8,128)(2,1)}, u32[]{:S(2)}) copy-start(bf16[2,512,512]{2,1,0:T(8,128)(2,1)} %w_dst.3) | copy-start | bytes 3145732
  17.2 1.7 %collective-permute-start = (bf16[256,512]{1,0:T(8,128)(2,1)S(1)}, bf16[256,512]{1,0:T(8,128)(2,1)S(1)}, u32[]{:S(2)}, u32[]{:S(2)}) collective-permute-start(bf16[256,512]{1,0:T(8,128)(2,1)S(1)} %get-tuple-element.20), channel_id=1, source_target_pairs={{0,1},{1,0},{2,3},{3,2},{4,5},{5,4},{6,7},{7,6},{8,9},{9,8},{10,11... | collective-permute-start | bytes 786440 | tf_op jit(solution)/shard_map/ppermute | solution.py:221
  18.8 9.1 %collective-permute-start.3 = (bf16[256,512]{1,0:T(8,128)(2,1)S(1)}, bf16[256,512]{1,0:T(8,128)(2,1)S(1)}, u32[]{:S(2)}, u32[]{:S(2)}) collective-permute-start(bf16[256,512]{1,0:T(8,128)(2,1)S(1)} %shard_map.156), channel_id=1, source_target_pairs={{0,2},{1,15},{2,4},{3,1},{4,6},{5,3},{6,8},{7,5},{8,10},{9,7},{10,... | collective-permute-start | bytes 786440 | tf_op jit(solution)/shard_map/ppermute | solution.py:230
  27.9 7.0 %copy-start.2 = (bf16[2,512,512]{2,1,0:T(8,128)(2,1)S(1)}, bf16[2,512,512]{2,1,0:T(8,128)(2,1)}, u32[]{:S(2)}) copy-start(bf16[2,512,512]{2,1,0:T(8,128)(2,1)} %w_out.4) | copy-start | bytes 3145732
  27.9 7.0 %copy-start.6 = (s32[256,6]{0,1:T(8,128)S(1)}, s32[256,6]{0,1:T(8,128)}, u32[]{:S(2)}) copy-start(s32[256,6]{0,1:T(8,128)} %param.21) | copy-start | bytes 18436
  28.4 2.4 %collective-permute-start.5 = (bf16[64,512]{1,0:T(8,128)(2,1)S(1)}, bf16[64,512]{1,0:T(8,128)(2,1)S(1)}, u32[]{:S(2)}, u32[]{:S(2)}) collective-permute-start(bf16[64,512]{1,0:T(8,128)(2,1)S(1)} %get-tuple-element.26), channel_id=1, source_target_pairs={{0,1},{1,0},{2,3},{3,2},{4,5},{5,4},{6,7},{7,6},{8,9},{9,8},{10,11... | collective-permute-start | bytes 196616 | tf_op jit(solution)/shard_map/ppermute | solution.py:221
  28.5 6.5 %collective-permute-start.4 = (bf16[64,512]{1,0:T(8,128)(2,1)S(1)}, bf16[64,512]{1,0:T(8,128)(2,1)S(1)}, u32[]{:S(2)}, u32[]{:S(2)}) collective-permute-start(bf16[64,512]{1,0:T(8,128)(2,1)S(1)} %get-tuple-element.26), channel_id=1, source_target_pairs={{0,15},{1,2},{2,1},{3,4},{4,3},{5,6},{6,5},{7,8},{8,7},{9,10},{10,... | collective-permute-start | bytes 196616 | tf_op jit(solution)/shard_map/ppermute | solution.py:224
  37.1 6.5 %copy-start.4 = (bf16[512,512]{1,0:T(8,128)(2,1)S(1)}, bf16[512,512]{1,0:T(8,128)(2,1)}, u32[]{:S(2)}) copy-start(bf16[512,512]{1,0:T(8,128)(2,1)} %w_next.1) | copy-start | bytes 1572868
  37.1 2.4 %collective-permute-start.7 = (bf16[64,512]{1,0:T(8,128)(2,1)S(1)}, bf16[64,512]{1,0:T(8,128)(2,1)S(1)}, u32[]{:S(2)}, u32[]{:S(2)}) collective-permute-start(bf16[64,512]{1,0:T(8,128)(2,1)S(1)} %get-tuple-element.30), channel_id=1, source_target_pairs={{0,1},{1,0},{2,3},{3,2},{4,5},{5,4},{6,7},{7,6},{8,9},{9,8},{10,11... | collective-permute-start | bytes 196616 | tf_op jit(solution)/shard_map/ppermute | solution.py:221
  37.2 6.5 %collective-permute-start.6 = (bf16[64,512]{1,0:T(8,128)(2,1)S(1)}, bf16[64,512]{1,0:T(8,128)(2,1)S(1)}, u32[]{:S(2)}, u32[]{:S(2)}) collective-permute-start(bf16[64,512]{1,0:T(8,128)(2,1)S(1)} %get-tuple-element.30), channel_id=1, source_target_pairs={{0,15},{1,2},{2,1},{3,4},{4,3},{5,6},{6,5},{7,8},{8,7},{9,10},{10,... | collective-permute-start | bytes 196616 | tf_op jit(solution)/shard_map/ppermute | solution.py:224
  39.4 20.7 %copy-start.8 = (s32[2048,1]{0,1:T(1,128)S(1)}, s32[2048,1]{0,1:T(1,128)}, u32[]{:S(2)}) copy-start(s32[2048,1]{0,1:T(1,128)} %param.18) | copy-start | bytes 24580
  39.4 20.7 %copy-start.10 = (s32[2048]{0:T(1024)S(1)}, s32[2048]{0:T(1024)}, u32[]{:S(2)}) copy-start(s32[2048]{0:T(1024)} %param.19) | copy-start | bytes 24580
  39.4 20.7 %copy-start.13 = (bf16[2048,512]{1,0:T(8,128)(2,1)S(1)}, bf16[2048,512]{1,0:T(8,128)(2,1)}, u32[]{:S(2)}) copy-start(bf16[2048,512]{1,0:T(8,128)(2,1)} %grid.3) | copy-start | bytes 6291460
  39.5 20.7 %copy-start.15 = (bf16[512,512]{1,0:T(8,128)(2,1)S(1)}, bf16[512,512]{1,0:T(8,128)(2,1)}, u32[]{:S(2)}) copy-start(bf16[512,512]{1,0:T(8,128)(2,1)} %w_grid.1) | copy-start | bytes 1572868
  45.8 17.6 %copy-start.16 = (bf16[512,512]{1,0:T(8,128)(2,1)S(1)}, bf16[512,512]{1,0:T(8,128)(2,1)}, u32[]{:S(2)}) copy-start(bf16[512,512]{1,0:T(8,128)(2,1)} %w_out.5) | copy-start | bytes 1572868
  45.8 14.3 %collective-permute-start.10 = (bf16[256,512]{1,0:T(8,128)(2,1)S(1)}, bf16[256,512]{1,0:T(8,128)(2,1)S(1)}, u32[]{:S(2)}, u32[]{:S(2)}) collective-permute-start(bf16[256,512]{1,0:T(8,128)(2,1)S(1)} %shard_map.161.own), channel_id=1, source_target_pairs={{0,14},{1,3},{2,0},{3,5},{4,2},{5,7},{6,4},{7,9},{8,6},{9,11},{10,... | collective-permute-start | bytes 786440 | tf_op jit(solution)/shard_map/ppermute | solution.py:227
  45.9 14.3 %collective-permute-start.8 = (bf16[256,512]{1,0:T(8,128)(2,1)S(1)}, bf16[256,512]{1,0:T(8,128)(2,1)S(1)}, u32[]{:S(2)}, u32[]{:S(2)}) collective-permute-start(bf16[256,512]{1,0:T(8,128)(2,1)S(1)} %shard_map.161.own), channel_id=1, source_target_pairs={{0,1},{1,0},{2,3},{3,2},{4,5},{5,4},{6,7},{7,6},{8,9},{9,8},{10,11... | collective-permute-start | bytes 786440 | tf_op jit(solution)/shard_map/ppermute | solution.py:221
  45.9 17.4 %collective-permute-start.9 = (bf16[256,512]{1,0:T(8,128)(2,1)S(1)}, bf16[256,512]{1,0:T(8,128)(2,1)S(1)}, u32[]{:S(2)}, u32[]{:S(2)}) collective-permute-start(bf16[256,512]{1,0:T(8,128)(2,1)S(1)} %shard_map.161.own), channel_id=1, source_target_pairs={{0,2},{1,15},{2,4},{3,1},{4,6},{5,3},{6,8},{7,5},{8,10},{9,7},{10,... | collective-permute-start | bytes 786440 | tf_op jit(solution)/shard_map/ppermute | solution.py:230
  60.1 3.2 %collective-permute-start.11 = (bf16[256,512]{1,0:T(8,128)(2,1)S(1)}, bf16[256,512]{1,0:T(8,128)(2,1)S(1)}, u32[]{:S(2)}, u32[]{:S(2)}) collective-permute-start(bf16[256,512]{1,0:T(8,128)(2,1)S(1)} %collective-permute-done.10.far), channel_id=1, source_target_pairs={{0,1},{1,0},{2,3},{3,2},{4,5},{5,4},{6,7},{7,6},{8,9},{9,8},{10,11... | collective-permute-start | bytes 786440 | tf_op jit(solution)/shard_map/ppermute | solution.py:221

commit v2 on v0

v2 whole, which is shorter than its diff:
```python
import functools

import jax
import jax.numpy as jnp
from jax import lax
from jax.experimental import pallas as pl
from jax.experimental.pallas import tpu as pltpu
from jax.sharding import PartitionSpec as P

L = 2
AXES = ("dom", "feat")
F32, BF16 = jnp.float32, jnp.bfloat16
MIB = 1 << 20
BLOCK = 512


def silu(x):
    half = 0.5 * x
    return half + half * jnp.tanh(half)


def dot(a, b):
    return jnp.dot(a, b, preferred_element_type=F32)


def slot_codes(owner, node, parts, mesh_rows):
    core = lax.axis_index("feat")
    me = lax.axis_index("dom") * 2 + core
    slot = (owner - me) * (1 - 2 * core) + 2
    slot = jnp.where(slot < 0, slot + parts, slot)
    slot = jnp.where(slot >= parts, slot - parts, slot)
    return slot * mesh_rows + node


def one_hot_down(code, first, rows):
    at = lax.broadcasted_iota(jnp.int32, (rows, code.shape[1]), 0)
    return jnp.where(at == code - first, 1.0, 0.0).astype(BF16)


def one_hot_across(row, width):
    n = row.shape[1]
    row = row.astype(F32)
    made = []
    for i in range(0, n, 128):
        cols = jnp.broadcast_to(row[:, i : i + 128], (128, 128)).T
        at = lax.broadcasted_iota(jnp.int32, cols.shape, 1).astype(F32)
        made.append(
            jnp.concatenate(
                [jnp.where(cols == at + float(j), 1.0, 0.0).astype(BF16) for j in range(0, width, 128)],
                axis=1,
            )
        )
    return jnp.concatenate(made, axis=0)


def encode_kernel(parts, owner, node, grid, w1, bias, hidden, near, cross, code, owner_v, node_v, grid_v, w1_v, bias_v, sems):
    small = [(owner, owner_v), (node, node_v), (w1, w1_v), (bias, bias_v)]
    copies = [pltpu.make_async_copy(a, b, sems.at[i]) for i, (a, b) in enumerate(small)]
    starts = range(0, grid.shape[0], BLOCK)
    blocks = [
        pltpu.make_async_copy(grid.at[pl.ds(r, BLOCK)], grid_v.at[pl.ds(r, BLOCK)], sems.at[4 + i])
        for i, r in enumerate(starts)
    ]
    for copy in copies + blocks:
        copy.start()
    for copy in copies:
        copy.wait()
    mesh_rows = near.shape[0]
    code[...] = slot_codes(owner_v[...], node_v[...], parts, mesh_rows)
    for r, copy in zip(starts, blocks):
        copy.wait()
        hidden[r : r + BLOCK] = silu(dot(grid_v[r : r + BLOCK], w1_v[...]) + bias_v[...]).astype(BF16)
    cross[...] = dot(one_hot_down(code[...], mesh_rows, mesh_rows), hidden[...]).astype(BF16)
    near[...] = dot(one_hot_down(code[...], 0, mesh_rows), hidden[...]).astype(BF16)


def far_kernel(code, hidden, crossed, far):
    rows = far.shape[0]
    far[...] = (dot(one_hot_down(code[...], 4 * rows, rows), hidden[...]) + crossed[...].astype(F32)).astype(BF16)


def chip_kernel(after, code, hidden, own, sibling):
    del after
    rows = own.shape[0]
    sibling[...] = dot(one_hot_down(code[...], 3 * rows, rows), hidden[...]).astype(BF16)
    own[...] = dot(one_hot_down(code[...], 2 * rows, rows), hidden[...])


def prepare_kernel(after, code, edges, halo_index, fetch, gather, gather_halo, pick):
    del after
    width = fetch.shape[1]
    for r in range(0, fetch.shape[0], BLOCK):
        fetch[r : r + BLOCK] = one_hot_across(code[:, r : r + BLOCK], width)
    n = edges.shape[1]
    own = gather.shape[1]
    for k in range(edges.shape[0]):
        one_hot = one_hot_across(edges[k : k + 1, :], own + gather_halo.shape[1])
        gather[k * n : (k + 1) * n] = one_hot[:, :own]
        gather_halo[k * n : (k + 1) * n] = one_hot[:, own:]
    pick[...] = one_hot_down(halo_index[...], 0, n)


def picked(pick, rows):
    return lax.dot_general(pick, rows, (((0,), (0,)), ((), ())), preferred_element_type=F32).astype(BF16)


def latent_kernel(mesh, own, sibling, near, far, w2, pick, latent, halo):
    sums = own[...] + sibling[...].astype(F32) + near[...].astype(F32) + far[...].astype(F32)
    rows = (mesh[...].astype(F32) + dot(sums.astype(BF16), w2[...])).astype(BF16)
    latent[...] = rows
    halo[...] = picked(pick[...], rows)


def project_kernel(layer, latent, w_src, w_dst, bias, gather, before):
    n = latent.shape[0]
    source = dot(latent[...], w_src[layer]).astype(BF16)
    target = dot(latent[...], w_dst[layer]) + bias[layer : layer + 1]
    for k in range(gather.shape[0] // n):
        before[k * n : (k + 1) * n] = dot(gather[k * n : (k + 1) * n], source) + target


def layer_kernel(layer, latent, before, across, beside, gather_halo, w_src, w_out, following, *outs):
    first = lax.axis_index("feat") == 0
    down = jnp.where(first, across[...], beside[...])
    up = jnp.where(first, beside[...], across[...])
    table = dot(jnp.concatenate([down, up], axis=0), w_src[layer]).astype(BF16)
    n = latent.shape[0]
    total = None
    for k in range(before.shape[0] // n):
        spot = slice(k * n, (k + 1) * n)
        message = silu(dot(gather_halo[spot], table) + before[spot]).astype(BF16).astype(F32)
        total = message if total is None else total + message
    rows = (latent[...].astype(F32) + dot(total.astype(BF16), w_out[layer])).astype(BF16)
    if layer == L - 1:
        outs[0][...] = dot(rows, following[...]).astype(BF16)
    else:
        outs[0][...] = rows
        outs[1][...] = picked(following[...], rows)


def base_kernel(grid, w_grid, fetch, own, sibling, base, stacked):
    width, rows = w_grid.shape[0], own.shape[0]
    stacked[:rows] = own[...]
    stacked[rows:] = sibling[...]
    for r in range(0, grid.shape[0], BLOCK):
        spot = slice(r, r + BLOCK)
        base[spot] = dot(grid[spot], w_grid[...]) + dot(fetch[spot, 2 * rows : 4 * rows], stacked[...])


def add_kernel(slot, fetch, base, table, out, *passed):
    rows = table.shape[0]
    for r in range(0, base.shape[0], BLOCK):
        spot = slice(r, r + BLOCK)
        out[spot] = base[spot] + dot(fetch[spot, slot * rows : (slot + 1) * rows], table[...])
    if passed:
        passed[0][...] = table[...]


def decode_kernel(slot, fetch, base, table, w_out, out, out_v, sems):
    rows = table.shape[0]
    copies = []
    for i, r in enumerate(range(0, base.shape[0], BLOCK)):
        spot = slice(r, r + BLOCK)
        hidden = silu(base[spot] + dot(fetch[spot, slot * rows : (slot + 1) * rows], table[...])).astype(BF16)
        out_v[spot] = dot(hidden, w_out[...]).astype(BF16)
        copies.append(pltpu.make_async_copy(out_v.at[pl.ds(r, BLOCK)], out.at[pl.ds(r, BLOCK)], sems.at[i]))
        copies[-1].start()
    for copy in copies:
        copy.wait()


VM = pltpu.VMEM


def call(kernel, ins, outs, flops, scratch=(), vmem=24, spaces=None, out_space=VM):
    moved = sum(a.size * a.dtype.itemsize for a in ins)
    spaces = spaces or [VM] * len(ins)
    ins = [pltpu.with_memory_space_constraint(a, s) if s is pltpu.HBM else a for a, s in zip(ins, spaces)]
    return pl.pallas_call(
        kernel,
        in_specs=[pl.BlockSpec(memory_space=space) for space in spaces],
        out_specs=[pl.BlockSpec(memory_space=out_space) for _ in outs],
        out_shape=[jax.ShapeDtypeStruct(shape, dtype) for shape, dtype in outs],
        scratch_shapes=list(scratch),
        compiler_params=pltpu.CompilerParams(vmem_limit_bytes=vmem * MIB),
        cost_estimate=pl.CostEstimate(flops=flops, bytes_accessed=moved if flops > 1 else 1, transcendentals=0),
    )(*ins)


def body(
    grid,
    mesh_feat,
    owner,
    node,
    halo_index,
    edge_src,
    w_enc1,
    enc_bias,
    w_enc2,
    proc_src,
    proc_dst,
    proc_bias,
    proc_out,
    dec_grid,
    dec_mesh,
    dec_out,
):
    parts = lax.axis_size(AXES)
    rows, width = grid.shape
    mesh_rows = mesh_feat.shape[0]
    border = halo_index.shape[0]
    degree = edge_src.shape[1]
    blocks = rows // BLOCK
    part = functools.partial

    def sided(step):
        return [(i, (i + step) % parts if i % 2 == 0 else (i - step) % parts) for i in range(parts)]

    def swap(value):
        return lax.ppermute(value, AXES, sided(1))

    def to_across(value):
        return lax.ppermute(value, AXES, sided(-1))

    def to_near(value):
        return lax.ppermute(value, AXES, sided(-2))

    def to_far(value):
        return lax.ppermute(value, AXES, sided(2))

    table = ((mesh_rows, width), BF16)
    unit = 2 * rows * width
    hidden, near, cross, code = call(
        part(encode_kernel, parts),
        [owner.reshape(1, rows), node.reshape(1, rows), grid, w_enc1, enc_bias.reshape(1, width)],
        [((rows, width), BF16), table, table, ((1, rows), jnp.int32)],
        unit * (width + 2 * mesh_rows),
        [
            VM((1, rows), jnp.int32),
            VM((1, rows), jnp.int32),
            VM((rows, width), BF16),
            VM((width, width), BF16),
            VM((1, width), F32),
            pltpu.SemaphoreType.DMA((4 + blocks,)),
        ],
        spaces=[pltpu.HBM] * 5,
    )
    crossed = swap(cross)
    near = to_near(near)
    (sent,) = call(far_kernel, [code, hidden, crossed], [table], unit * mesh_rows)
    far = to_far(sent)
    own, sibling = call(
        chip_kernel,
        [sent, code, hidden],
        [((mesh_rows, width), F32), table],
        unit * 2 * mesh_rows,
        spaces=[pl.ANY, VM, VM],
    )
    fetch, gather, gather_halo, pick = call(
        prepare_kernel,
        [sibling, code, edge_src.T, halo_index.reshape(1, border)],
        [
            ((rows, 5 * mesh_rows), BF16),
            ((degree * mesh_rows, mesh_rows), BF16),
            ((degree * mesh_rows, 2 * border), BF16),
            ((mesh_rows, border), BF16),
        ],
        unit * 2 * mesh_rows,
        spaces=[pl.ANY, VM, VM, VM],
    )
    sibling = swap(sibling)
    latent, halo = call(
        latent_kernel,
        [mesh_feat, own, sibling, near, far, w_enc2, pick],
        [table, ((border, width), BF16)],
        2 * mesh_rows * width * width,
    )
    for layer in range(L):
        last = layer == L - 1
        across = to_across(halo)
        beside = swap(halo)
        (before,) = call(
            part(project_kernel, layer),
            [latent, proc_src, proc_dst, proc_bias, gather],
            [((degree * mesh_rows, width), F32)],
            4 * mesh_rows * width * width + 2 * degree * mesh_rows * mesh_rows * width,
        )
        made = call(
            part(layer_kernel, layer),
            [latent, before, across, beside, gather_halo, proc_src, proc_out, dec_mesh if last else pick],
            [table] if last else [table, ((border, width), BF16)],
            2 * mesh_rows * width * (degree * 2 * border + 2 * width),
        )
        if last:
            (projected,) = made
        else:
            latent, halo = made
    far = to_near(projected)
    sibling = swap(projected)
    near = to_far(projected)
    f32_rows = ((rows, width), F32)
    (base,) = call(
        base_kernel,
        [grid, dec_grid, fetch, projected, sibling],
        [f32_rows],
        1,
        [VM((2 * mesh_rows, width), BF16)],
    )
    base, passed = call(part(add_kernel, 4), [fetch, base, far], [f32_rows, table], 1)
    cross = swap(passed)
    (base,) = call(part(add_kernel, 0), [fetch, base, near], [f32_rows], 1)
    (out,) = call(
        part(decode_kernel, 1),
        [fetch, base, cross, dec_out],
        [((rows, width), BF16)],
        unit * (width + mesh_rows),
        [VM((rows, width), BF16), pltpu.SemaphoreType.DMA((blocks,))],
        out_space=pltpu.HBM,
    )
    return out


def solution(mesh):
    rows = P(("group", "dom", "feat"), None)
    flat = P(("group", "dom", "feat"))
    return jax.shard_map(
        body,
        mesh=mesh,
        in_specs=(rows, rows, rows, flat, flat, rows) + (P(),) * 10,
        out_specs=rows,
        check_vma=False,
    )
```

time: 151 us -> 58.9 us (0.39); the launches traced: 148 us -> 58.7 us
  local copies, waits for them, and re-layouts: 63.8 us -> 0.07 us
  matrix products: 27 us -> 0 us
  Pallas kernels: 0 us -> 19.9 us
  starting transfers between devices: 31.9 us -> 17.5 us
  other arithmetic: 14.1 us -> 0 us
  waiting for transfers between devices: 10.6 us -> 20.8 us
    gather x9 -> x0, local copies, waits for them, and re-layouts: 42.9 us -> none  [the longest x4 19.1 us: body(): source_proj[edge_src] + node_proj[:, None, :]]
    dot_general x10 -> x0, matrix products: 27 us -> none  [the longest x1 6.72 us: body(): jnp.dot(hidden_dec, dec_out, preferred_element_type=jnp.float32)]
    pallas_call x0 -> x13, Pallas kernels: none -> 19.9 us  [call(): pl.pallas_call(kernel, in_specs=[pl.BlockSpec(memory_space=space) for spa...]
    scatter x2 -> x0, local copies, waits for them, and re-layouts: 18.4 us -> none  [the longest x1 10.1 us: body(): jnp.zeros((dump + 1, width), jnp.bfloat16).at[slots].set(message)[:dump]]
    ppermute x16 -> x12, starting transfers between devices: 31.9 us -> 17.5 us  [the longest x2 9.49 us: to_near(): return lax.ppermute(value, AXES, sided(-2))]
    ppermute x16 -> x12, waiting for transfers between devices: 10.6 us -> 20.8 us  [the longest x2 8.65 us: to_near(): return lax.ppermute(value, AXES, sided(-2))]
    reduce_sum x3 -> x0, other arithmetic: 10.1 us -> none  [the longest x2 9.29 us: body(): jnp.sum(edge_msg.astype(jnp.float32), axis=1).astype(jnp.bfloat16)]
    slice x5 -> x0, local copies, waits for them, and re-layouts: 2.14 us -> none  [the longest x1 0.99 us: return_rows(): backs.append(from_behind(outgoing[place], ('dom', 'feat'), -step))]
  transfers between devices with their start and end apart: 16 -> 12, of which waited for: 2 -> 6; matrix products, arithmetic and copies ran while one was open for 23% -> 0% of each run, Pallas kernels for 0% -> 15%
where the time goes in v2:
time: 58.9 us; the launch traced here: 58.7 us
  waiting for transfers between devices  20.8 us (35%)
  Pallas kernels  19.9 us (34%)
  starting transfers between devices  17.5 us (30%)
    pallas_call x13, Pallas kernels, call(): pl.pallas_call(kernel, in_specs=[pl.BlockSpec(memory_space=space) for spa...  19.9 us
    ppermute x2, starting transfers between devices, to_near(): return lax.ppermute(value, AXES, sided(-2))  9.49 us
    ppermute x2, waiting for transfers between devices, to_near(): return lax.ppermute(value, AXES, sided(-2))  8.65 us
    ppermute x2, waiting for transfers between devices, to_far(): return lax.ppermute(value, AXES, sided(2))  7.33 us
    ppermute x2, starting transfers between devices, to_across(): return lax.ppermute(value, AXES, sided(-1))  7.12 us
    ppermute x2, waiting for transfers between devices, to_across(): return lax.ppermute(value, AXES, sided(-1))  4.01 us
  transfers between devices with their start and end apart: 12, of which 6 were waited for; matrix products, arithmetic and copies ran while one was open for 0% of the time, Pallas kernels for 15%

profile of v2, /device:TPU:0, one launch (start us, length us, event | category | flops | bytes accessed | tf_op | source)
XLA Modules:
  0.0 58.7 jit_solution(8816639345423107875)
XLA Ops:
  0.0 4.6 %shard_map.154 = (bf16[2048,512]{1,0:T(8,128)(2,1)S(1)}, bf16[256,512]{1,0:T(8,128)(2,1)S(1)}, bf16[256,512]{1,0:T(8,128)(2,1)S(1)}, s32[1,2048]{1,0:T(1,128)S(1)}) custom-call(s32[1,2048]{1,0:T(1,128)} %bitcast.7, s32[1,2048]{1,0:T(1,128)} %bitcast.8, bf16[2048,512]{1,0:T(8,128)(2,1)} %grid.3, bf16[512,512]{1,0:T(8,128)(2,1)} %w1.1, f32[1,512]{1,0:T(1,128)} %bitcast.9), custom_call_target="tpu_custom_call" | custom-call | flops 2147483648 | bytes 2639872 | tf_op jit(solution)/shard_map/pallas_call | solution.py:179
  4.6 0.5 collective-permute-start
  5.1 5.6 %collective-permute-start.2 = (bf16[256,512]{1,0:T(8,128)(2,1)S(1)}, bf16[256,512]{1,0:T(8,128)(2,1)S(1)}, u32[]{:S(2)}, u32[]{:S(2)}) collective-permute-start(bf16[256,512]{1,0:T(8,128)(2,1)S(1)} %get-tuple-element.27), channel_id=1, source_target_pairs={{0,14},{1,3},{2,0},{3,5},{4,2},{5,7},{6,4},{7,9},{8,6},{9,11},{10,... | collective-permute-start | bytes 786440 | tf_op jit(solution)/shard_map/ppermute | solution.py:226
  10.7 0.7 %shard_map.155.after = bf16[256,512]{1,0:T(8,128)(2,1)S(1)} custom-call(s32[1,2048]{1,0:T(1,128)S(1)} %get-tuple-element.21.code, bf16[2048,512]{1,0:T(8,128)(2,1)S(1)} %get-tuple-element.22.hidden, bf16[256,512]{1,0:T(8,128)(2,1)S(1)} %collective-permute-done.crossed), custom_call_target="tpu_custom_call" | custom-call | flops 536870912 | bytes 2367488 | tf_op jit(solution)/shard_map/pallas_call | solution.py:179
  11.5 1.2 %shard_map.156 = (f32[256,512]{1,0:T(8,128)S(1)}, bf16[256,512]{1,0:T(8,128)(2,1)S(1)}) custom-call(bf16[256,512]{1,0:T(8,128)(2,1)S(1)} %shard_map.155.after, s32[1,2048]{1,0:T(1,128)S(1)} %get-tuple-element.21.code, bf16[2048,512]{1,0:T(8,128)(2,1)S(1)} %get-tuple-element.22.hidden), custom_call_target="tpu_custom_call" | custom-call | flops 1073741824 | bytes 2367488 | tf_op jit(solution)/shard_map/pallas_call | solution.py:179
  12.7 0.0 copy-start
  12.7 0.0 copy-start.1
  12.7 0.1 collective-permute-start.1
  12.8 0.1 collective-permute-start.3
  12.9 1.1 %shard_map.157 = (bf16[2048,1280]{1,0:T(8,128)(2,1)S(1)}, bf16[1536,256]{1,0:T(8,128)(2,1)S(1)}, bf16[1536,128]{1,0:T(8,128)(2,1)S(1)}, bf16[256,64]{1,0:T(8,128)(2,1)S(1)}) custom-call(bf16[256,512]{1,0:T(8,128)(2,1)S(1)} %get-tuple-element.24.after, s32[1,2048]{1,0:T(1,128)S(1)} %get-tuple-element.21.code, s32[6,256]{1,0:T(8,128)S(1)} %bitcast.5, ...), custom_call_target="tpu_custom_call" | custom-call | flops 1073741824 | bytes 276736 | tf_op jit(solution)/shard_map/pallas_call | solution.py:179
  14.1 0.6 collective-permute-done.2.near
  14.6 7.3 %collective-permute-done.3.far = bf16[256,512]{1,0:T(8,128)(2,1)S(1)} collective-permute-done((bf16[256,512]{1,0:T(8,128)(2,1)S(1)}, bf16[256,512]{1,0:T(8,128)(2,1)S(1)}, u32[]{:S(2)}, u32[]{:S(2)}) %collective-permute-start.3) | collective-permute-done | bytes 262176 | tf_op jit(solution)/shard_map/ppermute | solution.py:229
  21.9 0.4 shard_map.158
  22.4 0.1 collective-permute-start.5
  22.5 3.6 %collective-permute-start.4 = (bf16[64,512]{1,0:T(8,128)(2,1)S(1)}, bf16[64,512]{1,0:T(8,128)(2,1)S(1)}, u32[]{:S(2)}, u32[]{:S(2)}) collective-permute-start(bf16[64,512]{1,0:T(8,128)(2,1)S(1)} %get-tuple-element.31), channel_id=1, source_target_pairs={{0,15},{1,2},{2,1},{3,4},{4,3},{5,6},{6,5},{7,8},{8,7},{9,10},{10,... | collective-permute-start | bytes 196616 | tf_op jit(solution)/shard_map/ppermute | solution.py:223
  26.1 0.9 %shard_map.159.before = f32[1536,512]{1,0:T(8,128)S(1)} custom-call(bf16[256,512]{1,0:T(8,128)(2,1)S(1)} %get-tuple-element.29.latent, bf16[2,512,512]{2,1,0:T(8,128)(2,1)S(1)} %copy-done, bf16[2,512,512]{2,1,0:T(8,128)(2,1)S(1)} %copy-done.1, f32[2,512]{1,0:T(2,128)S(1)} %copy-done.9, bf16[1536,256]{1,0:T(8,128)(2,1)S(1)} %get-tuple-element.30.gather), custom_call_target="tpu_custom_call" | custom-call | flops 671088640 | bytes 3149824 | tf_op jit(solution)/shard_map/pallas_call | solution.py:179
  26.9 2.0 %collective-permute-done.4.across = bf16[64,512]{1,0:T(8,128)(2,1)S(1)} collective-permute-done((bf16[64,512]{1,0:T(8,128)(2,1)S(1)}, bf16[64,512]{1,0:T(8,128)(2,1)S(1)}, u32[]{:S(2)}, u32[]{:S(2)}) %collective-permute-start.4) | collective-permute-done | bytes 65568 | tf_op jit(solution)/shard_map/ppermute | solution.py:223
  28.9 1.6 %shard_map.160 = (bf16[256,512]{1,0:T(8,128)(2,1)S(1)}, bf16[64,512]{1,0:T(8,128)(2,1)S(1)}) custom-call(bf16[256,512]{1,0:T(8,128)(2,1)S(1)} %get-tuple-element.29.latent, f32[1536,512]{1,0:T(8,128)S(1)} %shard_map.159.before, bf16[64,512]{1,0:T(8,128)(2,1)S(1)} %collective-permute-done.4.across, bf16[64,512]{1,0:T(8,128)(2,1)S(1)} %collective-permute-done.5.beside, ...), custom_call_target="tpu_custom_call" | custom-call | flops 469762048 | bytes 6062080 | tf_op jit(solution)/shard_map/pallas_call | solution.py:179
  30.6 0.1 collective-permute-start.7
  30.7 3.6 %collective-permute-start.6 = (bf16[64,512]{1,0:T(8,128)(2,1)S(1)}, bf16[64,512]{1,0:T(8,128)(2,1)S(1)}, u32[]{:S(2)}, u32[]{:S(2)}) collective-permute-start(bf16[64,512]{1,0:T(8,128)(2,1)S(1)} %get-tuple-element.34), channel_id=1, source_target_pairs={{0,15},{1,2},{2,1},{3,4},{4,3},{5,6},{6,5},{7,8},{8,7},{9,10},{10,... | collective-permute-start | bytes 196616 | tf_op jit(solution)/shard_map/ppermute | solution.py:223
  34.2 0.8 %shard_map.161.before = f32[1536,512]{1,0:T(8,128)S(1)} custom-call(bf16[256,512]{1,0:T(8,128)(2,1)S(1)} %get-tuple-element.33.latent, bf16[2,512,512]{2,1,0:T(8,128)(2,1)S(1)} %copy-done, bf16[2,512,512]{2,1,0:T(8,128)(2,1)S(1)} %copy-done.1, f32[2,512]{1,0:T(2,128)S(1)} %copy-done.9, bf16[1536,256]{1,0:T(8,128)(2,1)S(1)} %get-tuple-element.30.gather), custom_call_target="tpu_custom_call" | custom-call | flops 671088640 | bytes 3149824 | tf_op jit(solution)/shard_map/pallas_call | solution.py:179
  35.1 2.0 %collective-permute-done.6.across = bf16[64,512]{1,0:T(8,128)(2,1)S(1)} collective-permute-done((bf16[64,512]{1,0:T(8,128)(2,1)S(1)}, bf16[64,512]{1,0:T(8,128)(2,1)S(1)}, u32[]{:S(2)}, u32[]{:S(2)}) %collective-permute-start.6) | collective-permute-done | bytes 65568 | tf_op jit(solution)/shard_map/ppermute | solution.py:223
  37.1 1.7 %shard_map.162.own = bf16[256,512]{1,0:T(8,128)(2,1)S(1)} custom-call(bf16[256,512]{1,0:T(8,128)(2,1)S(1)} %get-tuple-element.33.latent, f32[1536,512]{1,0:T(8,128)S(1)} %shard_map.161.before, bf16[64,512]{1,0:T(8,128)(2,1)S(1)} %collective-permute-done.6.across, bf16[64,512]{1,0:T(8,128)(2,1)S(1)} %collective-permute-done.7.beside, ...), custom_call_target="tpu_custom_call" | custom-call | flops 469762048 | bytes 6553600 | tf_op jit(solution)/shard_map/pallas_call | solution.py:179
  38.8 0.1 collective-permute-start.8
  38.9 3.9 %collective-permute-start.9 = (bf16[256,512]{1,0:T(8,128)(2,1)S(1)}, bf16[256,512]{1,0:T(8,128)(2,1)S(1)}, u32[]{:S(2)}, u32[]{:S(2)}) collective-permute-start(bf16[256,512]{1,0:T(8,128)(2,1)S(1)} %shard_map.162.own), channel_id=1, source_target_pairs={{0,14},{1,3},{2,0},{3,5},{4,2},{5,7},{6,4},{7,9},{8,6},{9,11},{10,... | collective-permute-start | bytes 786440 | tf_op jit(solution)/shard_map/ppermute | solution.py:226
  42.8 2.3 %shard_map.163.base = f32[2048,512]{1,0:T(8,128)S(1)} custom-call(bf16[2048,512]{1,0:T(8,128)(2,1)S(1)} %copy-done.3, bf16[512,512]{1,0:T(8,128)(2,1)S(1)} %copy-done.4, bf16[2048,1280]{1,0:T(8,128)(2,1)S(1)} %get-tuple-element.25.fetch, bf16[256,512]{1,0:T(8,128)(2,1)S(1)} %shard_map.162.own, bf16[256,512]{1,0:T(8,128)(2,1)S(1)} %collective-permute-done.8.sibling), custom_call_target="tpu_custom_call" | custom-call | flops 1 | bytes 1 | tf_op jit(solution)/shard_map/pallas_call | solution.py:179
  45.1 8.1 %collective-permute-done.9.table = bf16[256,512]{1,0:T(8,128)(2,1)S(1)} collective-permute-done((bf16[256,512]{1,0:T(8,128)(2,1)S(1)}, bf16[256,512]{1,0:T(8,128)(2,1)S(1)}, u32[]{:S(2)}, u32[]{:S(2)}) %collective-permute-start.9) | collective-permute-done | bytes 262176 | tf_op jit(solution)/shard_map/ppermute | solution.py:226
  53.3 0.7 %shard_map.164 = (f32[2048,512]{1,0:T(8,128)S(1)}, bf16[256,512]{1,0:T(8,128)(2,1)S(1)}) custom-call(bf16[2048,1280]{1,0:T(8,128)(2,1)S(1)} %get-tuple-element.25.fetch, f32[2048,512]{1,0:T(8,128)S(1)} %shard_map.163.base, bf16[256,512]{1,0:T(8,128)(2,1)S(1)} %collective-permute-done.9.table), custom_call_target="tpu_custom_call" | custom-call | flops 1 | bytes 1 | tf_op jit(solution)/shard_map/pallas_call | solution.py:179
  54.0 0.1 collective-permute-start.11
  54.1 0.7 %shard_map.165.base = f32[2048,512]{1,0:T(8,128)S(1)} custom-call(bf16[2048,1280]{1,0:T(8,128)(2,1)S(1)} %get-tuple-element.25.fetch, f32[2048,512]{1,0:T(8,128)S(1)} %get-tuple-element.35.base, bf16[256,512]{1,0:T(8,128)(2,1)S(1)} %collective-permute-done.10.table), custom_call_target="tpu_custom_call" | custom-call | flops 1 | bytes 1 | tf_op jit(solution)/shard_map/pallas_call | solution.py:179
  54.8 0.8 %collective-permute-done.11.table = bf16[256,512]{1,0:T(8,128)(2,1)S(1)} collective-permute-done((bf16[256,512]{1,0:T(8,128)(2,1)S(1)}, bf16[256,512]{1,0:T(8,128)(2,1)S(1)}, u32[]{:S(2)}, u32[]{:S(2)}) %collective-permute-start.11) | collective-permute-done | bytes 262176 | tf_op jit(solution)/shard_map/ppermute | solution.py:220
  55.6 3.0 %shard_map.166 = bf16[2048,512]{1,0:T(8,128)(2,1)} custom-call(bf16[2048,1280]{1,0:T(8,128)(2,1)S(1)} %get-tuple-element.25.fetch, f32[2048,512]{1,0:T(8,128)S(1)} %shard_map.165.base, bf16[256,512]{1,0:T(8,128)(2,1)S(1)} %collective-permute-done.11.table, bf16[512,512]{1,0:T(8,128)(2,1)S(1)} %copy-done.5), custom_call_target="tpu_custom_call" | custom-call | flops 1610612736 | bytes 10223616 | tf_op jit(solution)/shard_map/pallas_call | solution.py:179
  (29 shorter events, 0.1 us)
Async XLA Ops:
  4.6 6.1 %collective-permute-start = (bf16[256,512]{1,0:T(8,128)(2,1)S(1)}, bf16[256,512]{1,0:T(8,128)(2,1)S(1)}, u32[]{:S(2)}, u32[]{:S(2)}) collective-permute-start(bf16[256,512]{1,0:T(8,128)(2,1)S(1)} %get-tuple-element.23), channel_id=1, source_target_pairs={{0,1},{1,0},{2,3},{3,2},{4,5},{5,4},{6,7},{7,6},{8,9},{9,8},{10,11... | collective-permute-start | bytes 786440 | tf_op jit(solution)/shard_map/ppermute | solution.py:220
  5.1 9.5 %collective-permute-start.2 = (bf16[256,512]{1,0:T(8,128)(2,1)S(1)}, bf16[256,512]{1,0:T(8,128)(2,1)S(1)}, u32[]{:S(2)}, u32[]{:S(2)}) collective-permute-start(bf16[256,512]{1,0:T(8,128)(2,1)S(1)} %get-tuple-element.27), channel_id=1, source_target_pairs={{0,14},{1,3},{2,0},{3,5},{4,2},{5,7},{6,4},{7,9},{8,6},{9,11},{10,... | collective-permute-start | bytes 786440 | tf_op jit(solution)/shard_map/ppermute | solution.py:226
  10.7 2.2 %copy-start.10 = (s32[256,6]{0,1:T(8,128)S(1)}, s32[256,6]{0,1:T(8,128)}, u32[]{:S(2)}) copy-start(s32[256,6]{0,1:T(8,128)} %param.21) | copy-start | bytes 18436
  10.7 2.2 %copy-start.11 = (s32[64]{0:T(128)S(1)}, s32[64]{0:T(128)}, u32[]{:S(2)}) copy-start(s32[64]{0:T(128)} %param.20) | copy-start | bytes 772
  11.4 10.5 %copy-start.6 = (bf16[512,512]{1,0:T(8,128)(2,1)S(1)}, bf16[512,512]{1,0:T(8,128)(2,1)}, u32[]{:S(2)}) copy-start(bf16[512,512]{1,0:T(8,128)(2,1)} %w2.1) | copy-start | bytes 1572868
  11.4 10.5 %copy-start.8 = (bf16[256,512]{1,0:T(8,128)(2,1)S(1)}, bf16[256,512]{1,0:T(8,128)(2,1)}, u32[]{:S(2)}) copy-start(bf16[256,512]{1,0:T(8,128)(2,1)} %mesh.1) | copy-start | bytes 786436
  12.7 13.3 %copy-start = (bf16[2,512,512]{2,1,0:T(8,128)(2,1)S(1)}, bf16[2,512,512]{2,1,0:T(8,128)(2,1)}, u32[]{:S(2)}) copy-start(bf16[2,512,512]{2,1,0:T(8,128)(2,1)} %w_src.7) | copy-start | bytes 3145732
  12.7 13.3 %copy-start.1 = (bf16[2,512,512]{2,1,0:T(8,128)(2,1)S(1)}, bf16[2,512,512]{2,1,0:T(8,128)(2,1)}, u32[]{:S(2)}) copy-start(bf16[2,512,512]{2,1,0:T(8,128)(2,1)} %w_dst.3) | copy-start | bytes 3145732
  12.7 13.3 %copy-start.9 = (f32[2,512]{1,0:T(2,128)S(1)}, f32[2,512]{1,0:T(2,128)}, u32[]{:S(2)}) copy-start(f32[2,512]{1,0:T(2,128)} %bias.3) | copy-start | bytes 12292
  12.7 1.9 %collective-permute-start.1 = (bf16[256,512]{1,0:T(8,128)(2,1)S(1)}, bf16[256,512]{1,0:T(8,128)(2,1)S(1)}, u32[]{:S(2)}, u32[]{:S(2)}) collective-permute-start(bf16[256,512]{1,0:T(8,128)(2,1)S(1)} %get-tuple-element.24.after), channel_id=1, source_target_pairs={{0,1},{1,0},{2,3},{3,2},{4,5},{5,4},{6,7},{7,6},{8,9},{9,8},{10,11... | collective-permute-start | bytes 786440 | tf_op jit(solution)/shard_map/ppermute | solution.py:220
  12.8 9.1 %collective-permute-start.3 = (bf16[256,512]{1,0:T(8,128)(2,1)S(1)}, bf16[256,512]{1,0:T(8,128)(2,1)S(1)}, u32[]{:S(2)}, u32[]{:S(2)}) collective-permute-start(bf16[256,512]{1,0:T(8,128)(2,1)S(1)} %shard_map.155.after), channel_id=1, source_target_pairs={{0,2},{1,15},{2,4},{3,1},{4,6},{5,3},{6,8},{7,5},{8,10},{9,7},{10,... | collective-permute-start | bytes 786440 | tf_op jit(solution)/shard_map/ppermute | solution.py:229
  22.4 4.5 %collective-permute-start.5 = (bf16[64,512]{1,0:T(8,128)(2,1)S(1)}, bf16[64,512]{1,0:T(8,128)(2,1)S(1)}, u32[]{:S(2)}, u32[]{:S(2)}) collective-permute-start(bf16[64,512]{1,0:T(8,128)(2,1)S(1)} %get-tuple-element.31), channel_id=1, source_target_pairs={{0,1},{1,0},{2,3},{3,2},{4,5},{5,4},{6,7},{7,6},{8,9},{9,8},{10,11... | collective-permute-start | bytes 196616 | tf_op jit(solution)/shard_map/ppermute | solution.py:220
  22.5 6.5 %collective-permute-start.4 = (bf16[64,512]{1,0:T(8,128)(2,1)S(1)}, bf16[64,512]{1,0:T(8,128)(2,1)S(1)}, u32[]{:S(2)}, u32[]{:S(2)}) collective-permute-start(bf16[64,512]{1,0:T(8,128)(2,1)S(1)} %get-tuple-element.31), channel_id=1, source_target_pairs={{0,15},{1,2},{2,1},{3,4},{4,3},{5,6},{6,5},{7,8},{8,7},{9,10},{10,... | collective-permute-start | bytes 196616 | tf_op jit(solution)/shard_map/ppermute | solution.py:223
  26.0 2.9 %copy-start.2 = (bf16[2,512,512]{2,1,0:T(8,128)(2,1)S(1)}, bf16[2,512,512]{2,1,0:T(8,128)(2,1)}, u32[]{:S(2)}) copy-start(bf16[2,512,512]{2,1,0:T(8,128)(2,1)} %w_out.4) | copy-start | bytes 3145732
  30.6 4.5 %collective-permute-start.7 = (bf16[64,512]{1,0:T(8,128)(2,1)S(1)}, bf16[64,512]{1,0:T(8,128)(2,1)S(1)}, u32[]{:S(2)}, u32[]{:S(2)}) collective-permute-start(bf16[64,512]{1,0:T(8,128)(2,1)S(1)} %get-tuple-element.34), channel_id=1, source_target_pairs={{0,1},{1,0},{2,3},{3,2},{4,5},{5,4},{6,7},{7,6},{8,9},{9,8},{10,11... | collective-permute-start | bytes 196616 | tf_op jit(solution)/shard_map/ppermute | solution.py:220
  30.7 6.5 %collective-permute-start.6 = (bf16[64,512]{1,0:T(8,128)(2,1)S(1)}, bf16[64,512]{1,0:T(8,128)(2,1)S(1)}, u32[]{:S(2)}, u32[]{:S(2)}) collective-permute-start(bf16[64,512]{1,0:T(8,128)(2,1)S(1)} %get-tuple-element.34), channel_id=1, source_target_pairs={{0,15},{1,2},{2,1},{3,4},{4,3},{5,6},{6,5},{7,8},{8,7},{9,10},{10,... | collective-permute-start | bytes 196616 | tf_op jit(solution)/shard_map/ppermute | solution.py:223
  34.2 2.9 %copy-start.7 = (bf16[512,512]{1,0:T(8,128)(2,1)S(1)}, bf16[512,512]{1,0:T(8,128)(2,1)}, u32[]{:S(2)}) copy-start(bf16[512,512]{1,0:T(8,128)(2,1)} %following.1) | copy-start | bytes 1572868
  35.1 7.7 %copy-start.3 = (bf16[2048,512]{1,0:T(8,128)(2,1)S(1)}, bf16[2048,512]{1,0:T(8,128)(2,1)}, u32[]{:S(2)}) copy-start(bf16[2048,512]{1,0:T(8,128)(2,1)} %grid.3) | copy-start | bytes 6291460
  35.1 7.7 %copy-start.4 = (bf16[512,512]{1,0:T(8,128)(2,1)S(1)}, bf16[512,512]{1,0:T(8,128)(2,1)}, u32[]{:S(2)}) copy-start(bf16[512,512]{1,0:T(8,128)(2,1)} %w_grid.1) | copy-start | bytes 1572868
  38.8 4.0 %collective-permute-start.8 = (bf16[256,512]{1,0:T(8,128)(2,1)S(1)}, bf16[256,512]{1,0:T(8,128)(2,1)S(1)}, u32[]{:S(2)}, u32[]{:S(2)}) collective-permute-start(bf16[256,512]{1,0:T(8,128)(2,1)S(1)} %shard_map.162.own), channel_id=1, source_target_pairs={{0,1},{1,0},{2,3},{3,2},{4,5},{5,4},{6,7},{7,6},{8,9},{9,8},{10,11... | collective-permute-start | bytes 786440 | tf_op jit(solution)/shard_map/ppermute | solution.py:220
  38.9 14.3 %collective-permute-start.9 = (bf16[256,512]{1,0:T(8,128)(2,1)S(1)}, bf16[256,512]{1,0:T(8,128)(2,1)S(1)}, u32[]{:S(2)}, u32[]{:S(2)}) collective-permute-start(bf16[256,512]{1,0:T(8,128)(2,1)S(1)} %shard_map.162.own), channel_id=1, source_target_pairs={{0,14},{1,3},{2,0},{3,5},{4,2},{5,7},{6,4},{7,9},{8,6},{9,11},{10,... | collective-permute-start | bytes 786440 | tf_op jit(solution)/shard_map/ppermute | solution.py:226
  42.8 11.3 %collective-permute-start.10 = (bf16[256,512]{1,0:T(8,128)(2,1)S(1)}, bf16[256,512]{1,0:T(8,128)(2,1)S(1)}, u32[]{:S(2)}, u32[]{:S(2)}) collective-permute-start(bf16[256,512]{1,0:T(8,128)(2,1)S(1)} %shard_map.162.own), channel_id=1, source_target_pairs={{0,2},{1,15},{2,4},{3,1},{4,6},{5,3},{6,8},{7,5},{8,10},{9,7},{10,... | collective-permute-start | bytes 786440 | tf_op jit(solution)/shard_map/ppermute | solution.py:229
  54.0 1.6 %collective-permute-start.11 = (bf16[256,512]{1,0:T(8,128)(2,1)S(1)}, bf16[256,512]{1,0:T(8,128)(2,1)S(1)}, u32[]{:S(2)}, u32[]{:S(2)}) collective-permute-start(bf16[256,512]{1,0:T(8,128)(2,1)S(1)} %get-tuple-element.36), channel_id=1, source_target_pairs={{0,1},{1,0},{2,3},{3,2},{4,5},{5,4},{6,7},{7,6},{8,9},{9,8},{10,11... | collective-permute-start | bytes 786440 | tf_op jit(solution)/shard_map/ppermute | solution.py:220
  54.1 1.5 %copy-start.5 = (bf16[512,512]{1,0:T(8,128)(2,1)S(1)}, bf16[512,512]{1,0:T(8,128)(2,1)}, u32[]{:S(2)}) copy-start(bf16[512,512]{1,0:T(8,128)(2,1)} %w_out.5) | copy-start | bytes 1572868

commit v3 on v2

v3 whole, which is shorter than its diff:
```python
import functools

import jax
import jax.numpy as jnp
from jax import lax
from jax.experimental import pallas as pl
from jax.experimental.pallas import tpu as pltpu
from jax.sharding import PartitionSpec as P

L = 2
AXES = ("dom", "feat")
F32, BF16 = jnp.float32, jnp.bfloat16
MIB = 1 << 20
BLOCK = 512
ENCODE_BLOCK = 512
DECODE_BLOCK = 256
LONG = 40_000_000_000


def silu_of_twice(half):
    return half + half * jnp.tanh(half)


def dot(a, b):
    return jnp.dot(a, b, preferred_element_type=F32)


def slot_codes(owner, node, parts, mesh_rows):
    core = lax.axis_index("feat")
    me = lax.axis_index("dom") * 2 + core
    slot = (owner - me) * (1 - 2 * core) + 2
    slot = jnp.where(slot < 0, slot + parts, slot)
    slot = jnp.where(slot >= parts, slot - parts, slot)
    return slot * mesh_rows + node


def one_hot_down(code, first, rows):
    at = lax.broadcasted_iota(jnp.int32, (rows, code.shape[1]), 0)
    return jnp.where(at == code - first, 1.0, 0.0).astype(BF16)


def one_hot_across(row, width):
    n = row.shape[1]
    row = row.astype(F32)
    made = []
    for i in range(0, n, 128):
        cols = jnp.broadcast_to(row[:, i : i + 128], (128, 128)).T
        at = lax.broadcasted_iota(jnp.int32, cols.shape, 1).astype(F32)
        made.append(
            jnp.concatenate(
                [jnp.where(cols == at + float(j), 1.0, 0.0).astype(BF16) for j in range(0, width, 128)],
                axis=1,
            )
        )
    return jnp.concatenate(made, axis=0)


def encode_kernel(parts, owner, node, grid, w1, bias, hidden, near, code, owner_v, node_v, grid_v, w1_v, bias_v, one_hot, sems):
    small = [(owner, owner_v), (node, node_v), (w1, w1_v), (bias, bias_v)]
    copies = [pltpu.make_async_copy(a, b, sems.at[i]) for i, (a, b) in enumerate(small)]
    starts = range(0, grid.shape[0], ENCODE_BLOCK)
    blocks = [
        pltpu.make_async_copy(grid.at[pl.ds(r, ENCODE_BLOCK)], grid_v.at[pl.ds(r, ENCODE_BLOCK)], sems.at[4 + i])
        for i, r in enumerate(starts)
    ]
    for copy in copies + blocks:
        copy.start()
    copies[0].wait()
    copies[1].wait()
    code[...] = slot_codes(owner_v[...], node_v[...], parts, near.shape[0])
    one_hot[...] = one_hot_down(code[...], 0, near.shape[0])
    copies[2].wait()
    copies[3].wait()
    weights = w1_v[...] * 0.5
    offset = bias_v[...] * 0.5
    for r, copy in zip(starts, blocks):
        copy.wait()
        spot = slice(r, r + ENCODE_BLOCK)
        hidden[spot] = silu_of_twice(dot(grid_v[spot], weights) + offset).astype(BF16)
    near[...] = dot(one_hot[...], hidden[...]).astype(BF16)


def cross_kernel(code, hidden, cross):
    rows = cross.shape[0]
    cross[...] = dot(one_hot_down(code[...], rows, rows), hidden[...]).astype(BF16)


def far_kernel(code, hidden, crossed, far):
    rows = far.shape[0]
    far[...] = (dot(one_hot_down(code[...], 4 * rows, rows), hidden[...]) + crossed[...].astype(F32)).astype(BF16)


def chip_kernel(after, code, hidden, own, sibling):
    del after
    rows = own.shape[0]
    sibling[...] = dot(one_hot_down(code[...], 3 * rows, rows), hidden[...]).astype(BF16)
    own[...] = dot(one_hot_down(code[...], 2 * rows, rows), hidden[...])


def prepare_kernel(after, code, edges, halo_index, fetch, gather, gather_halo, pick, lead, lead_halo):
    del after
    width = fetch.shape[1]
    for r in range(0, fetch.shape[0], BLOCK):
        fetch[r : r + BLOCK] = one_hot_across(code[:, r : r + BLOCK], width)
    n, own = edges.shape[1], gather.shape[1]
    border = halo_index.shape[1]
    pick[...] = one_hot_down(halo_index[...], 0, n)
    for k in range(edges.shape[0]):
        one_hot = one_hot_across(edges[k : k + 1, :], own + gather_halo.shape[1])
        gather[k * n : (k + 1) * n] = one_hot[:, :own]
        gather_halo[k * n : (k + 1) * n] = one_hot[:, own:]
        ahead = picked(pick[...], one_hot)
        lead[k * border : (k + 1) * border] = ahead[:, :own]
        lead_halo[k * border : (k + 1) * border] = ahead[:, own:]


def picked(pick, rows):
    return lax.dot_general(pick, rows, (((0,), (0,)), ((), ())), preferred_element_type=F32).astype(BF16)


def latent_kernel(mesh, own, sibling, near, far, w2, pick, latent, halo):
    sums = own[...] + sibling[...].astype(F32) + near[...].astype(F32) + far[...].astype(F32)
    rows = (mesh[...].astype(F32) + dot(sums.astype(BF16), w2[...])).astype(BF16)
    latent[...] = rows
    halo[...] = picked(pick[...], rows)


def own_terms(layer, nodes, gather, source, w_dst, bias, before):
    n = nodes.shape[0]
    target = dot(nodes[...], w_dst[layer]) * 0.5 + bias[layer : layer + 1] * 0.5
    for k in range(gather.shape[0] // n):
        before[k * n : (k + 1) * n] = dot(gather[k * n : (k + 1) * n], source) + target


def project_kernel(layer, latent, w_src, w_dst, bias, gather, halo, *more):
    source = (dot(latent[...], w_src[layer]) * 0.5).astype(BF16)
    if len(more) > 2:
        lead, before, passed, before_lead = more
        own_terms(layer, halo, lead, source, w_dst, bias, before_lead)
    else:
        before, passed = more
    passed[...] = halo[...]
    own_terms(layer, latent, gather, source, w_dst, bias, before)


def halo_table(layer, across, beside, w_src):
    first = lax.axis_index("feat") == 0
    down = jnp.where(first, across[...], beside[...])
    up = jnp.where(first, beside[...], across[...])
    return (dot(jnp.concatenate([down, up], axis=0), w_src[layer]) * 0.5).astype(BF16)


def updated(layer, nodes, before, gather_halo, table, w_out):
    n = nodes.shape[0]
    total = None
    for k in range(before.shape[0] // n):
        spot = slice(k * n, (k + 1) * n)
        message = silu_of_twice(dot(gather_halo[spot], table) + before[spot])
        total = message if total is None else total + message
    return (nodes[...].astype(F32) + dot(total.astype(BF16), w_out[layer])).astype(BF16)


def lead_kernel(layer, halo, before, across, beside, gather_halo, w_src, w_out, new_halo, table):
    table[...] = halo_table(layer, across, beside, w_src)
    new_halo[...] = updated(layer, halo, before, gather_halo, table[...], w_out)


def layer_kernel(layer, latent, before, table, gather_halo, w_out, new):
    new[...] = updated(layer, latent, before, gather_halo, table[...], w_out)


def last_layer_kernel(layer, latent, before, across, beside, gather_halo, w_src, w_out, w_mesh, projected):
    table = halo_table(layer, across, beside, w_src)
    rows = updated(layer, latent, before, gather_halo, table, w_out)
    projected[...] = (dot(rows, w_mesh[...]) * 0.5).astype(BF16)


def base_kernel(grid, w_grid, fetch, own, base, passed):
    rows = own.shape[0]
    passed[...] = own[...]
    for r in range(0, grid.shape[0], BLOCK):
        spot = slice(r, r + BLOCK)
        base[spot] = dot(grid[spot], w_grid[...]) * 0.5 + dot(fetch[spot, 2 * rows : 3 * rows], own[...])


def add_kernel(fetch, base, sibling, far, out, stacked):
    rows = far.shape[0]
    stacked[:rows] = sibling[...]
    stacked[rows:] = far[...]
    for r in range(0, base.shape[0], BLOCK):
        spot = slice(r, r + BLOCK)
        out[spot] = base[spot] + dot(fetch[spot, 3 * rows : 5 * rows], stacked[...])


def pass_kernel(table, out):
    out[...] = table[...]


def decode_kernel(fetch, base, *refs):
    *tables, w_out, out, stacked, out_v, sems = refs
    rows = tables[0].shape[0]
    for i, table in enumerate(tables):
        stacked[i * rows : (i + 1) * rows] = table[...]
    def halved(r):
        spot = slice(r, r + DECODE_BLOCK)
        return base[spot] + dot(fetch[spot, : stacked.shape[0]], stacked[...])

    copies = []
    half = halved(0)
    for i, r in enumerate(range(0, base.shape[0], DECODE_BLOCK)):
        ahead = halved(r + DECODE_BLOCK) if r + DECODE_BLOCK < base.shape[0] else None
        out_v[r : r + DECODE_BLOCK] = dot(silu_of_twice(half).astype(BF16), w_out[...]).astype(BF16)
        half = ahead
        copies.append(pltpu.make_async_copy(out_v.at[pl.ds(r, DECODE_BLOCK)], out.at[pl.ds(r, DECODE_BLOCK)], sems.at[i]))
        copies[-1].start()
    for copy in copies:
        copy.wait()


VM = pltpu.VMEM


def call(kernel, ins, outs, flops, scratch=(), vmem=24, spaces=None, out_space=VM):
    moved = sum(a.size * a.dtype.itemsize for a in ins)
    spaces = spaces or [VM] * len(ins)
    ins = [pltpu.with_memory_space_constraint(a, s) if s is pltpu.HBM else a for a, s in zip(ins, spaces)]
    return pl.pallas_call(
        kernel,
        in_specs=[pl.BlockSpec(memory_space=space) for space in spaces],
        out_specs=[pl.BlockSpec(memory_space=out_space) for _ in outs],
        out_shape=[jax.ShapeDtypeStruct(shape, dtype) for shape, dtype in outs],
        scratch_shapes=list(scratch),
        compiler_params=pltpu.CompilerParams(vmem_limit_bytes=vmem * MIB),
        cost_estimate=pl.CostEstimate(flops=flops, bytes_accessed=moved if flops > 1 else 1, transcendentals=0),
    )(*ins)


def body(
    grid,
    mesh_feat,
    owner,
    node,
    halo_index,
    edge_src,
    w_enc1,
    enc_bias,
    w_enc2,
    proc_src,
    proc_dst,
    proc_bias,
    proc_out,
    dec_grid,
    dec_mesh,
    dec_out,
):
    parts = lax.axis_size(AXES)
    rows, width = grid.shape
    mesh_rows = mesh_feat.shape[0]
    border = halo_index.shape[0]
    degree = edge_src.shape[1]
    part = functools.partial

    def sided(step):
        return [(i, (i + step) % parts if i % 2 == 0 else (i - step) % parts) for i in range(parts)]

    def swap(value):
        return lax.ppermute(value, AXES, sided(1))

    def to_across(value):
        return lax.ppermute(value, AXES, sided(-1))

    def to_near(value):
        return lax.ppermute(value, AXES, sided(-2))

    def to_far(value):
        return lax.ppermute(value, AXES, sided(2))

    table = ((mesh_rows, width), BF16)
    border_rows = ((border, width), BF16)
    unit = 2 * rows * width
    hidden, near, code = call(
        part(encode_kernel, parts),
        [owner.reshape(1, rows), node.reshape(1, rows), grid, w_enc1, enc_bias.reshape(1, width)],
        [((rows, width), BF16), table, ((1, rows), jnp.int32)],
        unit * (width + mesh_rows),
        [
            VM((1, rows), jnp.int32),
            VM((1, rows), jnp.int32),
            VM((rows, width), BF16),
            VM((width, width), BF16),
            VM((1, width), F32),
            VM((mesh_rows, rows), BF16),
            pltpu.SemaphoreType.DMA((4 + rows // ENCODE_BLOCK,)),
        ],
        spaces=[pltpu.HBM] * 5,
    )
    near = to_near(near)
    (cross,) = call(cross_kernel, [code, hidden], [table], 1)
    crossed = swap(cross)
    (sent,) = call(far_kernel, [code, hidden, crossed], [table], 1)
    far = to_far(sent)
    own, sibling = call(
        chip_kernel,
        [sent, code, hidden],
        [((mesh_rows, width), F32), table],
        unit * 2 * mesh_rows,
        spaces=[pl.ANY, VM, VM],
    )
    fetch, gather, gather_halo, pick, lead, lead_halo = call(
        prepare_kernel,
        [near, code, edge_src.T, halo_index.reshape(1, border)],
        [
            ((rows, 5 * mesh_rows), BF16),
            ((degree * mesh_rows, mesh_rows), BF16),
            ((degree * mesh_rows, 2 * border), BF16),
            ((mesh_rows, border), BF16),
            ((degree * border, mesh_rows), BF16),
            ((degree * border, 2 * border), BF16),
        ],
        LONG,
        spaces=[pl.ANY, VM, VM, VM],
    )
    sibling = swap(sibling)
    latent, halo = call(
        latent_kernel,
        [mesh_feat, own, sibling, near, far, w_enc2, pick],
        [table, border_rows],
        2 * mesh_rows * width * width,
    )
    edge_terms = ((degree * mesh_rows, width), F32)
    for layer in range(L - 1):
        across = to_across(halo)
        before, passed, before_lead = call(
            part(project_kernel, layer),
            [latent, proc_src, proc_dst, proc_bias, gather, halo, lead],
            [edge_terms, border_rows, ((degree * border, width), F32)],
            1,
        )
        beside = swap(passed)
        (across,) = call(pass_kernel, [across], [border_rows], LONG)
        halo, received = call(
            part(lead_kernel, layer),
            [halo, before_lead, across, beside, lead_halo, proc_src, proc_out],
            [border_rows, ((2 * border, width), BF16)],
            2 * border * width * (degree * 2 * border + 3 * width),
        )
        (latent,) = call(
            part(layer_kernel, layer),
            [latent, before, received, gather_halo, proc_out],
            [table],
            1,
        )
    across = to_across(halo)
    before, passed = call(
        part(project_kernel, L - 1),
        [latent, proc_src, proc_dst, proc_bias, gather, halo],
        [edge_terms, border_rows],
        1,
    )
    beside = swap(passed)
    (across,) = call(pass_kernel, [across], [border_rows], LONG)
    (projected,) = call(
        part(last_layer_kernel, L - 1),
        [latent, before, across, beside, gather_halo, proc_src, proc_out, dec_mesh],
        [table],
        2 * mesh_rows * width * (degree * 2 * border + 2 * width),
    )
    far = to_near(projected)
    f32_rows = ((rows, width), F32)
    base, passed = call(
        base_kernel,
        [grid, dec_grid, fetch, projected],
        [f32_rows, table],
        1,
    )
    near = to_far(passed)
    sibling = swap(passed)
    pair = [VM((2 * mesh_rows, width), BF16)]
    (far,) = call(pass_kernel, [far], [table], LONG)
    cross = swap(far)
    (base,) = call(add_kernel, [fetch, base, sibling, far], [f32_rows], 1, pair)
    (near,) = call(pass_kernel, [near], [table], LONG)
    tables = [near, cross]
    (out,) = call(
        decode_kernel,
        [fetch, base, *tables, dec_out],
        [((rows, width), BF16)],
        unit * (width + mesh_rows),
        [
            VM((len(tables) * mesh_rows, width), BF16),
            VM((rows, width), BF16),
            pltpu.SemaphoreType.DMA((rows // DECODE_BLOCK,)),
        ],
        out_space=pltpu.HBM,
    )
    return out


def solution(mesh):
    rows = P(("group", "dom", "feat"), None)
    flat = P(("group", "dom", "feat"))
    return jax.shard_map(
        body,
        mesh=mesh,
        in_specs=(rows, rows, rows, flat, flat, rows) + (P(),) * 10,
        out_specs=rows,
        check_vma=False,
    )
```

time: 58.9 us -> 55.1 us (0.935); the launches traced: 58.7 us -> 54.3 us
  waiting for transfers between devices: 20.8 us -> 18.2 us
  starting transfers between devices: 17.5 us -> 15.7 us
    ppermute x2, waiting for transfers between devices: 7.33 us -> 2.97 us  [to_far(): return lax.ppermute(value, AXES, sided(2))]
    ppermute x2, starting transfers between devices: 9.49 us -> 6.96 us  [to_near(): return lax.ppermute(value, AXES, sided(-2))]
    ppermute x2, waiting for transfers between devices: 8.65 us -> 11 us  [to_near(): return lax.ppermute(value, AXES, sided(-2))]
    ppermute x2, starting transfers between devices: 7.12 us -> 5.55 us  [to_across(): return lax.ppermute(value, AXES, sided(-1))]
    ppermute x6, starting transfers between devices: 0.87 us -> 2.15 us  [swap(): return lax.ppermute(value, AXES, sided(1))]
    ppermute x2, starting transfers between devices: 0.06 us -> 1.05 us  [to_far(): return lax.ppermute(value, AXES, sided(2))]
    pallas_call x13 -> x18, Pallas kernels: 19.9 us -> 19.9 us  [call(): pl.pallas_call(kernel, in_specs=[pl.BlockSpec(memory_space=space) for spa...]
  transfers between devices with their start and end apart: 12 -> 12, of which waited for: 6 -> 6; matrix products, arithmetic and copies ran while one was open for 0% -> 0% of each run, Pallas kernels for 15% -> 18%
where the time goes in v3:
time: 55.1 us; the launch traced here: 54.3 us
  Pallas kernels  19.9 us (36%)
  waiting for transfers between devices  18.2 us (33%)
  starting transfers between devices  15.7 us (28%)
    pallas_call x18, Pallas kernels, call(): pl.pallas_call(kernel, in_specs=[pl.BlockSpec(memory_space=space) for spa...  19.9 us
    ppermute x2, waiting for transfers between devices, to_near(): return lax.ppermute(value, AXES, sided(-2))  11 us
    ppermute x2, starting transfers between devices, to_near(): return lax.ppermute(value, AXES, sided(-2))  6.96 us
    ppermute x2, starting transfers between devices, to_across(): return lax.ppermute(value, AXES, sided(-1))  5.55 us
    ppermute x2, waiting for transfers between devices, to_across(): return lax.ppermute(value, AXES, sided(-1))  3.99 us
    ppermute x2, waiting for transfers between devices, to_far(): return lax.ppermute(value, AXES, sided(2))  2.97 us
    ppermute x6, starting transfers between devices, swap(): return lax.ppermute(value, AXES, sided(1))  2.15 us
  transfers between devices with their start and end apart: 12, of which 6 were waited for; matrix products, arithmetic and copies ran while one was open for 0% of the time, Pallas kernels for 18%

profile of v3, /device:TPU:0, one launch (start us, length us, event | category | flops | bytes accessed | tf_op | source)
XLA Modules:
  0.0 54.3 jit_solution(17765124368878345061)
XLA Ops:
  0.0 3.7 %shard_map.154 = (bf16[2048,512]{1,0:T(8,128)(2,1)S(1)}, bf16[256,512]{1,0:T(8,128)(2,1)S(1)}, s32[1,2048]{1,0:T(1,128)S(1)}) custom-call(s32[1,2048]{1,0:T(1,128)} %bitcast.7, s32[1,2048]{1,0:T(1,128)} %bitcast.8, bf16[2048,512]{1,0:T(8,128)(2,1)} %grid.3, bf16[512,512]{1,0:T(8,128)(2,1)} %w1.1, f32[1,512]{1,0:T(1,128)} %bitcast.9), custom_call_target="tpu_custom_call" | custom-call | flops 1610612736 | bytes 2639872 | tf_op jit(solution)/shard_map/pallas_call | solution.py:227
  3.7 0.7 %shard_map.156 = bf16[256,512]{1,0:T(8,128)(2,1)S(1)} custom-call(s32[1,2048]{1,0:T(1,128)S(1)} %get-tuple-element.28.code, bf16[2048,512]{1,0:T(8,128)(2,1)S(1)} %get-tuple-element.30.hidden), custom_call_target="tpu_custom_call" | custom-call | flops 1 | bytes 1 | tf_op jit(solution)/shard_map/pallas_call | solution.py:227
  4.4 0.5 collective-permute-start.1
  4.9 5.6 %collective-permute-start = (bf16[256,512]{1,0:T(8,128)(2,1)S(1)}, bf16[256,512]{1,0:T(8,128)(2,1)S(1)}, u32[]{:S(2)}, u32[]{:S(2)}) collective-permute-start(bf16[256,512]{1,0:T(8,128)(2,1)S(1)} %get-tuple-element.27), channel_id=1, source_target_pairs={{0,14},{1,3},{2,0},{3,5},{4,2},{5,7},{6,4},{7,9},{8,6},{9,11},{10,... | collective-permute-start | bytes 786440 | tf_op jit(solution)/shard_map/ppermute | solution.py:273
  10.6 0.7 %shard_map.157.after = bf16[256,512]{1,0:T(8,128)(2,1)S(1)} custom-call(s32[1,2048]{1,0:T(1,128)S(1)} %get-tuple-element.28.code, bf16[2048,512]{1,0:T(8,128)(2,1)S(1)} %get-tuple-element.30.hidden, bf16[256,512]{1,0:T(8,128)(2,1)S(1)} %collective-permute-done.1.crossed), custom_call_target="tpu_custom_call" | custom-call | flops 1 | bytes 1 | tf_op jit(solution)/shard_map/pallas_call | solution.py:227
  11.3 0.1 collective-permute-start.3
  11.4 1.2 %shard_map.158 = (f32[256,512]{1,0:T(8,128)S(1)}, bf16[256,512]{1,0:T(8,128)(2,1)S(1)}) custom-call(bf16[256,512]{1,0:T(8,128)(2,1)S(1)} %shard_map.157.after, s32[1,2048]{1,0:T(1,128)S(1)} %get-tuple-element.28.code, bf16[2048,512]{1,0:T(8,128)(2,1)S(1)} %get-tuple-element.30.hidden), custom_call_target="tpu_custom_call" | custom-call | flops 1073741824 | bytes 2367488 | tf_op jit(solution)/shard_map/pallas_call | solution.py:227
  12.6 1.3 %collective-permute-start.2 = (bf16[256,512]{1,0:T(8,128)(2,1)S(1)}, bf16[256,512]{1,0:T(8,128)(2,1)S(1)}, u32[]{:S(2)}, u32[]{:S(2)}) collective-permute-start(bf16[256,512]{1,0:T(8,128)(2,1)S(1)} %get-tuple-element.32), channel_id=1, source_target_pairs={{0,1},{1,0},{2,3},{3,2},{4,5},{5,4},{6,7},{7,6},{8,9},{9,8},{10,11... | collective-permute-start | bytes 786440 | tf_op jit(solution)/shard_map/ppermute | solution.py:267
  14.0 1.9 %collective-permute-done.after.near = bf16[256,512]{1,0:T(8,128)(2,1)S(1)} collective-permute-done((bf16[256,512]{1,0:T(8,128)(2,1)S(1)}, bf16[256,512]{1,0:T(8,128)(2,1)S(1)}, u32[]{:S(2)}, u32[]{:S(2)}) %collective-permute-start) | collective-permute-done | bytes 262176 | tf_op jit(solution)/shard_map/ppermute | solution.py:273
  15.9 1.5 %shard_map.155 = (bf16[2048,1280]{1,0:T(8,128)(2,1)S(1)}, bf16[1536,256]{1,0:T(8,128)(2,1)S(1)}, bf16[1536,128]{1,0:T(8,128)(2,1)S(1)}, bf16[256,64]{1,0:T(8,128...) custom-call(bf16[256,512]{1,0:T(8,128)(2,1)S(1)} %collective-permute-done.after.near, ...), custom_call_target="tpu_custom_call" | custom-call | flops 40000000000 | bytes 276736 | tf_op jit(solution)/shard_map/pallas_call | solution.py:227
  17.5 3.0 %collective-permute-done.3.far = bf16[256,512]{1,0:T(8,128)(2,1)S(1)} collective-permute-done((bf16[256,512]{1,0:T(8,128)(2,1)S(1)}, bf16[256,512]{1,0:T(8,128)(2,1)S(1)}, u32[]{:S(2)}, u32[]{:S(2)}) %collective-permute-start.3) | collective-permute-done | bytes 262176 | tf_op jit(solution)/shard_map/ppermute | solution.py:276
  20.4 0.5 shard_map.159
  20.9 2.8 %collective-permute-start.4 = (bf16[64,512]{1,0:T(8,128)(2,1)S(1)}, bf16[64,512]{1,0:T(8,128)(2,1)S(1)}, u32[]{:S(2)}, u32[]{:S(2)}) collective-permute-start(bf16[64,512]{1,0:T(8,128)(2,1)S(1)} %get-tuple-element.36.halo), channel_id=1, source_target_pairs={{0,15},{1,2},{2,1},{3,4},{4,3},{5,6},{6,5},{7,8},{8,7},{9,10},{10,... | collective-permute-start | bytes 196616 | tf_op jit(solution)/shard_map/ppermute | solution.py:270
  23.7 1.3 %shard_map.160 = (f32[1536,512]{1,0:T(8,128)S(1)}, bf16[64,512]{1,0:T(8,128)(2,1)S(1)}, f32[384,512]{1,0:T(8,128)S(1)}) custom-call(bf16[256,512]{1,0:T(8,128)(2,1)S(1)} %get-tuple-element.34.latent, bf16[2,512,512]{2,1,0:T(8,128)(2,1)S(1)} %copy-done, bf16[2,512,512]{2,1,0:T(8,128)(2,1)S(1)} %copy-done.2, f32[2,512]{1,0:T(2,128)S(1)} %copy-done.9, ...), custom_call_target="tpu_custom_call" | custom-call | flops 1 | bytes 1 | tf_op jit(solution)/shard_map/pallas_call | solution.py:227
  25.0 0.1 collective-permute-start.5
  25.1 2.3 %collective-permute-done.4.table = bf16[64,512]{1,0:T(8,128)(2,1)S(1)} collective-permute-done((bf16[64,512]{1,0:T(8,128)(2,1)S(1)}, bf16[64,512]{1,0:T(8,128)(2,1)S(1)}, u32[]{:S(2)}, u32[]{:S(2)}) %collective-permute-start.4) | collective-permute-done | bytes 65568 | tf_op jit(solution)/shard_map/ppermute | solution.py:270
  27.4 0.7 %shard_map.162 = (bf16[64,512]{1,0:T(8,128)(2,1)S(1)}, bf16[128,512]{1,0:T(8,128)(2,1)S(1)}) custom-call(bf16[64,512]{1,0:T(8,128)(2,1)S(1)} %get-tuple-element.36.halo, f32[384,512]{1,0:T(8,128)S(1)} %get-tuple-element.39.before, bf16[64,512]{1,0:T(8,128)(2,1)S(1)} %shard_map.161.across, bf16[64,512]{1,0:T(8,128)(2,1)S(1)} %collective-permute-done.5.beside, ...), custom_call_target="tpu_custom_call" | custom-call | flops 150994944 | bytes 3178496 | tf_op jit(solution)/shard_map/pallas_call | solution.py:227
  28.1 2.8 %collective-permute-start.6 = (bf16[64,512]{1,0:T(8,128)(2,1)S(1)}, bf16[64,512]{1,0:T(8,128)(2,1)S(1)}, u32[]{:S(2)}, u32[]{:S(2)}) collective-permute-start(bf16[64,512]{1,0:T(8,128)(2,1)S(1)} %get-tuple-element.44.halo), channel_id=1, source_target_pairs={{0,15},{1,2},{2,1},{3,4},{4,3},{5,6},{6,5},{7,8},{8,7},{9,10},{10,... | collective-permute-start | bytes 196616 | tf_op jit(solution)/shard_map/ppermute | solution.py:270
  30.8 1.0 %shard_map.163.latent = bf16[256,512]{1,0:T(8,128)(2,1)S(1)} custom-call(bf16[256,512]{1,0:T(8,128)(2,1)S(1)} %get-tuple-element.34.latent, f32[1536,512]{1,0:T(8,128)S(1)} %get-tuple-element.38.before, bf16[128,512]{1,0:T(8,128)(2,1)S(1)} %get-tuple-element.42.table, bf16[1536,128]{1,0:T(8,128)(2,1)S(1)} %get-tuple-element.43.gather_halo, ...), custom_call_target="tpu_custom_call" | custom-call | flops 1 | bytes 1 | tf_op jit(solution)/shard_map/pallas_call | solution.py:227
  31.9 0.8 %shard_map.164 = (f32[1536,512]{1,0:T(8,128)S(1)}, bf16[64,512]{1,0:T(8,128)(2,1)S(1)}) custom-call(bf16[256,512]{1,0:T(8,128)(2,1)S(1)} %shard_map.163.latent, bf16[2,512,512]{2,1,0:T(8,128)(2,1)S(1)} %copy-done, bf16[2,512,512]{2,1,0:T(8,128)(2,1)S(1)} %copy-done.2, f32[2,512]{1,0:T(2,128)S(1)} %copy-done.9, ...), custom_call_target="tpu_custom_call" | custom-call | flops 1 | bytes 1 | tf_op jit(solution)/shard_map/pallas_call | solution.py:227
  32.7 0.1 collective-permute-start.7
  32.8 1.7 %collective-permute-done.6.table = bf16[64,512]{1,0:T(8,128)(2,1)S(1)} collective-permute-done((bf16[64,512]{1,0:T(8,128)(2,1)S(1)}, bf16[64,512]{1,0:T(8,128)(2,1)S(1)}, u32[]{:S(2)}, u32[]{:S(2)}) %collective-permute-start.6) | collective-permute-done | bytes 65568 | tf_op jit(solution)/shard_map/ppermute | solution.py:270
  34.6 1.4 %shard_map.166.own = bf16[256,512]{1,0:T(8,128)(2,1)S(1)} custom-call(bf16[256,512]{1,0:T(8,128)(2,1)S(1)} %shard_map.163.latent, f32[1536,512]{1,0:T(8,128)S(1)} %get-tuple-element.45.before, bf16[64,512]{1,0:T(8,128)(2,1)S(1)} %shard_map.165.across, bf16[64,512]{1,0:T(8,128)(2,1)S(1)} %collective-permute-done.7.beside, ...), custom_call_target="tpu_custom_call" | custom-call | flops 469762048 | bytes 6553600 | tf_op jit(solution)/shard_map/pallas_call | solution.py:227
  36.0 1.3 %collective-permute-start.9 = (bf16[256,512]{1,0:T(8,128)(2,1)S(1)}, bf16[256,512]{1,0:T(8,128)(2,1)S(1)}, u32[]{:S(2)}, u32[]{:S(2)}) collective-permute-start(bf16[256,512]{1,0:T(8,128)(2,1)S(1)} %shard_map.166.own), channel_id=1, source_target_pairs={{0,14},{1,3},{2,0},{3,5},{4,2},{5,7},{6,4},{7,9},{8,6},{9,11},{10,... | collective-permute-start | bytes 786440 | tf_op jit(solution)/shard_map/ppermute | solution.py:273
  37.3 1.8 %shard_map.167 = (f32[2048,512]{1,0:T(8,128)S(1)}, bf16[256,512]{1,0:T(8,128)(2,1)S(1)}) custom-call(bf16[2048,512]{1,0:T(8,128)(2,1)S(1)} %copy-done.3, bf16[512,512]{1,0:T(8,128)(2,1)S(1)} %copy-done.4, bf16[2048,1280]{1,0:T(8,128)(2,1)S(1)} %get-tuple-element.29.fetch, bf16[256,512]{1,0:T(8,128)(2,1)S(1)} %shard_map.166.own), custom_call_target="tpu_custom_call" | custom-call | flops 1 | bytes 1 | tf_op jit(solution)/shard_map/pallas_call | solution.py:227
  39.1 0.1 collective-permute-start.8
  39.2 1.0 %collective-permute-start.10 = (bf16[256,512]{1,0:T(8,128)(2,1)S(1)}, bf16[256,512]{1,0:T(8,128)(2,1)S(1)}, u32[]{:S(2)}, u32[]{:S(2)}) collective-permute-start(bf16[256,512]{1,0:T(8,128)(2,1)S(1)} %get-tuple-element.48), channel_id=1, source_target_pairs={{0,2},{1,15},{2,4},{3,1},{4,6},{5,3},{6,8},{7,5},{8,10},{9,7},{10,... | collective-permute-start | bytes 786440 | tf_op jit(solution)/shard_map/ppermute | solution.py:276
  40.2 9.1 %collective-permute-done.9.table = bf16[256,512]{1,0:T(8,128)(2,1)S(1)} collective-permute-done((bf16[256,512]{1,0:T(8,128)(2,1)S(1)}, bf16[256,512]{1,0:T(8,128)(2,1)S(1)}, u32[]{:S(2)}, u32[]{:S(2)}) %collective-permute-start.9) | collective-permute-done | bytes 262176 | tf_op jit(solution)/shard_map/ppermute | solution.py:273
  49.3 0.1 collective-permute-start.11
  49.5 1.3 %shard_map.169.base = f32[2048,512]{1,0:T(8,128)S(1)} custom-call(bf16[2048,1280]{1,0:T(8,128)(2,1)S(1)} %get-tuple-element.29.fetch, f32[2048,512]{1,0:T(8,128)S(1)} %get-tuple-element.47.base, bf16[256,512]{1,0:T(8,128)(2,1)S(1)} %collective-permute-done.8.sibling, bf16[256,512]{1,0:T(8,128)(2,1)S(1)} %shard_map.168.far), custom_call_target="tpu_custom_call" | custom-call | flops 1 | bytes 1 | tf_op jit(solution)/shard_map/pallas_call | solution.py:227
  50.7 0.2 collective-permute-done.11.refs_1_
  50.9 3.2 %shard_map.171 = bf16[2048,512]{1,0:T(8,128)(2,1)} custom-call(bf16[2048,1280]{1,0:T(8,128)(2,1)S(1)} %get-tuple-element.29.fetch, f32[2048,512]{1,0:T(8,128)S(1)} %shard_map.169.base, bf16[256,512]{1,0:T(8,128)(2,1)S(1)} %shard_map.170.refs_0_, bf16[256,512]{1,0:T(8,128)(2,1)S(1)} %collective-permute-done.11.refs_1_, bf16[512,512]{1,0:T(8,128)(2,1)S(1)} %copy-done.5), custom_call_target="tpu_custom_call" | custom-call | flops 1610612736 | bytes 10485760 | tf_op jit(solution)/shard_map/pallas_call | solution.py:227
  (34 shorter events, 0.1 us)
Async XLA Ops:
  4.4 6.2 %collective-permute-start.1 = (bf16[256,512]{1,0:T(8,128)(2,1)S(1)}, bf16[256,512]{1,0:T(8,128)(2,1)S(1)}, u32[]{:S(2)}, u32[]{:S(2)}) collective-permute-start(bf16[256,512]{1,0:T(8,128)(2,1)S(1)} %shard_map.156), channel_id=1, source_target_pairs={{0,1},{1,0},{2,3},{3,2},{4,5},{5,4},{6,7},{7,6},{8,9},{9,8},{10,11... | collective-permute-start | bytes 786440 | tf_op jit(solution)/shard_map/ppermute | solution.py:267
  4.9 10.9 %copy-start.10 = (s32[256,6]{0,1:T(8,128)S(1)}, s32[256,6]{0,1:T(8,128)}, u32[]{:S(2)}) copy-start(s32[256,6]{0,1:T(8,128)} %param.21) | copy-start | bytes 18436
  4.9 10.9 %copy-start.11 = (s32[64]{0:T(128)S(1)}, s32[64]{0:T(128)}, u32[]{:S(2)}) copy-start(s32[64]{0:T(128)} %param.20) | copy-start | bytes 772
  4.9 10.9 %collective-permute-start = (bf16[256,512]{1,0:T(8,128)(2,1)S(1)}, bf16[256,512]{1,0:T(8,128)(2,1)S(1)}, u32[]{:S(2)}, u32[]{:S(2)}) collective-permute-start(bf16[256,512]{1,0:T(8,128)(2,1)S(1)} %get-tuple-element.27), channel_id=1, source_target_pairs={{0,14},{1,3},{2,0},{3,5},{4,2},{5,7},{6,4},{7,9},{8,6},{9,11},{10,... | collective-permute-start | bytes 786440 | tf_op jit(solution)/shard_map/ppermute | solution.py:273
  11.3 9.1 %collective-permute-start.3 = (bf16[256,512]{1,0:T(8,128)(2,1)S(1)}, bf16[256,512]{1,0:T(8,128)(2,1)S(1)}, u32[]{:S(2)}, u32[]{:S(2)}) collective-permute-start(bf16[256,512]{1,0:T(8,128)(2,1)S(1)} %shard_map.157.after), channel_id=1, source_target_pairs={{0,2},{1,15},{2,4},{3,1},{4,6},{5,3},{6,8},{7,5},{8,10},{9,7},{10,... | collective-permute-start | bytes 786440 | tf_op jit(solution)/shard_map/ppermute | solution.py:276
  12.6 4.8 %collective-permute-start.2 = (bf16[256,512]{1,0:T(8,128)(2,1)S(1)}, bf16[256,512]{1,0:T(8,128)(2,1)S(1)}, u32[]{:S(2)}, u32[]{:S(2)}) collective-permute-start(bf16[256,512]{1,0:T(8,128)(2,1)S(1)} %get-tuple-element.32), channel_id=1, source_target_pairs={{0,1},{1,0},{2,3},{3,2},{4,5},{5,4},{6,7},{7,6},{8,9},{9,8},{10,11... | collective-permute-start | bytes 786440 | tf_op jit(solution)/shard_map/ppermute | solution.py:267
  15.9 4.6 %copy-start.6 = (bf16[512,512]{1,0:T(8,128)(2,1)S(1)}, bf16[512,512]{1,0:T(8,128)(2,1)}, u32[]{:S(2)}) copy-start(bf16[512,512]{1,0:T(8,128)(2,1)} %w2.1) | copy-start | bytes 1572868
  15.9 4.6 %copy-start.8 = (bf16[256,512]{1,0:T(8,128)(2,1)S(1)}, bf16[256,512]{1,0:T(8,128)(2,1)}, u32[]{:S(2)}) copy-start(bf16[256,512]{1,0:T(8,128)(2,1)} %mesh.1) | copy-start | bytes 786436
  15.9 7.8 %copy-start = (bf16[2,512,512]{2,1,0:T(8,128)(2,1)S(1)}, bf16[2,512,512]{2,1,0:T(8,128)(2,1)}, u32[]{:S(2)}) copy-start(bf16[2,512,512]{2,1,0:T(8,128)(2,1)} %w_src.7) | copy-start | bytes 3145732
  15.9 7.8 %copy-start.2 = (bf16[2,512,512]{2,1,0:T(8,128)(2,1)S(1)}, bf16[2,512,512]{2,1,0:T(8,128)(2,1)}, u32[]{:S(2)}) copy-start(bf16[2,512,512]{2,1,0:T(8,128)(2,1)} %w_dst.3) | copy-start | bytes 3145732
  15.9 7.8 %copy-start.9 = (f32[2,512]{1,0:T(2,128)S(1)}, f32[2,512]{1,0:T(2,128)}, u32[]{:S(2)}) copy-start(f32[2,512]{1,0:T(2,128)} %bias.3) | copy-start | bytes 12292
  20.9 6.5 %collective-permute-start.4 = (bf16[64,512]{1,0:T(8,128)(2,1)S(1)}, bf16[64,512]{1,0:T(8,128)(2,1)S(1)}, u32[]{:S(2)}, u32[]{:S(2)}) collective-permute-start(bf16[64,512]{1,0:T(8,128)(2,1)S(1)} %get-tuple-element.36.halo), channel_id=1, source_target_pairs={{0,15},{1,2},{2,1},{3,4},{4,3},{5,6},{6,5},{7,8},{8,7},{9,10},{10,... | collective-permute-start | bytes 196616 | tf_op jit(solution)/shard_map/ppermute | solution.py:270
  25.0 2.4 %copy-start.1 = (bf16[2,512,512]{2,1,0:T(8,128)(2,1)S(1)}, bf16[2,512,512]{2,1,0:T(8,128)(2,1)}, u32[]{:S(2)}) copy-start(bf16[2,512,512]{2,1,0:T(8,128)(2,1)} %w_out.5) | copy-start | bytes 3145732
  25.0 2.4 %collective-permute-start.5 = (bf16[64,512]{1,0:T(8,128)(2,1)S(1)}, bf16[64,512]{1,0:T(8,128)(2,1)S(1)}, u32[]{:S(2)}, u32[]{:S(2)}) collective-permute-start(bf16[64,512]{1,0:T(8,128)(2,1)S(1)} %get-tuple-element.40), channel_id=1, source_target_pairs={{0,1},{1,0},{2,3},{3,2},{4,5},{5,4},{6,7},{7,6},{8,9},{9,8},{10,11... | collective-permute-start | bytes 196616 | tf_op jit(solution)/shard_map/ppermute | solution.py:267
  28.1 6.5 %collective-permute-start.6 = (bf16[64,512]{1,0:T(8,128)(2,1)S(1)}, bf16[64,512]{1,0:T(8,128)(2,1)S(1)}, u32[]{:S(2)}, u32[]{:S(2)}) collective-permute-start(bf16[64,512]{1,0:T(8,128)(2,1)S(1)} %get-tuple-element.44.halo), channel_id=1, source_target_pairs={{0,15},{1,2},{2,1},{3,4},{4,3},{5,6},{6,5},{7,8},{8,7},{9,10},{10,... | collective-permute-start | bytes 196616 | tf_op jit(solution)/shard_map/ppermute | solution.py:270
  32.7 1.8 %copy-start.7 = (bf16[512,512]{1,0:T(8,128)(2,1)S(1)}, bf16[512,512]{1,0:T(8,128)(2,1)}, u32[]{:S(2)}) copy-start(bf16[512,512]{1,0:T(8,128)(2,1)} %w_mesh.1) | copy-start | bytes 1572868
  32.7 1.8 %collective-permute-start.7 = (bf16[64,512]{1,0:T(8,128)(2,1)S(1)}, bf16[64,512]{1,0:T(8,128)(2,1)S(1)}, u32[]{:S(2)}, u32[]{:S(2)}) collective-permute-start(bf16[64,512]{1,0:T(8,128)(2,1)S(1)} %get-tuple-element.46), channel_id=1, source_target_pairs={{0,1},{1,0},{2,3},{3,2},{4,5},{5,4},{6,7},{7,6},{8,9},{9,8},{10,11... | collective-permute-start | bytes 196616 | tf_op jit(solution)/shard_map/ppermute | solution.py:267
  34.5 2.8 %copy-start.3 = (bf16[2048,512]{1,0:T(8,128)(2,1)S(1)}, bf16[2048,512]{1,0:T(8,128)(2,1)}, u32[]{:S(2)}) copy-start(bf16[2048,512]{1,0:T(8,128)(2,1)} %grid.3) | copy-start | bytes 6291460
  34.5 2.8 %copy-start.4 = (bf16[512,512]{1,0:T(8,128)(2,1)S(1)}, bf16[512,512]{1,0:T(8,128)(2,1)}, u32[]{:S(2)}) copy-start(bf16[512,512]{1,0:T(8,128)(2,1)} %w_grid.1) | copy-start | bytes 1572868
  36.0 13.3 %collective-permute-start.9 = (bf16[256,512]{1,0:T(8,128)(2,1)S(1)}, bf16[256,512]{1,0:T(8,128)(2,1)S(1)}, u32[]{:S(2)}, u32[]{:S(2)}) collective-permute-start(bf16[256,512]{1,0:T(8,128)(2,1)S(1)} %shard_map.166.own), channel_id=1, source_target_pairs={{0,14},{1,3},{2,0},{3,5},{4,2},{5,7},{6,4},{7,9},{8,6},{9,11},{10,... | collective-permute-start | bytes 786440 | tf_op jit(solution)/shard_map/ppermute | solution.py:273
  39.1 10.3 %collective-permute-start.8 = (bf16[256,512]{1,0:T(8,128)(2,1)S(1)}, bf16[256,512]{1,0:T(8,128)(2,1)S(1)}, u32[]{:S(2)}, u32[]{:S(2)}) collective-permute-start(bf16[256,512]{1,0:T(8,128)(2,1)S(1)} %get-tuple-element.48), channel_id=1, source_target_pairs={{0,1},{1,0},{2,3},{3,2},{4,5},{5,4},{6,7},{7,6},{8,9},{9,8},{10,11... | collective-permute-start | bytes 786440 | tf_op jit(solution)/shard_map/ppermute | solution.py:267
  39.2 10.2 %collective-permute-start.10 = (bf16[256,512]{1,0:T(8,128)(2,1)S(1)}, bf16[256,512]{1,0:T(8,128)(2,1)S(1)}, u32[]{:S(2)}, u32[]{:S(2)}) collective-permute-start(bf16[256,512]{1,0:T(8,128)(2,1)S(1)} %get-tuple-element.48), channel_id=1, source_target_pairs={{0,2},{1,15},{2,4},{3,1},{4,6},{5,3},{6,8},{7,5},{8,10},{9,7},{10,... | collective-permute-start | bytes 786440 | tf_op jit(solution)/shard_map/ppermute | solution.py:276
  49.3 1.6 %collective-permute-start.11 = (bf16[256,512]{1,0:T(8,128)(2,1)S(1)}, bf16[256,512]{1,0:T(8,128)(2,1)S(1)}, u32[]{:S(2)}, u32[]{:S(2)}) collective-permute-start(bf16[256,512]{1,0:T(8,128)(2,1)S(1)} %shard_map.168.far), channel_id=1, source_target_pairs={{0,1},{1,0},{2,3},{3,2},{4,5},{5,4},{6,7},{7,6},{8,9},{9,8},{10,11... | collective-permute-start | bytes 786440 | tf_op jit(solution)/shard_map/ppermute | solution.py:267
  49.5 1.5 %copy-start.5 = (bf16[512,512]{1,0:T(8,128)(2,1)S(1)}, bf16[512,512]{1,0:T(8,128)(2,1)}, u32[]{:S(2)}) copy-start(bf16[512,512]{1,0:T(8,128)(2,1)} %refs_2_.1) | copy-start | bytes 1572868

commit v4 on v3

--- a/solution.py
+++ b/solution.py
@@ -12,7 +12,7 @@
 F32, BF16 = jnp.float32, jnp.bfloat16
 MIB = 1 << 20
 BLOCK = 512
-ENCODE_BLOCK = 512
+ENCODE_BLOCK = 1024
 DECODE_BLOCK = 256
 LONG = 40_000_000_000
 
@@ -55,7 +55,7 @@
     return jnp.concatenate(made, axis=0)
 
 
-def encode_kernel(parts, owner, node, grid, w1, bias, hidden, near, code, owner_v, node_v, grid_v, w1_v, bias_v, one_hot, sems):
+def encode_kernel(parts, owner, node, grid, w1, bias, hidden, near, cross, code, owner_v, node_v, grid_v, w1_v, bias_v, one_hot, sems):
     small = [(owner, owner_v), (node, node_v), (w1, w1_v), (bias, bias_v)]
     copies = [pltpu.make_async_copy(a, b, sems.at[i]) for i, (a, b) in enumerate(small)]
     starts = range(0, grid.shape[0], ENCODE_BLOCK)
@@ -63,12 +63,14 @@
         pltpu.make_async_copy(grid.at[pl.ds(r, ENCODE_BLOCK)], grid_v.at[pl.ds(r, ENCODE_BLOCK)], sems.at[4 + i])
         for i, r in enumerate(starts)
     ]
-    for copy in copies + blocks:
+    for copy in copies + blocks[:1]:
         copy.start()
     copies[0].wait()
     copies[1].wait()
+    for copy in blocks[1:]:
+        copy.start()
     code[...] = slot_codes(owner_v[...], node_v[...], parts, near.shape[0])
-    one_hot[...] = one_hot_down(code[...], 0, near.shape[0])
+    one_hot[...] = one_hot_down(code[...], 0, one_hot.shape[0])
     copies[2].wait()
     copies[3].wait()
     weights = w1_v[...] * 0.5
@@ -77,12 +79,9 @@
         copy.wait()
         spot = slice(r, r + ENCODE_BLOCK)
         hidden[spot] = silu_of_twice(dot(grid_v[spot], weights) + offset).astype(BF16)
-    near[...] = dot(one_hot[...], hidden[...]).astype(BF16)
-
-
-def cross_kernel(code, hidden, cross):
-    rows = cross.shape[0]
-    cross[...] = dot(one_hot_down(code[...], rows, rows), hidden[...]).astype(BF16)
+    rows = near.shape[0]
+    cross[...] = dot(one_hot[rows:], hidden[...]).astype(BF16)
+    near[...] = dot(one_hot[:rows], hidden[...]).astype(BF16)
 
 
 def far_kernel(code, hidden, crossed, far):
@@ -97,11 +96,9 @@
     own[...] = dot(one_hot_down(code[...], 2 * rows, rows), hidden[...])
 
 
-def prepare_kernel(after, code, edges, halo_index, fetch, gather, gather_halo, pick, lead, lead_halo):
+def prepare_kernel(after, edges, halo_index, w_out, w_mesh, gather, gather_halo, pick, lead, lead_halo, joined):
     del after
-    width = fetch.shape[1]
-    for r in range(0, fetch.shape[0], BLOCK):
-        fetch[r : r + BLOCK] = one_hot_across(code[:, r : r + BLOCK], width)
+    joined[...] = (dot(w_out[L - 1], w_mesh[...]) * 0.5).astype(BF16)
     n, own = edges.shape[1], gather.shape[1]
     border = halo_index.shape[1]
     pick[...] = one_hot_down(halo_index[...], 0, n)
@@ -132,13 +129,12 @@
         before[k * n : (k + 1) * n] = dot(gather[k * n : (k + 1) * n], source) + target
 
 
-def project_kernel(layer, latent, w_src, w_dst, bias, gather, halo, *more):
+def project_kernel(layer, latent, w_src, w_dst, bias, gather, halo, more_in, before, passed, more_out):
     source = (dot(latent[...], w_src[layer]) * 0.5).astype(BF16)
-    if len(more) > 2:
-        lead, before, passed, before_lead = more
-        own_terms(layer, halo, lead, source, w_dst, bias, before_lead)
+    if layer == L - 1:
+        more_out[...] = dot(latent[...], more_in[...]) * 0.5
     else:
-        before, passed = more
+        own_terms(layer, halo, more_in, source, w_dst, bias, more_out)
     passed[...] = halo[...]
     own_terms(layer, latent, gather, source, w_dst, bias, before)
 
@@ -150,14 +146,18 @@
     return (dot(jnp.concatenate([down, up], axis=0), w_src[layer]) * 0.5).astype(BF16)
 
 
-def updated(layer, nodes, before, gather_halo, table, w_out):
-    n = nodes.shape[0]
+def edge_sums(n, before, gather_halo, table):
     total = None
     for k in range(before.shape[0] // n):
         spot = slice(k * n, (k + 1) * n)
         message = silu_of_twice(dot(gather_halo[spot], table) + before[spot])
         total = message if total is None else total + message
-    return (nodes[...].astype(F32) + dot(total.astype(BF16), w_out[layer])).astype(BF16)
+    return total.astype(BF16)
+
+
+def updated(layer, nodes, before, gather_halo, table, w_out):
+    sums = edge_sums(nodes.shape[0], before, gather_halo, table)
+    return (nodes[...].astype(F32) + dot(sums, w_out[layer])).astype(BF16)
 
 
 def lead_kernel(layer, halo, before, across, beside, gather_halo, w_src, w_out, new_halo, table):
@@ -169,27 +169,50 @@
     new[...] = updated(layer, latent, before, gather_halo, table[...], w_out)
 
 
-def last_layer_kernel(layer, latent, before, across, beside, gather_halo, w_src, w_out, w_mesh, projected):
-    table = halo_table(layer, across, beside, w_src)
-    rows = updated(layer, latent, before, gather_halo, table, w_out)
-    projected[...] = (dot(rows, w_mesh[...]) * 0.5).astype(BF16)
-
-
-def base_kernel(grid, w_grid, fetch, own, base, passed):
+def last_layer_kernel(layer, before, across, beside, gather_halo, w_src, kept, joined, projected):
+    sums = edge_sums(kept.shape[0], before, gather_halo, halo_table(layer, across, beside, w_src))
+    projected[...] = (kept[...] + dot(sums, joined[...])).astype(BF16)
+
+
+def base_kernel(code, grid, w_grid, own, fetch, base, *pieces):
+    rows = own.shape[0]
+    cut_kernel(own, *pieces)
+    for r in range(0, grid.shape[0], BLOCK):
+        spot = slice(r, r + BLOCK)
+        fetch[spot] = one_hot_across(code[:, spot], fetch.shape[1])
+        base[spot] = dot(grid[spot], w_grid[...]) * 0.5 + dot(fetch[spot, 2 * rows : 3 * rows], own[...])
+
+
+def sibling_kernel(fetch, base, own, *refs):
+    *pieces, out, passed = refs
     rows = own.shape[0]
     passed[...] = own[...]
-    for r in range(0, grid.shape[0], BLOCK):
-        spot = slice(r, r + BLOCK)
-        base[spot] = dot(grid[spot], w_grid[...]) * 0.5 + dot(fetch[spot, 2 * rows : 3 * rows], own[...])
-
-
-def add_kernel(fetch, base, sibling, far, out, stacked):
-    rows = far.shape[0]
-    stacked[:rows] = sibling[...]
-    stacked[rows:] = far[...]
+    table = jnp.concatenate([piece[...] for piece in pieces], axis=0)
     for r in range(0, base.shape[0], BLOCK):
         spot = slice(r, r + BLOCK)
-        out[spot] = base[spot] + dot(fetch[spot, 3 * rows : 5 * rows], stacked[...])
+        out[spot] = base[spot] + dot(fetch[spot, 3 * rows : 4 * rows], table)
+
+
+def far_add_kernel(fetch, base, far, out):
+    rows = far.shape[0]
+    for r in range(0, base.shape[0], BLOCK):
+        spot = slice(r, r + BLOCK)
+        out[spot] = base[spot] + dot(fetch[spot, 4 * rows : 5 * rows], far[...])
+
+
+def cross_add_kernel(fetch, base, *refs):
+    *pieces, out = refs
+    table = jnp.concatenate([piece[...] for piece in pieces], axis=0)
+    rows = table.shape[0]
+    for r in range(0, base.shape[0], BLOCK):
+        spot = slice(r, r + BLOCK)
+        out[spot] = base[spot] + dot(fetch[spot, rows : 2 * rows], table)
+
+
+def cut_kernel(table, *pieces):
+    rows = pieces[0].shape[0]
+    for i, piece in enumerate(pieces):
+        piece[...] = table[i * rows : (i + 1) * rows]
 
 
 def pass_kernel(table, out):
@@ -198,9 +221,10 @@
 
 def decode_kernel(fetch, base, *refs):
     *tables, w_out, out, stacked, out_v, sems = refs
-    rows = tables[0].shape[0]
-    for i, table in enumerate(tables):
-        stacked[i * rows : (i + 1) * rows] = table[...]
+    low = 0
+    for table in tables:
+        stacked[low : low + table.shape[0]] = table[...]
+        low += table.shape[0]
     def halved(r):
         spot = slice(r, r + DECODE_BLOCK)
         return base[spot] + dot(fetch[spot, : stacked.shape[0]], stacked[...])
@@ -278,24 +302,23 @@
     table = ((mesh_rows, width), BF16)
     border_rows = ((border, width), BF16)
     unit = 2 * rows * width
-    hidden, near, code = call(
+    hidden, near, cross, code = call(
         part(encode_kernel, parts),
         [owner.reshape(1, rows), node.reshape(1, rows), grid, w_enc1, enc_bias.reshape(1, width)],
-        [((rows, width), BF16), table, ((1, rows), jnp.int32)],
-        unit * (width + mesh_rows),
+        [((rows, width), BF16), table, table, ((1, rows), jnp.int32)],
+        unit * (width + 2 * mesh_rows),
         [
             VM((1, rows), jnp.int32),
             VM((1, rows), jnp.int32),
             VM((rows, width), BF16),
             VM((width, width), BF16),
             VM((1, width), F32),
-            VM((mesh_rows, rows), BF16),
+            VM((2 * mesh_rows, rows), BF16),
             pltpu.SemaphoreType.DMA((4 + rows // ENCODE_BLOCK,)),
         ],
         spaces=[pltpu.HBM] * 5,
     )
     near = to_near(near)
-    (cross,) = call(cross_kernel, [code, hidden], [table], 1)
     crossed = swap(cross)
     (sent,) = call(far_kernel, [code, hidden, crossed], [table], 1)
     far = to_far(sent)
@@ -306,19 +329,19 @@
         unit * 2 * mesh_rows,
         spaces=[pl.ANY, VM, VM],
     )
-    fetch, gather, gather_halo, pick, lead, lead_halo = call(
+    gather, gather_halo, pick, lead, lead_halo, joined = call(
         prepare_kernel,
-        [near, code, edge_src.T, halo_index.reshape(1, border)],
+        [near, edge_src.T, halo_index.reshape(1, border), proc_out, dec_mesh],
         [
-            ((rows, 5 * mesh_rows), BF16),
             ((degree * mesh_rows, mesh_rows), BF16),
             ((degree * mesh_rows, 2 * border), BF16),
             ((mesh_rows, border), BF16),
             ((degree * border, mesh_rows), BF16),
             ((degree * border, 2 * border), BF16),
+            ((width, width), BF16),
         ],
         LONG,
-        spaces=[pl.ANY, VM, VM, VM],
+        spaces=[pl.ANY, VM, VM, VM, VM],
     )
     sibling = swap(sibling)
     latent, halo = call(
@@ -351,43 +374,44 @@
             1,
         )
     across = to_across(halo)
-    before, passed = call(
+    before, passed, kept = call(
         part(project_kernel, L - 1),
-        [latent, proc_src, proc_dst, proc_bias, gather, halo],
-        [edge_terms, border_rows],
+        [latent, proc_src, proc_dst, proc_bias, gather, halo, dec_mesh],
+        [edge_terms, border_rows, ((mesh_rows, width), F32)],
         1,
     )
     beside = swap(passed)
     (across,) = call(pass_kernel, [across], [border_rows], LONG)
     (projected,) = call(
         part(last_layer_kernel, L - 1),
-        [latent, before, across, beside, gather_halo, proc_src, proc_out, dec_mesh],
+        [before, across, beside, gather_halo, proc_src, kept, joined],
         [table],
         2 * mesh_rows * width * (degree * 2 * border + 2 * width),
     )
     far = to_near(projected)
     f32_rows = ((rows, width), F32)
-    base, passed = call(
+    pieces = [((mesh_rows // 2, width), BF16)] * 2
+    fetch, base, *passed = call(
         base_kernel,
-        [grid, dec_grid, fetch, projected],
-        [f32_rows, table],
+        [code, grid, dec_grid, projected],
+        [((rows, 5 * mesh_rows), BF16), f32_rows, *pieces],
         1,
     )
+    sibling = [swap(piece) for piece in passed]
+    base, passed = call(sibling_kernel, [fetch, base, projected, *sibling], [f32_rows, table], 1)
     near = to_far(passed)
-    sibling = swap(passed)
-    pair = [VM((2 * mesh_rows, width), BF16)]
-    (far,) = call(pass_kernel, [far], [table], LONG)
-    cross = swap(far)
-    (base,) = call(add_kernel, [fetch, base, sibling, far], [f32_rows], 1, pair)
-    (near,) = call(pass_kernel, [near], [table], LONG)
-    tables = [near, cross]
+    passed = call(cut_kernel, [far], pieces, 1)
+    cross = [swap(piece) for piece in passed]
+    (base,) = call(far_add_kernel, [fetch, base, far], [f32_rows], 1)
+    (base,) = call(cross_add_kernel, [fetch, base, *cross], [f32_rows], 1)
+    tables = [near]
     (out,) = call(
         decode_kernel,
         [fetch, base, *tables, dec_out],
         [((rows, width), BF16)],
         unit * (width + mesh_rows),
         [
-            VM((len(tables) * mesh_rows, width), BF16),
+            VM((mesh_rows, width), BF16),
             VM((rows, width), BF16),
             pltpu.SemaphoreType.DMA((rows // DECODE_BLOCK,)),
         ],

time: 55.1 us -> 53.9 us (0.978); the launches traced: 54.3 us -> 53.7 us
  waiting for transfers between devices: 18.2 us -> 16.9 us
  starting transfers between devices: 15.7 us -> 16.7 us
    ppermute x2, waiting for transfers between devices: 11 us -> 4.24 us  [to_near(): return lax.ppermute(value, AXES, sided(-2))]
    ppermute x2, waiting for transfers between devices: 2.97 us -> 7.47 us  [to_far(): return lax.ppermute(value, AXES, sided(2))]
    ppermute x6 -> x8, waiting for transfers between devices: 0.21 us -> 1.33 us  [swap(): return lax.ppermute(value, AXES, sided(1))]
    ppermute x6 -> x8, starting transfers between devices: 2.15 us -> 3.16 us  [swap(): return lax.ppermute(value, AXES, sided(1))]
  transfers between devices with their start and end apart: 12 -> 14, of which waited for: 6 -> 10; matrix products, arithmetic and copies ran while one was open for 0% -> 0% of each run, Pallas kernels for 18% -> 20%
where the time goes in v4:
time: 53.9 us; the launch traced here: 53.7 us
  Pallas kernels  19.6 us (36%)
  waiting for transfers between devices  16.9 us (31%)
  starting transfers between devices  16.7 us (31%)
    pallas_call x18, Pallas kernels, call(): pl.pallas_call(kernel, in_specs=[pl.BlockSpec(memory_space=space) for spa...  19.6 us
    ppermute x2, waiting for transfers between devices, to_far(): return lax.ppermute(value, AXES, sided(2))  7.47 us
    ppermute x2, starting transfers between devices, to_near(): return lax.ppermute(value, AXES, sided(-2))  7.26 us
    ppermute x2, starting transfers between devices, to_across(): return lax.ppermute(value, AXES, sided(-1))  5.56 us
    ppermute x2, waiting for transfers between devices, to_near(): return lax.ppermute(value, AXES, sided(-2))  4.24 us
    ppermute x2, waiting for transfers between devices, to_across(): return lax.ppermute(value, AXES, sided(-1))  3.85 us
    ppermute x8, starting transfers between devices, swap(): return lax.ppermute(value, AXES, sided(1))  3.16 us
    ppermute x8, waiting for transfers between devices, swap(): return lax.ppermute(value, AXES, sided(1))  1.33 us
  transfers between devices with their start and end apart: 14, of which 10 were waited for; matrix products, arithmetic and copies ran while one was open for 0% of the time, Pallas kernels for 20%

profile of v4, /device:TPU:0, one launch (start us, length us, event | category | flops | bytes accessed | tf_op | source)
XLA Modules:
  0.0 53.7 jit_solution(16545646247656939214)
XLA Ops:
  0.0 4.1 %shard_map.154 = (bf16[2048,512]{1,0:T(8,128)(2,1)S(1)}, bf16[256,512]{1,0:T(8,128)(2,1)S(1)}, bf16[256,512]{1,0:T(8,128)(2,1)S(1)}, s32[1,2048]{1,0:T(1,128)S(1)}) custom-call(s32[1,2048]{1,0:T(1,128)} %bitcast.7, s32[1,2048]{1,0:T(1,128)} %bitcast.8, bf16[2048,512]{1,0:T(8,128)(2,1)} %grid.3, bf16[512,512]{1,0:T(8,128)(2,1)} %w1.1, f32[1,512]{1,0:T(1,128)} %bitcast.9), custom_call_target="tpu_custom_call" | custom-call | flops 2147483648 | bytes 2639872 | tf_op jit(solution)/shard_map/pallas_call | solution.py:251
  4.1 0.5 collective-permute-start
  4.7 5.6 %collective-permute-start.2 = (bf16[256,512]{1,0:T(8,128)(2,1)S(1)}, bf16[256,512]{1,0:T(8,128)(2,1)S(1)}, u32[]{:S(2)}, u32[]{:S(2)}) collective-permute-start(bf16[256,512]{1,0:T(8,128)(2,1)S(1)} %get-tuple-element.40), channel_id=1, source_target_pairs={{0,14},{1,3},{2,0},{3,5},{4,2},{5,7},{6,4},{7,9},{8,6},{9,11},{10,... | collective-permute-start | bytes 786440 | tf_op jit(solution)/shard_map/ppermute | solution.py:297
  10.3 0.7 %shard_map.155.after = bf16[256,512]{1,0:T(8,128)(2,1)S(1)} custom-call(s32[1,2048]{1,0:T(1,128)S(1)} %get-tuple-element.35.code, bf16[2048,512]{1,0:T(8,128)(2,1)S(1)} %get-tuple-element.36.hidden, bf16[256,512]{1,0:T(8,128)(2,1)S(1)} %collective-permute-done.crossed), custom_call_target="tpu_custom_call" | custom-call | flops 1 | bytes 1 | tf_op jit(solution)/shard_map/pallas_call | solution.py:251
  11.1 1.2 %shard_map.156 = (f32[256,512]{1,0:T(8,128)S(1)}, bf16[256,512]{1,0:T(8,128)(2,1)S(1)}) custom-call(bf16[256,512]{1,0:T(8,128)(2,1)S(1)} %shard_map.155.after, s32[1,2048]{1,0:T(1,128)S(1)} %get-tuple-element.35.code, bf16[2048,512]{1,0:T(8,128)(2,1)S(1)} %get-tuple-element.36.hidden), custom_call_target="tpu_custom_call" | custom-call | flops 1073741824 | bytes 2367488 | tf_op jit(solution)/shard_map/pallas_call | solution.py:251
  12.3 1.4 %collective-permute-start.1 = (bf16[256,512]{1,0:T(8,128)(2,1)S(1)}, bf16[256,512]{1,0:T(8,128)(2,1)S(1)}, u32[]{:S(2)}, u32[]{:S(2)}) collective-permute-start(bf16[256,512]{1,0:T(8,128)(2,1)S(1)} %get-tuple-element.39), channel_id=1, source_target_pairs={{0,1},{1,0},{2,3},{3,2},{4,5},{5,4},{6,7},{7,6},{8,9},{9,8},{10,11... | collective-permute-start | bytes 786440 | tf_op jit(solution)/shard_map/ppermute | solution.py:291
  13.7 1.8 %collective-permute-done.2.after.near = bf16[256,512]{1,0:T(8,128)(2,1)S(1)} collective-permute-done((bf16[256,512]{1,0:T(8,128)(2,1)S(1)}, bf16[256,512]{1,0:T(8,128)(2,1)S(1)}, u32[]{:S(2)}, u32[]{:S(2)}) %collective-permute-start.2) | collective-permute-done | bytes 262176 | tf_op jit(solution)/shard_map/ppermute | solution.py:297
  15.6 0.8 %shard_map.157 = (bf16[1536,256]{1,0:T(8,128)(2,1)S(1)}, bf16[1536,128]{1,0:T(8,128)(2,1)S(1)}, bf16[256,64]{1,0:T(8,128)(2,1)S(1)}, bf16[384,256]{1,0:T(8,128)(...) custom-call(bf16[256,512]{1,0:T(8,128)(2,1)S(1)} %collective-permute-done.2.after.near, ...), custom_call_target="tpu_custom_call" | custom-call | flops 40000000000 | bytes 1841408 | tf_op jit(solution)/shard_map/pallas_call | solution.py:251
  16.4 3.7 %collective-permute-done.3.far = bf16[256,512]{1,0:T(8,128)(2,1)S(1)} collective-permute-done((bf16[256,512]{1,0:T(8,128)(2,1)S(1)}, bf16[256,512]{1,0:T(8,128)(2,1)S(1)}, u32[]{:S(2)}, u32[]{:S(2)}) %collective-permute-start.3) | collective-permute-done | bytes 262176 | tf_op jit(solution)/shard_map/ppermute | solution.py:300
  20.1 0.4 shard_map.158
  20.6 2.8 %collective-permute-start.4 = (bf16[64,512]{1,0:T(8,128)(2,1)S(1)}, bf16[64,512]{1,0:T(8,128)(2,1)S(1)}, u32[]{:S(2)}, u32[]{:S(2)}) collective-permute-start(bf16[64,512]{1,0:T(8,128)(2,1)S(1)} %get-tuple-element.44.halo), channel_id=1, source_target_pairs={{0,15},{1,2},{2,1},{3,4},{4,3},{5,6},{6,5},{7,8},{8,7},{9,10},{10,... | collective-permute-start | bytes 196616 | tf_op jit(solution)/shard_map/ppermute | solution.py:294
  23.4 1.3 %shard_map.159 = (f32[1536,512]{1,0:T(8,128)S(1)}, bf16[64,512]{1,0:T(8,128)(2,1)S(1)}, f32[384,512]{1,0:T(8,128)S(1)}) custom-call(bf16[256,512]{1,0:T(8,128)(2,1)S(1)} %get-tuple-element.42.latent, bf16[2,512,512]{2,1,0:T(8,128)(2,1)S(1)} %copy-done, bf16[2,512,512]{2,1,0:T(8,128)(2,1)S(1)} %copy-done.2, f32[2,512]{1,0:T(2,128)S(1)} %copy-done.9, ...), custom_call_target="tpu_custom_call" | custom-call | flops 1 | bytes 1 | tf_op jit(solution)/shard_map/pallas_call | solution.py:251
  24.7 2.3 %collective-permute-done.4.table = bf16[64,512]{1,0:T(8,128)(2,1)S(1)} collective-permute-done((bf16[64,512]{1,0:T(8,128)(2,1)S(1)}, bf16[64,512]{1,0:T(8,128)(2,1)S(1)}, u32[]{:S(2)}, u32[]{:S(2)}) %collective-permute-start.4) | collective-permute-done | bytes 65568 | tf_op jit(solution)/shard_map/ppermute | solution.py:294
  27.0 0.7 %shard_map.161 = (bf16[64,512]{1,0:T(8,128)(2,1)S(1)}, bf16[128,512]{1,0:T(8,128)(2,1)S(1)}) custom-call(bf16[64,512]{1,0:T(8,128)(2,1)S(1)} %get-tuple-element.44.halo, f32[384,512]{1,0:T(8,128)S(1)} %get-tuple-element.47.before, bf16[64,512]{1,0:T(8,128)(2,1)S(1)} %shard_map.160.across, bf16[64,512]{1,0:T(8,128)(2,1)S(1)} %collective-permute-done.5.beside, ...), custom_call_target="tpu_custom_call" | custom-call | flops 150994944 | bytes 3178496 | tf_op jit(solution)/shard_map/pallas_call | solution.py:251
  27.7 2.8 %collective-permute-start.6 = (bf16[64,512]{1,0:T(8,128)(2,1)S(1)}, bf16[64,512]{1,0:T(8,128)(2,1)S(1)}, u32[]{:S(2)}, u32[]{:S(2)}) collective-permute-start(bf16[64,512]{1,0:T(8,128)(2,1)S(1)} %get-tuple-element.52.halo), channel_id=1, source_target_pairs={{0,15},{1,2},{2,1},{3,4},{4,3},{5,6},{6,5},{7,8},{8,7},{9,10},{10,... | collective-permute-start | bytes 196616 | tf_op jit(solution)/shard_map/ppermute | solution.py:294
  30.5 1.0 %shard_map.162.latent = bf16[256,512]{1,0:T(8,128)(2,1)S(1)} custom-call(bf16[256,512]{1,0:T(8,128)(2,1)S(1)} %get-tuple-element.42.latent, f32[1536,512]{1,0:T(8,128)S(1)} %get-tuple-element.46.before, bf16[128,512]{1,0:T(8,128)(2,1)S(1)} %get-tuple-element.50.table, bf16[1536,128]{1,0:T(8,128)(2,1)S(1)} %get-tuple-element.51.gather_halo, ...), custom_call_target="tpu_custom_call" | custom-call | flops 1 | bytes 1 | tf_op jit(solution)/shard_map/pallas_call | solution.py:251
  31.5 1.0 %shard_map.163 = (f32[1536,512]{1,0:T(8,128)S(1)}, bf16[64,512]{1,0:T(8,128)(2,1)S(1)}, f32[256,512]{1,0:T(8,128)S(1)}) custom-call(bf16[256,512]{1,0:T(8,128)(2,1)S(1)} %shard_map.162.latent, bf16[2,512,512]{2,1,0:T(8,128)(2,1)S(1)} %copy-done, bf16[2,512,512]{2,1,0:T(8,128)(2,1)S(1)} %copy-done.2, f32[2,512]{1,0:T(2,128)S(1)} %copy-done.9, ...), custom_call_target="tpu_custom_call" | custom-call | flops 1 | bytes 1 | tf_op jit(solution)/shard_map/pallas_call | solution.py:251
  32.6 1.6 %collective-permute-done.6.table = bf16[64,512]{1,0:T(8,128)(2,1)S(1)} collective-permute-done((bf16[64,512]{1,0:T(8,128)(2,1)S(1)}, bf16[64,512]{1,0:T(8,128)(2,1)S(1)}, u32[]{:S(2)}, u32[]{:S(2)}) %collective-permute-start.6) | collective-permute-done | bytes 65568 | tf_op jit(solution)/shard_map/ppermute | solution.py:294
  34.2 1.2 %shard_map.165.own = bf16[256,512]{1,0:T(8,128)(2,1)S(1)} custom-call(f32[1536,512]{1,0:T(8,128)S(1)} %get-tuple-element.53.before, bf16[64,512]{1,0:T(8,128)(2,1)S(1)} %shard_map.164.across, bf16[64,512]{1,0:T(8,128)(2,1)S(1)} %collective-permute-done.7.beside, bf16[1536,128]{1,0:T(8,128)(2,1)S(1)} %get-tuple-element.51.gather_halo, ...), custom_call_target="tpu_custom_call" | custom-call | flops 469762048 | bytes 5767168 | tf_op jit(solution)/shard_map/pallas_call | solution.py:251
  35.4 1.7 %collective-permute-start.10 = (bf16[256,512]{1,0:T(8,128)(2,1)S(1)}, bf16[256,512]{1,0:T(8,128)(2,1)S(1)}, u32[]{:S(2)}, u32[]{:S(2)}) collective-permute-start(bf16[256,512]{1,0:T(8,128)(2,1)S(1)} %shard_map.165.own), channel_id=1, source_target_pairs={{0,14},{1,3},{2,0},{3,5},{4,2},{5,7},{6,4},{7,9},{8,6},{9,11},{10,... | collective-permute-start | bytes 786440 | tf_op jit(solution)/shard_map/ppermute | solution.py:297
  37.1 2.3 %shard_map.166 = (bf16[2048,1280]{1,0:T(8,128)(2,1)S(1)}, f32[2048,512]{1,0:T(8,128)S(1)}, bf16[128,512]{1,0:T(8,128)(2,1)S(1)}, bf16[128,512]{1,0:T(8,128)(2,1)S(1)}) custom-call(s32[1,2048]{1,0:T(1,128)S(1)} %get-tuple-element.35.code, bf16[2048,512]{1,0:T(8,128)(2,1)S(1)} %copy-done.3, bf16[512,512]{1,0:T(8,128)(2,1)S(1)} %copy-done.7, ...), custom_call_target="tpu_custom_call" | custom-call | flops 1 | bytes 1 | tf_op jit(solution)/shard_map/pallas_call | solution.py:251
  39.5 0.5 collective-permute-start.9
  40.0 0.8 %collective-permute-done.8.refs_0_ = bf16[128,512]{1,0:T(8,128)(2,1)S(1)} collective-permute-done((bf16[128,512]{1,0:T(8,128)(2,1)S(1)}, bf16[128,512]{1,0:T(8,128)(2,1)S(1)}, u32[]{:S(2)}, u32[]{:S(2)}) %collective-permute-start.8) | collective-permute-done | bytes 131104 | tf_op jit(solution)/shard_map/ppermute | solution.py:291
  40.9 0.2 collective-permute-done.9.refs_1_
  41.0 0.7 %shard_map.167 = (f32[2048,512]{1,0:T(8,128)S(1)}, bf16[256,512]{1,0:T(8,128)(2,1)S(1)}) custom-call(bf16[2048,1280]{1,0:T(8,128)(2,1)S(1)} %get-tuple-element.57.fetch, f32[2048,512]{1,0:T(8,128)S(1)} %get-tuple-element.58.base, bf16[256,512]{1,0:T(8,128)(2,1)S(1)} %shard_map.165.own, bf16[128,512]{1,0:T(8,128)(2,1)S(1)} %collective-permute-done.8.refs_0_, ...), custom_call_target="tpu_custom_call" | custom-call | flops 1 | bytes 1 | tf_op jit(solution)/shard_map/pallas_call | solution.py:251
  41.8 0.7 %collective-permute-start.13 = (bf16[256,512]{1,0:T(8,128)(2,1)S(1)}, bf16[256,512]{1,0:T(8,128)(2,1)S(1)}, u32[]{:S(2)}, u32[]{:S(2)}) collective-permute-start(bf16[256,512]{1,0:T(8,128)(2,1)S(1)} %get-tuple-element.64), channel_id=1, source_target_pairs={{0,2},{1,15},{2,4},{3,1},{4,6},{5,3},{6,8},{7,5},{8,10},{9,7},{10,... | collective-permute-start | bytes 786440 | tf_op jit(solution)/shard_map/ppermute | solution.py:300
  42.5 2.4 %collective-permute-done.10.far.table = bf16[256,512]{1,0:T(8,128)(2,1)S(1)} collective-permute-done((bf16[256,512]{1,0:T(8,128)(2,1)S(1)}, bf16[256,512]{1,0:T(8,128)(2,1)S(1)}, u32[]{:S(2)}, u32[]{:S(2)}) %collective-permute-start.10) | collective-permute-done | bytes 262176 | tf_op jit(solution)/shard_map/ppermute | solution.py:297
  45.0 0.5 collective-permute-start.12
  45.5 0.7 %shard_map.168.base = f32[2048,512]{1,0:T(8,128)S(1)} custom-call(bf16[2048,1280]{1,0:T(8,128)(2,1)S(1)} %get-tuple-element.57.fetch, f32[2048,512]{1,0:T(8,128)S(1)} %get-tuple-element.61.base, bf16[256,512]{1,0:T(8,128)(2,1)S(1)} %collective-permute-done.10.far.table), custom_call_target="tpu_custom_call" | custom-call | flops 1 | bytes 1 | tf_op jit(solution)/shard_map/pallas_call | solution.py:251
  46.5 0.7 %shard_map.170.base = f32[2048,512]{1,0:T(8,128)S(1)} custom-call(bf16[2048,1280]{1,0:T(8,128)(2,1)S(1)} %get-tuple-element.57.fetch, f32[2048,512]{1,0:T(8,128)S(1)} %shard_map.168.base, bf16[128,512]{1,0:T(8,128)(2,1)S(1)} %collective-permute-done.11.refs_0_, bf16[128,512]{1,0:T(8,128)(2,1)S(1)} %collective-permute-done.12.refs_1_), custom_call_target="tpu_custom_call" | custom-call | flops 1 | bytes 1 | tf_op jit(solution)/shard_map/pallas_call | solution.py:251
  47.2 3.7 %collective-permute-done.13.refs_0_ = bf16[256,512]{1,0:T(8,128)(2,1)S(1)} collective-permute-done((bf16[256,512]{1,0:T(8,128)(2,1)S(1)}, bf16[256,512]{1,0:T(8,128)(2,1)S(1)}, u32[]{:S(2)}, u32[]{:S(2)}) %collective-permute-start.13) | collective-permute-done | bytes 262176 | tf_op jit(solution)/shard_map/ppermute | solution.py:300
  50.9 2.6 %shard_map.171 = bf16[2048,512]{1,0:T(8,128)(2,1)} custom-call(bf16[2048,1280]{1,0:T(8,128)(2,1)S(1)} %get-tuple-element.57.fetch, f32[2048,512]{1,0:T(8,128)S(1)} %shard_map.170.base, bf16[256,512]{1,0:T(8,128)(2,1)S(1)} %collective-permute-done.13.refs_0_, bf16[512,512]{1,0:T(8,128)(2,1)S(1)} %copy-done.4), custom_call_target="tpu_custom_call" | custom-call | flops 1610612736 | bytes 10223616 | tf_op jit(solution)/shard_map/pallas_call | solution.py:251
  (38 shorter events, 0.8 us)
Async XLA Ops:
  4.1 11.4 %copy-start.1 = (bf16[2,512,512]{2,1,0:T(8,128)(2,1)S(1)}, bf16[2,512,512]{2,1,0:T(8,128)(2,1)}, u32[]{:S(2)}) copy-start(bf16[2,512,512]{2,1,0:T(8,128)(2,1)} %w_out.5) | copy-start | bytes 3145732
  4.1 11.4 %copy-start.6 = (bf16[512,512]{1,0:T(8,128)(2,1)S(1)}, bf16[512,512]{1,0:T(8,128)(2,1)}, u32[]{:S(2)}) copy-start(bf16[512,512]{1,0:T(8,128)(2,1)} %more_in.1) | copy-start | bytes 1572868
  4.1 11.4 %copy-start.10 = (s32[256,6]{0,1:T(8,128)S(1)}, s32[256,6]{0,1:T(8,128)}, u32[]{:S(2)}) copy-start(s32[256,6]{0,1:T(8,128)} %param.21) | copy-start | bytes 18436
  4.1 11.4 %copy-start.11 = (s32[64]{0:T(128)S(1)}, s32[64]{0:T(128)}, u32[]{:S(2)}) copy-start(s32[64]{0:T(128)} %param.20) | copy-start | bytes 772
  4.1 6.1 %collective-permute-start = (bf16[256,512]{1,0:T(8,128)(2,1)S(1)}, bf16[256,512]{1,0:T(8,128)(2,1)S(1)}, u32[]{:S(2)}, u32[]{:S(2)}) collective-permute-start(bf16[256,512]{1,0:T(8,128)(2,1)S(1)} %get-tuple-element.37), channel_id=1, source_target_pairs={{0,1},{1,0},{2,3},{3,2},{4,5},{5,4},{6,7},{7,6},{8,9},{9,8},{10,11... | collective-permute-start | bytes 786440 | tf_op jit(solution)/shard_map/ppermute | solution.py:291
  4.7 10.9 %collective-permute-start.2 = (bf16[256,512]{1,0:T(8,128)(2,1)S(1)}, bf16[256,512]{1,0:T(8,128)(2,1)S(1)}, u32[]{:S(2)}, u32[]{:S(2)}) collective-permute-start(bf16[256,512]{1,0:T(8,128)(2,1)S(1)} %get-tuple-element.40), channel_id=1, source_target_pairs={{0,14},{1,3},{2,0},{3,5},{4,2},{5,7},{6,4},{7,9},{8,6},{9,11},{10,... | collective-permute-start | bytes 786440 | tf_op jit(solution)/shard_map/ppermute | solution.py:297
  11.0 9.1 %collective-permute-start.3 = (bf16[256,512]{1,0:T(8,128)(2,1)S(1)}, bf16[256,512]{1,0:T(8,128)(2,1)S(1)}, u32[]{:S(2)}, u32[]{:S(2)}) collective-permute-start(bf16[256,512]{1,0:T(8,128)(2,1)S(1)} %shard_map.155.after), channel_id=1, source_target_pairs={{0,2},{1,15},{2,4},{3,1},{4,6},{5,3},{6,8},{7,5},{8,10},{9,7},{10,... | collective-permute-start | bytes 786440 | tf_op jit(solution)/shard_map/ppermute | solution.py:300
  12.3 4.1 %collective-permute-start.1 = (bf16[256,512]{1,0:T(8,128)(2,1)S(1)}, bf16[256,512]{1,0:T(8,128)(2,1)S(1)}, u32[]{:S(2)}, u32[]{:S(2)}) collective-permute-start(bf16[256,512]{1,0:T(8,128)(2,1)S(1)} %get-tuple-element.39), channel_id=1, source_target_pairs={{0,1},{1,0},{2,3},{3,2},{4,5},{5,4},{6,7},{7,6},{8,9},{9,8},{10,11... | collective-permute-start | bytes 786440 | tf_op jit(solution)/shard_map/ppermute | solution.py:291
  15.5 4.6 %copy-start.5 = (bf16[512,512]{1,0:T(8,128)(2,1)S(1)}, bf16[512,512]{1,0:T(8,128)(2,1)}, u32[]{:S(2)}) copy-start(bf16[512,512]{1,0:T(8,128)(2,1)} %w2.1) | copy-start | bytes 1572868
  15.5 4.6 %copy-start.8 = (bf16[256,512]{1,0:T(8,128)(2,1)S(1)}, bf16[256,512]{1,0:T(8,128)(2,1)}, u32[]{:S(2)}) copy-start(bf16[256,512]{1,0:T(8,128)(2,1)} %mesh.1) | copy-start | bytes 786436
  15.6 7.8 %copy-start = (bf16[2,512,512]{2,1,0:T(8,128)(2,1)S(1)}, bf16[2,512,512]{2,1,0:T(8,128)(2,1)}, u32[]{:S(2)}) copy-start(bf16[2,512,512]{2,1,0:T(8,128)(2,1)} %w_src.7) | copy-start | bytes 3145732
  15.6 7.8 %copy-start.2 = (bf16[2,512,512]{2,1,0:T(8,128)(2,1)S(1)}, bf16[2,512,512]{2,1,0:T(8,128)(2,1)}, u32[]{:S(2)}) copy-start(bf16[2,512,512]{2,1,0:T(8,128)(2,1)} %w_dst.3) | copy-start | bytes 3145732
  15.6 7.8 %copy-start.9 = (f32[2,512]{1,0:T(2,128)S(1)}, f32[2,512]{1,0:T(2,128)}, u32[]{:S(2)}) copy-start(f32[2,512]{1,0:T(2,128)} %bias.3) | copy-start | bytes 12292
  20.6 6.5 %collective-permute-start.4 = (bf16[64,512]{1,0:T(8,128)(2,1)S(1)}, bf16[64,512]{1,0:T(8,128)(2,1)S(1)}, u32[]{:S(2)}, u32[]{:S(2)}) collective-permute-start(bf16[64,512]{1,0:T(8,128)(2,1)S(1)} %get-tuple-element.44.halo), channel_id=1, source_target_pairs={{0,15},{1,2},{2,1},{3,4},{4,3},{5,6},{6,5},{7,8},{8,7},{9,10},{10,... | collective-permute-start | bytes 196616 | tf_op jit(solution)/shard_map/ppermute | solution.py:294
  24.7 2.4 %collective-permute-start.5 = (bf16[64,512]{1,0:T(8,128)(2,1)S(1)}, bf16[64,512]{1,0:T(8,128)(2,1)S(1)}, u32[]{:S(2)}, u32[]{:S(2)}) collective-permute-start(bf16[64,512]{1,0:T(8,128)(2,1)S(1)} %get-tuple-element.48), channel_id=1, source_target_pairs={{0,1},{1,0},{2,3},{3,2},{4,5},{5,4},{6,7},{7,6},{8,9},{9,8},{10,11... | collective-permute-start | bytes 196616 | tf_op jit(solution)/shard_map/ppermute | solution.py:291
  27.7 6.5 %collective-permute-start.6 = (bf16[64,512]{1,0:T(8,128)(2,1)S(1)}, bf16[64,512]{1,0:T(8,128)(2,1)S(1)}, u32[]{:S(2)}, u32[]{:S(2)}) collective-permute-start(bf16[64,512]{1,0:T(8,128)(2,1)S(1)} %get-tuple-element.52.halo), channel_id=1, source_target_pairs={{0,15},{1,2},{2,1},{3,4},{4,3},{5,6},{6,5},{7,8},{8,7},{9,10},{10,... | collective-permute-start | bytes 196616 | tf_op jit(solution)/shard_map/ppermute | solution.py:294
  32.5 1.7 %collective-permute-start.7 = (bf16[64,512]{1,0:T(8,128)(2,1)S(1)}, bf16[64,512]{1,0:T(8,128)(2,1)S(1)}, u32[]{:S(2)}, u32[]{:S(2)}) collective-permute-start(bf16[64,512]{1,0:T(8,128)(2,1)S(1)} %get-tuple-element.54), channel_id=1, source_target_pairs={{0,1},{1,0},{2,3},{3,2},{4,5},{5,4},{6,7},{7,6},{8,9},{9,8},{10,11... | collective-permute-start | bytes 196616 | tf_op jit(solution)/shard_map/ppermute | solution.py:291
  34.2 2.9 %copy-start.3 = (bf16[2048,512]{1,0:T(8,128)(2,1)S(1)}, bf16[2048,512]{1,0:T(8,128)(2,1)}, u32[]{:S(2)}) copy-start(bf16[2048,512]{1,0:T(8,128)(2,1)} %grid.3) | copy-start | bytes 6291460
  34.2 2.9 %copy-start.7 = (bf16[512,512]{1,0:T(8,128)(2,1)S(1)}, bf16[512,512]{1,0:T(8,128)(2,1)}, u32[]{:S(2)}) copy-start(bf16[512,512]{1,0:T(8,128)(2,1)} %w_grid.1) | copy-start | bytes 1572868
  35.4 9.4 %collective-permute-start.10 = (bf16[256,512]{1,0:T(8,128)(2,1)S(1)}, bf16[256,512]{1,0:T(8,128)(2,1)S(1)}, u32[]{:S(2)}, u32[]{:S(2)}) collective-permute-start(bf16[256,512]{1,0:T(8,128)(2,1)S(1)} %shard_map.165.own), channel_id=1, source_target_pairs={{0,14},{1,3},{2,0},{3,5},{4,2},{5,7},{6,4},{7,9},{8,6},{9,11},{10,... | collective-permute-start | bytes 786440 | tf_op jit(solution)/shard_map/ppermute | solution.py:297
  39.4 1.4 %collective-permute-start.8 = (bf16[128,512]{1,0:T(8,128)(2,1)S(1)}, bf16[128,512]{1,0:T(8,128)(2,1)S(1)}, u32[]{:S(2)}, u32[]{:S(2)}) collective-permute-start(bf16[128,512]{1,0:T(8,128)(2,1)S(1)} %get-tuple-element.59), channel_id=1, source_target_pairs={{0,1},{1,0},{2,3},{3,2},{4,5},{5,4},{6,7},{7,6},{8,9},{9,8},{10,11... | collective-permute-start | bytes 393224 | tf_op jit(solution)/shard_map/ppermute | solution.py:291
  39.5 1.5 %collective-permute-start.9 = (bf16[128,512]{1,0:T(8,128)(2,1)S(1)}, bf16[128,512]{1,0:T(8,128)(2,1)S(1)}, u32[]{:S(2)}, u32[]{:S(2)}) collective-permute-start(bf16[128,512]{1,0:T(8,128)(2,1)S(1)} %get-tuple-element.60), channel_id=1, source_target_pairs={{0,1},{1,0},{2,3},{3,2},{4,5},{5,4},{6,7},{7,6},{8,9},{9,8},{10,11... | collective-permute-start | bytes 393224 | tf_op jit(solution)/shard_map/ppermute | solution.py:291
  41.8 9.1 %collective-permute-start.13 = (bf16[256,512]{1,0:T(8,128)(2,1)S(1)}, bf16[256,512]{1,0:T(8,128)(2,1)S(1)}, u32[]{:S(2)}, u32[]{:S(2)}) collective-permute-start(bf16[256,512]{1,0:T(8,128)(2,1)S(1)} %get-tuple-element.64), channel_id=1, source_target_pairs={{0,2},{1,15},{2,4},{3,1},{4,6},{5,3},{6,8},{7,5},{8,10},{9,7},{10,... | collective-permute-start | bytes 786440 | tf_op jit(solution)/shard_map/ppermute | solution.py:300
  44.9 1.4 %collective-permute-start.11 = (bf16[128,512]{1,0:T(8,128)(2,1)S(1)}, bf16[128,512]{1,0:T(8,128)(2,1)S(1)}, u32[]{:S(2)}, u32[]{:S(2)}) collective-permute-start(bf16[128,512]{1,0:T(8,128)(2,1)S(1)} %get-tuple-element.62), channel_id=1, source_target_pairs={{0,1},{1,0},{2,3},{3,2},{4,5},{5,4},{6,7},{7,6},{8,9},{9,8},{10,11... | collective-permute-start | bytes 393224 | tf_op jit(solution)/shard_map/ppermute | solution.py:291
  45.0 1.5 %collective-permute-start.12 = (bf16[128,512]{1,0:T(8,128)(2,1)S(1)}, bf16[128,512]{1,0:T(8,128)(2,1)S(1)}, u32[]{:S(2)}, u32[]{:S(2)}) collective-permute-start(bf16[128,512]{1,0:T(8,128)(2,1)S(1)} %get-tuple-element.63), channel_id=1, source_target_pairs={{0,1},{1,0},{2,3},{3,2},{4,5},{5,4},{6,7},{7,6},{8,9},{9,8},{10,11... | collective-permute-start | bytes 393224 | tf_op jit(solution)/shard_map/ppermute | solution.py:291
  46.2 4.8 %copy-start.4 = (bf16[512,512]{1,0:T(8,128)(2,1)S(1)}, bf16[512,512]{1,0:T(8,128)(2,1)}, u32[]{:S(2)}) copy-start(bf16[512,512]{1,0:T(8,128)(2,1)} %refs_1_.1) | copy-start | bytes 1572868

commit v5 on v4

--- a/solution.py
+++ b/solution.py
@@ -184,9 +184,10 @@
 
 
 def sibling_kernel(fetch, base, own, *refs):
-    *pieces, out, passed = refs
-    rows = own.shape[0]
-    passed[...] = own[...]
+    *pieces, out, left, right = refs
+    rows, half = left.shape
+    left[...] = own[:, :half]
+    right[...] = own[:, half:]
     table = jnp.concatenate([piece[...] for piece in pieces], axis=0)
     for r in range(0, base.shape[0], BLOCK):
         spot = slice(r, r + BLOCK)
@@ -219,24 +220,45 @@
     out[...] = table[...]
 
 
-def decode_kernel(fetch, base, *refs):
-    *tables, w_out, out, stacked, out_v, sems = refs
-    low = 0
-    for table in tables:
-        stacked[low : low + table.shape[0]] = table[...]
-        low += table.shape[0]
+def ahead_of(block, starts, halved, finish):
+    half = halved(0)
+    for r in starts:
+        ahead = halved(r + block) if r + block <= starts[-1] else None
+        finish(r, silu_of_twice(half).astype(BF16))
+        half = ahead
+
+
+def decode_left_kernel(fetch, base, near, w_out, partial):
+    rows, width = near.shape
+    starts = range(0, base.shape[0], DECODE_BLOCK)
+
     def halved(r):
         spot = slice(r, r + DECODE_BLOCK)
-        return base[spot] + dot(fetch[spot, : stacked.shape[0]], stacked[...])
-
+        return base[spot, :width] + dot(fetch[spot, :rows], near[...])
+
+    def finish(r, hidden):
+        partial[r : r + DECODE_BLOCK] = dot(hidden, w_out[:width])
+
+    ahead_of(DECODE_BLOCK, starts, halved, finish)
+
+
+def decode_kernel(fetch, base, near, w_out, partial, out, out_v, sems):
+    rows, width = near.shape
+    starts = range(0, base.shape[0], DECODE_BLOCK)
     copies = []
-    half = halved(0)
-    for i, r in enumerate(range(0, base.shape[0], DECODE_BLOCK)):
-        ahead = halved(r + DECODE_BLOCK) if r + DECODE_BLOCK < base.shape[0] else None
-        out_v[r : r + DECODE_BLOCK] = dot(silu_of_twice(half).astype(BF16), w_out[...]).astype(BF16)
-        half = ahead
-        copies.append(pltpu.make_async_copy(out_v.at[pl.ds(r, DECODE_BLOCK)], out.at[pl.ds(r, DECODE_BLOCK)], sems.at[i]))
+
+    def halved(r):
+        spot = slice(r, r + DECODE_BLOCK)
+        return base[spot, width:] + dot(fetch[spot, :rows], near[...])
+
+    def finish(r, hidden):
+        spot = slice(r, r + DECODE_BLOCK)
+        out_v[spot] = (partial[spot] + dot(hidden, w_out[width:])).astype(BF16)
+        place = pl.ds(r, DECODE_BLOCK)
+        copies.append(pltpu.make_async_copy(out_v.at[place], out.at[place], sems.at[len(copies)]))
         copies[-1].start()
+
+    ahead_of(DECODE_BLOCK, starts, halved, finish)
     for copy in copies:
         copy.wait()
 
@@ -398,23 +420,21 @@
         1,
     )
     sibling = [swap(piece) for piece in passed]
-    base, passed = call(sibling_kernel, [fetch, base, projected, *sibling], [f32_rows, table], 1)
-    near = to_far(passed)
-    passed = call(cut_kernel, [far], pieces, 1)
+    half = ((mesh_rows, width // 2), BF16)
+    base, left, right = call(sibling_kernel, [fetch, base, projected, *sibling], [f32_rows, half, half], 1)
+    left = to_far(left)
+    right = to_far(right)
+    passed = call(cut_kernel, [far], [((mesh_rows // 8, width), BF16)] * 8, 1)
     cross = [swap(piece) for piece in passed]
     (base,) = call(far_add_kernel, [fetch, base, far], [f32_rows], 1)
     (base,) = call(cross_add_kernel, [fetch, base, *cross], [f32_rows], 1)
-    tables = [near]
+    (partial,) = call(decode_left_kernel, [fetch, base, left, dec_out], [f32_rows], 1)
     (out,) = call(
         decode_kernel,
-        [fetch, base, *tables, dec_out],
+        [fetch, base, right, dec_out, partial],
         [((rows, width), BF16)],
         unit * (width + mesh_rows),
-        [
-            VM((mesh_rows, width), BF16),
-            VM((rows, width), BF16),
-            pltpu.SemaphoreType.DMA((rows // DECODE_BLOCK,)),
-        ],
+        [VM((rows, width), BF16), pltpu.SemaphoreType.DMA((rows // DECODE_BLOCK,))],
         out_space=pltpu.HBM,
     )
     return out

time: 53.9 us -> 53.2 us (0.987)
  waiting for transfers between devices: 16.9 us -> 14.3 us
  starting transfers between devices: 16.7 us -> 18.1 us
    ppermute x2 -> x3, waiting for transfers between devices: 7.47 us -> 3.87 us  [to_far(): return lax.ppermute(value, AXES, sided(2))]
    ppermute x8 -> x14, starting transfers between devices: 3.16 us -> 4.43 us  [swap(): return lax.ppermute(value, AXES, sided(1))]
    ppermute x8 -> x14, waiting for transfers between devices: 1.33 us -> 2.3 us  [swap(): return lax.ppermute(value, AXES, sided(1))]
    pallas_call x18 -> x19, Pallas kernels: 19.6 us -> 19.9 us  [call(): pl.pallas_call(kernel, in_specs=[pl.BlockSpec(memory_space=space) for spa...]
  transfers between devices with their start and end apart: 14 -> 21, of which waited for: 10 -> 11; matrix products, arithmetic and copies ran while one was open for 0% -> 0% of each run, Pallas kernels for 20% -> 22%
where the time goes in v5:
time: 53.2 us; the launch traced here: 53 us
  Pallas kernels  19.9 us (37%)
  starting transfers between devices  18.1 us (34%)
  waiting for transfers between devices  14.3 us (27%)
    pallas_call x19, Pallas kernels, call(): pl.pallas_call(kernel, in_specs=[pl.BlockSpec(memory_space=space) for spa...  19.9 us
    ppermute x2, starting transfers between devices, to_near(): return lax.ppermute(value, AXES, sided(-2))  7.24 us
    ppermute x2, starting transfers between devices, to_across(): return lax.ppermute(value, AXES, sided(-1))  5.56 us
    ppermute x14, starting transfers between devices, swap(): return lax.ppermute(value, AXES, sided(1))  4.43 us
    ppermute x2, waiting for transfers between devices, to_near(): return lax.ppermute(value, AXES, sided(-2))  4.3 us
    ppermute x3, waiting for transfers between devices, to_far(): return lax.ppermute(value, AXES, sided(2))  3.87 us
    ppermute x2, waiting for transfers between devices, to_across(): return lax.ppermute(value, AXES, sided(-1))  3.85 us
    ppermute x14, waiting for transfers between devices, swap(): return lax.ppermute(value, AXES, sided(1))  2.3 us
  transfers between devices with their start and end apart: 21, of which 11 were waited for; matrix products, arithmetic and copies ran while one was open for 0% of the time, Pallas kernels for 22%

profile of v5, /device:TPU:0, one launch (start us, length us, event | category | flops | bytes accessed | tf_op | source)
XLA Modules:
  0.0 53.0 jit_solution(9945828548466672431)
XLA Ops:
  0.0 4.1 %shard_map.154 = (bf16[2048,512]{1,0:T(8,128)(2,1)S(1)}, bf16[256,512]{1,0:T(8,128)(2,1)S(1)}, bf16[256,512]{1,0:T(8,128)(2,1)S(1)}, s32[1,2048]{1,0:T(1,128)S(1)}) custom-call(s32[1,2048]{1,0:T(1,128)} %bitcast.7, s32[1,2048]{1,0:T(1,128)} %bitcast.8, bf16[2048,512]{1,0:T(8,128)(2,1)} %grid.3, bf16[512,512]{1,0:T(8,128)(2,1)} %w1.1, f32[1,512]{1,0:T(1,128)} %bitcast.9), custom_call_target="tpu_custom_call" | custom-call | flops 2147483648 | bytes 2639872 | tf_op jit(solution)/shard_map/pallas_call | solution.py:273
  4.1 0.5 collective-permute-start
  4.7 5.6 %collective-permute-start.2 = (bf16[256,512]{1,0:T(8,128)(2,1)S(1)}, bf16[256,512]{1,0:T(8,128)(2,1)S(1)}, u32[]{:S(2)}, u32[]{:S(2)}) collective-permute-start(bf16[256,512]{1,0:T(8,128)(2,1)S(1)} %get-tuple-element.47), channel_id=1, source_target_pairs={{0,14},{1,3},{2,0},{3,5},{4,2},{5,7},{6,4},{7,9},{8,6},{9,11},{10,... | collective-permute-start | bytes 786440 | tf_op jit(solution)/shard_map/ppermute | solution.py:319
  10.3 0.7 %shard_map.155.after = bf16[256,512]{1,0:T(8,128)(2,1)S(1)} custom-call(s32[1,2048]{1,0:T(1,128)S(1)} %get-tuple-element.42.code, bf16[2048,512]{1,0:T(8,128)(2,1)S(1)} %get-tuple-element.43.hidden, bf16[256,512]{1,0:T(8,128)(2,1)S(1)} %collective-permute-done.crossed), custom_call_target="tpu_custom_call" | custom-call | flops 1 | bytes 1 | tf_op jit(solution)/shard_map/pallas_call | solution.py:273
  11.1 1.2 %shard_map.156 = (f32[256,512]{1,0:T(8,128)S(1)}, bf16[256,512]{1,0:T(8,128)(2,1)S(1)}) custom-call(bf16[256,512]{1,0:T(8,128)(2,1)S(1)} %shard_map.155.after, s32[1,2048]{1,0:T(1,128)S(1)} %get-tuple-element.42.code, bf16[2048,512]{1,0:T(8,128)(2,1)S(1)} %get-tuple-element.43.hidden), custom_call_target="tpu_custom_call" | custom-call | flops 1073741824 | bytes 2367488 | tf_op jit(solution)/shard_map/pallas_call | solution.py:273
  12.3 1.4 %collective-permute-start.1 = (bf16[256,512]{1,0:T(8,128)(2,1)S(1)}, bf16[256,512]{1,0:T(8,128)(2,1)S(1)}, u32[]{:S(2)}, u32[]{:S(2)}) collective-permute-start(bf16[256,512]{1,0:T(8,128)(2,1)S(1)} %get-tuple-element.46), channel_id=1, source_target_pairs={{0,1},{1,0},{2,3},{3,2},{4,5},{5,4},{6,7},{7,6},{8,9},{9,8},{10,11... | collective-permute-start | bytes 786440 | tf_op jit(solution)/shard_map/ppermute | solution.py:313
  13.7 1.8 %collective-permute-done.2.after.near = bf16[256,512]{1,0:T(8,128)(2,1)S(1)} collective-permute-done((bf16[256,512]{1,0:T(8,128)(2,1)S(1)}, bf16[256,512]{1,0:T(8,128)(2,1)S(1)}, u32[]{:S(2)}, u32[]{:S(2)}) %collective-permute-start.2) | collective-permute-done | bytes 262176 | tf_op jit(solution)/shard_map/ppermute | solution.py:319
  15.6 0.8 %shard_map.157 = (bf16[1536,256]{1,0:T(8,128)(2,1)S(1)}, bf16[1536,128]{1,0:T(8,128)(2,1)S(1)}, bf16[256,64]{1,0:T(8,128)(2,1)S(1)}, bf16[384,256]{1,0:T(8,128)(...) custom-call(bf16[256,512]{1,0:T(8,128)(2,1)S(1)} %collective-permute-done.2.after.near, ...), custom_call_target="tpu_custom_call" | custom-call | flops 40000000000 | bytes 1841408 | tf_op jit(solution)/shard_map/pallas_call | solution.py:273
  16.4 3.7 %collective-permute-done.3.far = bf16[256,512]{1,0:T(8,128)(2,1)S(1)} collective-permute-done((bf16[256,512]{1,0:T(8,128)(2,1)S(1)}, bf16[256,512]{1,0:T(8,128)(2,1)S(1)}, u32[]{:S(2)}, u32[]{:S(2)}) %collective-permute-start.3) | collective-permute-done | bytes 262176 | tf_op jit(solution)/shard_map/ppermute | solution.py:322
  20.6 2.8 %collective-permute-start.4 = (bf16[64,512]{1,0:T(8,128)(2,1)S(1)}, bf16[64,512]{1,0:T(8,128)(2,1)S(1)}, u32[]{:S(2)}, u32[]{:S(2)}) collective-permute-start(bf16[64,512]{1,0:T(8,128)(2,1)S(1)} %get-tuple-element.51.halo), channel_id=1, source_target_pairs={{0,15},{1,2},{2,1},{3,4},{4,3},{5,6},{6,5},{7,8},{8,7},{9,10},{10,... | collective-permute-start | bytes 196616 | tf_op jit(solution)/shard_map/ppermute | solution.py:316
  23.4 1.3 %shard_map.159 = (f32[1536,512]{1,0:T(8,128)S(1)}, bf16[64,512]{1,0:T(8,128)(2,1)S(1)}, f32[384,512]{1,0:T(8,128)S(1)}) custom-call(bf16[256,512]{1,0:T(8,128)(2,1)S(1)} %get-tuple-element.49.latent, bf16[2,512,512]{2,1,0:T(8,128)(2,1)S(1)} %copy-done, bf16[2,512,512]{2,1,0:T(8,128)(2,1)S(1)} %copy-done.2, f32[2,512]{1,0:T(2,128)S(1)} %copy-done.9, ...), custom_call_target="tpu_custom_call" | custom-call | flops 1 | bytes 1 | tf_op jit(solution)/shard_map/pallas_call | solution.py:273
  24.7 2.3 %collective-permute-done.4.table = bf16[64,512]{1,0:T(8,128)(2,1)S(1)} collective-permute-done((bf16[64,512]{1,0:T(8,128)(2,1)S(1)}, bf16[64,512]{1,0:T(8,128)(2,1)S(1)}, u32[]{:S(2)}, u32[]{:S(2)}) %collective-permute-start.4) | collective-permute-done | bytes 65568 | tf_op jit(solution)/shard_map/ppermute | solution.py:316
  27.0 0.7 %shard_map.161 = (bf16[64,512]{1,0:T(8,128)(2,1)S(1)}, bf16[128,512]{1,0:T(8,128)(2,1)S(1)}) custom-call(bf16[64,512]{1,0:T(8,128)(2,1)S(1)} %get-tuple-element.51.halo, f32[384,512]{1,0:T(8,128)S(1)} %get-tuple-element.54.before, bf16[64,512]{1,0:T(8,128)(2,1)S(1)} %shard_map.160.across, bf16[64,512]{1,0:T(8,128)(2,1)S(1)} %collective-permute-done.5.beside, ...), custom_call_target="tpu_custom_call" | custom-call | flops 150994944 | bytes 3178496 | tf_op jit(solution)/shard_map/pallas_call | solution.py:273
  27.7 2.8 %collective-permute-start.6 = (bf16[64,512]{1,0:T(8,128)(2,1)S(1)}, bf16[64,512]{1,0:T(8,128)(2,1)S(1)}, u32[]{:S(2)}, u32[]{:S(2)}) collective-permute-start(bf16[64,512]{1,0:T(8,128)(2,1)S(1)} %get-tuple-element.59.halo), channel_id=1, source_target_pairs={{0,15},{1,2},{2,1},{3,4},{4,3},{5,6},{6,5},{7,8},{8,7},{9,10},{10,... | collective-permute-start | bytes 196616 | tf_op jit(solution)/shard_map/ppermute | solution.py:316
  30.5 1.0 %shard_map.162.latent = bf16[256,512]{1,0:T(8,128)(2,1)S(1)} custom-call(bf16[256,512]{1,0:T(8,128)(2,1)S(1)} %get-tuple-element.49.latent, f32[1536,512]{1,0:T(8,128)S(1)} %get-tuple-element.53.before, bf16[128,512]{1,0:T(8,128)(2,1)S(1)} %get-tuple-element.57.table, bf16[1536,128]{1,0:T(8,128)(2,1)S(1)} %get-tuple-element.58.gather_halo, ...), custom_call_target="tpu_custom_call" | custom-call | flops 1 | bytes 1 | tf_op jit(solution)/shard_map/pallas_call | solution.py:273
  31.5 1.0 %shard_map.163 = (f32[1536,512]{1,0:T(8,128)S(1)}, bf16[64,512]{1,0:T(8,128)(2,1)S(1)}, f32[256,512]{1,0:T(8,128)S(1)}) custom-call(bf16[256,512]{1,0:T(8,128)(2,1)S(1)} %shard_map.162.latent, bf16[2,512,512]{2,1,0:T(8,128)(2,1)S(1)} %copy-done, bf16[2,512,512]{2,1,0:T(8,128)(2,1)S(1)} %copy-done.2, f32[2,512]{1,0:T(2,128)S(1)} %copy-done.9, ...), custom_call_target="tpu_custom_call" | custom-call | flops 1 | bytes 1 | tf_op jit(solution)/shard_map/pallas_call | solution.py:273
  32.6 1.6 %collective-permute-done.6.table = bf16[64,512]{1,0:T(8,128)(2,1)S(1)} collective-permute-done((bf16[64,512]{1,0:T(8,128)(2,1)S(1)}, bf16[64,512]{1,0:T(8,128)(2,1)S(1)}, u32[]{:S(2)}, u32[]{:S(2)}) %collective-permute-start.6) | collective-permute-done | bytes 65568 | tf_op jit(solution)/shard_map/ppermute | solution.py:316
  34.2 1.2 %shard_map.165.own = bf16[256,512]{1,0:T(8,128)(2,1)S(1)} custom-call(f32[1536,512]{1,0:T(8,128)S(1)} %get-tuple-element.60.before, bf16[64,512]{1,0:T(8,128)(2,1)S(1)} %shard_map.164.across, bf16[64,512]{1,0:T(8,128)(2,1)S(1)} %collective-permute-done.7.beside, bf16[1536,128]{1,0:T(8,128)(2,1)S(1)} %get-tuple-element.58.gather_halo, ...), custom_call_target="tpu_custom_call" | custom-call | flops 469762048 | bytes 5767168 | tf_op jit(solution)/shard_map/pallas_call | solution.py:273
  35.4 1.6 %collective-permute-start.10 = (bf16[256,512]{1,0:T(8,128)(2,1)S(1)}, bf16[256,512]{1,0:T(8,128)(2,1)S(1)}, u32[]{:S(2)}, u32[]{:S(2)}) collective-permute-start(bf16[256,512]{1,0:T(8,128)(2,1)S(1)} %shard_map.165.own), channel_id=1, source_target_pairs={{0,14},{1,3},{2,0},{3,5},{4,2},{5,7},{6,4},{7,9},{8,6},{9,11},{10,... | collective-permute-start | bytes 786440 | tf_op jit(solution)/shard_map/ppermute | solution.py:319
  37.1 2.3 %shard_map.166 = (bf16[2048,1280]{1,0:T(8,128)(2,1)S(1)}, f32[2048,512]{1,0:T(8,128)S(1)}, bf16[128,512]{1,0:T(8,128)(2,1)S(1)}, bf16[128,512]{1,0:T(8,128)(2,1)S(1)}) custom-call(s32[1,2048]{1,0:T(1,128)S(1)} %get-tuple-element.42.code, bf16[2048,512]{1,0:T(8,128)(2,1)S(1)} %copy-done.4, bf16[512,512]{1,0:T(8,128)(2,1)S(1)} %copy-done.7, ...), custom_call_target="tpu_custom_call" | custom-call | flops 1 | bytes 1 | tf_op jit(solution)/shard_map/pallas_call | solution.py:273
  39.5 0.5 collective-permute-start.9
  40.0 0.8 %collective-permute-done.8.refs_0_ = bf16[128,512]{1,0:T(8,128)(2,1)S(1)} collective-permute-done((bf16[128,512]{1,0:T(8,128)(2,1)S(1)}, bf16[128,512]{1,0:T(8,128)(2,1)S(1)}, u32[]{:S(2)}, u32[]{:S(2)}) %collective-permute-start.8) | collective-permute-done | bytes 131104 | tf_op jit(solution)/shard_map/ppermute | solution.py:313
  41.0 0.7 %shard_map.167 = (f32[2048,512]{1,0:T(8,128)S(1)}, bf16[256,256]{1,0:T(8,128)(2,1)S(1)}, bf16[256,256]{1,0:T(8,128)(2,1)S(1)}) custom-call(bf16[2048,1280]{1,0:T(8,128)(2,1)S(1)} %get-tuple-element.64.fetch, f32[2048,512]{1,0:T(8,128)S(1)} %get-tuple-element.65.base, bf16[256,512]{1,0:T(8,128)(2,1)S(1)} %shard_map.165.own, ...), custom_call_target="tpu_custom_call" | custom-call | flops 1 | bytes 1 | tf_op jit(solution)/shard_map/pallas_call | solution.py:273
  41.7 0.7 %collective-permute-start.20 = (bf16[256,256]{1,0:T(8,128)(2,1)S(1)}, bf16[256,256]{1,0:T(8,128)(2,1)S(1)}, u32[]{:S(2)}, u32[]{:S(2)}) collective-permute-start(bf16[256,256]{1,0:T(8,128)(2,1)S(1)} %get-tuple-element.78), channel_id=1, source_target_pairs={{0,2},{1,15},{2,4},{3,1},{4,6},{5,3},{6,8},{7,5},{8,10},{9,7},{10,... | collective-permute-start | bytes 393224 | tf_op jit(solution)/shard_map/ppermute | solution.py:322
  42.5 2.5 %collective-permute-done.10.far.table = bf16[256,512]{1,0:T(8,128)(2,1)S(1)} collective-permute-done((bf16[256,512]{1,0:T(8,128)(2,1)S(1)}, bf16[256,512]{1,0:T(8,128)(2,1)S(1)}, u32[]{:S(2)}, u32[]{:S(2)}) %collective-permute-start.10) | collective-permute-done | bytes 262176 | tf_op jit(solution)/shard_map/ppermute | solution.py:319
  45.1 0.5 collective-permute-start.12
  45.6 0.6 %collective-permute-done.11.refs_0_ = bf16[32,512]{1,0:T(8,128)(2,1)S(1)} collective-permute-done((bf16[32,512]{1,0:T(8,128)(2,1)S(1)}, bf16[32,512]{1,0:T(8,128)(2,1)S(1)}, u32[]{:S(2)}, u32[]{:S(2)}) %collective-permute-start.11) | collective-permute-done | bytes 32800 | tf_op jit(solution)/shard_map/ppermute | solution.py:313
  46.9 0.5 collective-permute-done.14.refs_3_
  48.0 0.7 %shard_map.168.base = f32[2048,512]{1,0:T(8,128)S(1)} custom-call(bf16[2048,1280]{1,0:T(8,128)(2,1)S(1)} %get-tuple-element.64.fetch, f32[2048,512]{1,0:T(8,128)S(1)} %get-tuple-element.68.base, bf16[256,512]{1,0:T(8,128)(2,1)S(1)} %collective-permute-done.10.far.table), custom_call_target="tpu_custom_call" | custom-call | flops 1 | bytes 1 | tf_op jit(solution)/shard_map/pallas_call | solution.py:273
  48.8 0.7 %shard_map.170.base = f32[2048,512]{1,0:T(8,128)S(1)} custom-call(bf16[2048,1280]{1,0:T(8,128)(2,1)S(1)} %get-tuple-element.64.fetch, f32[2048,512]{1,0:T(8,128)S(1)} %shard_map.168.base, bf16[32,512]{1,0:T(8,128)(2,1)S(1)} %collective-permute-done.11.refs_0_, bf16[32,512]{1,0:T(8,128)(2,1)S(1)} %collective-permute-done.12.refs_1_, ...), custom_call_target="tpu_custom_call" | custom-call | flops 1 | bytes 1 | tf_op jit(solution)/shard_map/pallas_call | solution.py:273
  49.7 1.1 %shard_map.171.partial = f32[2048,512]{1,0:T(8,128)S(1)} custom-call(bf16[2048,1280]{1,0:T(8,128)(2,1)S(1)} %get-tuple-element.64.fetch, f32[2048,512]{1,0:T(8,128)S(1)} %shard_map.170.base, bf16[256,256]{1,0:T(8,128)(2,1)S(1)} %collective-permute-done.20.near, bf16[512,512]{1,0:T(8,128)(2,1)S(1)} %copy-done.3), custom_call_target="tpu_custom_call" | custom-call | flops 1 | bytes 1 | tf_op jit(solution)/shard_map/pallas_call | solution.py:273
  51.0 1.9 %shard_map.172 = bf16[2048,512]{1,0:T(8,128)(2,1)} custom-call(bf16[2048,1280]{1,0:T(8,128)(2,1)S(1)} %get-tuple-element.64.fetch, f32[2048,512]{1,0:T(8,128)S(1)} %shard_map.170.base, bf16[256,256]{1,0:T(8,128)(2,1)S(1)} %collective-permute-done.19.near, bf16[512,512]{1,0:T(8,128)(2,1)S(1)} %copy-done.3, f32[2048,512]{1,0:T(8,128)S(1)} %shard_map.171.partial), custom_call_target="tpu_custom_call" | custom-call | flops 1610612736 | bytes 14286848 | tf_op jit(solution)/shard_map/pallas_call | solution.py:273
  (53 shorter events, 2.8 us)
Async XLA Ops:
  4.1 11.4 %copy-start.1 = (bf16[2,512,512]{2,1,0:T(8,128)(2,1)S(1)}, bf16[2,512,512]{2,1,0:T(8,128)(2,1)}, u32[]{:S(2)}) copy-start(bf16[2,512,512]{2,1,0:T(8,128)(2,1)} %w_out.7) | copy-start | bytes 3145732
  4.1 11.4 %copy-start.6 = (bf16[512,512]{1,0:T(8,128)(2,1)S(1)}, bf16[512,512]{1,0:T(8,128)(2,1)}, u32[]{:S(2)}) copy-start(bf16[512,512]{1,0:T(8,128)(2,1)} %more_in.1) | copy-start | bytes 1572868
  4.1 11.4 %copy-start.10 = (s32[256,6]{0,1:T(8,128)S(1)}, s32[256,6]{0,1:T(8,128)}, u32[]{:S(2)}) copy-start(s32[256,6]{0,1:T(8,128)} %param.21) | copy-start | bytes 18436
  4.1 11.4 %copy-start.11 = (s32[64]{0:T(128)S(1)}, s32[64]{0:T(128)}, u32[]{:S(2)}) copy-start(s32[64]{0:T(128)} %param.20) | copy-start | bytes 772
  4.1 6.1 %collective-permute-start = (bf16[256,512]{1,0:T(8,128)(2,1)S(1)}, bf16[256,512]{1,0:T(8,128)(2,1)S(1)}, u32[]{:S(2)}, u32[]{:S(2)}) collective-permute-start(bf16[256,512]{1,0:T(8,128)(2,1)S(1)} %get-tuple-element.44), channel_id=1, source_target_pairs={{0,1},{1,0},{2,3},{3,2},{4,5},{5,4},{6,7},{7,6},{8,9},{9,8},{10,11... | collective-permute-start | bytes 786440 | tf_op jit(solution)/shard_map/ppermute | solution.py:313
  4.7 10.9 %collective-permute-start.2 = (bf16[256,512]{1,0:T(8,128)(2,1)S(1)}, bf16[256,512]{1,0:T(8,128)(2,1)S(1)}, u32[]{:S(2)}, u32[]{:S(2)}) collective-permute-start(bf16[256,512]{1,0:T(8,128)(2,1)S(1)} %get-tuple-element.47), channel_id=1, source_target_pairs={{0,14},{1,3},{2,0},{3,5},{4,2},{5,7},{6,4},{7,9},{8,6},{9,11},{10,... | collective-permute-start | bytes 786440 | tf_op jit(solution)/shard_map/ppermute | solution.py:319
  11.0 9.1 %collective-permute-start.3 = (bf16[256,512]{1,0:T(8,128)(2,1)S(1)}, bf16[256,512]{1,0:T(8,128)(2,1)S(1)}, u32[]{:S(2)}, u32[]{:S(2)}) collective-permute-start(bf16[256,512]{1,0:T(8,128)(2,1)S(1)} %shard_map.155.after), channel_id=1, source_target_pairs={{0,2},{1,15},{2,4},{3,1},{4,6},{5,3},{6,8},{7,5},{8,10},{9,7},{10,... | collective-permute-start | bytes 786440 | tf_op jit(solution)/shard_map/ppermute | solution.py:322
  12.3 4.1 %collective-permute-start.1 = (bf16[256,512]{1,0:T(8,128)(2,1)S(1)}, bf16[256,512]{1,0:T(8,128)(2,1)S(1)}, u32[]{:S(2)}, u32[]{:S(2)}) collective-permute-start(bf16[256,512]{1,0:T(8,128)(2,1)S(1)} %get-tuple-element.46), channel_id=1, source_target_pairs={{0,1},{1,0},{2,3},{3,2},{4,5},{5,4},{6,7},{7,6},{8,9},{9,8},{10,11... | collective-permute-start | bytes 786440 | tf_op jit(solution)/shard_map/ppermute | solution.py:313
  15.5 4.6 %copy-start.5 = (bf16[512,512]{1,0:T(8,128)(2,1)S(1)}, bf16[512,512]{1,0:T(8,128)(2,1)}, u32[]{:S(2)}) copy-start(bf16[512,512]{1,0:T(8,128)(2,1)} %w2.1) | copy-start | bytes 1572868
  15.5 4.6 %copy-start.8 = (bf16[256,512]{1,0:T(8,128)(2,1)S(1)}, bf16[256,512]{1,0:T(8,128)(2,1)}, u32[]{:S(2)}) copy-start(bf16[256,512]{1,0:T(8,128)(2,1)} %mesh.1) | copy-start | bytes 786436
  15.6 7.8 %copy-start = (bf16[2,512,512]{2,1,0:T(8,128)(2,1)S(1)}, bf16[2,512,512]{2,1,0:T(8,128)(2,1)}, u32[]{:S(2)}) copy-start(bf16[2,512,512]{2,1,0:T(8,128)(2,1)} %w_src.7) | copy-start | bytes 3145732
  15.6 7.8 %copy-start.2 = (bf16[2,512,512]{2,1,0:T(8,128)(2,1)S(1)}, bf16[2,512,512]{2,1,0:T(8,128)(2,1)}, u32[]{:S(2)}) copy-start(bf16[2,512,512]{2,1,0:T(8,128)(2,1)} %w_dst.3) | copy-start | bytes 3145732
  15.6 7.8 %copy-start.9 = (f32[2,512]{1,0:T(2,128)S(1)}, f32[2,512]{1,0:T(2,128)}, u32[]{:S(2)}) copy-start(f32[2,512]{1,0:T(2,128)} %bias.3) | copy-start | bytes 12292
  20.6 6.5 %collective-permute-start.4 = (bf16[64,512]{1,0:T(8,128)(2,1)S(1)}, bf16[64,512]{1,0:T(8,128)(2,1)S(1)}, u32[]{:S(2)}, u32[]{:S(2)}) collective-permute-start(bf16[64,512]{1,0:T(8,128)(2,1)S(1)} %get-tuple-element.51.halo), channel_id=1, source_target_pairs={{0,15},{1,2},{2,1},{3,4},{4,3},{5,6},{6,5},{7,8},{8,7},{9,10},{10,... | collective-permute-start | bytes 196616 | tf_op jit(solution)/shard_map/ppermute | solution.py:316
  24.7 2.4 %collective-permute-start.5 = (bf16[64,512]{1,0:T(8,128)(2,1)S(1)}, bf16[64,512]{1,0:T(8,128)(2,1)S(1)}, u32[]{:S(2)}, u32[]{:S(2)}) collective-permute-start(bf16[64,512]{1,0:T(8,128)(2,1)S(1)} %get-tuple-element.55), channel_id=1, source_target_pairs={{0,1},{1,0},{2,3},{3,2},{4,5},{5,4},{6,7},{7,6},{8,9},{9,8},{10,11... | collective-permute-start | bytes 196616 | tf_op jit(solution)/shard_map/ppermute | solution.py:313
  27.7 6.5 %collective-permute-start.6 = (bf16[64,512]{1,0:T(8,128)(2,1)S(1)}, bf16[64,512]{1,0:T(8,128)(2,1)S(1)}, u32[]{:S(2)}, u32[]{:S(2)}) collective-permute-start(bf16[64,512]{1,0:T(8,128)(2,1)S(1)} %get-tuple-element.59.halo), channel_id=1, source_target_pairs={{0,15},{1,2},{2,1},{3,4},{4,3},{5,6},{6,5},{7,8},{8,7},{9,10},{10,... | collective-permute-start | bytes 196616 | tf_op jit(solution)/shard_map/ppermute | solution.py:316
  32.5 1.7 %collective-permute-start.7 = (bf16[64,512]{1,0:T(8,128)(2,1)S(1)}, bf16[64,512]{1,0:T(8,128)(2,1)S(1)}, u32[]{:S(2)}, u32[]{:S(2)}) collective-permute-start(bf16[64,512]{1,0:T(8,128)(2,1)S(1)} %get-tuple-element.61), channel_id=1, source_target_pairs={{0,1},{1,0},{2,3},{3,2},{4,5},{5,4},{6,7},{7,6},{8,9},{9,8},{10,11... | collective-permute-start | bytes 196616 | tf_op jit(solution)/shard_map/ppermute | solution.py:313
  34.2 2.9 %copy-start.4 = (bf16[2048,512]{1,0:T(8,128)(2,1)S(1)}, bf16[2048,512]{1,0:T(8,128)(2,1)}, u32[]{:S(2)}) copy-start(bf16[2048,512]{1,0:T(8,128)(2,1)} %grid.3) | copy-start | bytes 6291460
  34.2 2.9 %copy-start.7 = (bf16[512,512]{1,0:T(8,128)(2,1)S(1)}, bf16[512,512]{1,0:T(8,128)(2,1)}, u32[]{:S(2)}) copy-start(bf16[512,512]{1,0:T(8,128)(2,1)} %w_grid.1) | copy-start | bytes 1572868
  35.4 9.5 %collective-permute-start.10 = (bf16[256,512]{1,0:T(8,128)(2,1)S(1)}, bf16[256,512]{1,0:T(8,128)(2,1)S(1)}, u32[]{:S(2)}, u32[]{:S(2)}) collective-permute-start(bf16[256,512]{1,0:T(8,128)(2,1)S(1)} %shard_map.165.own), channel_id=1, source_target_pairs={{0,14},{1,3},{2,0},{3,5},{4,2},{5,7},{6,4},{7,9},{8,6},{9,11},{10,... | collective-permute-start | bytes 786440 | tf_op jit(solution)/shard_map/ppermute | solution.py:319
  39.4 1.4 %collective-permute-start.8 = (bf16[128,512]{1,0:T(8,128)(2,1)S(1)}, bf16[128,512]{1,0:T(8,128)(2,1)S(1)}, u32[]{:S(2)}, u32[]{:S(2)}) collective-permute-start(bf16[128,512]{1,0:T(8,128)(2,1)S(1)} %get-tuple-element.66), channel_id=1, source_target_pairs={{0,1},{1,0},{2,3},{3,2},{4,5},{5,4},{6,7},{7,6},{8,9},{9,8},{10,11... | collective-permute-start | bytes 393224 | tf_op jit(solution)/shard_map/ppermute | solution.py:313
  39.5 1.5 %collective-permute-start.9 = (bf16[128,512]{1,0:T(8,128)(2,1)S(1)}, bf16[128,512]{1,0:T(8,128)(2,1)S(1)}, u32[]{:S(2)}, u32[]{:S(2)}) collective-permute-start(bf16[128,512]{1,0:T(8,128)(2,1)S(1)} %get-tuple-element.67), channel_id=1, source_target_pairs={{0,1},{1,0},{2,3},{3,2},{4,5},{5,4},{6,7},{7,6},{8,9},{9,8},{10,11... | collective-permute-start | bytes 393224 | tf_op jit(solution)/shard_map/ppermute | solution.py:313
  41.7 7.8 %collective-permute-start.20 = (bf16[256,256]{1,0:T(8,128)(2,1)S(1)}, bf16[256,256]{1,0:T(8,128)(2,1)S(1)}, u32[]{:S(2)}, u32[]{:S(2)}) collective-permute-start(bf16[256,256]{1,0:T(8,128)(2,1)S(1)} %get-tuple-element.78), channel_id=1, source_target_pairs={{0,2},{1,15},{2,4},{3,1},{4,6},{5,3},{6,8},{7,5},{8,10},{9,7},{10,... | collective-permute-start | bytes 393224 | tf_op jit(solution)/shard_map/ppermute | solution.py:322
  42.4 8.5 %collective-permute-start.19 = (bf16[256,256]{1,0:T(8,128)(2,1)S(1)}, bf16[256,256]{1,0:T(8,128)(2,1)S(1)}, u32[]{:S(2)}, u32[]{:S(2)}) collective-permute-start(bf16[256,256]{1,0:T(8,128)(2,1)S(1)} %get-tuple-element.77), channel_id=1, source_target_pairs={{0,2},{1,15},{2,4},{3,1},{4,6},{5,3},{6,8},{7,5},{8,10},{9,7},{10,... | collective-permute-start | bytes 393224 | tf_op jit(solution)/shard_map/ppermute | solution.py:322
  45.0 1.3 %collective-permute-start.11 = (bf16[32,512]{1,0:T(8,128)(2,1)S(1)}, bf16[32,512]{1,0:T(8,128)(2,1)S(1)}, u32[]{:S(2)}, u32[]{:S(2)}) collective-permute-start(bf16[32,512]{1,0:T(8,128)(2,1)S(1)} %get-tuple-element.69), channel_id=1, source_target_pairs={{0,1},{1,0},{2,3},{3,2},{4,5},{5,4},{6,7},{7,6},{8,9},{9,8},{10,11... | collective-permute-start | bytes 98312 | tf_op jit(solution)/shard_map/ppermute | solution.py:313
  45.1 1.4 %collective-permute-start.12 = (bf16[32,512]{1,0:T(8,128)(2,1)S(1)}, bf16[32,512]{1,0:T(8,128)(2,1)S(1)}, u32[]{:S(2)}, u32[]{:S(2)}) collective-permute-start(bf16[32,512]{1,0:T(8,128)(2,1)S(1)} %get-tuple-element.70), channel_id=1, source_target_pairs={{0,1},{1,0},{2,3},{3,2},{4,5},{5,4},{6,7},{7,6},{8,9},{9,8},{10,11... | collective-permute-start | bytes 98312 | tf_op jit(solution)/shard_map/ppermute | solution.py:313
  45.6 1.2 %collective-permute-start.13 = (bf16[32,512]{1,0:T(8,128)(2,1)S(1)}, bf16[32,512]{1,0:T(8,128)(2,1)S(1)}, u32[]{:S(2)}, u32[]{:S(2)}) collective-permute-start(bf16[32,512]{1,0:T(8,128)(2,1)S(1)} %get-tuple-element.71), channel_id=1, source_target_pairs={{0,1},{1,0},{2,3},{3,2},{4,5},{5,4},{6,7},{7,6},{8,9},{9,8},{10,11... | collective-permute-start | bytes 98312 | tf_op jit(solution)/shard_map/ppermute | solution.py:313
  46.3 1.2 %collective-permute-start.14 = (bf16[32,512]{1,0:T(8,128)(2,1)S(1)}, bf16[32,512]{1,0:T(8,128)(2,1)S(1)}, u32[]{:S(2)}, u32[]{:S(2)}) collective-permute-start(bf16[32,512]{1,0:T(8,128)(2,1)S(1)} %get-tuple-element.72), channel_id=1, source_target_pairs={{0,1},{1,0},{2,3},{3,2},{4,5},{5,4},{6,7},{7,6},{8,9},{9,8},{10,11... | collective-permute-start | bytes 98312 | tf_op jit(solution)/shard_map/ppermute | solution.py:313
  46.4 1.2 %collective-permute-start.15 = (bf16[32,512]{1,0:T(8,128)(2,1)S(1)}, bf16[32,512]{1,0:T(8,128)(2,1)S(1)}, u32[]{:S(2)}, u32[]{:S(2)}) collective-permute-start(bf16[32,512]{1,0:T(8,128)(2,1)S(1)} %get-tuple-element.73), channel_id=1, source_target_pairs={{0,1},{1,0},{2,3},{3,2},{4,5},{5,4},{6,7},{7,6},{8,9},{9,8},{10,11... | collective-permute-start | bytes 98312 | tf_op jit(solution)/shard_map/ppermute | solution.py:313
  46.8 1.9 %collective-permute-start.16 = (bf16[32,512]{1,0:T(8,128)(2,1)S(1)}, bf16[32,512]{1,0:T(8,128)(2,1)S(1)}, u32[]{:S(2)}, u32[]{:S(2)}) collective-permute-start(bf16[32,512]{1,0:T(8,128)(2,1)S(1)} %get-tuple-element.74), channel_id=1, source_target_pairs={{0,1},{1,0},{2,3},{3,2},{4,5},{5,4},{6,7},{7,6},{8,9},{9,8},{10,11... | collective-permute-start | bytes 98312 | tf_op jit(solution)/shard_map/ppermute | solution.py:313
  47.5 1.3 %collective-permute-start.17 = (bf16[32,512]{1,0:T(8,128)(2,1)S(1)}, bf16[32,512]{1,0:T(8,128)(2,1)S(1)}, u32[]{:S(2)}, u32[]{:S(2)}) collective-permute-start(bf16[32,512]{1,0:T(8,128)(2,1)S(1)} %get-tuple-element.75), channel_id=1, source_target_pairs={{0,1},{1,0},{2,3},{3,2},{4,5},{5,4},{6,7},{7,6},{8,9},{9,8},{10,11... | collective-permute-start | bytes 98312 | tf_op jit(solution)/shard_map/ppermute | solution.py:313
  47.6 1.2 %collective-permute-start.18 = (bf16[32,512]{1,0:T(8,128)(2,1)S(1)}, bf16[32,512]{1,0:T(8,128)(2,1)S(1)}, u32[]{:S(2)}, u32[]{:S(2)}) collective-permute-start(bf16[32,512]{1,0:T(8,128)(2,1)S(1)} %get-tuple-element.76), channel_id=1, source_target_pairs={{0,1},{1,0},{2,3},{3,2},{4,5},{5,4},{6,7},{7,6},{8,9},{9,8},{10,11... | collective-permute-start | bytes 98312 | tf_op jit(solution)/shard_map/ppermute | solution.py:313
  (1 other events, 1.0 us)

commit v6 on v5

--- a/solution.py
+++ b/solution.py
@@ -89,19 +89,29 @@
     far[...] = (dot(one_hot_down(code[...], 4 * rows, rows), hidden[...]) + crossed[...].astype(F32)).astype(BF16)
 
 
-def chip_kernel(after, code, hidden, own, sibling):
+def chip_kernel(after, code, hidden, halo_index, *refs):
     del after
+    held, (own, sibling, pick, joined, kept), buffers, sems = refs[:5], refs[5:10], refs[10:15], refs[15]
+    copies = [pltpu.make_async_copy(a, b, sems.at[i]) for i, (a, b) in enumerate(zip(held, buffers))]
+    for copy in copies:
+        copy.start()
     rows = own.shape[0]
     sibling[...] = dot(one_hot_down(code[...], 3 * rows, rows), hidden[...]).astype(BF16)
     own[...] = dot(one_hot_down(code[...], 2 * rows, rows), hidden[...])
-
-
-def prepare_kernel(after, edges, halo_index, w_out, w_mesh, gather, gather_halo, pick, lead, lead_halo, joined):
+    for copy in copies:
+        copy.wait()
+    mesh, w2, w_src, w_out, w_mesh = buffers
+    pairs = [(w2[...], w_src[0])] + [(w_out[i], w_src[i + 1]) for i in range(L - 1)] + [(w_out[L - 1], w_mesh[...])]
+    for i, (first, second) in enumerate(pairs):
+        joined[i] = (dot(first, second) * 0.5).astype(BF16)
+    pick[...] = one_hot_down(halo_index[...], 0, rows)
+    kept[...] = dot(picked(pick[...], mesh[...]), w_src[0]) * 0.5
+
+
+def prepare_kernel(after, edges, pick, gather, gather_halo, lead, lead_halo):
     del after
-    joined[...] = (dot(w_out[L - 1], w_mesh[...]) * 0.5).astype(BF16)
     n, own = edges.shape[1], gather.shape[1]
-    border = halo_index.shape[1]
-    pick[...] = one_hot_down(halo_index[...], 0, n)
+    border = pick.shape[1]
     for k in range(edges.shape[0]):
         one_hot = one_hot_across(edges[k : k + 1, :], own + gather_halo.shape[1])
         gather[k * n : (k + 1) * n] = one_hot[:, :own]
@@ -115,11 +125,15 @@
     return lax.dot_general(pick, rows, (((0,), (0,)), ((), ())), preferred_element_type=F32).astype(BF16)
 
 
-def latent_kernel(mesh, own, sibling, near, far, w2, pick, latent, halo):
-    sums = own[...] + sibling[...].astype(F32) + near[...].astype(F32) + far[...].astype(F32)
-    rows = (mesh[...].astype(F32) + dot(sums.astype(BF16), w2[...])).astype(BF16)
-    latent[...] = rows
-    halo[...] = picked(pick[...], rows)
+def sums_kernel(after, own, sibling, near, far, pick, joined, kept, sums, halo):
+    del after
+    total = own[...] + sibling[...].astype(F32) + near[...].astype(F32) + far[...].astype(F32)
+    sums[...] = total.astype(BF16)
+    halo[...] = (kept[...] + dot(picked(pick[...], sums[...]), joined[0])).astype(BF16)
+
+
+def latent_kernel(mesh, sums, w2, latent):
+    latent[...] = (mesh[...].astype(F32) + dot(sums[...], w2[...])).astype(BF16)
 
 
 def own_terms(layer, nodes, gather, source, w_dst, bias, before):
@@ -129,21 +143,25 @@
         before[k * n : (k + 1) * n] = dot(gather[k * n : (k + 1) * n], source) + target
 
 
-def project_kernel(layer, latent, w_src, w_dst, bias, gather, halo, more_in, before, passed, more_out):
+def project_kernel(layer, latent, w_src, w_dst, bias, gather, halo, w_next, *refs):
     source = (dot(latent[...], w_src[layer]) * 0.5).astype(BF16)
     if layer == L - 1:
-        more_out[...] = dot(latent[...], more_in[...]) * 0.5
+        before, passed, kept = refs
+        kept[...] = dot(latent[...], w_next[...]) * 0.5
     else:
-        own_terms(layer, halo, more_in, source, w_dst, bias, more_out)
+        pick, lead, before, passed, kept, before_lead = refs
+        nodes = picked(pick[...], latent[...])
+        kept[...] = dot(nodes, w_next[layer + 1]) * 0.5
+        own_terms(layer, nodes, lead, source, w_dst, bias, before_lead)
     passed[...] = halo[...]
     own_terms(layer, latent, gather, source, w_dst, bias, before)
 
 
-def halo_table(layer, across, beside, w_src):
+def halo_table(across, beside):
     first = lax.axis_index("feat") == 0
     down = jnp.where(first, across[...], beside[...])
     up = jnp.where(first, beside[...], across[...])
-    return (dot(jnp.concatenate([down, up], axis=0), w_src[layer]) * 0.5).astype(BF16)
+    return jnp.concatenate([down, up], axis=0)
 
 
 def edge_sums(n, before, gather_halo, table):
@@ -155,23 +173,19 @@
     return total.astype(BF16)
 
 
-def updated(layer, nodes, before, gather_halo, table, w_out):
-    sums = edge_sums(nodes.shape[0], before, gather_halo, table)
-    return (nodes[...].astype(F32) + dot(sums, w_out[layer])).astype(BF16)
-
-
-def lead_kernel(layer, halo, before, across, beside, gather_halo, w_src, w_out, new_halo, table):
-    table[...] = halo_table(layer, across, beside, w_src)
-    new_halo[...] = updated(layer, halo, before, gather_halo, table[...], w_out)
-
-
-def layer_kernel(layer, latent, before, table, gather_halo, w_out, new):
-    new[...] = updated(layer, latent, before, gather_halo, table[...], w_out)
-
-
-def last_layer_kernel(layer, before, across, beside, gather_halo, w_src, kept, joined, projected):
-    sums = edge_sums(kept.shape[0], before, gather_halo, halo_table(layer, across, beside, w_src))
-    projected[...] = (kept[...] + dot(sums, joined[...])).astype(BF16)
+def lead_kernel(layer, before, across, beside, gather_halo, joined, kept, halo):
+    sums = edge_sums(kept.shape[0], before, gather_halo, halo_table(across, beside))
+    halo[...] = (kept[...] + dot(sums, joined[layer + 1])).astype(BF16)
+
+
+def layer_kernel(layer, latent, before, across, beside, gather_halo, w_out, new):
+    sums = edge_sums(latent.shape[0], before, gather_halo, halo_table(across, beside))
+    new[...] = (latent[...].astype(F32) + dot(sums, w_out[layer])).astype(BF16)
+
+
+def last_layer_kernel(before, across, beside, gather_halo, kept, joined, projected):
+    sums = edge_sums(kept.shape[0], before, gather_halo, halo_table(across, beside))
+    projected[...] = (kept[...] + dot(sums, joined[L])).astype(BF16)
 
 
 def base_kernel(code, grid, w_grid, own, fetch, base, *pieces):
@@ -211,9 +225,13 @@
 
 
 def cut_kernel(table, *pieces):
-    rows = pieces[0].shape[0]
-    for i, piece in enumerate(pieces):
-        piece[...] = table[i * rows : (i + 1) * rows]
+    row = column = 0
+    for piece in pieces:
+        rows, width = piece.shape
+        piece[...] = table[row : row + rows, column : column + width]
+        row += rows
+        if row == table.shape[0]:
+            row, column = 0, column + width
 
 
 def pass_kernel(table, out):
@@ -344,58 +362,73 @@
     crossed = swap(cross)
     (sent,) = call(far_kernel, [code, hidden, crossed], [table], 1)
     far = to_far(sent)
-    own, sibling = call(
+    own, sibling, pick, joined, kept = call(
         chip_kernel,
-        [sent, code, hidden],
-        [((mesh_rows, width), F32), table],
+        [sent, code, hidden, halo_index.reshape(1, border), mesh_feat, w_enc2, proc_src, proc_out, dec_mesh],
+        [
+            ((mesh_rows, width), F32),
+            table,
+            ((mesh_rows, border), BF16),
+            ((L + 1, width, width), BF16),
+            ((border, width), F32),
+        ],
         unit * 2 * mesh_rows,
-        spaces=[pl.ANY, VM, VM],
-    )
-    gather, gather_halo, pick, lead, lead_halo, joined = call(
+        [
+            VM((mesh_rows, width), BF16),
+            VM((width, width), BF16),
+            VM((L, width, width), BF16),
+            VM((L, width, width), BF16),
+            VM((width, width), BF16),
+            pltpu.SemaphoreType.DMA((5,)),
+        ],
+        spaces=[pl.ANY] + [VM] * 3 + [pltpu.HBM] * 5,
+    )
+    gather, gather_halo, lead, lead_halo = call(
         prepare_kernel,
-        [near, edge_src.T, halo_index.reshape(1, border), proc_out, dec_mesh],
+        [near, edge_src.T, pick],
         [
             ((degree * mesh_rows, mesh_rows), BF16),
             ((degree * mesh_rows, 2 * border), BF16),
-            ((mesh_rows, border), BF16),
             ((degree * border, mesh_rows), BF16),
             ((degree * border, 2 * border), BF16),
-            ((width, width), BF16),
         ],
         LONG,
-        spaces=[pl.ANY, VM, VM, VM, VM],
+        spaces=[pl.ANY, VM, VM],
     )
     sibling = swap(sibling)
-    latent, halo = call(
-        latent_kernel,
-        [mesh_feat, own, sibling, near, far, w_enc2, pick],
+    sums, halo = call(
+        sums_kernel,
+        [lead_halo, own, sibling, near, far, pick, joined, kept],
         [table, border_rows],
         2 * mesh_rows * width * width,
-    )
+        spaces=[pl.ANY] + [VM] * 7,
+    )
+    across = to_across(halo)
+    (latent,) = call(latent_kernel, [mesh_feat, sums, w_enc2], [table], 1)
     edge_terms = ((degree * mesh_rows, width), F32)
     for layer in range(L - 1):
-        across = to_across(halo)
-        before, passed, before_lead = call(
+        before, passed, kept, before_lead = call(
             part(project_kernel, layer),
-            [latent, proc_src, proc_dst, proc_bias, gather, halo, lead],
-            [edge_terms, border_rows, ((degree * border, width), F32)],
+            [latent, proc_src, proc_dst, proc_bias, gather, halo, proc_src, pick, lead],
+            [edge_terms, border_rows, ((border, width), F32), ((degree * border, width), F32)],
             1,
         )
         beside = swap(passed)
         (across,) = call(pass_kernel, [across], [border_rows], LONG)
-        halo, received = call(
+        (halo,) = call(
             part(lead_kernel, layer),
-            [halo, before_lead, across, beside, lead_halo, proc_src, proc_out],
-            [border_rows, ((2 * border, width), BF16)],
+            [before_lead, across, beside, lead_halo, joined, kept],
+            [border_rows],
             2 * border * width * (degree * 2 * border + 3 * width),
         )
+        arrived = (across, beside)
+        across = to_across(halo)
         (latent,) = call(
             part(layer_kernel, layer),
-            [latent, before, received, gather_halo, proc_out],
+            [latent, before, *arrived, gather_halo, proc_out],
             [table],
             1,
         )
-    across = to_across(halo)
     before, passed, kept = call(
         part(project_kernel, L - 1),
         [latent, proc_src, proc_dst, proc_bias, gather, halo, dec_mesh],
@@ -405,8 +438,8 @@
     beside = swap(passed)
     (across,) = call(pass_kernel, [across], [border_rows], LONG)
     (projected,) = call(
-        part(last_layer_kernel, L - 1),
-        [before, across, beside, gather_halo, proc_src, kept, joined],
+        last_layer_kernel,
+        [before, across, beside, gather_halo, kept, joined],
         [table],
         2 * mesh_rows * width * (degree * 2 * border + 2 * width),
     )
@@ -424,7 +457,7 @@
     base, left, right = call(sibling_kernel, [fetch, base, projected, *sibling], [f32_rows, half, half], 1)
     left = to_far(left)
     right = to_far(right)
-    passed = call(cut_kernel, [far], [((mesh_rows // 8, width), BF16)] * 8, 1)
+    passed = call(cut_kernel, [far], [((mesh_rows * part_rows // 256, width), BF16) for part_rows in (48, 48, 48, 48, 32, 32)], 1)
     cross = [swap(piece) for piece in passed]
     (base,) = call(far_add_kernel, [fetch, base, far], [f32_rows], 1)
     (base,) = call(cross_add_kernel, [fetch, base, *cross], [f32_rows], 1)

time: 53.2 us -> 52.8 us (level)
  Pallas kernels: 19.9 us -> 22.8 us
  waiting for transfers between devices: 14.3 us -> 11.7 us
    pallas_call x19 -> x20, Pallas kernels: 19.9 us -> 22.8 us  [call(): pl.pallas_call(kernel, in_specs=[pl.BlockSpec(memory_space=space) for spa...]
    ppermute x2, waiting for transfers between devices: 4.3 us -> 2.44 us  [to_near(): return lax.ppermute(value, AXES, sided(-2))]
    ppermute x14 -> x12, waiting for transfers between devices: 2.3 us -> 1.96 us  [swap(): return lax.ppermute(value, AXES, sided(1))]
    ppermute x14 -> x12, starting transfers between devices: 4.43 us -> 4.1 us  [swap(): return lax.ppermute(value, AXES, sided(1))]
  transfers between devices with their start and end apart: 21 -> 19, of which waited for: 11 -> 10; matrix products, arithmetic and copies ran while one was open for 0% -> 0% of each run, Pallas kernels for 22% -> 28%
where the time goes in v6:
time: 52.8 us; the launch traced here: 52.7 us
  Pallas kernels  22.8 us (43%)
  starting transfers between devices  17.7 us (34%)
  waiting for transfers between devices  11.7 us (22%)
    pallas_call x20, Pallas kernels, call(): pl.pallas_call(kernel, in_specs=[pl.BlockSpec(memory_space=space) for spa...  22.8 us
    ppermute x2, starting transfers between devices, to_near(): return lax.ppermute(value, AXES, sided(-2))  7.26 us
    ppermute x2, starting transfers between devices, to_across(): return lax.ppermute(value, AXES, sided(-1))  5.54 us
    ppermute x12, starting transfers between devices, swap(): return lax.ppermute(value, AXES, sided(1))  4.1 us
    ppermute x3, waiting for transfers between devices, to_far(): return lax.ppermute(value, AXES, sided(2))  3.92 us
    ppermute x2, waiting for transfers between devices, to_across(): return lax.ppermute(value, AXES, sided(-1))  3.35 us
    ppermute x2, waiting for transfers between devices, to_near(): return lax.ppermute(value, AXES, sided(-2))  2.44 us
    ppermute x12, waiting for transfers between devices, swap(): return lax.ppermute(value, AXES, sided(1))  1.96 us
  transfers between devices with their start and end apart: 19, of which 10 were waited for; matrix products, arithmetic and copies ran while one was open for 0% of the time, Pallas kernels for 28%

profile of v6, /device:TPU:0, one launch (start us, length us, event | category | flops | bytes accessed | tf_op | source)
XLA Modules:
  0.0 52.7 jit_solution(13585394397955319309)
XLA Ops:
  0.0 4.2 %shard_map.154 = (bf16[2048,512]{1,0:T(8,128)(2,1)S(1)}, bf16[256,512]{1,0:T(8,128)(2,1)S(1)}, bf16[256,512]{1,0:T(8,128)(2,1)S(1)}, s32[1,2048]{1,0:T(1,128)S(1)}) custom-call(s32[1,2048]{1,0:T(1,128)} %bitcast.7, s32[1,2048]{1,0:T(1,128)} %bitcast.8, bf16[2048,512]{1,0:T(8,128)(2,1)} %grid.3, bf16[512,512]{1,0:T(8,128)(2,1)} %w1.1, f32[1,512]{1,0:T(1,128)} %bitcast.9), custom_call_target="tpu_custom_call" | custom-call | flops 2147483648 | bytes 2639872 | tf_op jit(solution)/shard_map/pallas_call | solution.py:291
  4.2 0.5 collective-permute-start.1
  4.7 5.6 %collective-permute-start = (bf16[256,512]{1,0:T(8,128)(2,1)S(1)}, bf16[256,512]{1,0:T(8,128)(2,1)S(1)}, u32[]{:S(2)}, u32[]{:S(2)}) collective-permute-start(bf16[256,512]{1,0:T(8,128)(2,1)S(1)} %get-tuple-element.41), channel_id=1, source_target_pairs={{0,14},{1,3},{2,0},{3,5},{4,2},{5,7},{6,4},{7,9},{8,6},{9,11},{10,... | collective-permute-start | bytes 786440 | tf_op jit(solution)/shard_map/ppermute | solution.py:337
  10.3 0.7 %shard_map.155.after = bf16[256,512]{1,0:T(8,128)(2,1)S(1)} custom-call(s32[1,2048]{1,0:T(1,128)S(1)} %get-tuple-element.40.code, bf16[2048,512]{1,0:T(8,128)(2,1)S(1)} %get-tuple-element.42.hidden, bf16[256,512]{1,0:T(8,128)(2,1)S(1)} %collective-permute-done.1.crossed), custom_call_target="tpu_custom_call" | custom-call | flops 1 | bytes 1 | tf_op jit(solution)/shard_map/pallas_call | solution.py:291
  11.1 4.2 %shard_map.156 = (f32[256,512]{1,0:T(8,128)S(1)}, bf16[256,512]{1,0:T(8,128)(2,1)S(1)}, bf16[256,64]{1,0:T(8,128)(2,1)S(1)}, bf16[3,512,512]{2,1,0:T(8,128)(2,1)S(1)}, f32[64,512]{1,0:T(8,128)S(1)}) custom-call(bf16[256,512]{1,0:T(8,128)(2,1)S(1)} %shard_map.155.after, s32[1,2048]{1,0:T(1,128)S(1)} %get-tuple-element.40.code, ...), custom_call_target="tpu_custom_call" | custom-call | flops 1073741824 | bytes 5775616 | tf_op jit(solution)/shard_map/pallas_call | solution.py:291
  15.3 1.4 %collective-permute-start.2 = (bf16[256,512]{1,0:T(8,128)(2,1)S(1)}, bf16[256,512]{1,0:T(8,128)(2,1)S(1)}, u32[]{:S(2)}, u32[]{:S(2)}) collective-permute-start(bf16[256,512]{1,0:T(8,128)(2,1)S(1)} %get-tuple-element.47), channel_id=1, source_target_pairs={{0,1},{1,0},{2,3},{3,2},{4,5},{5,4},{6,7},{7,6},{8,9},{9,8},{10,11... | collective-permute-start | bytes 786440 | tf_op jit(solution)/shard_map/ppermute | solution.py:331
  16.7 0.6 %shard_map.157 = (bf16[1536,256]{1,0:T(8,128)(2,1)S(1)}, bf16[1536,128]{1,0:T(8,128)(2,1)S(1)}, bf16[384,256]{1,0:T(8,128)(2,1)S(1)}, bf16[384,128]{1,0:T(8,128)(2,1)S(1)}) custom-call(bf16[256,512]{1,0:T(8,128)(2,1)S(1)} %collective-permute-done.after.near, s32[6,256]{1,0:T(8,128)S(1)} %bitcast.6, bf16[256,64]{1,0:T(8,128)(2,1)S(1)} %get-tuple-element.44.pick.refs_0_), custom_call_target="tpu_custom_call" | custom-call | flops 40000000000 | bytes 301056 | tf_op jit(solution)/shard_map/pallas_call | solution.py:291
  17.3 2.8 %collective-permute-done.3.far = bf16[256,512]{1,0:T(8,128)(2,1)S(1)} collective-permute-done((bf16[256,512]{1,0:T(8,128)(2,1)S(1)}, bf16[256,512]{1,0:T(8,128)(2,1)S(1)}, u32[]{:S(2)}, u32[]{:S(2)}) %collective-permute-start.3) | collective-permute-done | bytes 262176 | tf_op jit(solution)/shard_map/ppermute | solution.py:340
  20.2 0.4 shard_map.158
  20.6 2.8 %collective-permute-start.4 = (bf16[64,512]{1,0:T(8,128)(2,1)S(1)}, bf16[64,512]{1,0:T(8,128)(2,1)S(1)}, u32[]{:S(2)}, u32[]{:S(2)}) collective-permute-start(bf16[64,512]{1,0:T(8,128)(2,1)S(1)} %get-tuple-element.52.halo), channel_id=1, source_target_pairs={{0,15},{1,2},{2,1},{3,4},{4,3},{5,6},{6,5},{7,8},{8,7},{9,10},{10,... | collective-permute-start | bytes 196616 | tf_op jit(solution)/shard_map/ppermute | solution.py:334
  23.7 1.5 %shard_map.160 = (f32[1536,512]{1,0:T(8,128)S(1)}, bf16[64,512]{1,0:T(8,128)(2,1)S(1)}, f32[64,512]{1,0:T(8,128)S(1)}, f32[384,512]{1,0:T(8,128)S(1)}) custom-call(bf16[256,512]{1,0:T(8,128)(2,1)S(1)} %shard_map.159.latent, bf16[2,512,512]{2,1,0:T(8,128)(2,1)S(1)} %copy-done, bf16[2,512,512]{2,1,0:T(8,128)(2,1)S(1)} %copy-done.1, f32[2,512]{1,0:T(2,128)S(1)} %copy-done.9, ...), custom_call_target="tpu_custom_call" | custom-call | flops 1 | bytes 1 | tf_op jit(solution)/shard_map/pallas_call | solution.py:291
  25.3 1.8 %collective-permute-done.4.table = bf16[64,512]{1,0:T(8,128)(2,1)S(1)} collective-permute-done((bf16[64,512]{1,0:T(8,128)(2,1)S(1)}, bf16[64,512]{1,0:T(8,128)(2,1)S(1)}, u32[]{:S(2)}, u32[]{:S(2)}) %collective-permute-start.4) | collective-permute-done | bytes 65568 | tf_op jit(solution)/shard_map/ppermute | solution.py:334
  27.1 0.5 shard_map.163.halo
  27.5 2.8 %collective-permute-start.6 = (bf16[64,512]{1,0:T(8,128)(2,1)S(1)}, bf16[64,512]{1,0:T(8,128)(2,1)S(1)}, u32[]{:S(2)}, u32[]{:S(2)}) collective-permute-start(bf16[64,512]{1,0:T(8,128)(2,1)S(1)} %shard_map.163.halo), channel_id=1, source_target_pairs={{0,15},{1,2},{2,1},{3,4},{4,3},{5,6},{6,5},{7,8},{8,7},{9,10},{10,... | collective-permute-start | bytes 196616 | tf_op jit(solution)/shard_map/ppermute | solution.py:334
  30.3 1.0 %shard_map.162.latent = bf16[256,512]{1,0:T(8,128)(2,1)S(1)} custom-call(bf16[256,512]{1,0:T(8,128)(2,1)S(1)} %shard_map.159.latent, f32[1536,512]{1,0:T(8,128)S(1)} %get-tuple-element.54.before, bf16[64,512]{1,0:T(8,128)(2,1)S(1)} %shard_map.161.across, bf16[64,512]{1,0:T(8,128)(2,1)S(1)} %collective-permute-done.5.beside, ...), custom_call_target="tpu_custom_call" | custom-call | flops 1 | bytes 1 | tf_op jit(solution)/shard_map/pallas_call | solution.py:291
  31.3 1.0 %shard_map.164 = (f32[1536,512]{1,0:T(8,128)S(1)}, bf16[64,512]{1,0:T(8,128)(2,1)S(1)}, f32[256,512]{1,0:T(8,128)S(1)}) custom-call(bf16[256,512]{1,0:T(8,128)(2,1)S(1)} %shard_map.162.latent, bf16[2,512,512]{2,1,0:T(8,128)(2,1)S(1)} %copy-done, bf16[2,512,512]{2,1,0:T(8,128)(2,1)S(1)} %copy-done.1, f32[2,512]{1,0:T(2,128)S(1)} %copy-done.9, ...), custom_call_target="tpu_custom_call" | custom-call | flops 1 | bytes 1 | tf_op jit(solution)/shard_map/pallas_call | solution.py:291
  32.4 1.6 %collective-permute-done.6.table = bf16[64,512]{1,0:T(8,128)(2,1)S(1)} collective-permute-done((bf16[64,512]{1,0:T(8,128)(2,1)S(1)}, bf16[64,512]{1,0:T(8,128)(2,1)S(1)}, u32[]{:S(2)}, u32[]{:S(2)}) %collective-permute-start.6) | collective-permute-done | bytes 65568 | tf_op jit(solution)/shard_map/ppermute | solution.py:334
  34.0 1.0 %shard_map.166.own = bf16[256,512]{1,0:T(8,128)(2,1)S(1)} custom-call(f32[1536,512]{1,0:T(8,128)S(1)} %get-tuple-element.59.before, bf16[64,512]{1,0:T(8,128)(2,1)S(1)} %shard_map.165.across, bf16[64,512]{1,0:T(8,128)(2,1)S(1)} %collective-permute-done.7.beside, bf16[1536,128]{1,0:T(8,128)(2,1)S(1)} %get-tuple-element.56.gather_halo, ...), custom_call_target="tpu_custom_call" | custom-call | flops 469762048 | bytes 5767168 | tf_op jit(solution)/shard_map/pallas_call | solution.py:291
  35.1 1.7 %collective-permute-start.10 = (bf16[256,512]{1,0:T(8,128)(2,1)S(1)}, bf16[256,512]{1,0:T(8,128)(2,1)S(1)}, u32[]{:S(2)}, u32[]{:S(2)}) collective-permute-start(bf16[256,512]{1,0:T(8,128)(2,1)S(1)} %shard_map.166.own), channel_id=1, source_target_pairs={{0,14},{1,3},{2,0},{3,5},{4,2},{5,7},{6,4},{7,9},{8,6},{9,11},{10,... | collective-permute-start | bytes 786440 | tf_op jit(solution)/shard_map/ppermute | solution.py:337
  36.7 2.3 %shard_map.167 = (bf16[2048,1280]{1,0:T(8,128)(2,1)S(1)}, f32[2048,512]{1,0:T(8,128)S(1)}, bf16[128,512]{1,0:T(8,128)(2,1)S(1)}, bf16[128,512]{1,0:T(8,128)(2,1)S(1)}) custom-call(s32[1,2048]{1,0:T(1,128)S(1)} %get-tuple-element.40.code, bf16[2048,512]{1,0:T(8,128)(2,1)S(1)} %copy-done.5, bf16[512,512]{1,0:T(8,128)(2,1)S(1)} %copy-done.8, ...), custom_call_target="tpu_custom_call" | custom-call | flops 1 | bytes 1 | tf_op jit(solution)/shard_map/pallas_call | solution.py:291
  39.1 0.5 collective-permute-start.9
  39.6 0.8 %collective-permute-done.8.refs_0_ = bf16[128,512]{1,0:T(8,128)(2,1)S(1)} collective-permute-done((bf16[128,512]{1,0:T(8,128)(2,1)S(1)}, bf16[128,512]{1,0:T(8,128)(2,1)S(1)}, u32[]{:S(2)}, u32[]{:S(2)}) %collective-permute-start.8) | collective-permute-done | bytes 131104 | tf_op jit(solution)/shard_map/ppermute | solution.py:331
  40.6 0.7 %shard_map.168 = (f32[2048,512]{1,0:T(8,128)S(1)}, bf16[256,256]{1,0:T(8,128)(2,1)S(1)}, bf16[256,256]{1,0:T(8,128)(2,1)S(1)}) custom-call(bf16[2048,1280]{1,0:T(8,128)(2,1)S(1)} %get-tuple-element.62.fetch, f32[2048,512]{1,0:T(8,128)S(1)} %get-tuple-element.63.base, bf16[256,512]{1,0:T(8,128)(2,1)S(1)} %shard_map.166.own, ...), custom_call_target="tpu_custom_call" | custom-call | flops 1 | bytes 1 | tf_op jit(solution)/shard_map/pallas_call | solution.py:291
  41.4 0.6 %collective-permute-start.18 = (bf16[256,256]{1,0:T(8,128)(2,1)S(1)}, bf16[256,256]{1,0:T(8,128)(2,1)S(1)}, u32[]{:S(2)}, u32[]{:S(2)}) collective-permute-start(bf16[256,256]{1,0:T(8,128)(2,1)S(1)} %get-tuple-element.74), channel_id=1, source_target_pairs={{0,2},{1,15},{2,4},{3,1},{4,6},{5,3},{6,8},{7,5},{8,10},{9,7},{10,... | collective-permute-start | bytes 393224 | tf_op jit(solution)/shard_map/ppermute | solution.py:340
  42.1 2.4 %collective-permute-done.10.far.table = bf16[256,512]{1,0:T(8,128)(2,1)S(1)} collective-permute-done((bf16[256,512]{1,0:T(8,128)(2,1)S(1)}, bf16[256,512]{1,0:T(8,128)(2,1)S(1)}, u32[]{:S(2)}, u32[]{:S(2)}) %collective-permute-start.10) | collective-permute-done | bytes 262176 | tf_op jit(solution)/shard_map/ppermute | solution.py:337
  44.6 0.5 collective-permute-start.15
  45.2 0.8 %collective-permute-done.15.refs_4_ = bf16[32,512]{1,0:T(8,128)(2,1)S(1)} collective-permute-done((bf16[32,512]{1,0:T(8,128)(2,1)S(1)}, bf16[32,512]{1,0:T(8,128)(2,1)S(1)}, u32[]{:S(2)}, u32[]{:S(2)}) %collective-permute-start.15) | collective-permute-done | bytes 32800 | tf_op jit(solution)/shard_map/ppermute | solution.py:331
  46.9 0.7 %shard_map.169.base = f32[2048,512]{1,0:T(8,128)S(1)} custom-call(bf16[2048,1280]{1,0:T(8,128)(2,1)S(1)} %get-tuple-element.62.fetch, f32[2048,512]{1,0:T(8,128)S(1)} %get-tuple-element.66.base, bf16[256,512]{1,0:T(8,128)(2,1)S(1)} %collective-permute-done.10.far.table), custom_call_target="tpu_custom_call" | custom-call | flops 1 | bytes 1 | tf_op jit(solution)/shard_map/pallas_call | solution.py:291
  47.7 0.7 %shard_map.171.base = f32[2048,512]{1,0:T(8,128)S(1)} custom-call(bf16[2048,1280]{1,0:T(8,128)(2,1)S(1)} %get-tuple-element.62.fetch, f32[2048,512]{1,0:T(8,128)S(1)} %shard_map.169.base, bf16[48,512]{1,0:T(8,128)(2,1)S(1)} %collective-permute-done.11.refs_0_, bf16[48,512]{1,0:T(8,128)(2,1)S(1)} %collective-permute-done.12.refs_1_, ...), custom_call_target="tpu_custom_call" | custom-call | flops 1 | bytes 1 | tf_op jit(solution)/shard_map/pallas_call | solution.py:291
  48.5 0.7 %collective-permute-done.18.near = bf16[256,256]{1,0:T(8,128)(2,1)S(1)} collective-permute-done((bf16[256,256]{1,0:T(8,128)(2,1)S(1)}, bf16[256,256]{1,0:T(8,128)(2,1)S(1)}, u32[]{:S(2)}, u32[]{:S(2)}) %collective-permute-start.18) | collective-permute-done | bytes 131104 | tf_op jit(solution)/shard_map/ppermute | solution.py:340
  49.2 1.1 %shard_map.172.partial = f32[2048,512]{1,0:T(8,128)S(1)} custom-call(bf16[2048,1280]{1,0:T(8,128)(2,1)S(1)} %get-tuple-element.62.fetch, f32[2048,512]{1,0:T(8,128)S(1)} %shard_map.171.base, bf16[256,256]{1,0:T(8,128)(2,1)S(1)} %collective-permute-done.18.near, bf16[512,512]{1,0:T(8,128)(2,1)S(1)} %copy-done.3), custom_call_target="tpu_custom_call" | custom-call | flops 1 | bytes 1 | tf_op jit(solution)/shard_map/pallas_call | solution.py:291
  50.6 1.9 %shard_map.173 = bf16[2048,512]{1,0:T(8,128)(2,1)} custom-call(bf16[2048,1280]{1,0:T(8,128)(2,1)S(1)} %get-tuple-element.62.fetch, f32[2048,512]{1,0:T(8,128)S(1)} %shard_map.171.base, bf16[256,256]{1,0:T(8,128)(2,1)S(1)} %collective-permute-done.17.near, bf16[512,512]{1,0:T(8,128)(2,1)S(1)} %copy-done.3, f32[2048,512]{1,0:T(8,128)S(1)} %shard_map.172.partial), custom_call_target="tpu_custom_call" | custom-call | flops 1610612736 | bytes 14286848 | tf_op jit(solution)/shard_map/pallas_call | solution.py:291
  (50 shorter events, 2.4 us)
Async XLA Ops:
  0.0 11.1 %copy-start.10 = (s32[64]{0:T(128)S(1)}, s32[64]{0:T(128)}, u32[]{:S(2)}) copy-start(s32[64]{0:T(128)} %param.20) | copy-start | bytes 772
  4.2 6.1 %collective-permute-start.1 = (bf16[256,512]{1,0:T(8,128)(2,1)S(1)}, bf16[256,512]{1,0:T(8,128)(2,1)S(1)}, u32[]{:S(2)}, u32[]{:S(2)}) collective-permute-start(bf16[256,512]{1,0:T(8,128)(2,1)S(1)} %get-tuple-element.43), channel_id=1, source_target_pairs={{0,1},{1,0},{2,3},{3,2},{4,5},{5,4},{6,7},{7,6},{8,9},{9,8},{10,11... | collective-permute-start | bytes 786440 | tf_op jit(solution)/shard_map/ppermute | solution.py:331
  4.7 11.9 %collective-permute-start = (bf16[256,512]{1,0:T(8,128)(2,1)S(1)}, bf16[256,512]{1,0:T(8,128)(2,1)S(1)}, u32[]{:S(2)}, u32[]{:S(2)}) collective-permute-start(bf16[256,512]{1,0:T(8,128)(2,1)S(1)} %get-tuple-element.41), channel_id=1, source_target_pairs={{0,14},{1,3},{2,0},{3,5},{4,2},{5,7},{6,4},{7,9},{8,6},{9,11},{10,... | collective-permute-start | bytes 786440 | tf_op jit(solution)/shard_map/ppermute | solution.py:337
  10.3 6.3 %copy-start.11 = (s32[256,6]{0,1:T(8,128)S(1)}, s32[256,6]{0,1:T(8,128)}, u32[]{:S(2)}) copy-start(s32[256,6]{0,1:T(8,128)} %param.21) | copy-start | bytes 18436
  11.0 9.1 %collective-permute-start.3 = (bf16[256,512]{1,0:T(8,128)(2,1)S(1)}, bf16[256,512]{1,0:T(8,128)(2,1)S(1)}, u32[]{:S(2)}, u32[]{:S(2)}) collective-permute-start(bf16[256,512]{1,0:T(8,128)(2,1)S(1)} %shard_map.155.after), channel_id=1, source_target_pairs={{0,2},{1,15},{2,4},{3,1},{4,6},{5,3},{6,8},{7,5},{8,10},{9,7},{10,... | collective-permute-start | bytes 786440 | tf_op jit(solution)/shard_map/ppermute | solution.py:340
  15.3 4.9 %collective-permute-start.2 = (bf16[256,512]{1,0:T(8,128)(2,1)S(1)}, bf16[256,512]{1,0:T(8,128)(2,1)S(1)}, u32[]{:S(2)}, u32[]{:S(2)}) collective-permute-start(bf16[256,512]{1,0:T(8,128)(2,1)S(1)} %get-tuple-element.47), channel_id=1, source_target_pairs={{0,1},{1,0},{2,3},{3,2},{4,5},{5,4},{6,7},{7,6},{8,9},{9,8},{10,11... | collective-permute-start | bytes 786440 | tf_op jit(solution)/shard_map/ppermute | solution.py:331
  16.7 6.7 %copy-start.4 = (bf16[512,512]{1,0:T(8,128)(2,1)S(1)}, bf16[512,512]{1,0:T(8,128)(2,1)}, u32[]{:S(2)}) copy-start(bf16[512,512]{1,0:T(8,128)(2,1)} %w2.1) | copy-start | bytes 1572868
  16.7 6.7 %copy-start.7 = (bf16[256,512]{1,0:T(8,128)(2,1)S(1)}, bf16[256,512]{1,0:T(8,128)(2,1)}, u32[]{:S(2)}) copy-start(bf16[256,512]{1,0:T(8,128)(2,1)} %mesh.1) | copy-start | bytes 786436
  17.3 6.4 %copy-start = (bf16[2,512,512]{2,1,0:T(8,128)(2,1)S(1)}, bf16[2,512,512]{2,1,0:T(8,128)(2,1)}, u32[]{:S(2)}) copy-start(bf16[2,512,512]{2,1,0:T(8,128)(2,1)} %w_src.3) | copy-start | bytes 3145732
  17.3 6.4 %copy-start.1 = (bf16[2,512,512]{2,1,0:T(8,128)(2,1)S(1)}, bf16[2,512,512]{2,1,0:T(8,128)(2,1)}, u32[]{:S(2)}) copy-start(bf16[2,512,512]{2,1,0:T(8,128)(2,1)} %w_dst.3) | copy-start | bytes 3145732
  17.3 6.4 %copy-start.9 = (f32[2,512]{1,0:T(2,128)S(1)}, f32[2,512]{1,0:T(2,128)}, u32[]{:S(2)}) copy-start(f32[2,512]{1,0:T(2,128)} %bias.3) | copy-start | bytes 12292
  20.6 6.5 %collective-permute-start.4 = (bf16[64,512]{1,0:T(8,128)(2,1)S(1)}, bf16[64,512]{1,0:T(8,128)(2,1)S(1)}, u32[]{:S(2)}, u32[]{:S(2)}) collective-permute-start(bf16[64,512]{1,0:T(8,128)(2,1)S(1)} %get-tuple-element.52.halo), channel_id=1, source_target_pairs={{0,15},{1,2},{2,1},{3,4},{4,3},{5,6},{6,5},{7,8},{8,7},{9,10},{10,... | collective-permute-start | bytes 196616 | tf_op jit(solution)/shard_map/ppermute | solution.py:334
  25.2 5.1 %copy-start.2 = (bf16[2,512,512]{2,1,0:T(8,128)(2,1)S(1)}, bf16[2,512,512]{2,1,0:T(8,128)(2,1)}, u32[]{:S(2)}) copy-start(bf16[2,512,512]{2,1,0:T(8,128)(2,1)} %w_out.3) | copy-start | bytes 3145732
  25.2 1.9 %collective-permute-start.5 = (bf16[64,512]{1,0:T(8,128)(2,1)S(1)}, bf16[64,512]{1,0:T(8,128)(2,1)S(1)}, u32[]{:S(2)}, u32[]{:S(2)}) collective-permute-start(bf16[64,512]{1,0:T(8,128)(2,1)S(1)} %get-tuple-element.55), channel_id=1, source_target_pairs={{0,1},{1,0},{2,3},{3,2},{4,5},{5,4},{6,7},{7,6},{8,9},{9,8},{10,11... | collective-permute-start | bytes 196616 | tf_op jit(solution)/shard_map/ppermute | solution.py:331
  27.1 4.3 %copy-start.6 = (bf16[512,512]{1,0:T(8,128)(2,1)S(1)}, bf16[512,512]{1,0:T(8,128)(2,1)}, u32[]{:S(2)}) copy-start(bf16[512,512]{1,0:T(8,128)(2,1)} %w_next.3) | copy-start | bytes 1572868
  27.5 6.5 %collective-permute-start.6 = (bf16[64,512]{1,0:T(8,128)(2,1)S(1)}, bf16[64,512]{1,0:T(8,128)(2,1)S(1)}, u32[]{:S(2)}, u32[]{:S(2)}) collective-permute-start(bf16[64,512]{1,0:T(8,128)(2,1)S(1)} %shard_map.163.halo), channel_id=1, source_target_pairs={{0,15},{1,2},{2,1},{3,4},{4,3},{5,6},{6,5},{7,8},{8,7},{9,10},{10,... | collective-permute-start | bytes 196616 | tf_op jit(solution)/shard_map/ppermute | solution.py:334
  32.3 1.7 %collective-permute-start.7 = (bf16[64,512]{1,0:T(8,128)(2,1)S(1)}, bf16[64,512]{1,0:T(8,128)(2,1)S(1)}, u32[]{:S(2)}, u32[]{:S(2)}) collective-permute-start(bf16[64,512]{1,0:T(8,128)(2,1)S(1)} %get-tuple-element.60), channel_id=1, source_target_pairs={{0,1},{1,0},{2,3},{3,2},{4,5},{5,4},{6,7},{7,6},{8,9},{9,8},{10,11... | collective-permute-start | bytes 196616 | tf_op jit(solution)/shard_map/ppermute | solution.py:331
  34.0 2.7 %copy-start.5 = (bf16[2048,512]{1,0:T(8,128)(2,1)S(1)}, bf16[2048,512]{1,0:T(8,128)(2,1)}, u32[]{:S(2)}) copy-start(bf16[2048,512]{1,0:T(8,128)(2,1)} %grid.3) | copy-start | bytes 6291460
  34.0 2.7 %copy-start.8 = (bf16[512,512]{1,0:T(8,128)(2,1)S(1)}, bf16[512,512]{1,0:T(8,128)(2,1)}, u32[]{:S(2)}) copy-start(bf16[512,512]{1,0:T(8,128)(2,1)} %w_grid.1) | copy-start | bytes 1572868
  35.1 9.5 %collective-permute-start.10 = (bf16[256,512]{1,0:T(8,128)(2,1)S(1)}, bf16[256,512]{1,0:T(8,128)(2,1)S(1)}, u32[]{:S(2)}, u32[]{:S(2)}) collective-permute-start(bf16[256,512]{1,0:T(8,128)(2,1)S(1)} %shard_map.166.own), channel_id=1, source_target_pairs={{0,14},{1,3},{2,0},{3,5},{4,2},{5,7},{6,4},{7,9},{8,6},{9,11},{10,... | collective-permute-start | bytes 786440 | tf_op jit(solution)/shard_map/ppermute | solution.py:337
  39.0 1.4 %collective-permute-start.8 = (bf16[128,512]{1,0:T(8,128)(2,1)S(1)}, bf16[128,512]{1,0:T(8,128)(2,1)S(1)}, u32[]{:S(2)}, u32[]{:S(2)}) collective-permute-start(bf16[128,512]{1,0:T(8,128)(2,1)S(1)} %get-tuple-element.64), channel_id=1, source_target_pairs={{0,1},{1,0},{2,3},{3,2},{4,5},{5,4},{6,7},{7,6},{8,9},{9,8},{10,11... | collective-permute-start | bytes 393224 | tf_op jit(solution)/shard_map/ppermute | solution.py:331
  39.1 1.5 %collective-permute-start.9 = (bf16[128,512]{1,0:T(8,128)(2,1)S(1)}, bf16[128,512]{1,0:T(8,128)(2,1)S(1)}, u32[]{:S(2)}, u32[]{:S(2)}) collective-permute-start(bf16[128,512]{1,0:T(8,128)(2,1)S(1)} %get-tuple-element.65), channel_id=1, source_target_pairs={{0,1},{1,0},{2,3},{3,2},{4,5},{5,4},{6,7},{7,6},{8,9},{9,8},{10,11... | collective-permute-start | bytes 393224 | tf_op jit(solution)/shard_map/ppermute | solution.py:331
  41.4 7.8 %collective-permute-start.18 = (bf16[256,256]{1,0:T(8,128)(2,1)S(1)}, bf16[256,256]{1,0:T(8,128)(2,1)S(1)}, u32[]{:S(2)}, u32[]{:S(2)}) collective-permute-start(bf16[256,256]{1,0:T(8,128)(2,1)S(1)} %get-tuple-element.74), channel_id=1, source_target_pairs={{0,2},{1,15},{2,4},{3,1},{4,6},{5,3},{6,8},{7,5},{8,10},{9,7},{10,... | collective-permute-start | bytes 393224 | tf_op jit(solution)/shard_map/ppermute | solution.py:340
  42.0 8.6 %collective-permute-start.17 = (bf16[256,256]{1,0:T(8,128)(2,1)S(1)}, bf16[256,256]{1,0:T(8,128)(2,1)S(1)}, u32[]{:S(2)}, u32[]{:S(2)}) collective-permute-start(bf16[256,256]{1,0:T(8,128)(2,1)S(1)} %get-tuple-element.73), channel_id=1, source_target_pairs={{0,2},{1,15},{2,4},{3,1},{4,6},{5,3},{6,8},{7,5},{8,10},{9,7},{10,... | collective-permute-start | bytes 393224 | tf_op jit(solution)/shard_map/ppermute | solution.py:340
  44.5 2.0 %collective-permute-start.11 = (bf16[48,512]{1,0:T(8,128)(2,1)S(1)}, bf16[48,512]{1,0:T(8,128)(2,1)S(1)}, u32[]{:S(2)}, u32[]{:S(2)}) collective-permute-start(bf16[48,512]{1,0:T(8,128)(2,1)S(1)} %get-tuple-element.67), channel_id=1, source_target_pairs={{0,1},{1,0},{2,3},{3,2},{4,5},{5,4},{6,7},{7,6},{8,9},{9,8},{10,11... | collective-permute-start | bytes 147464 | tf_op jit(solution)/shard_map/ppermute | solution.py:331
  44.6 1.4 %collective-permute-start.15 = (bf16[32,512]{1,0:T(8,128)(2,1)S(1)}, bf16[32,512]{1,0:T(8,128)(2,1)S(1)}, u32[]{:S(2)}, u32[]{:S(2)}) collective-permute-start(bf16[32,512]{1,0:T(8,128)(2,1)S(1)} %get-tuple-element.71), channel_id=1, source_target_pairs={{0,1},{1,0},{2,3},{3,2},{4,5},{5,4},{6,7},{7,6},{8,9},{9,8},{10,11... | collective-permute-start | bytes 98312 | tf_op jit(solution)/shard_map/ppermute | solution.py:331
  45.1 1.2 %collective-permute-start.16 = (bf16[32,512]{1,0:T(8,128)(2,1)S(1)}, bf16[32,512]{1,0:T(8,128)(2,1)S(1)}, u32[]{:S(2)}, u32[]{:S(2)}) collective-permute-start(bf16[32,512]{1,0:T(8,128)(2,1)S(1)} %get-tuple-element.72), channel_id=1, source_target_pairs={{0,1},{1,0},{2,3},{3,2},{4,5},{5,4},{6,7},{7,6},{8,9},{9,8},{10,11... | collective-permute-start | bytes 98312 | tf_op jit(solution)/shard_map/ppermute | solution.py:331
  46.0 1.6 %collective-permute-start.12 = (bf16[48,512]{1,0:T(8,128)(2,1)S(1)}, bf16[48,512]{1,0:T(8,128)(2,1)S(1)}, u32[]{:S(2)}, u32[]{:S(2)}) collective-permute-start(bf16[48,512]{1,0:T(8,128)(2,1)S(1)} %get-tuple-element.68), channel_id=1, source_target_pairs={{0,1},{1,0},{2,3},{3,2},{4,5},{5,4},{6,7},{7,6},{8,9},{9,8},{10,11... | collective-permute-start | bytes 147464 | tf_op jit(solution)/shard_map/ppermute | solution.py:331
  46.3 1.3 %collective-permute-start.13 = (bf16[48,512]{1,0:T(8,128)(2,1)S(1)}, bf16[48,512]{1,0:T(8,128)(2,1)S(1)}, u32[]{:S(2)}, u32[]{:S(2)}) collective-permute-start(bf16[48,512]{1,0:T(8,128)(2,1)S(1)} %get-tuple-element.69), channel_id=1, source_target_pairs={{0,1},{1,0},{2,3},{3,2},{4,5},{5,4},{6,7},{7,6},{8,9},{9,8},{10,11... | collective-permute-start | bytes 147464 | tf_op jit(solution)/shard_map/ppermute | solution.py:331
  46.5 1.2 %collective-permute-start.14 = (bf16[48,512]{1,0:T(8,128)(2,1)S(1)}, bf16[48,512]{1,0:T(8,128)(2,1)S(1)}, u32[]{:S(2)}, u32[]{:S(2)}) collective-permute-start(bf16[48,512]{1,0:T(8,128)(2,1)S(1)} %get-tuple-element.70), channel_id=1, source_target_pairs={{0,1},{1,0},{2,3},{3,2},{4,5},{5,4},{6,7},{7,6},{8,9},{9,8},{10,11... | collective-permute-start | bytes 147464 | tf_op jit(solution)/shard_map/ppermute | solution.py:331
  47.6 1.6 %copy-start.3 = (bf16[512,512]{1,0:T(8,128)(2,1)S(1)}, bf16[512,512]{1,0:T(8,128)(2,1)}, u32[]{:S(2)}) copy-start(bf16[512,512]{1,0:T(8,128)(2,1)} %w_out.5) | copy-start | bytes 1572868

commit v7 on v6

--- a/solution.py
+++ b/solution.py
@@ -91,13 +91,15 @@
 
 def chip_kernel(after, code, hidden, halo_index, *refs):
     del after
-    held, (own, sibling, pick, joined, kept), buffers, sems = refs[:5], refs[5:10], refs[10:15], refs[15]
+    held, (own, sibling, pick, joined, kept, fetch), buffers, sems = refs[:5], refs[5:11], refs[11:16], refs[16]
     copies = [pltpu.make_async_copy(a, b, sems.at[i]) for i, (a, b) in enumerate(zip(held, buffers))]
     for copy in copies:
         copy.start()
     rows = own.shape[0]
     sibling[...] = dot(one_hot_down(code[...], 3 * rows, rows), hidden[...]).astype(BF16)
     own[...] = dot(one_hot_down(code[...], 2 * rows, rows), hidden[...])
+    for r in range(0, fetch.shape[0], BLOCK):
+        fetch[r : r + BLOCK] = one_hot_across(code[:, r : r + BLOCK], fetch.shape[1])
     for copy in copies:
         copy.wait()
     mesh, w2, w_src, w_out, w_mesh = buffers
@@ -188,12 +190,11 @@
     projected[...] = (kept[...] + dot(sums, joined[L])).astype(BF16)
 
 
-def base_kernel(code, grid, w_grid, own, fetch, base, *pieces):
+def base_kernel(grid, w_grid, fetch, own, base, *pieces):
     rows = own.shape[0]
     cut_kernel(own, *pieces)
     for r in range(0, grid.shape[0], BLOCK):
         spot = slice(r, r + BLOCK)
-        fetch[spot] = one_hot_across(code[:, spot], fetch.shape[1])
         base[spot] = dot(grid[spot], w_grid[...]) * 0.5 + dot(fetch[spot, 2 * rows : 3 * rows], own[...])
 
 
@@ -362,7 +363,7 @@
     crossed = swap(cross)
     (sent,) = call(far_kernel, [code, hidden, crossed], [table], 1)
     far = to_far(sent)
-    own, sibling, pick, joined, kept = call(
+    own, sibling, pick, joined, kept, fetch = call(
         chip_kernel,
         [sent, code, hidden, halo_index.reshape(1, border), mesh_feat, w_enc2, proc_src, proc_out, dec_mesh],
         [
@@ -371,6 +372,7 @@
             ((mesh_rows, border), BF16),
             ((L + 1, width, width), BF16),
             ((border, width), F32),
+            ((rows, 5 * mesh_rows), BF16),
         ],
         unit * 2 * mesh_rows,
         [
@@ -446,10 +448,10 @@
     far = to_near(projected)
     f32_rows = ((rows, width), F32)
     pieces = [((mesh_rows // 2, width), BF16)] * 2
-    fetch, base, *passed = call(
+    base, *passed = call(
         base_kernel,
-        [code, grid, dec_grid, projected],
-        [((rows, 5 * mesh_rows), BF16), f32_rows, *pieces],
+        [grid, dec_grid, fetch, projected],
+        [f32_rows, *pieces],
         1,
     )
     sibling = [swap(piece) for piece in passed]
@@ -457,7 +459,7 @@
     base, left, right = call(sibling_kernel, [fetch, base, projected, *sibling], [f32_rows, half, half], 1)
     left = to_far(left)
     right = to_far(right)
-    passed = call(cut_kernel, [far], [((mesh_rows * part_rows // 256, width), BF16) for part_rows in (48, 48, 48, 48, 32, 32)], 1)
+    passed = call(cut_kernel, [far], [((mesh_rows * part_rows // 256, width), BF16) for part_rows in (64, 48, 48, 48, 48)], 1)
     cross = [swap(piece) for piece in passed]
     (base,) = call(far_add_kernel, [fetch, base, far], [f32_rows], 1)
     (base,) = call(cross_add_kernel, [fetch, base, *cross], [f32_rows], 1)

time: 52.8 us -> 52.1 us (0.987)
  Pallas kernels: 22.8 us -> 21.1 us
  waiting for transfers between devices: 11.7 us -> 12.9 us
    pallas_call x20, Pallas kernels: 22.8 us -> 21.1 us  [call(): pl.pallas_call(kernel, in_specs=[pl.BlockSpec(memory_space=space) for spa...]
    ppermute x2, waiting for transfers between devices: 2.44 us -> 3.56 us  [to_near(): return lax.ppermute(value, AXES, sided(-2))]
    ppermute x12 -> x11, starting transfers between devices: 4.1 us -> 3.75 us  [swap(): return lax.ppermute(value, AXES, sided(1))]
    ppermute x12 -> x11, waiting for transfers between devices: 1.96 us -> 1.83 us  [swap(): return lax.ppermute(value, AXES, sided(1))]
  transfers between devices with their start and end apart: 19 -> 18, of which waited for: 10 -> 9; matrix products, arithmetic and copies ran while one was open for 0% -> 0% of each run, Pallas kernels for 28% -> 25%
where the time goes in v7:
time: 52.1 us; the launch traced here: 51.9 us
  Pallas kernels  21.1 us (40%)
  starting transfers between devices  17.3 us (33%)
  waiting for transfers between devices  12.9 us (25%)
    pallas_call x20, Pallas kernels, call(): pl.pallas_call(kernel, in_specs=[pl.BlockSpec(memory_space=space) for spa...  21.1 us
    ppermute x2, starting transfers between devices, to_near(): return lax.ppermute(value, AXES, sided(-2))  7.16 us
    ppermute x2, starting transfers between devices, to_across(): return lax.ppermute(value, AXES, sided(-1))  5.54 us
    ppermute x3, waiting for transfers between devices, to_far(): return lax.ppermute(value, AXES, sided(2))  4.03 us
    ppermute x11, starting transfers between devices, swap(): return lax.ppermute(value, AXES, sided(1))  3.75 us
    ppermute x2, waiting for transfers between devices, to_near(): return lax.ppermute(value, AXES, sided(-2))  3.56 us
    ppermute x2, waiting for transfers between devices, to_across(): return lax.ppermute(value, AXES, sided(-1))  3.45 us
    ppermute x11, waiting for transfers between devices, swap(): return lax.ppermute(value, AXES, sided(1))  1.83 us
  transfers between devices with their start and end apart: 18, of which 9 were waited for; matrix products, arithmetic and copies ran while one was open for 0% of the time, Pallas kernels for 25%

profile of v7, /device:TPU:0, one launch (start us, length us, event | category | flops | bytes accessed | tf_op | source)
XLA Modules:
  0.0 51.9 jit_solution(15552548544026180788)
XLA Ops:
  0.0 4.2 %shard_map.154 = (bf16[2048,512]{1,0:T(8,128)(2,1)S(1)}, bf16[256,512]{1,0:T(8,128)(2,1)S(1)}, bf16[256,512]{1,0:T(8,128)(2,1)S(1)}, s32[1,2048]{1,0:T(1,128)S(1)}) custom-call(s32[1,2048]{1,0:T(1,128)} %bitcast.7, s32[1,2048]{1,0:T(1,128)} %bitcast.8, bf16[2048,512]{1,0:T(8,128)(2,1)} %grid.3, bf16[512,512]{1,0:T(8,128)(2,1)} %w1.1, f32[1,512]{1,0:T(1,128)} %bitcast.9), custom_call_target="tpu_custom_call" | custom-call | flops 2147483648 | bytes 2639872 | tf_op jit(solution)/shard_map/pallas_call | solution.py:292
  4.2 0.5 collective-permute-start
  4.7 5.6 %collective-permute-start.1 = (bf16[256,512]{1,0:T(8,128)(2,1)S(1)}, bf16[256,512]{1,0:T(8,128)(2,1)S(1)}, u32[]{:S(2)}, u32[]{:S(2)}) collective-permute-start(bf16[256,512]{1,0:T(8,128)(2,1)S(1)} %get-tuple-element.43), channel_id=1, source_target_pairs={{0,14},{1,3},{2,0},{3,5},{4,2},{5,7},{6,4},{7,9},{8,6},{9,11},{10,... | collective-permute-start | bytes 786440 | tf_op jit(solution)/shard_map/ppermute | solution.py:338
  10.3 0.7 %shard_map.155.after = bf16[256,512]{1,0:T(8,128)(2,1)S(1)} custom-call(s32[1,2048]{1,0:T(1,128)S(1)} %get-tuple-element.39.code, bf16[2048,512]{1,0:T(8,128)(2,1)S(1)} %get-tuple-element.40.hidden, bf16[256,512]{1,0:T(8,128)(2,1)S(1)} %collective-permute-done.crossed), custom_call_target="tpu_custom_call" | custom-call | flops 1 | bytes 1 | tf_op jit(solution)/shard_map/pallas_call | solution.py:292
  11.1 3.1 %shard_map.156 = (f32[256,512]{1,0:T(8,128)S(1)}, bf16[256,512]{1,0:T(8,128)(2,1)S(1)}, bf16[256,64]{1,0:T(8,128)(2,1)S(1)}, bf16[3,512,512]{2,1,0:T(8,128)(2,1)...) custom-call(bf16[256,512]{1,0:T(8,128)(2,1)S(1)} %shard_map.155.after, ...), custom_call_target="tpu_custom_call" | custom-call | flops 1073741824 | bytes 5775616 | tf_op jit(solution)/shard_map/pallas_call | solution.py:292
  14.3 1.4 %collective-permute-start.2 = (bf16[256,512]{1,0:T(8,128)(2,1)S(1)}, bf16[256,512]{1,0:T(8,128)(2,1)S(1)}, u32[]{:S(2)}, u32[]{:S(2)}) collective-permute-start(bf16[256,512]{1,0:T(8,128)(2,1)S(1)} %get-tuple-element.47), channel_id=1, source_target_pairs={{0,1},{1,0},{2,3},{3,2},{4,5},{5,4},{6,7},{7,6},{8,9},{9,8},{10,11... | collective-permute-start | bytes 786440 | tf_op jit(solution)/shard_map/ppermute | solution.py:332
  15.7 0.6 %shard_map.157 = (bf16[1536,256]{1,0:T(8,128)(2,1)S(1)}, bf16[1536,128]{1,0:T(8,128)(2,1)S(1)}, bf16[384,256]{1,0:T(8,128)(2,1)S(1)}, bf16[384,128]{1,0:T(8,128)(2,1)S(1)}) custom-call(bf16[256,512]{1,0:T(8,128)(2,1)S(1)} %collective-permute-done.1.after.near, s32[6,256]{1,0:T(8,128)S(1)} %bitcast.6, bf16[256,64]{1,0:T(8,128)(2,1)S(1)} %get-tuple-element.44.pick.refs_0_), custom_call_target="tpu_custom_call" | custom-call | flops 40000000000 | bytes 301056 | tf_op jit(solution)/shard_map/pallas_call | solution.py:292
  16.3 3.8 %collective-permute-done.3.far = bf16[256,512]{1,0:T(8,128)(2,1)S(1)} collective-permute-done((bf16[256,512]{1,0:T(8,128)(2,1)S(1)}, bf16[256,512]{1,0:T(8,128)(2,1)S(1)}, u32[]{:S(2)}, u32[]{:S(2)}) %collective-permute-start.3) | collective-permute-done | bytes 262176 | tf_op jit(solution)/shard_map/ppermute | solution.py:341
  20.2 0.4 shard_map.158
  20.6 2.8 %collective-permute-start.4 = (bf16[64,512]{1,0:T(8,128)(2,1)S(1)}, bf16[64,512]{1,0:T(8,128)(2,1)S(1)}, u32[]{:S(2)}, u32[]{:S(2)}) collective-permute-start(bf16[64,512]{1,0:T(8,128)(2,1)S(1)} %get-tuple-element.52.halo), channel_id=1, source_target_pairs={{0,15},{1,2},{2,1},{3,4},{4,3},{5,6},{6,5},{7,8},{8,7},{9,10},{10,... | collective-permute-start | bytes 196616 | tf_op jit(solution)/shard_map/ppermute | solution.py:335
  23.7 1.5 %shard_map.160 = (f32[1536,512]{1,0:T(8,128)S(1)}, bf16[64,512]{1,0:T(8,128)(2,1)S(1)}, f32[64,512]{1,0:T(8,128)S(1)}, f32[384,512]{1,0:T(8,128)S(1)}) custom-call(bf16[256,512]{1,0:T(8,128)(2,1)S(1)} %shard_map.159.latent, bf16[2,512,512]{2,1,0:T(8,128)(2,1)S(1)} %copy-done, bf16[2,512,512]{2,1,0:T(8,128)(2,1)S(1)} %copy-done.1, f32[2,512]{1,0:T(2,128)S(1)} %copy-done.9, ...), custom_call_target="tpu_custom_call" | custom-call | flops 1 | bytes 1 | tf_op jit(solution)/shard_map/pallas_call | solution.py:292
  25.3 1.8 %collective-permute-done.4.table = bf16[64,512]{1,0:T(8,128)(2,1)S(1)} collective-permute-done((bf16[64,512]{1,0:T(8,128)(2,1)S(1)}, bf16[64,512]{1,0:T(8,128)(2,1)S(1)}, u32[]{:S(2)}, u32[]{:S(2)}) %collective-permute-start.4) | collective-permute-done | bytes 65568 | tf_op jit(solution)/shard_map/ppermute | solution.py:335
  27.1 0.5 shard_map.163.halo
  27.5 2.8 %collective-permute-start.6 = (bf16[64,512]{1,0:T(8,128)(2,1)S(1)}, bf16[64,512]{1,0:T(8,128)(2,1)S(1)}, u32[]{:S(2)}, u32[]{:S(2)}) collective-permute-start(bf16[64,512]{1,0:T(8,128)(2,1)S(1)} %shard_map.163.halo), channel_id=1, source_target_pairs={{0,15},{1,2},{2,1},{3,4},{4,3},{5,6},{6,5},{7,8},{8,7},{9,10},{10,... | collective-permute-start | bytes 196616 | tf_op jit(solution)/shard_map/ppermute | solution.py:335
  30.3 0.9 %shard_map.162.latent = bf16[256,512]{1,0:T(8,128)(2,1)S(1)} custom-call(bf16[256,512]{1,0:T(8,128)(2,1)S(1)} %shard_map.159.latent, f32[1536,512]{1,0:T(8,128)S(1)} %get-tuple-element.54.before, bf16[64,512]{1,0:T(8,128)(2,1)S(1)} %shard_map.161.across, bf16[64,512]{1,0:T(8,128)(2,1)S(1)} %collective-permute-done.5.beside, ...), custom_call_target="tpu_custom_call" | custom-call | flops 1 | bytes 1 | tf_op jit(solution)/shard_map/pallas_call | solution.py:292
  31.2 1.0 %shard_map.164 = (f32[1536,512]{1,0:T(8,128)S(1)}, bf16[64,512]{1,0:T(8,128)(2,1)S(1)}, f32[256,512]{1,0:T(8,128)S(1)}) custom-call(bf16[256,512]{1,0:T(8,128)(2,1)S(1)} %shard_map.162.latent, bf16[2,512,512]{2,1,0:T(8,128)(2,1)S(1)} %copy-done, bf16[2,512,512]{2,1,0:T(8,128)(2,1)S(1)} %copy-done.1, f32[2,512]{1,0:T(2,128)S(1)} %copy-done.9, ...), custom_call_target="tpu_custom_call" | custom-call | flops 1 | bytes 1 | tf_op jit(solution)/shard_map/pallas_call | solution.py:292
  32.3 1.7 %collective-permute-done.6.table = bf16[64,512]{1,0:T(8,128)(2,1)S(1)} collective-permute-done((bf16[64,512]{1,0:T(8,128)(2,1)S(1)}, bf16[64,512]{1,0:T(8,128)(2,1)S(1)}, u32[]{:S(2)}, u32[]{:S(2)}) %collective-permute-start.6) | collective-permute-done | bytes 65568 | tf_op jit(solution)/shard_map/ppermute | solution.py:335
  34.0 0.9 %shard_map.166.own = bf16[256,512]{1,0:T(8,128)(2,1)S(1)} custom-call(f32[1536,512]{1,0:T(8,128)S(1)} %get-tuple-element.59.before, bf16[64,512]{1,0:T(8,128)(2,1)S(1)} %shard_map.165.across, bf16[64,512]{1,0:T(8,128)(2,1)S(1)} %collective-permute-done.7.beside, bf16[1536,128]{1,0:T(8,128)(2,1)S(1)} %get-tuple-element.56.gather_halo, ...), custom_call_target="tpu_custom_call" | custom-call | flops 469762048 | bytes 5767168 | tf_op jit(solution)/shard_map/pallas_call | solution.py:292
  35.0 1.6 %collective-permute-start.10 = (bf16[256,512]{1,0:T(8,128)(2,1)S(1)}, bf16[256,512]{1,0:T(8,128)(2,1)S(1)}, u32[]{:S(2)}, u32[]{:S(2)}) collective-permute-start(bf16[256,512]{1,0:T(8,128)(2,1)S(1)} %shard_map.166.own), channel_id=1, source_target_pairs={{0,14},{1,3},{2,0},{3,5},{4,2},{5,7},{6,4},{7,9},{8,6},{9,11},{10,... | collective-permute-start | bytes 786440 | tf_op jit(solution)/shard_map/ppermute | solution.py:338
  36.5 1.8 %shard_map.167 = (f32[2048,512]{1,0:T(8,128)S(1)}, bf16[128,512]{1,0:T(8,128)(2,1)S(1)}, bf16[128,512]{1,0:T(8,128)(2,1)S(1)}) custom-call(bf16[2048,512]{1,0:T(8,128)(2,1)S(1)} %copy-done.6, bf16[512,512]{1,0:T(8,128)(2,1)S(1)} %copy-done.8, bf16[2048,1280]{1,0:T(8,128)(2,1)S(1)} %get-tuple-element.42.fetch, bf16[256,512]{1,0:T(8,128)(2,1)S(1)} %shard_map.166.own), custom_call_target="tpu_custom_call" | custom-call | flops 1 | bytes 1 | tf_op jit(solution)/shard_map/pallas_call | solution.py:292
  38.4 0.5 collective-permute-start.9
  38.9 0.8 %collective-permute-done.8.refs_0_ = bf16[128,512]{1,0:T(8,128)(2,1)S(1)} collective-permute-done((bf16[128,512]{1,0:T(8,128)(2,1)S(1)}, bf16[128,512]{1,0:T(8,128)(2,1)S(1)}, u32[]{:S(2)}, u32[]{:S(2)}) %collective-permute-start.8) | collective-permute-done | bytes 131104 | tf_op jit(solution)/shard_map/ppermute | solution.py:332
  39.9 0.7 %shard_map.168 = (f32[2048,512]{1,0:T(8,128)S(1)}, bf16[256,256]{1,0:T(8,128)(2,1)S(1)}, bf16[256,256]{1,0:T(8,128)(2,1)S(1)}) custom-call(bf16[2048,1280]{1,0:T(8,128)(2,1)S(1)} %get-tuple-element.42.fetch, f32[2048,512]{1,0:T(8,128)S(1)} %get-tuple-element.62.base, bf16[256,512]{1,0:T(8,128)(2,1)S(1)} %shard_map.166.own, ...), custom_call_target="tpu_custom_call" | custom-call | flops 1 | bytes 1 | tf_op jit(solution)/shard_map/pallas_call | solution.py:292
  40.7 0.8 %collective-permute-start.17 = (bf16[256,256]{1,0:T(8,128)(2,1)S(1)}, bf16[256,256]{1,0:T(8,128)(2,1)S(1)}, u32[]{:S(2)}, u32[]{:S(2)}) collective-permute-start(bf16[256,256]{1,0:T(8,128)(2,1)S(1)} %get-tuple-element.72), channel_id=1, source_target_pairs={{0,2},{1,15},{2,4},{3,1},{4,6},{5,3},{6,8},{7,5},{8,10},{9,7},{10,... | collective-permute-start | bytes 393224 | tf_op jit(solution)/shard_map/ppermute | solution.py:341
  41.5 3.6 %collective-permute-done.10.far.table = bf16[256,512]{1,0:T(8,128)(2,1)S(1)} collective-permute-done((bf16[256,512]{1,0:T(8,128)(2,1)S(1)}, bf16[256,512]{1,0:T(8,128)(2,1)S(1)}, u32[]{:S(2)}, u32[]{:S(2)}) %collective-permute-start.10) | collective-permute-done | bytes 262176 | tf_op jit(solution)/shard_map/ppermute | solution.py:338
  45.2 0.5 collective-permute-start.13
  45.7 0.6 %collective-permute-done.12.refs_1_ = bf16[48,512]{1,0:T(8,128)(2,1)S(1)} collective-permute-done((bf16[48,512]{1,0:T(8,128)(2,1)S(1)}, bf16[48,512]{1,0:T(8,128)(2,1)S(1)}, u32[]{:S(2)}, u32[]{:S(2)}) %collective-permute-start.12) | collective-permute-done | bytes 49184 | tf_op jit(solution)/shard_map/ppermute | solution.py:332
  46.5 0.3 collective-permute-start.15
  46.9 0.7 %shard_map.169.base = f32[2048,512]{1,0:T(8,128)S(1)} custom-call(bf16[2048,1280]{1,0:T(8,128)(2,1)S(1)} %get-tuple-element.42.fetch, f32[2048,512]{1,0:T(8,128)S(1)} %get-tuple-element.65.base, bf16[256,512]{1,0:T(8,128)(2,1)S(1)} %collective-permute-done.10.far.table), custom_call_target="tpu_custom_call" | custom-call | flops 1 | bytes 1 | tf_op jit(solution)/shard_map/pallas_call | solution.py:292
  47.8 0.7 %shard_map.171.base = f32[2048,512]{1,0:T(8,128)S(1)} custom-call(bf16[2048,1280]{1,0:T(8,128)(2,1)S(1)} %get-tuple-element.42.fetch, f32[2048,512]{1,0:T(8,128)S(1)} %shard_map.169.base, bf16[64,512]{1,0:T(8,128)(2,1)S(1)} %collective-permute-done.11.refs_0_, bf16[48,512]{1,0:T(8,128)(2,1)S(1)} %collective-permute-done.12.refs_1_, ...), custom_call_target="tpu_custom_call" | custom-call | flops 1 | bytes 1 | tf_op jit(solution)/shard_map/pallas_call | solution.py:292
  48.7 1.1 %shard_map.172.partial = f32[2048,512]{1,0:T(8,128)S(1)} custom-call(bf16[2048,1280]{1,0:T(8,128)(2,1)S(1)} %get-tuple-element.42.fetch, f32[2048,512]{1,0:T(8,128)S(1)} %shard_map.171.base, bf16[256,256]{1,0:T(8,128)(2,1)S(1)} %collective-permute-done.17.near, bf16[512,512]{1,0:T(8,128)(2,1)S(1)} %copy-done.3), custom_call_target="tpu_custom_call" | custom-call | flops 1 | bytes 1 | tf_op jit(solution)/shard_map/pallas_call | solution.py:292
  49.9 1.9 %shard_map.173 = bf16[2048,512]{1,0:T(8,128)(2,1)} custom-call(bf16[2048,1280]{1,0:T(8,128)(2,1)S(1)} %get-tuple-element.42.fetch, f32[2048,512]{1,0:T(8,128)S(1)} %shard_map.171.base, bf16[256,256]{1,0:T(8,128)(2,1)S(1)} %collective-permute-done.16.near, bf16[512,512]{1,0:T(8,128)(2,1)S(1)} %copy-done.3, f32[2048,512]{1,0:T(8,128)S(1)} %shard_map.172.partial), custom_call_target="tpu_custom_call" | custom-call | flops 1610612736 | bytes 14286848 | tf_op jit(solution)/shard_map/pallas_call | solution.py:292
  (48 shorter events, 1.7 us)
Async XLA Ops:
  0.0 11.1 %copy-start.10 = (s32[64]{0:T(128)S(1)}, s32[64]{0:T(128)}, u32[]{:S(2)}) copy-start(s32[64]{0:T(128)} %param.20) | copy-start | bytes 772
  4.2 6.1 %collective-permute-start = (bf16[256,512]{1,0:T(8,128)(2,1)S(1)}, bf16[256,512]{1,0:T(8,128)(2,1)S(1)}, u32[]{:S(2)}, u32[]{:S(2)}) collective-permute-start(bf16[256,512]{1,0:T(8,128)(2,1)S(1)} %get-tuple-element.41), channel_id=1, source_target_pairs={{0,1},{1,0},{2,3},{3,2},{4,5},{5,4},{6,7},{7,6},{8,9},{9,8},{10,11... | collective-permute-start | bytes 786440 | tf_op jit(solution)/shard_map/ppermute | solution.py:332
  4.7 10.9 %collective-permute-start.1 = (bf16[256,512]{1,0:T(8,128)(2,1)S(1)}, bf16[256,512]{1,0:T(8,128)(2,1)S(1)}, u32[]{:S(2)}, u32[]{:S(2)}) collective-permute-start(bf16[256,512]{1,0:T(8,128)(2,1)S(1)} %get-tuple-element.43), channel_id=1, source_target_pairs={{0,14},{1,3},{2,0},{3,5},{4,2},{5,7},{6,4},{7,9},{8,6},{9,11},{10,... | collective-permute-start | bytes 786440 | tf_op jit(solution)/shard_map/ppermute | solution.py:338
  10.3 5.3 %copy-start.11 = (s32[256,6]{0,1:T(8,128)S(1)}, s32[256,6]{0,1:T(8,128)}, u32[]{:S(2)}) copy-start(s32[256,6]{0,1:T(8,128)} %param.21) | copy-start | bytes 18436
  11.0 9.1 %collective-permute-start.3 = (bf16[256,512]{1,0:T(8,128)(2,1)S(1)}, bf16[256,512]{1,0:T(8,128)(2,1)S(1)}, u32[]{:S(2)}, u32[]{:S(2)}) collective-permute-start(bf16[256,512]{1,0:T(8,128)(2,1)S(1)} %shard_map.155.after), channel_id=1, source_target_pairs={{0,2},{1,15},{2,4},{3,1},{4,6},{5,3},{6,8},{7,5},{8,10},{9,7},{10,... | collective-permute-start | bytes 786440 | tf_op jit(solution)/shard_map/ppermute | solution.py:341
  14.3 5.9 %collective-permute-start.2 = (bf16[256,512]{1,0:T(8,128)(2,1)S(1)}, bf16[256,512]{1,0:T(8,128)(2,1)S(1)}, u32[]{:S(2)}, u32[]{:S(2)}) collective-permute-start(bf16[256,512]{1,0:T(8,128)(2,1)S(1)} %get-tuple-element.47), channel_id=1, source_target_pairs={{0,1},{1,0},{2,3},{3,2},{4,5},{5,4},{6,7},{7,6},{8,9},{9,8},{10,11... | collective-permute-start | bytes 786440 | tf_op jit(solution)/shard_map/ppermute | solution.py:332
  15.6 7.7 %copy-start.4 = (bf16[512,512]{1,0:T(8,128)(2,1)S(1)}, bf16[512,512]{1,0:T(8,128)(2,1)}, u32[]{:S(2)}) copy-start(bf16[512,512]{1,0:T(8,128)(2,1)} %w2.1) | copy-start | bytes 1572868
  15.6 7.7 %copy-start.7 = (bf16[256,512]{1,0:T(8,128)(2,1)S(1)}, bf16[256,512]{1,0:T(8,128)(2,1)}, u32[]{:S(2)}) copy-start(bf16[256,512]{1,0:T(8,128)(2,1)} %mesh.1) | copy-start | bytes 786436
  16.3 7.4 %copy-start = (bf16[2,512,512]{2,1,0:T(8,128)(2,1)S(1)}, bf16[2,512,512]{2,1,0:T(8,128)(2,1)}, u32[]{:S(2)}) copy-start(bf16[2,512,512]{2,1,0:T(8,128)(2,1)} %w_src.3) | copy-start | bytes 3145732
  16.3 7.4 %copy-start.1 = (bf16[2,512,512]{2,1,0:T(8,128)(2,1)S(1)}, bf16[2,512,512]{2,1,0:T(8,128)(2,1)}, u32[]{:S(2)}) copy-start(bf16[2,512,512]{2,1,0:T(8,128)(2,1)} %w_dst.3) | copy-start | bytes 3145732
  16.3 7.4 %copy-start.9 = (f32[2,512]{1,0:T(2,128)S(1)}, f32[2,512]{1,0:T(2,128)}, u32[]{:S(2)}) copy-start(f32[2,512]{1,0:T(2,128)} %bias.3) | copy-start | bytes 12292
  20.6 6.5 %collective-permute-start.4 = (bf16[64,512]{1,0:T(8,128)(2,1)S(1)}, bf16[64,512]{1,0:T(8,128)(2,1)S(1)}, u32[]{:S(2)}, u32[]{:S(2)}) collective-permute-start(bf16[64,512]{1,0:T(8,128)(2,1)S(1)} %get-tuple-element.52.halo), channel_id=1, source_target_pairs={{0,15},{1,2},{2,1},{3,4},{4,3},{5,6},{6,5},{7,8},{8,7},{9,10},{10,... | collective-permute-start | bytes 196616 | tf_op jit(solution)/shard_map/ppermute | solution.py:335
  25.2 5.1 %copy-start.2 = (bf16[2,512,512]{2,1,0:T(8,128)(2,1)S(1)}, bf16[2,512,512]{2,1,0:T(8,128)(2,1)}, u32[]{:S(2)}) copy-start(bf16[2,512,512]{2,1,0:T(8,128)(2,1)} %w_out.3) | copy-start | bytes 3145732
  25.2 1.9 %collective-permute-start.5 = (bf16[64,512]{1,0:T(8,128)(2,1)S(1)}, bf16[64,512]{1,0:T(8,128)(2,1)S(1)}, u32[]{:S(2)}, u32[]{:S(2)}) collective-permute-start(bf16[64,512]{1,0:T(8,128)(2,1)S(1)} %get-tuple-element.55), channel_id=1, source_target_pairs={{0,1},{1,0},{2,3},{3,2},{4,5},{5,4},{6,7},{7,6},{8,9},{9,8},{10,11... | collective-permute-start | bytes 196616 | tf_op jit(solution)/shard_map/ppermute | solution.py:332
  27.1 4.2 %copy-start.5 = (bf16[512,512]{1,0:T(8,128)(2,1)S(1)}, bf16[512,512]{1,0:T(8,128)(2,1)}, u32[]{:S(2)}) copy-start(bf16[512,512]{1,0:T(8,128)(2,1)} %w_next.3) | copy-start | bytes 1572868
  27.5 6.5 %collective-permute-start.6 = (bf16[64,512]{1,0:T(8,128)(2,1)S(1)}, bf16[64,512]{1,0:T(8,128)(2,1)S(1)}, u32[]{:S(2)}, u32[]{:S(2)}) collective-permute-start(bf16[64,512]{1,0:T(8,128)(2,1)S(1)} %shard_map.163.halo), channel_id=1, source_target_pairs={{0,15},{1,2},{2,1},{3,4},{4,3},{5,6},{6,5},{7,8},{8,7},{9,10},{10,... | collective-permute-start | bytes 196616 | tf_op jit(solution)/shard_map/ppermute | solution.py:335
  32.2 1.8 %collective-permute-start.7 = (bf16[64,512]{1,0:T(8,128)(2,1)S(1)}, bf16[64,512]{1,0:T(8,128)(2,1)S(1)}, u32[]{:S(2)}, u32[]{:S(2)}) collective-permute-start(bf16[64,512]{1,0:T(8,128)(2,1)S(1)} %get-tuple-element.60), channel_id=1, source_target_pairs={{0,1},{1,0},{2,3},{3,2},{4,5},{5,4},{6,7},{7,6},{8,9},{9,8},{10,11... | collective-permute-start | bytes 196616 | tf_op jit(solution)/shard_map/ppermute | solution.py:332
  34.0 2.5 %copy-start.6 = (bf16[2048,512]{1,0:T(8,128)(2,1)S(1)}, bf16[2048,512]{1,0:T(8,128)(2,1)}, u32[]{:S(2)}) copy-start(bf16[2048,512]{1,0:T(8,128)(2,1)} %grid.3) | copy-start | bytes 6291460
  34.0 2.5 %copy-start.8 = (bf16[512,512]{1,0:T(8,128)(2,1)S(1)}, bf16[512,512]{1,0:T(8,128)(2,1)}, u32[]{:S(2)}) copy-start(bf16[512,512]{1,0:T(8,128)(2,1)} %w_grid.1) | copy-start | bytes 1572868
  35.0 10.1 %collective-permute-start.10 = (bf16[256,512]{1,0:T(8,128)(2,1)S(1)}, bf16[256,512]{1,0:T(8,128)(2,1)S(1)}, u32[]{:S(2)}, u32[]{:S(2)}) collective-permute-start(bf16[256,512]{1,0:T(8,128)(2,1)S(1)} %shard_map.166.own), channel_id=1, source_target_pairs={{0,14},{1,3},{2,0},{3,5},{4,2},{5,7},{6,4},{7,9},{8,6},{9,11},{10,... | collective-permute-start | bytes 786440 | tf_op jit(solution)/shard_map/ppermute | solution.py:338
  38.3 1.4 %collective-permute-start.8 = (bf16[128,512]{1,0:T(8,128)(2,1)S(1)}, bf16[128,512]{1,0:T(8,128)(2,1)S(1)}, u32[]{:S(2)}, u32[]{:S(2)}) collective-permute-start(bf16[128,512]{1,0:T(8,128)(2,1)S(1)} %get-tuple-element.63), channel_id=1, source_target_pairs={{0,1},{1,0},{2,3},{3,2},{4,5},{5,4},{6,7},{7,6},{8,9},{9,8},{10,11... | collective-permute-start | bytes 393224 | tf_op jit(solution)/shard_map/ppermute | solution.py:332
  38.4 1.5 %collective-permute-start.9 = (bf16[128,512]{1,0:T(8,128)(2,1)S(1)}, bf16[128,512]{1,0:T(8,128)(2,1)S(1)}, u32[]{:S(2)}, u32[]{:S(2)}) collective-permute-start(bf16[128,512]{1,0:T(8,128)(2,1)S(1)} %get-tuple-element.64), channel_id=1, source_target_pairs={{0,1},{1,0},{2,3},{3,2},{4,5},{5,4},{6,7},{7,6},{8,9},{9,8},{10,11... | collective-permute-start | bytes 393224 | tf_op jit(solution)/shard_map/ppermute | solution.py:332
  40.7 7.8 %collective-permute-start.17 = (bf16[256,256]{1,0:T(8,128)(2,1)S(1)}, bf16[256,256]{1,0:T(8,128)(2,1)S(1)}, u32[]{:S(2)}, u32[]{:S(2)}) collective-permute-start(bf16[256,256]{1,0:T(8,128)(2,1)S(1)} %get-tuple-element.72), channel_id=1, source_target_pairs={{0,2},{1,15},{2,4},{3,1},{4,6},{5,3},{6,8},{7,5},{8,10},{9,7},{10,... | collective-permute-start | bytes 393224 | tf_op jit(solution)/shard_map/ppermute | solution.py:341
  41.4 8.5 %collective-permute-start.16 = (bf16[256,256]{1,0:T(8,128)(2,1)S(1)}, bf16[256,256]{1,0:T(8,128)(2,1)S(1)}, u32[]{:S(2)}, u32[]{:S(2)}) collective-permute-start(bf16[256,256]{1,0:T(8,128)(2,1)S(1)} %get-tuple-element.71), channel_id=1, source_target_pairs={{0,2},{1,15},{2,4},{3,1},{4,6},{5,3},{6,8},{7,5},{8,10},{9,7},{10,... | collective-permute-start | bytes 393224 | tf_op jit(solution)/shard_map/ppermute | solution.py:341
  45.1 1.3 %collective-permute-start.12 = (bf16[48,512]{1,0:T(8,128)(2,1)S(1)}, bf16[48,512]{1,0:T(8,128)(2,1)S(1)}, u32[]{:S(2)}, u32[]{:S(2)}) collective-permute-start(bf16[48,512]{1,0:T(8,128)(2,1)S(1)} %get-tuple-element.67), channel_id=1, source_target_pairs={{0,1},{1,0},{2,3},{3,2},{4,5},{5,4},{6,7},{7,6},{8,9},{9,8},{10,11... | collective-permute-start | bytes 147464 | tf_op jit(solution)/shard_map/ppermute | solution.py:332
  45.2 1.4 %collective-permute-start.13 = (bf16[48,512]{1,0:T(8,128)(2,1)S(1)}, bf16[48,512]{1,0:T(8,128)(2,1)S(1)}, u32[]{:S(2)}, u32[]{:S(2)}) collective-permute-start(bf16[48,512]{1,0:T(8,128)(2,1)S(1)} %get-tuple-element.68), channel_id=1, source_target_pairs={{0,1},{1,0},{2,3},{3,2},{4,5},{5,4},{6,7},{7,6},{8,9},{9,8},{10,11... | collective-permute-start | bytes 147464 | tf_op jit(solution)/shard_map/ppermute | solution.py:332
  45.7 2.1 %collective-permute-start.11 = (bf16[64,512]{1,0:T(8,128)(2,1)S(1)}, bf16[64,512]{1,0:T(8,128)(2,1)S(1)}, u32[]{:S(2)}, u32[]{:S(2)}) collective-permute-start(bf16[64,512]{1,0:T(8,128)(2,1)S(1)} %get-tuple-element.66), channel_id=1, source_target_pairs={{0,1},{1,0},{2,3},{3,2},{4,5},{5,4},{6,7},{7,6},{8,9},{9,8},{10,11... | collective-permute-start | bytes 196616 | tf_op jit(solution)/shard_map/ppermute | solution.py:332
  46.4 1.2 %collective-permute-start.14 = (bf16[48,512]{1,0:T(8,128)(2,1)S(1)}, bf16[48,512]{1,0:T(8,128)(2,1)S(1)}, u32[]{:S(2)}, u32[]{:S(2)}) collective-permute-start(bf16[48,512]{1,0:T(8,128)(2,1)S(1)} %get-tuple-element.69), channel_id=1, source_target_pairs={{0,1},{1,0},{2,3},{3,2},{4,5},{5,4},{6,7},{7,6},{8,9},{9,8},{10,11... | collective-permute-start | bytes 147464 | tf_op jit(solution)/shard_map/ppermute | solution.py:332
  46.5 1.2 %collective-permute-start.15 = (bf16[48,512]{1,0:T(8,128)(2,1)S(1)}, bf16[48,512]{1,0:T(8,128)(2,1)S(1)}, u32[]{:S(2)}, u32[]{:S(2)}) collective-permute-start(bf16[48,512]{1,0:T(8,128)(2,1)S(1)} %get-tuple-element.70), channel_id=1, source_target_pairs={{0,1},{1,0},{2,3},{3,2},{4,5},{5,4},{6,7},{7,6},{8,9},{9,8},{10,11... | collective-permute-start | bytes 147464 | tf_op jit(solution)/shard_map/ppermute | solution.py:332
  47.6 1.0 %copy-start.3 = (bf16[512,512]{1,0:T(8,128)(2,1)S(1)}, bf16[512,512]{1,0:T(8,128)(2,1)}, u32[]{:S(2)}) copy-start(bf16[512,512]{1,0:T(8,128)(2,1)} %w_out.5) | copy-start | bytes 1572868

commit v8 on v7

--- a/solution.py
+++ b/solution.py
@@ -192,18 +192,23 @@
 
 def base_kernel(grid, w_grid, fetch, own, base, *pieces):
     rows = own.shape[0]
-    cut_kernel(own, *pieces)
+    cut_kernel(None, own, *pieces)
     for r in range(0, grid.shape[0], BLOCK):
         spot = slice(r, r + BLOCK)
         base[spot] = dot(grid[spot], w_grid[...]) * 0.5 + dot(fetch[spot, 2 * rows : 3 * rows], own[...])
 
 
-def sibling_kernel(fetch, base, own, *refs):
-    *pieces, out, left, right = refs
-    rows, half = left.shape
+def halve_kernel(first_after, after, own, left, right):
+    del first_after, after
+    half = left.shape[1]
     left[...] = own[:, :half]
     right[...] = own[:, half:]
+
+
+def sibling_kernel(fetch, base, *refs):
+    *pieces, out = refs
     table = jnp.concatenate([piece[...] for piece in pieces], axis=0)
+    rows = table.shape[0]
     for r in range(0, base.shape[0], BLOCK):
         spot = slice(r, r + BLOCK)
         out[spot] = base[spot] + dot(fetch[spot, 3 * rows : 4 * rows], table)
@@ -225,7 +230,8 @@
         out[spot] = base[spot] + dot(fetch[spot, rows : 2 * rows], table)
 
 
-def cut_kernel(table, *pieces):
+def cut_kernel(after, table, *pieces):
+    del after
     row = column = 0
     for piece in pieces:
         rows, width = piece.shape
@@ -456,10 +462,12 @@
     )
     sibling = [swap(piece) for piece in passed]
     half = ((mesh_rows, width // 2), BF16)
-    base, left, right = call(sibling_kernel, [fetch, base, projected, *sibling], [f32_rows, half, half], 1)
+    left, right = call(halve_kernel, [*sibling, projected], [half, half], 1, spaces=[pl.ANY, pl.ANY, VM])
+    (base,) = call(sibling_kernel, [fetch, base, *sibling], [f32_rows], 1)
     left = to_far(left)
     right = to_far(right)
-    passed = call(cut_kernel, [far], [((mesh_rows * part_rows // 256, width), BF16) for part_rows in (64, 48, 48, 48, 48)], 1)
+    shares = [((mesh_rows * share // 256, width), BF16) for share in (112, 80, 64)]
+    passed = call(cut_kernel, [base, far], shares, 1, spaces=[pl.ANY, VM])
     cross = [swap(piece) for piece in passed]
     (base,) = call(far_add_kernel, [fetch, base, far], [f32_rows], 1)
     (base,) = call(cross_add_kernel, [fetch, base, *cross], [f32_rows], 1)

time: 52.1 us -> 51.6 us (level)
    ppermute x2, waiting for transfers between devices: 3.56 us -> 4.12 us  [to_near(): return lax.ppermute(value, AXES, sided(-2))]
    ppermute x11 -> x9, starting transfers between devices: 3.75 us -> 3.24 us  [swap(): return lax.ppermute(value, AXES, sided(1))]
    ppermute x11 -> x9, waiting for transfers between devices: 1.83 us -> 1.49 us  [swap(): return lax.ppermute(value, AXES, sided(1))]
    pallas_call x20 -> x21, Pallas kernels: 21.1 us -> 21.1 us  [call(): pl.pallas_call(kernel, in_specs=[pl.BlockSpec(memory_space=space) for spa...]
  transfers between devices with their start and end apart: 18 -> 16, of which waited for: 9 -> 7; matrix products, arithmetic and copies ran while one was open for 0% -> 0% of each run, Pallas kernels for 25% -> 26%
where the time goes in v8:
time: 51.6 us; the launch traced here: 51.3 us
  Pallas kernels  21.1 us (41%)
  starting transfers between devices  16.8 us (33%)
  waiting for transfers between devices  12.9 us (25%)
    pallas_call x21, Pallas kernels, call(): pl.pallas_call(kernel, in_specs=[pl.BlockSpec(memory_space=space) for spa...  21.1 us
    ppermute x2, starting transfers between devices, to_near(): return lax.ppermute(value, AXES, sided(-2))  7.15 us
    ppermute x2, starting transfers between devices, to_across(): return lax.ppermute(value, AXES, sided(-1))  5.54 us
    ppermute x2, waiting for transfers between devices, to_near(): return lax.ppermute(value, AXES, sided(-2))  4.12 us
    ppermute x3, waiting for transfers between devices, to_far(): return lax.ppermute(value, AXES, sided(2))  3.85 us
    ppermute x2, waiting for transfers between devices, to_across(): return lax.ppermute(value, AXES, sided(-1))  3.45 us
    ppermute x9, starting transfers between devices, swap(): return lax.ppermute(value, AXES, sided(1))  3.24 us
    ppermute x9, waiting for transfers between devices, swap(): return lax.ppermute(value, AXES, sided(1))  1.49 us
  transfers between devices with their start and end apart: 16, of which 7 were waited for; matrix products, arithmetic and copies ran while one was open for 0% of the time, Pallas kernels for 26%

profile of v8, /device:TPU:0, one launch (start us, length us, event | category | flops | bytes accessed | tf_op | source)
XLA Modules:
  0.0 51.3 jit_solution(4275567462554989314)
XLA Ops:
  0.0 4.2 %shard_map.154 = (bf16[2048,512]{1,0:T(8,128)(2,1)S(1)}, bf16[256,512]{1,0:T(8,128)(2,1)S(1)}, bf16[256,512]{1,0:T(8,128)(2,1)S(1)}, s32[1,2048]{1,0:T(1,128)S(1)}) custom-call(s32[1,2048]{1,0:T(1,128)} %bitcast.7, s32[1,2048]{1,0:T(1,128)} %bitcast.8, bf16[2048,512]{1,0:T(8,128)(2,1)} %grid.3, bf16[512,512]{1,0:T(8,128)(2,1)} %w1.1, f32[1,512]{1,0:T(1,128)} %bitcast.9), custom_call_target="tpu_custom_call" | custom-call | flops 2147483648 | bytes 2639872 | tf_op jit(solution)/shard_map/pallas_call | solution.py:298
  4.2 0.5 %collective-permute-start = (bf16[256,512]{1,0:T(8,128)(2,1)S(1)}, bf16[256,512]{1,0:T(8,128)(2,1)S(1)}, u32[]{:S(2)}, u32[]{:S(2)}) collective-permute-start(bf16[256,512]{1,0:T(8,128)(2,1)S(1)} %get-tuple-element.38), channel_id=1, source_target_pairs={{0,1},{1,0},{2,3},{3,2},{4,5},{5,4},{6,7},{7,6},{8,9},{9,8},{10,11... | collective-permute-start | bytes 786440 | tf_op jit(solution)/shard_map/ppermute | solution.py:338
  4.7 5.6 %collective-permute-start.1 = (bf16[256,512]{1,0:T(8,128)(2,1)S(1)}, bf16[256,512]{1,0:T(8,128)(2,1)S(1)}, u32[]{:S(2)}, u32[]{:S(2)}) collective-permute-start(bf16[256,512]{1,0:T(8,128)(2,1)S(1)} %get-tuple-element.40), channel_id=1, source_target_pairs={{0,14},{1,3},{2,0},{3,5},{4,2},{5,7},{6,4},{7,9},{8,6},{9,11},{10,... | collective-permute-start | bytes 786440 | tf_op jit(solution)/shard_map/ppermute | solution.py:344
  10.3 0.7 %shard_map.155.after = bf16[256,512]{1,0:T(8,128)(2,1)S(1)} custom-call(s32[1,2048]{1,0:T(1,128)S(1)} %get-tuple-element.36.code, bf16[2048,512]{1,0:T(8,128)(2,1)S(1)} %get-tuple-element.37.hidden, bf16[256,512]{1,0:T(8,128)(2,1)S(1)} %collective-permute-done.crossed), custom_call_target="tpu_custom_call" | custom-call | flops 1 | bytes 1 | tf_op jit(solution)/shard_map/pallas_call | solution.py:298
  11.1 3.1 %shard_map.156 = (f32[256,512]{1,0:T(8,128)S(1)}, bf16[256,512]{1,0:T(8,128)(2,1)S(1)}, bf16[256,64]{1,0:T(8,128)(2,1)S(1)}, bf16[3,512,512]{2,1,0:T(8,128)(2,1)...) custom-call(bf16[256,512]{1,0:T(8,128)(2,1)S(1)} %shard_map.155.after, ...), custom_call_target="tpu_custom_call" | custom-call | flops 1073741824 | bytes 5775616 | tf_op jit(solution)/shard_map/pallas_call | solution.py:298
  14.3 1.4 %collective-permute-start.2 = (bf16[256,512]{1,0:T(8,128)(2,1)S(1)}, bf16[256,512]{1,0:T(8,128)(2,1)S(1)}, u32[]{:S(2)}, u32[]{:S(2)}) collective-permute-start(bf16[256,512]{1,0:T(8,128)(2,1)S(1)} %get-tuple-element.44), channel_id=1, source_target_pairs={{0,1},{1,0},{2,3},{3,2},{4,5},{5,4},{6,7},{7,6},{8,9},{9,8},{10,11... | collective-permute-start | bytes 786440 | tf_op jit(solution)/shard_map/ppermute | solution.py:338
  15.7 0.6 %shard_map.157 = (bf16[1536,256]{1,0:T(8,128)(2,1)S(1)}, bf16[1536,128]{1,0:T(8,128)(2,1)S(1)}, bf16[384,256]{1,0:T(8,128)(2,1)S(1)}, bf16[384,128]{1,0:T(8,128)(2,1)S(1)}) custom-call(bf16[256,512]{1,0:T(8,128)(2,1)S(1)} %collective-permute-done.1.after.near, s32[6,256]{1,0:T(8,128)S(1)} %bitcast.6, bf16[256,64]{1,0:T(8,128)(2,1)S(1)} %get-tuple-element.41.pick.refs_0_), custom_call_target="tpu_custom_call" | custom-call | flops 40000000000 | bytes 301056 | tf_op jit(solution)/shard_map/pallas_call | solution.py:298
  16.3 3.8 %collective-permute-done.3.far = bf16[256,512]{1,0:T(8,128)(2,1)S(1)} collective-permute-done((bf16[256,512]{1,0:T(8,128)(2,1)S(1)}, bf16[256,512]{1,0:T(8,128)(2,1)S(1)}, u32[]{:S(2)}, u32[]{:S(2)}) %collective-permute-start.3) | collective-permute-done | bytes 262176 | tf_op jit(solution)/shard_map/ppermute | solution.py:347
  20.2 0.4 shard_map.158
  20.6 2.8 %collective-permute-start.4 = (bf16[64,512]{1,0:T(8,128)(2,1)S(1)}, bf16[64,512]{1,0:T(8,128)(2,1)S(1)}, u32[]{:S(2)}, u32[]{:S(2)}) collective-permute-start(bf16[64,512]{1,0:T(8,128)(2,1)S(1)} %get-tuple-element.49.halo), channel_id=1, source_target_pairs={{0,15},{1,2},{2,1},{3,4},{4,3},{5,6},{6,5},{7,8},{8,7},{9,10},{10,... | collective-permute-start | bytes 196616 | tf_op jit(solution)/shard_map/ppermute | solution.py:341
  23.4 0.3 shard_map.159.latent
  23.7 1.5 %shard_map.160 = (f32[1536,512]{1,0:T(8,128)S(1)}, bf16[64,512]{1,0:T(8,128)(2,1)S(1)}, f32[64,512]{1,0:T(8,128)S(1)}, f32[384,512]{1,0:T(8,128)S(1)}) custom-call(bf16[256,512]{1,0:T(8,128)(2,1)S(1)} %shard_map.159.latent, bf16[2,512,512]{2,1,0:T(8,128)(2,1)S(1)} %copy-done, bf16[2,512,512]{2,1,0:T(8,128)(2,1)S(1)} %copy-done.1, f32[2,512]{1,0:T(2,128)S(1)} %copy-done.9, ...), custom_call_target="tpu_custom_call" | custom-call | flops 1 | bytes 1 | tf_op jit(solution)/shard_map/pallas_call | solution.py:298
  25.3 1.8 %collective-permute-done.4.table = bf16[64,512]{1,0:T(8,128)(2,1)S(1)} collective-permute-done((bf16[64,512]{1,0:T(8,128)(2,1)S(1)}, bf16[64,512]{1,0:T(8,128)(2,1)S(1)}, u32[]{:S(2)}, u32[]{:S(2)}) %collective-permute-start.4) | collective-permute-done | bytes 65568 | tf_op jit(solution)/shard_map/ppermute | solution.py:341
  27.1 0.5 shard_map.163.halo
  27.5 2.8 %collective-permute-start.6 = (bf16[64,512]{1,0:T(8,128)(2,1)S(1)}, bf16[64,512]{1,0:T(8,128)(2,1)S(1)}, u32[]{:S(2)}, u32[]{:S(2)}) collective-permute-start(bf16[64,512]{1,0:T(8,128)(2,1)S(1)} %shard_map.163.halo), channel_id=1, source_target_pairs={{0,15},{1,2},{2,1},{3,4},{4,3},{5,6},{6,5},{7,8},{8,7},{9,10},{10,... | collective-permute-start | bytes 196616 | tf_op jit(solution)/shard_map/ppermute | solution.py:341
  30.3 0.9 %shard_map.162.latent = bf16[256,512]{1,0:T(8,128)(2,1)S(1)} custom-call(bf16[256,512]{1,0:T(8,128)(2,1)S(1)} %shard_map.159.latent, f32[1536,512]{1,0:T(8,128)S(1)} %get-tuple-element.51.before, bf16[64,512]{1,0:T(8,128)(2,1)S(1)} %shard_map.161.across, bf16[64,512]{1,0:T(8,128)(2,1)S(1)} %collective-permute-done.5.beside, ...), custom_call_target="tpu_custom_call" | custom-call | flops 1 | bytes 1 | tf_op jit(solution)/shard_map/pallas_call | solution.py:298
  31.2 1.0 %shard_map.164 = (f32[1536,512]{1,0:T(8,128)S(1)}, bf16[64,512]{1,0:T(8,128)(2,1)S(1)}, f32[256,512]{1,0:T(8,128)S(1)}) custom-call(bf16[256,512]{1,0:T(8,128)(2,1)S(1)} %shard_map.162.latent, bf16[2,512,512]{2,1,0:T(8,128)(2,1)S(1)} %copy-done, bf16[2,512,512]{2,1,0:T(8,128)(2,1)S(1)} %copy-done.1, f32[2,512]{1,0:T(2,128)S(1)} %copy-done.9, ...), custom_call_target="tpu_custom_call" | custom-call | flops 1 | bytes 1 | tf_op jit(solution)/shard_map/pallas_call | solution.py:298
  32.3 1.7 %collective-permute-done.6.table = bf16[64,512]{1,0:T(8,128)(2,1)S(1)} collective-permute-done((bf16[64,512]{1,0:T(8,128)(2,1)S(1)}, bf16[64,512]{1,0:T(8,128)(2,1)S(1)}, u32[]{:S(2)}, u32[]{:S(2)}) %collective-permute-start.6) | collective-permute-done | bytes 65568 | tf_op jit(solution)/shard_map/ppermute | solution.py:341
  34.0 0.9 %shard_map.166.own = bf16[256,512]{1,0:T(8,128)(2,1)S(1)} custom-call(f32[1536,512]{1,0:T(8,128)S(1)} %get-tuple-element.56.before, bf16[64,512]{1,0:T(8,128)(2,1)S(1)} %shard_map.165.across, bf16[64,512]{1,0:T(8,128)(2,1)S(1)} %collective-permute-done.7.beside, bf16[1536,128]{1,0:T(8,128)(2,1)S(1)} %get-tuple-element.53.gather_halo, ...), custom_call_target="tpu_custom_call" | custom-call | flops 469762048 | bytes 5767168 | tf_op jit(solution)/shard_map/pallas_call | solution.py:298
  35.0 1.5 %collective-permute-start.10 = (bf16[256,512]{1,0:T(8,128)(2,1)S(1)}, bf16[256,512]{1,0:T(8,128)(2,1)S(1)}, u32[]{:S(2)}, u32[]{:S(2)}) collective-permute-start(bf16[256,512]{1,0:T(8,128)(2,1)S(1)} %shard_map.166.own), channel_id=1, source_target_pairs={{0,14},{1,3},{2,0},{3,5},{4,2},{5,7},{6,4},{7,9},{8,6},{9,11},{10,... | collective-permute-start | bytes 786440 | tf_op jit(solution)/shard_map/ppermute | solution.py:344
  36.5 1.8 %shard_map.167 = (f32[2048,512]{1,0:T(8,128)S(1)}, bf16[128,512]{1,0:T(8,128)(2,1)S(1)}, bf16[128,512]{1,0:T(8,128)(2,1)S(1)}) custom-call(bf16[2048,512]{1,0:T(8,128)(2,1)S(1)} %copy-done.6, bf16[512,512]{1,0:T(8,128)(2,1)S(1)} %copy-done.8, bf16[2048,1280]{1,0:T(8,128)(2,1)S(1)} %get-tuple-element.39.fetch, bf16[256,512]{1,0:T(8,128)(2,1)S(1)} %shard_map.166.own), custom_call_target="tpu_custom_call" | custom-call | flops 1 | bytes 1 | tf_op jit(solution)/shard_map/pallas_call | solution.py:298
  38.4 0.5 collective-permute-start.9
  38.9 0.8 %collective-permute-done.8.refs_0_.first_after = bf16[128,512]{1,0:T(8,128)(2,1)S(1)} collective-permute-done((bf16[128,512]{1,0:T(8,128)(2,1)S(1)}, bf16[128,512]{1,0:T(8,128)(2,1)S(1)}, u32[]{:S(2)}, u32[]{:S(2)}) %collective-permute-start.8) | collective-permute-done | bytes 131104 | tf_op jit(solution)/shard_map/ppermute | solution.py:338
  39.9 0.8 %collective-permute-start.15 = (bf16[256,256]{1,0:T(8,128)(2,1)S(1)}, bf16[256,256]{1,0:T(8,128)(2,1)S(1)}, u32[]{:S(2)}, u32[]{:S(2)}) collective-permute-start(bf16[256,256]{1,0:T(8,128)(2,1)S(1)} %get-tuple-element.66), channel_id=1, source_target_pairs={{0,2},{1,15},{2,4},{3,1},{4,6},{5,3},{6,8},{7,5},{8,10},{9,7},{10,... | collective-permute-start | bytes 393224 | tf_op jit(solution)/shard_map/ppermute | solution.py:347
  40.8 0.7 %shard_map.168.base.after = f32[2048,512]{1,0:T(8,128)S(1)} custom-call(bf16[2048,1280]{1,0:T(8,128)(2,1)S(1)} %get-tuple-element.39.fetch, f32[2048,512]{1,0:T(8,128)S(1)} %get-tuple-element.59.base, bf16[128,512]{1,0:T(8,128)(2,1)S(1)} %collective-permute-done.8.refs_0_.first_after, bf16[128,512]{1,0:T(8,128)(2,1)S(1)} %collective-permute-done.9.refs_1_.after), custom_call_target="tpu_custom_call" | custom-call | flops 1 | bytes 1 | tf_op jit(solution)/shard_map/pallas_call | solution.py:298
  41.5 4.1 %collective-permute-done.10.far.table = bf16[256,512]{1,0:T(8,128)(2,1)S(1)} collective-permute-done((bf16[256,512]{1,0:T(8,128)(2,1)S(1)}, bf16[256,512]{1,0:T(8,128)(2,1)S(1)}, u32[]{:S(2)}, u32[]{:S(2)}) %collective-permute-start.10) | collective-permute-done | bytes 262176 | tf_op jit(solution)/shard_map/ppermute | solution.py:344
  45.7 0.5 collective-permute-start.12
  46.3 0.7 %shard_map.169.base = f32[2048,512]{1,0:T(8,128)S(1)} custom-call(bf16[2048,1280]{1,0:T(8,128)(2,1)S(1)} %get-tuple-element.39.fetch, f32[2048,512]{1,0:T(8,128)S(1)} %shard_map.168.base.after, bf16[256,512]{1,0:T(8,128)(2,1)S(1)} %collective-permute-done.10.far.table), custom_call_target="tpu_custom_call" | custom-call | flops 1 | bytes 1 | tf_op jit(solution)/shard_map/pallas_call | solution.py:298
  47.0 0.4 collective-permute-done.13.refs_2_
  47.5 0.7 %shard_map.171.base = f32[2048,512]{1,0:T(8,128)S(1)} custom-call(bf16[2048,1280]{1,0:T(8,128)(2,1)S(1)} %get-tuple-element.39.fetch, f32[2048,512]{1,0:T(8,128)S(1)} %shard_map.169.base, bf16[112,512]{1,0:T(8,128)(2,1)S(1)} %collective-permute-done.11.refs_0_, bf16[80,512]{1,0:T(8,128)(2,1)S(1)} %collective-permute-done.12.refs_1_, ...), custom_call_target="tpu_custom_call" | custom-call | flops 1 | bytes 1 | tf_op jit(solution)/shard_map/pallas_call | solution.py:298
  48.2 1.1 %shard_map.173.partial = f32[2048,512]{1,0:T(8,128)S(1)} custom-call(bf16[2048,1280]{1,0:T(8,128)(2,1)S(1)} %get-tuple-element.39.fetch, f32[2048,512]{1,0:T(8,128)S(1)} %shard_map.171.base, bf16[256,256]{1,0:T(8,128)(2,1)S(1)} %collective-permute-done.15.near, bf16[512,512]{1,0:T(8,128)(2,1)S(1)} %copy-done.3), custom_call_target="tpu_custom_call" | custom-call | flops 1 | bytes 1 | tf_op jit(solution)/shard_map/pallas_call | solution.py:298
  49.3 1.9 %shard_map.174 = bf16[2048,512]{1,0:T(8,128)(2,1)} custom-call(bf16[2048,1280]{1,0:T(8,128)(2,1)S(1)} %get-tuple-element.39.fetch, f32[2048,512]{1,0:T(8,128)S(1)} %shard_map.171.base, bf16[256,256]{1,0:T(8,128)(2,1)S(1)} %collective-permute-done.14.near, bf16[512,512]{1,0:T(8,128)(2,1)S(1)} %copy-done.3, f32[2048,512]{1,0:T(8,128)S(1)} %shard_map.173.partial), custom_call_target="tpu_custom_call" | custom-call | flops 1610612736 | bytes 14286848 | tf_op jit(solution)/shard_map/pallas_call | solution.py:298
  (45 shorter events, 0.8 us)
Async XLA Ops:
  0.0 11.1 %copy-start.10 = (s32[64]{0:T(128)S(1)}, s32[64]{0:T(128)}, u32[]{:S(2)}) copy-start(s32[64]{0:T(128)} %param.20) | copy-start | bytes 772
  4.2 6.1 %collective-permute-start = (bf16[256,512]{1,0:T(8,128)(2,1)S(1)}, bf16[256,512]{1,0:T(8,128)(2,1)S(1)}, u32[]{:S(2)}, u32[]{:S(2)}) collective-permute-start(bf16[256,512]{1,0:T(8,128)(2,1)S(1)} %get-tuple-element.38), channel_id=1, source_target_pairs={{0,1},{1,0},{2,3},{3,2},{4,5},{5,4},{6,7},{7,6},{8,9},{9,8},{10,11... | collective-permute-start | bytes 786440 | tf_op jit(solution)/shard_map/ppermute | solution.py:338
  4.7 10.9 %collective-permute-start.1 = (bf16[256,512]{1,0:T(8,128)(2,1)S(1)}, bf16[256,512]{1,0:T(8,128)(2,1)S(1)}, u32[]{:S(2)}, u32[]{:S(2)}) collective-permute-start(bf16[256,512]{1,0:T(8,128)(2,1)S(1)} %get-tuple-element.40), channel_id=1, source_target_pairs={{0,14},{1,3},{2,0},{3,5},{4,2},{5,7},{6,4},{7,9},{8,6},{9,11},{10,... | collective-permute-start | bytes 786440 | tf_op jit(solution)/shard_map/ppermute | solution.py:344
  10.3 5.3 %copy-start.11 = (s32[256,6]{0,1:T(8,128)S(1)}, s32[256,6]{0,1:T(8,128)}, u32[]{:S(2)}) copy-start(s32[256,6]{0,1:T(8,128)} %param.21) | copy-start | bytes 18436
  11.0 9.1 %collective-permute-start.3 = (bf16[256,512]{1,0:T(8,128)(2,1)S(1)}, bf16[256,512]{1,0:T(8,128)(2,1)S(1)}, u32[]{:S(2)}, u32[]{:S(2)}) collective-permute-start(bf16[256,512]{1,0:T(8,128)(2,1)S(1)} %shard_map.155.after), channel_id=1, source_target_pairs={{0,2},{1,15},{2,4},{3,1},{4,6},{5,3},{6,8},{7,5},{8,10},{9,7},{10,... | collective-permute-start | bytes 786440 | tf_op jit(solution)/shard_map/ppermute | solution.py:347
  14.3 5.9 %collective-permute-start.2 = (bf16[256,512]{1,0:T(8,128)(2,1)S(1)}, bf16[256,512]{1,0:T(8,128)(2,1)S(1)}, u32[]{:S(2)}, u32[]{:S(2)}) collective-permute-start(bf16[256,512]{1,0:T(8,128)(2,1)S(1)} %get-tuple-element.44), channel_id=1, source_target_pairs={{0,1},{1,0},{2,3},{3,2},{4,5},{5,4},{6,7},{7,6},{8,9},{9,8},{10,11... | collective-permute-start | bytes 786440 | tf_op jit(solution)/shard_map/ppermute | solution.py:338
  15.6 7.7 %copy-start.4 = (bf16[512,512]{1,0:T(8,128)(2,1)S(1)}, bf16[512,512]{1,0:T(8,128)(2,1)}, u32[]{:S(2)}) copy-start(bf16[512,512]{1,0:T(8,128)(2,1)} %w2.1) | copy-start | bytes 1572868
  15.6 7.7 %copy-start.7 = (bf16[256,512]{1,0:T(8,128)(2,1)S(1)}, bf16[256,512]{1,0:T(8,128)(2,1)}, u32[]{:S(2)}) copy-start(bf16[256,512]{1,0:T(8,128)(2,1)} %mesh.1) | copy-start | bytes 786436
  16.3 7.4 %copy-start = (bf16[2,512,512]{2,1,0:T(8,128)(2,1)S(1)}, bf16[2,512,512]{2,1,0:T(8,128)(2,1)}, u32[]{:S(2)}) copy-start(bf16[2,512,512]{2,1,0:T(8,128)(2,1)} %w_src.3) | copy-start | bytes 3145732
  16.3 7.4 %copy-start.1 = (bf16[2,512,512]{2,1,0:T(8,128)(2,1)S(1)}, bf16[2,512,512]{2,1,0:T(8,128)(2,1)}, u32[]{:S(2)}) copy-start(bf16[2,512,512]{2,1,0:T(8,128)(2,1)} %w_dst.3) | copy-start | bytes 3145732
  16.3 7.4 %copy-start.9 = (f32[2,512]{1,0:T(2,128)S(1)}, f32[2,512]{1,0:T(2,128)}, u32[]{:S(2)}) copy-start(f32[2,512]{1,0:T(2,128)} %bias.3) | copy-start | bytes 12292
  20.6 6.5 %collective-permute-start.4 = (bf16[64,512]{1,0:T(8,128)(2,1)S(1)}, bf16[64,512]{1,0:T(8,128)(2,1)S(1)}, u32[]{:S(2)}, u32[]{:S(2)}) collective-permute-start(bf16[64,512]{1,0:T(8,128)(2,1)S(1)} %get-tuple-element.49.halo), channel_id=1, source_target_pairs={{0,15},{1,2},{2,1},{3,4},{4,3},{5,6},{6,5},{7,8},{8,7},{9,10},{10,... | collective-permute-start | bytes 196616 | tf_op jit(solution)/shard_map/ppermute | solution.py:341
  25.2 5.1 %copy-start.2 = (bf16[2,512,512]{2,1,0:T(8,128)(2,1)S(1)}, bf16[2,512,512]{2,1,0:T(8,128)(2,1)}, u32[]{:S(2)}) copy-start(bf16[2,512,512]{2,1,0:T(8,128)(2,1)} %w_out.3) | copy-start | bytes 3145732
  25.2 1.9 %collective-permute-start.5 = (bf16[64,512]{1,0:T(8,128)(2,1)S(1)}, bf16[64,512]{1,0:T(8,128)(2,1)S(1)}, u32[]{:S(2)}, u32[]{:S(2)}) collective-permute-start(bf16[64,512]{1,0:T(8,128)(2,1)S(1)} %get-tuple-element.52), channel_id=1, source_target_pairs={{0,1},{1,0},{2,3},{3,2},{4,5},{5,4},{6,7},{7,6},{8,9},{9,8},{10,11... | collective-permute-start | bytes 196616 | tf_op jit(solution)/shard_map/ppermute | solution.py:338
  27.1 4.2 %copy-start.5 = (bf16[512,512]{1,0:T(8,128)(2,1)S(1)}, bf16[512,512]{1,0:T(8,128)(2,1)}, u32[]{:S(2)}) copy-start(bf16[512,512]{1,0:T(8,128)(2,1)} %w_next.3) | copy-start | bytes 1572868
  27.5 6.5 %collective-permute-start.6 = (bf16[64,512]{1,0:T(8,128)(2,1)S(1)}, bf16[64,512]{1,0:T(8,128)(2,1)S(1)}, u32[]{:S(2)}, u32[]{:S(2)}) collective-permute-start(bf16[64,512]{1,0:T(8,128)(2,1)S(1)} %shard_map.163.halo), channel_id=1, source_target_pairs={{0,15},{1,2},{2,1},{3,4},{4,3},{5,6},{6,5},{7,8},{8,7},{9,10},{10,... | collective-permute-start | bytes 196616 | tf_op jit(solution)/shard_map/ppermute | solution.py:341
  32.2 1.8 %collective-permute-start.7 = (bf16[64,512]{1,0:T(8,128)(2,1)S(1)}, bf16[64,512]{1,0:T(8,128)(2,1)S(1)}, u32[]{:S(2)}, u32[]{:S(2)}) collective-permute-start(bf16[64,512]{1,0:T(8,128)(2,1)S(1)} %get-tuple-element.57), channel_id=1, source_target_pairs={{0,1},{1,0},{2,3},{3,2},{4,5},{5,4},{6,7},{7,6},{8,9},{9,8},{10,11... | collective-permute-start | bytes 196616 | tf_op jit(solution)/shard_map/ppermute | solution.py:338
  34.0 2.5 %copy-start.6 = (bf16[2048,512]{1,0:T(8,128)(2,1)S(1)}, bf16[2048,512]{1,0:T(8,128)(2,1)}, u32[]{:S(2)}) copy-start(bf16[2048,512]{1,0:T(8,128)(2,1)} %grid.3) | copy-start | bytes 6291460
  34.0 2.5 %copy-start.8 = (bf16[512,512]{1,0:T(8,128)(2,1)S(1)}, bf16[512,512]{1,0:T(8,128)(2,1)}, u32[]{:S(2)}) copy-start(bf16[512,512]{1,0:T(8,128)(2,1)} %w_grid.1) | copy-start | bytes 1572868
  35.0 10.6 %collective-permute-start.10 = (bf16[256,512]{1,0:T(8,128)(2,1)S(1)}, bf16[256,512]{1,0:T(8,128)(2,1)S(1)}, u32[]{:S(2)}, u32[]{:S(2)}) collective-permute-start(bf16[256,512]{1,0:T(8,128)(2,1)S(1)} %shard_map.166.own), channel_id=1, source_target_pairs={{0,14},{1,3},{2,0},{3,5},{4,2},{5,7},{6,4},{7,9},{8,6},{9,11},{10,... | collective-permute-start | bytes 786440 | tf_op jit(solution)/shard_map/ppermute | solution.py:344
  38.3 1.4 %collective-permute-start.8 = (bf16[128,512]{1,0:T(8,128)(2,1)S(1)}, bf16[128,512]{1,0:T(8,128)(2,1)S(1)}, u32[]{:S(2)}, u32[]{:S(2)}) collective-permute-start(bf16[128,512]{1,0:T(8,128)(2,1)S(1)} %get-tuple-element.60), channel_id=1, source_target_pairs={{0,1},{1,0},{2,3},{3,2},{4,5},{5,4},{6,7},{7,6},{8,9},{9,8},{10,11... | collective-permute-start | bytes 393224 | tf_op jit(solution)/shard_map/ppermute | solution.py:338
  38.4 1.5 %collective-permute-start.9 = (bf16[128,512]{1,0:T(8,128)(2,1)S(1)}, bf16[128,512]{1,0:T(8,128)(2,1)S(1)}, u32[]{:S(2)}, u32[]{:S(2)}) collective-permute-start(bf16[128,512]{1,0:T(8,128)(2,1)S(1)} %get-tuple-element.61), channel_id=1, source_target_pairs={{0,1},{1,0},{2,3},{3,2},{4,5},{5,4},{6,7},{7,6},{8,9},{9,8},{10,11... | collective-permute-start | bytes 393224 | tf_op jit(solution)/shard_map/ppermute | solution.py:338
  39.9 8.2 %collective-permute-start.15 = (bf16[256,256]{1,0:T(8,128)(2,1)S(1)}, bf16[256,256]{1,0:T(8,128)(2,1)S(1)}, u32[]{:S(2)}, u32[]{:S(2)}) collective-permute-start(bf16[256,256]{1,0:T(8,128)(2,1)S(1)} %get-tuple-element.66), channel_id=1, source_target_pairs={{0,2},{1,15},{2,4},{3,1},{4,6},{5,3},{6,8},{7,5},{8,10},{9,7},{10,... | collective-permute-start | bytes 393224 | tf_op jit(solution)/shard_map/ppermute | solution.py:347
  40.7 8.6 %collective-permute-start.14 = (bf16[256,256]{1,0:T(8,128)(2,1)S(1)}, bf16[256,256]{1,0:T(8,128)(2,1)S(1)}, u32[]{:S(2)}, u32[]{:S(2)}) collective-permute-start(bf16[256,256]{1,0:T(8,128)(2,1)S(1)} %get-tuple-element.65), channel_id=1, source_target_pairs={{0,2},{1,15},{2,4},{3,1},{4,6},{5,3},{6,8},{7,5},{8,10},{9,7},{10,... | collective-permute-start | bytes 393224 | tf_op jit(solution)/shard_map/ppermute | solution.py:347
  45.6 1.8 %collective-permute-start.11 = (bf16[112,512]{1,0:T(8,128)(2,1)S(1)}, bf16[112,512]{1,0:T(8,128)(2,1)S(1)}, u32[]{:S(2)}, u32[]{:S(2)}) collective-permute-start(bf16[112,512]{1,0:T(8,128)(2,1)S(1)} %get-tuple-element.62), channel_id=1, source_target_pairs={{0,1},{1,0},{2,3},{3,2},{4,5},{5,4},{6,7},{7,6},{8,9},{9,8},{10,11... | collective-permute-start | bytes 344072 | tf_op jit(solution)/shard_map/ppermute | solution.py:338
  45.7 1.8 %collective-permute-start.12 = (bf16[80,512]{1,0:T(8,128)(2,1)S(1)}, bf16[80,512]{1,0:T(8,128)(2,1)S(1)}, u32[]{:S(2)}, u32[]{:S(2)}) collective-permute-start(bf16[80,512]{1,0:T(8,128)(2,1)S(1)} %get-tuple-element.63), channel_id=1, source_target_pairs={{0,1},{1,0},{2,3},{3,2},{4,5},{5,4},{6,7},{7,6},{8,9},{9,8},{10,11... | collective-permute-start | bytes 245768 | tf_op jit(solution)/shard_map/ppermute | solution.py:338
  46.2 1.3 %collective-permute-start.13 = (bf16[64,512]{1,0:T(8,128)(2,1)S(1)}, bf16[64,512]{1,0:T(8,128)(2,1)S(1)}, u32[]{:S(2)}, u32[]{:S(2)}) collective-permute-start(bf16[64,512]{1,0:T(8,128)(2,1)S(1)} %get-tuple-element.64), channel_id=1, source_target_pairs={{0,1},{1,0},{2,3},{3,2},{4,5},{5,4},{6,7},{7,6},{8,9},{9,8},{10,11... | collective-permute-start | bytes 196616 | tf_op jit(solution)/shard_map/ppermute | solution.py:338
  47.0 1.2 %copy-start.3 = (bf16[512,512]{1,0:T(8,128)(2,1)S(1)}, bf16[512,512]{1,0:T(8,128)(2,1)}, u32[]{:S(2)}) copy-start(bf16[512,512]{1,0:T(8,128)(2,1)} %w_out.5) | copy-start | bytes 1572868

commit v9 on v8

--- a/solution.py
+++ b/solution.py
@@ -255,16 +255,16 @@
 
 def decode_left_kernel(fetch, base, near, w_out, partial):
     rows, width = near.shape
-    starts = range(0, base.shape[0], DECODE_BLOCK)
+    starts = range(0, base.shape[0], BLOCK)
 
     def halved(r):
-        spot = slice(r, r + DECODE_BLOCK)
+        spot = slice(r, r + BLOCK)
         return base[spot, :width] + dot(fetch[spot, :rows], near[...])
 
     def finish(r, hidden):
-        partial[r : r + DECODE_BLOCK] = dot(hidden, w_out[:width])
-
-    ahead_of(DECODE_BLOCK, starts, halved, finish)
+        partial[r : r + BLOCK] = dot(hidden, w_out[:width])
+
+    ahead_of(BLOCK, starts, halved, finish)
 
 
 def decode_kernel(fetch, base, near, w_out, partial, out, out_v, sems):

time: 51.6 us -> 51.6 us (level)
  no operation moved by 1% of the time
where the time goes in v9:
time: 51.6 us; the launch traced here: 51.3 us
  Pallas kernels  21 us (41%)
  starting transfers between devices  16.8 us (33%)
  waiting for transfers between devices  12.9 us (25%)
    pallas_call x21, Pallas kernels, call(): pl.pallas_call(kernel, in_specs=[pl.BlockSpec(memory_space=space) for spa...  21 us
    ppermute x2, starting transfers between devices, to_near(): return lax.ppermute(value, AXES, sided(-2))  7.15 us
    ppermute x2, starting transfers between devices, to_across(): return lax.ppermute(value, AXES, sided(-1))  5.54 us
    ppermute x2, waiting for transfers between devices, to_near(): return lax.ppermute(value, AXES, sided(-2))  4.12 us
    ppermute x3, waiting for transfers between devices, to_far(): return lax.ppermute(value, AXES, sided(2))  3.85 us
    ppermute x2, waiting for transfers between devices, to_across(): return lax.ppermute(value, AXES, sided(-1))  3.45 us
    ppermute x9, starting transfers between devices, swap(): return lax.ppermute(value, AXES, sided(1))  3.24 us
    ppermute x9, waiting for transfers between devices, swap(): return lax.ppermute(value, AXES, sided(1))  1.49 us
  transfers between devices with their start and end apart: 16, of which 7 were waited for; matrix products, arithmetic and copies ran while one was open for 0% of the time, Pallas kernels for 26%

profile of v9, /device:TPU:0, one launch (start us, length us, event | category | flops | bytes accessed | tf_op | source)
XLA Modules:
  0.0 51.3 jit_solution(10363310433290740096)
XLA Ops:
  0.0 4.2 %shard_map.154 = (bf16[2048,512]{1,0:T(8,128)(2,1)S(1)}, bf16[256,512]{1,0:T(8,128)(2,1)S(1)}, bf16[256,512]{1,0:T(8,128)(2,1)S(1)}, s32[1,2048]{1,0:T(1,128)S(1)}) custom-call(s32[1,2048]{1,0:T(1,128)} %bitcast.7, s32[1,2048]{1,0:T(1,128)} %bitcast.8, bf16[2048,512]{1,0:T(8,128)(2,1)} %grid.3, bf16[512,512]{1,0:T(8,128)(2,1)} %w1.1, f32[1,512]{1,0:T(1,128)} %bitcast.9), custom_call_target="tpu_custom_call" | custom-call | flops 2147483648 | bytes 2639872 | tf_op jit(solution)/shard_map/pallas_call | solution.py:298
  4.2 0.5 %collective-permute-start = (bf16[256,512]{1,0:T(8,128)(2,1)S(1)}, bf16[256,512]{1,0:T(8,128)(2,1)S(1)}, u32[]{:S(2)}, u32[]{:S(2)}) collective-permute-start(bf16[256,512]{1,0:T(8,128)(2,1)S(1)} %get-tuple-element.38), channel_id=1, source_target_pairs={{0,1},{1,0},{2,3},{3,2},{4,5},{5,4},{6,7},{7,6},{8,9},{9,8},{10,11... | collective-permute-start | bytes 786440 | tf_op jit(solution)/shard_map/ppermute | solution.py:338
  4.7 5.6 %collective-permute-start.1 = (bf16[256,512]{1,0:T(8,128)(2,1)S(1)}, bf16[256,512]{1,0:T(8,128)(2,1)S(1)}, u32[]{:S(2)}, u32[]{:S(2)}) collective-permute-start(bf16[256,512]{1,0:T(8,128)(2,1)S(1)} %get-tuple-element.40), channel_id=1, source_target_pairs={{0,14},{1,3},{2,0},{3,5},{4,2},{5,7},{6,4},{7,9},{8,6},{9,11},{10,... | collective-permute-start | bytes 786440 | tf_op jit(solution)/shard_map/ppermute | solution.py:344
  10.3 0.7 %shard_map.155.after = bf16[256,512]{1,0:T(8,128)(2,1)S(1)} custom-call(s32[1,2048]{1,0:T(1,128)S(1)} %get-tuple-element.36.code, bf16[2048,512]{1,0:T(8,128)(2,1)S(1)} %get-tuple-element.37.hidden, bf16[256,512]{1,0:T(8,128)(2,1)S(1)} %collective-permute-done.crossed), custom_call_target="tpu_custom_call" | custom-call | flops 1 | bytes 1 | tf_op jit(solution)/shard_map/pallas_call | solution.py:298
  11.1 3.1 %shard_map.156 = (f32[256,512]{1,0:T(8,128)S(1)}, bf16[256,512]{1,0:T(8,128)(2,1)S(1)}, bf16[256,64]{1,0:T(8,128)(2,1)S(1)}, bf16[3,512,512]{2,1,0:T(8,128)(2,1)...) custom-call(bf16[256,512]{1,0:T(8,128)(2,1)S(1)} %shard_map.155.after, ...), custom_call_target="tpu_custom_call" | custom-call | flops 1073741824 | bytes 5775616 | tf_op jit(solution)/shard_map/pallas_call | solution.py:298
  14.3 1.4 %collective-permute-start.2 = (bf16[256,512]{1,0:T(8,128)(2,1)S(1)}, bf16[256,512]{1,0:T(8,128)(2,1)S(1)}, u32[]{:S(2)}, u32[]{:S(2)}) collective-permute-start(bf16[256,512]{1,0:T(8,128)(2,1)S(1)} %get-tuple-element.44), channel_id=1, source_target_pairs={{0,1},{1,0},{2,3},{3,2},{4,5},{5,4},{6,7},{7,6},{8,9},{9,8},{10,11... | collective-permute-start | bytes 786440 | tf_op jit(solution)/shard_map/ppermute | solution.py:338
  15.7 0.6 %shard_map.157 = (bf16[1536,256]{1,0:T(8,128)(2,1)S(1)}, bf16[1536,128]{1,0:T(8,128)(2,1)S(1)}, bf16[384,256]{1,0:T(8,128)(2,1)S(1)}, bf16[384,128]{1,0:T(8,128)(2,1)S(1)}) custom-call(bf16[256,512]{1,0:T(8,128)(2,1)S(1)} %collective-permute-done.1.after.near, s32[6,256]{1,0:T(8,128)S(1)} %bitcast.6, bf16[256,64]{1,0:T(8,128)(2,1)S(1)} %get-tuple-element.41.pick.refs_0_), custom_call_target="tpu_custom_call" | custom-call | flops 40000000000 | bytes 301056 | tf_op jit(solution)/shard_map/pallas_call | solution.py:298
  16.3 3.8 %collective-permute-done.3.far = bf16[256,512]{1,0:T(8,128)(2,1)S(1)} collective-permute-done((bf16[256,512]{1,0:T(8,128)(2,1)S(1)}, bf16[256,512]{1,0:T(8,128)(2,1)S(1)}, u32[]{:S(2)}, u32[]{:S(2)}) %collective-permute-start.3) | collective-permute-done | bytes 262176 | tf_op jit(solution)/shard_map/ppermute | solution.py:347
  20.2 0.4 shard_map.158
  20.6 2.8 %collective-permute-start.4 = (bf16[64,512]{1,0:T(8,128)(2,1)S(1)}, bf16[64,512]{1,0:T(8,128)(2,1)S(1)}, u32[]{:S(2)}, u32[]{:S(2)}) collective-permute-start(bf16[64,512]{1,0:T(8,128)(2,1)S(1)} %get-tuple-element.49.halo), channel_id=1, source_target_pairs={{0,15},{1,2},{2,1},{3,4},{4,3},{5,6},{6,5},{7,8},{8,7},{9,10},{10,... | collective-permute-start | bytes 196616 | tf_op jit(solution)/shard_map/ppermute | solution.py:341
  23.4 0.3 shard_map.159.latent
  23.7 1.5 %shard_map.160 = (f32[1536,512]{1,0:T(8,128)S(1)}, bf16[64,512]{1,0:T(8,128)(2,1)S(1)}, f32[64,512]{1,0:T(8,128)S(1)}, f32[384,512]{1,0:T(8,128)S(1)}) custom-call(bf16[256,512]{1,0:T(8,128)(2,1)S(1)} %shard_map.159.latent, bf16[2,512,512]{2,1,0:T(8,128)(2,1)S(1)} %copy-done, bf16[2,512,512]{2,1,0:T(8,128)(2,1)S(1)} %copy-done.1, f32[2,512]{1,0:T(2,128)S(1)} %copy-done.9, ...), custom_call_target="tpu_custom_call" | custom-call | flops 1 | bytes 1 | tf_op jit(solution)/shard_map/pallas_call | solution.py:298
  25.3 1.8 %collective-permute-done.4.table = bf16[64,512]{1,0:T(8,128)(2,1)S(1)} collective-permute-done((bf16[64,512]{1,0:T(8,128)(2,1)S(1)}, bf16[64,512]{1,0:T(8,128)(2,1)S(1)}, u32[]{:S(2)}, u32[]{:S(2)}) %collective-permute-start.4) | collective-permute-done | bytes 65568 | tf_op jit(solution)/shard_map/ppermute | solution.py:341
  27.1 0.5 shard_map.163.halo
  27.5 2.8 %collective-permute-start.6 = (bf16[64,512]{1,0:T(8,128)(2,1)S(1)}, bf16[64,512]{1,0:T(8,128)(2,1)S(1)}, u32[]{:S(2)}, u32[]{:S(2)}) collective-permute-start(bf16[64,512]{1,0:T(8,128)(2,1)S(1)} %shard_map.163.halo), channel_id=1, source_target_pairs={{0,15},{1,2},{2,1},{3,4},{4,3},{5,6},{6,5},{7,8},{8,7},{9,10},{10,... | collective-permute-start | bytes 196616 | tf_op jit(solution)/shard_map/ppermute | solution.py:341
  30.3 0.9 %shard_map.162.latent = bf16[256,512]{1,0:T(8,128)(2,1)S(1)} custom-call(bf16[256,512]{1,0:T(8,128)(2,1)S(1)} %shard_map.159.latent, f32[1536,512]{1,0:T(8,128)S(1)} %get-tuple-element.51.before, bf16[64,512]{1,0:T(8,128)(2,1)S(1)} %shard_map.161.across, bf16[64,512]{1,0:T(8,128)(2,1)S(1)} %collective-permute-done.5.beside, ...), custom_call_target="tpu_custom_call" | custom-call | flops 1 | bytes 1 | tf_op jit(solution)/shard_map/pallas_call | solution.py:298
  31.2 1.0 %shard_map.164 = (f32[1536,512]{1,0:T(8,128)S(1)}, bf16[64,512]{1,0:T(8,128)(2,1)S(1)}, f32[256,512]{1,0:T(8,128)S(1)}) custom-call(bf16[256,512]{1,0:T(8,128)(2,1)S(1)} %shard_map.162.latent, bf16[2,512,512]{2,1,0:T(8,128)(2,1)S(1)} %copy-done, bf16[2,512,512]{2,1,0:T(8,128)(2,1)S(1)} %copy-done.1, f32[2,512]{1,0:T(2,128)S(1)} %copy-done.9, ...), custom_call_target="tpu_custom_call" | custom-call | flops 1 | bytes 1 | tf_op jit(solution)/shard_map/pallas_call | solution.py:298
  32.3 1.7 %collective-permute-done.6.table = bf16[64,512]{1,0:T(8,128)(2,1)S(1)} collective-permute-done((bf16[64,512]{1,0:T(8,128)(2,1)S(1)}, bf16[64,512]{1,0:T(8,128)(2,1)S(1)}, u32[]{:S(2)}, u32[]{:S(2)}) %collective-permute-start.6) | collective-permute-done | bytes 65568 | tf_op jit(solution)/shard_map/ppermute | solution.py:341
  34.0 0.9 %shard_map.166.own = bf16[256,512]{1,0:T(8,128)(2,1)S(1)} custom-call(f32[1536,512]{1,0:T(8,128)S(1)} %get-tuple-element.56.before, bf16[64,512]{1,0:T(8,128)(2,1)S(1)} %shard_map.165.across, bf16[64,512]{1,0:T(8,128)(2,1)S(1)} %collective-permute-done.7.beside, bf16[1536,128]{1,0:T(8,128)(2,1)S(1)} %get-tuple-element.53.gather_halo, ...), custom_call_target="tpu_custom_call" | custom-call | flops 469762048 | bytes 5767168 | tf_op jit(solution)/shard_map/pallas_call | solution.py:298
  35.0 1.5 %collective-permute-start.10 = (bf16[256,512]{1,0:T(8,128)(2,1)S(1)}, bf16[256,512]{1,0:T(8,128)(2,1)S(1)}, u32[]{:S(2)}, u32[]{:S(2)}) collective-permute-start(bf16[256,512]{1,0:T(8,128)(2,1)S(1)} %shard_map.166.own), channel_id=1, source_target_pairs={{0,14},{1,3},{2,0},{3,5},{4,2},{5,7},{6,4},{7,9},{8,6},{9,11},{10,... | collective-permute-start | bytes 786440 | tf_op jit(solution)/shard_map/ppermute | solution.py:344
  36.5 1.8 %shard_map.167 = (f32[2048,512]{1,0:T(8,128)S(1)}, bf16[128,512]{1,0:T(8,128)(2,1)S(1)}, bf16[128,512]{1,0:T(8,128)(2,1)S(1)}) custom-call(bf16[2048,512]{1,0:T(8,128)(2,1)S(1)} %copy-done.6, bf16[512,512]{1,0:T(8,128)(2,1)S(1)} %copy-done.8, bf16[2048,1280]{1,0:T(8,128)(2,1)S(1)} %get-tuple-element.39.fetch, bf16[256,512]{1,0:T(8,128)(2,1)S(1)} %shard_map.166.own), custom_call_target="tpu_custom_call" | custom-call | flops 1 | bytes 1 | tf_op jit(solution)/shard_map/pallas_call | solution.py:298
  38.4 0.5 collective-permute-start.9
  38.9 0.8 %collective-permute-done.8.refs_0_.first_after = bf16[128,512]{1,0:T(8,128)(2,1)S(1)} collective-permute-done((bf16[128,512]{1,0:T(8,128)(2,1)S(1)}, bf16[128,512]{1,0:T(8,128)(2,1)S(1)}, u32[]{:S(2)}, u32[]{:S(2)}) %collective-permute-start.8) | collective-permute-done | bytes 131104 | tf_op jit(solution)/shard_map/ppermute | solution.py:338
  39.9 0.8 %collective-permute-start.15 = (bf16[256,256]{1,0:T(8,128)(2,1)S(1)}, bf16[256,256]{1,0:T(8,128)(2,1)S(1)}, u32[]{:S(2)}, u32[]{:S(2)}) collective-permute-start(bf16[256,256]{1,0:T(8,128)(2,1)S(1)} %get-tuple-element.66), channel_id=1, source_target_pairs={{0,2},{1,15},{2,4},{3,1},{4,6},{5,3},{6,8},{7,5},{8,10},{9,7},{10,... | collective-permute-start | bytes 393224 | tf_op jit(solution)/shard_map/ppermute | solution.py:347
  40.8 0.7 %shard_map.168.base.after = f32[2048,512]{1,0:T(8,128)S(1)} custom-call(bf16[2048,1280]{1,0:T(8,128)(2,1)S(1)} %get-tuple-element.39.fetch, f32[2048,512]{1,0:T(8,128)S(1)} %get-tuple-element.59.base, bf16[128,512]{1,0:T(8,128)(2,1)S(1)} %collective-permute-done.8.refs_0_.first_after, bf16[128,512]{1,0:T(8,128)(2,1)S(1)} %collective-permute-done.9.refs_1_.after), custom_call_target="tpu_custom_call" | custom-call | flops 1 | bytes 1 | tf_op jit(solution)/shard_map/pallas_call | solution.py:298
  41.5 4.1 %collective-permute-done.10.far.table = bf16[256,512]{1,0:T(8,128)(2,1)S(1)} collective-permute-done((bf16[256,512]{1,0:T(8,128)(2,1)S(1)}, bf16[256,512]{1,0:T(8,128)(2,1)S(1)}, u32[]{:S(2)}, u32[]{:S(2)}) %collective-permute-start.10) | collective-permute-done | bytes 262176 | tf_op jit(solution)/shard_map/ppermute | solution.py:344
  45.7 0.5 collective-permute-start.12
  46.3 0.7 %shard_map.169.base = f32[2048,512]{1,0:T(8,128)S(1)} custom-call(bf16[2048,1280]{1,0:T(8,128)(2,1)S(1)} %get-tuple-element.39.fetch, f32[2048,512]{1,0:T(8,128)S(1)} %shard_map.168.base.after, bf16[256,512]{1,0:T(8,128)(2,1)S(1)} %collective-permute-done.10.far.table), custom_call_target="tpu_custom_call" | custom-call | flops 1 | bytes 1 | tf_op jit(solution)/shard_map/pallas_call | solution.py:298
  47.0 0.4 collective-permute-done.13.refs_2_
  47.5 0.7 %shard_map.171.base = f32[2048,512]{1,0:T(8,128)S(1)} custom-call(bf16[2048,1280]{1,0:T(8,128)(2,1)S(1)} %get-tuple-element.39.fetch, f32[2048,512]{1,0:T(8,128)S(1)} %shard_map.169.base, bf16[112,512]{1,0:T(8,128)(2,1)S(1)} %collective-permute-done.11.refs_0_, bf16[80,512]{1,0:T(8,128)(2,1)S(1)} %collective-permute-done.12.refs_1_, ...), custom_call_target="tpu_custom_call" | custom-call | flops 1 | bytes 1 | tf_op jit(solution)/shard_map/pallas_call | solution.py:298
  48.2 1.0 %shard_map.173.partial = f32[2048,512]{1,0:T(8,128)S(1)} custom-call(bf16[2048,1280]{1,0:T(8,128)(2,1)S(1)} %get-tuple-element.39.fetch, f32[2048,512]{1,0:T(8,128)S(1)} %shard_map.171.base, bf16[256,256]{1,0:T(8,128)(2,1)S(1)} %collective-permute-done.15.near, bf16[512,512]{1,0:T(8,128)(2,1)S(1)} %copy-done.3), custom_call_target="tpu_custom_call" | custom-call | flops 1 | bytes 1 | tf_op jit(solution)/shard_map/pallas_call | solution.py:298
  49.2 1.9 %shard_map.174 = bf16[2048,512]{1,0:T(8,128)(2,1)} custom-call(bf16[2048,1280]{1,0:T(8,128)(2,1)S(1)} %get-tuple-element.39.fetch, f32[2048,512]{1,0:T(8,128)S(1)} %shard_map.171.base, bf16[256,256]{1,0:T(8,128)(2,1)S(1)} %collective-permute-done.14.near, bf16[512,512]{1,0:T(8,128)(2,1)S(1)} %copy-done.3, f32[2048,512]{1,0:T(8,128)S(1)} %shard_map.173.partial), custom_call_target="tpu_custom_call" | custom-call | flops 1610612736 | bytes 14286848 | tf_op jit(solution)/shard_map/pallas_call | solution.py:298
  (45 shorter events, 0.8 us)
Async XLA Ops:
  0.0 11.1 %copy-start.10 = (s32[64]{0:T(128)S(1)}, s32[64]{0:T(128)}, u32[]{:S(2)}) copy-start(s32[64]{0:T(128)} %param.20) | copy-start | bytes 772
  4.2 6.1 %collective-permute-start = (bf16[256,512]{1,0:T(8,128)(2,1)S(1)}, bf16[256,512]{1,0:T(8,128)(2,1)S(1)}, u32[]{:S(2)}, u32[]{:S(2)}) collective-permute-start(bf16[256,512]{1,0:T(8,128)(2,1)S(1)} %get-tuple-element.38), channel_id=1, source_target_pairs={{0,1},{1,0},{2,3},{3,2},{4,5},{5,4},{6,7},{7,6},{8,9},{9,8},{10,11... | collective-permute-start | bytes 786440 | tf_op jit(solution)/shard_map/ppermute | solution.py:338
  4.7 10.9 %collective-permute-start.1 = (bf16[256,512]{1,0:T(8,128)(2,1)S(1)}, bf16[256,512]{1,0:T(8,128)(2,1)S(1)}, u32[]{:S(2)}, u32[]{:S(2)}) collective-permute-start(bf16[256,512]{1,0:T(8,128)(2,1)S(1)} %get-tuple-element.40), channel_id=1, source_target_pairs={{0,14},{1,3},{2,0},{3,5},{4,2},{5,7},{6,4},{7,9},{8,6},{9,11},{10,... | collective-permute-start | bytes 786440 | tf_op jit(solution)/shard_map/ppermute | solution.py:344
  10.3 5.3 %copy-start.11 = (s32[256,6]{0,1:T(8,128)S(1)}, s32[256,6]{0,1:T(8,128)}, u32[]{:S(2)}) copy-start(s32[256,6]{0,1:T(8,128)} %param.21) | copy-start | bytes 18436
  11.0 9.1 %collective-permute-start.3 = (bf16[256,512]{1,0:T(8,128)(2,1)S(1)}, bf16[256,512]{1,0:T(8,128)(2,1)S(1)}, u32[]{:S(2)}, u32[]{:S(2)}) collective-permute-start(bf16[256,512]{1,0:T(8,128)(2,1)S(1)} %shard_map.155.after), channel_id=1, source_target_pairs={{0,2},{1,15},{2,4},{3,1},{4,6},{5,3},{6,8},{7,5},{8,10},{9,7},{10,... | collective-permute-start | bytes 786440 | tf_op jit(solution)/shard_map/ppermute | solution.py:347
  14.3 5.9 %collective-permute-start.2 = (bf16[256,512]{1,0:T(8,128)(2,1)S(1)}, bf16[256,512]{1,0:T(8,128)(2,1)S(1)}, u32[]{:S(2)}, u32[]{:S(2)}) collective-permute-start(bf16[256,512]{1,0:T(8,128)(2,1)S(1)} %get-tuple-element.44), channel_id=1, source_target_pairs={{0,1},{1,0},{2,3},{3,2},{4,5},{5,4},{6,7},{7,6},{8,9},{9,8},{10,11... | collective-permute-start | bytes 786440 | tf_op jit(solution)/shard_map/ppermute | solution.py:338
  15.6 7.7 %copy-start.4 = (bf16[512,512]{1,0:T(8,128)(2,1)S(1)}, bf16[512,512]{1,0:T(8,128)(2,1)}, u32[]{:S(2)}) copy-start(bf16[512,512]{1,0:T(8,128)(2,1)} %w2.1) | copy-start | bytes 1572868
  15.6 7.7 %copy-start.7 = (bf16[256,512]{1,0:T(8,128)(2,1)S(1)}, bf16[256,512]{1,0:T(8,128)(2,1)}, u32[]{:S(2)}) copy-start(bf16[256,512]{1,0:T(8,128)(2,1)} %mesh.1) | copy-start | bytes 786436
  16.3 7.4 %copy-start = (bf16[2,512,512]{2,1,0:T(8,128)(2,1)S(1)}, bf16[2,512,512]{2,1,0:T(8,128)(2,1)}, u32[]{:S(2)}) copy-start(bf16[2,512,512]{2,1,0:T(8,128)(2,1)} %w_src.3) | copy-start | bytes 3145732
  16.3 7.4 %copy-start.1 = (bf16[2,512,512]{2,1,0:T(8,128)(2,1)S(1)}, bf16[2,512,512]{2,1,0:T(8,128)(2,1)}, u32[]{:S(2)}) copy-start(bf16[2,512,512]{2,1,0:T(8,128)(2,1)} %w_dst.3) | copy-start | bytes 3145732
  16.3 7.4 %copy-start.9 = (f32[2,512]{1,0:T(2,128)S(1)}, f32[2,512]{1,0:T(2,128)}, u32[]{:S(2)}) copy-start(f32[2,512]{1,0:T(2,128)} %bias.3) | copy-start | bytes 12292
  20.6 6.5 %collective-permute-start.4 = (bf16[64,512]{1,0:T(8,128)(2,1)S(1)}, bf16[64,512]{1,0:T(8,128)(2,1)S(1)}, u32[]{:S(2)}, u32[]{:S(2)}) collective-permute-start(bf16[64,512]{1,0:T(8,128)(2,1)S(1)} %get-tuple-element.49.halo), channel_id=1, source_target_pairs={{0,15},{1,2},{2,1},{3,4},{4,3},{5,6},{6,5},{7,8},{8,7},{9,10},{10,... | collective-permute-start | bytes 196616 | tf_op jit(solution)/shard_map/ppermute | solution.py:341
  25.2 5.1 %copy-start.2 = (bf16[2,512,512]{2,1,0:T(8,128)(2,1)S(1)}, bf16[2,512,512]{2,1,0:T(8,128)(2,1)}, u32[]{:S(2)}) copy-start(bf16[2,512,512]{2,1,0:T(8,128)(2,1)} %w_out.3) | copy-start | bytes 3145732
  25.2 1.9 %collective-permute-start.5 = (bf16[64,512]{1,0:T(8,128)(2,1)S(1)}, bf16[64,512]{1,0:T(8,128)(2,1)S(1)}, u32[]{:S(2)}, u32[]{:S(2)}) collective-permute-start(bf16[64,512]{1,0:T(8,128)(2,1)S(1)} %get-tuple-element.52), channel_id=1, source_target_pairs={{0,1},{1,0},{2,3},{3,2},{4,5},{5,4},{6,7},{7,6},{8,9},{9,8},{10,11... | collective-permute-start | bytes 196616 | tf_op jit(solution)/shard_map/ppermute | solution.py:338
  27.1 4.2 %copy-start.5 = (bf16[512,512]{1,0:T(8,128)(2,1)S(1)}, bf16[512,512]{1,0:T(8,128)(2,1)}, u32[]{:S(2)}) copy-start(bf16[512,512]{1,0:T(8,128)(2,1)} %w_next.3) | copy-start | bytes 1572868
  27.5 6.5 %collective-permute-start.6 = (bf16[64,512]{1,0:T(8,128)(2,1)S(1)}, bf16[64,512]{1,0:T(8,128)(2,1)S(1)}, u32[]{:S(2)}, u32[]{:S(2)}) collective-permute-start(bf16[64,512]{1,0:T(8,128)(2,1)S(1)} %shard_map.163.halo), channel_id=1, source_target_pairs={{0,15},{1,2},{2,1},{3,4},{4,3},{5,6},{6,5},{7,8},{8,7},{9,10},{10,... | collective-permute-start | bytes 196616 | tf_op jit(solution)/shard_map/ppermute | solution.py:341
  32.2 1.8 %collective-permute-start.7 = (bf16[64,512]{1,0:T(8,128)(2,1)S(1)}, bf16[64,512]{1,0:T(8,128)(2,1)S(1)}, u32[]{:S(2)}, u32[]{:S(2)}) collective-permute-start(bf16[64,512]{1,0:T(8,128)(2,1)S(1)} %get-tuple-element.57), channel_id=1, source_target_pairs={{0,1},{1,0},{2,3},{3,2},{4,5},{5,4},{6,7},{7,6},{8,9},{9,8},{10,11... | collective-permute-start | bytes 196616 | tf_op jit(solution)/shard_map/ppermute | solution.py:338
  34.0 2.5 %copy-start.6 = (bf16[2048,512]{1,0:T(8,128)(2,1)S(1)}, bf16[2048,512]{1,0:T(8,128)(2,1)}, u32[]{:S(2)}) copy-start(bf16[2048,512]{1,0:T(8,128)(2,1)} %grid.3) | copy-start | bytes 6291460
  34.0 2.5 %copy-start.8 = (bf16[512,512]{1,0:T(8,128)(2,1)S(1)}, bf16[512,512]{1,0:T(8,128)(2,1)}, u32[]{:S(2)}) copy-start(bf16[512,512]{1,0:T(8,128)(2,1)} %w_grid.1) | copy-start | bytes 1572868
  35.0 10.6 %collective-permute-start.10 = (bf16[256,512]{1,0:T(8,128)(2,1)S(1)}, bf16[256,512]{1,0:T(8,128)(2,1)S(1)}, u32[]{:S(2)}, u32[]{:S(2)}) collective-permute-start(bf16[256,512]{1,0:T(8,128)(2,1)S(1)} %shard_map.166.own), channel_id=1, source_target_pairs={{0,14},{1,3},{2,0},{3,5},{4,2},{5,7},{6,4},{7,9},{8,6},{9,11},{10,... | collective-permute-start | bytes 786440 | tf_op jit(solution)/shard_map/ppermute | solution.py:344
  38.3 1.4 %collective-permute-start.8 = (bf16[128,512]{1,0:T(8,128)(2,1)S(1)}, bf16[128,512]{1,0:T(8,128)(2,1)S(1)}, u32[]{:S(2)}, u32[]{:S(2)}) collective-permute-start(bf16[128,512]{1,0:T(8,128)(2,1)S(1)} %get-tuple-element.60), channel_id=1, source_target_pairs={{0,1},{1,0},{2,3},{3,2},{4,5},{5,4},{6,7},{7,6},{8,9},{9,8},{10,11... | collective-permute-start | bytes 393224 | tf_op jit(solution)/shard_map/ppermute | solution.py:338
  38.4 1.5 %collective-permute-start.9 = (bf16[128,512]{1,0:T(8,128)(2,1)S(1)}, bf16[128,512]{1,0:T(8,128)(2,1)S(1)}, u32[]{:S(2)}, u32[]{:S(2)}) collective-permute-start(bf16[128,512]{1,0:T(8,128)(2,1)S(1)} %get-tuple-element.61), channel_id=1, source_target_pairs={{0,1},{1,0},{2,3},{3,2},{4,5},{5,4},{6,7},{7,6},{8,9},{9,8},{10,11... | collective-permute-start | bytes 393224 | tf_op jit(solution)/shard_map/ppermute | solution.py:338
  39.9 8.2 %collective-permute-start.15 = (bf16[256,256]{1,0:T(8,128)(2,1)S(1)}, bf16[256,256]{1,0:T(8,128)(2,1)S(1)}, u32[]{:S(2)}, u32[]{:S(2)}) collective-permute-start(bf16[256,256]{1,0:T(8,128)(2,1)S(1)} %get-tuple-element.66), channel_id=1, source_target_pairs={{0,2},{1,15},{2,4},{3,1},{4,6},{5,3},{6,8},{7,5},{8,10},{9,7},{10,... | collective-permute-start | bytes 393224 | tf_op jit(solution)/shard_map/ppermute | solution.py:347
  40.7 8.5 %collective-permute-start.14 = (bf16[256,256]{1,0:T(8,128)(2,1)S(1)}, bf16[256,256]{1,0:T(8,128)(2,1)S(1)}, u32[]{:S(2)}, u32[]{:S(2)}) collective-permute-start(bf16[256,256]{1,0:T(8,128)(2,1)S(1)} %get-tuple-element.65), channel_id=1, source_target_pairs={{0,2},{1,15},{2,4},{3,1},{4,6},{5,3},{6,8},{7,5},{8,10},{9,7},{10,... | collective-permute-start | bytes 393224 | tf_op jit(solution)/shard_map/ppermute | solution.py:347
  45.6 1.8 %collective-permute-start.11 = (bf16[112,512]{1,0:T(8,128)(2,1)S(1)}, bf16[112,512]{1,0:T(8,128)(2,1)S(1)}, u32[]{:S(2)}, u32[]{:S(2)}) collective-permute-start(bf16[112,512]{1,0:T(8,128)(2,1)S(1)} %get-tuple-element.62), channel_id=1, source_target_pairs={{0,1},{1,0},{2,3},{3,2},{4,5},{5,4},{6,7},{7,6},{8,9},{9,8},{10,11... | collective-permute-start | bytes 344072 | tf_op jit(solution)/shard_map/ppermute | solution.py:338
  45.7 1.8 %collective-permute-start.12 = (bf16[80,512]{1,0:T(8,128)(2,1)S(1)}, bf16[80,512]{1,0:T(8,128)(2,1)S(1)}, u32[]{:S(2)}, u32[]{:S(2)}) collective-permute-start(bf16[80,512]{1,0:T(8,128)(2,1)S(1)} %get-tuple-element.63), channel_id=1, source_target_pairs={{0,1},{1,0},{2,3},{3,2},{4,5},{5,4},{6,7},{7,6},{8,9},{9,8},{10,11... | collective-permute-start | bytes 245768 | tf_op jit(solution)/shard_map/ppermute | solution.py:338
  46.2 1.3 %collective-permute-start.13 = (bf16[64,512]{1,0:T(8,128)(2,1)S(1)}, bf16[64,512]{1,0:T(8,128)(2,1)S(1)}, u32[]{:S(2)}, u32[]{:S(2)}) collective-permute-start(bf16[64,512]{1,0:T(8,128)(2,1)S(1)} %get-tuple-element.64), channel_id=1, source_target_pairs={{0,1},{1,0},{2,3},{3,2},{4,5},{5,4},{6,7},{7,6},{8,9},{9,8},{10,11... | collective-permute-start | bytes 196616 | tf_op jit(solution)/shard_map/ppermute | solution.py:338
  47.0 1.2 %copy-start.3 = (bf16[512,512]{1,0:T(8,128)(2,1)S(1)}, bf16[512,512]{1,0:T(8,128)(2,1)}, u32[]{:S(2)}) copy-start(bf16[512,512]{1,0:T(8,128)(2,1)} %w_out.5) | copy-start | bytes 1572868

commit v10 on v9

--- a/solution.py
+++ b/solution.py
@@ -13,6 +13,7 @@
 MIB = 1 << 20
 BLOCK = 512
 ENCODE_BLOCK = 1024
+ENCODE_STEP = 512
 DECODE_BLOCK = 256
 LONG = 40_000_000_000
 
@@ -75,10 +76,16 @@
     copies[3].wait()
     weights = w1_v[...] * 0.5
     offset = bias_v[...] * 0.5
-    for r, copy in zip(starts, blocks):
-        copy.wait()
-        spot = slice(r, r + ENCODE_BLOCK)
-        hidden[spot] = silu_of_twice(dot(grid_v[spot], weights) + offset).astype(BF16)
+    def halved(r):
+        if r % ENCODE_BLOCK == 0:
+            blocks[r // ENCODE_BLOCK].wait()
+        return dot(grid_v[r : r + ENCODE_STEP], weights) + offset
+
+    half = halved(0)
+    for r in range(0, grid.shape[0], ENCODE_STEP):
+        ahead = halved(r + ENCODE_STEP) if r + ENCODE_STEP < grid.shape[0] else None
+        hidden[r : r + ENCODE_STEP] = silu_of_twice(half).astype(BF16)
+        half = ahead
     rows = near.shape[0]
     cross[...] = dot(one_hot[rows:], hidden[...]).astype(BF16)
     near[...] = dot(one_hot[:rows], hidden[...]).astype(BF16)

time: 51.6 us -> 51.6 us (level)
  no operation moved by 1% of the time
where the time goes in v10:
time: 51.6 us; the launch traced here: 51.3 us
  Pallas kernels  21 us (41%)
  starting transfers between devices  16.8 us (33%)
  waiting for transfers between devices  12.9 us (25%)
    pallas_call x21, Pallas kernels, call(): pl.pallas_call(kernel, in_specs=[pl.BlockSpec(memory_space=space) for spa...  21 us
    ppermute x2, starting transfers between devices, to_near(): return lax.ppermute(value, AXES, sided(-2))  7.16 us
    ppermute x2, starting transfers between devices, to_across(): return lax.ppermute(value, AXES, sided(-1))  5.55 us
    ppermute x2, waiting for transfers between devices, to_near(): return lax.ppermute(value, AXES, sided(-2))  4.11 us
    ppermute x3, waiting for transfers between devices, to_far(): return lax.ppermute(value, AXES, sided(2))  3.85 us
    ppermute x2, waiting for transfers between devices, to_across(): return lax.ppermute(value, AXES, sided(-1))  3.44 us
    ppermute x9, starting transfers between devices, swap(): return lax.ppermute(value, AXES, sided(1))  3.23 us
    ppermute x9, waiting for transfers between devices, swap(): return lax.ppermute(value, AXES, sided(1))  1.49 us
  transfers between devices with their start and end apart: 16, of which 7 were waited for; matrix products, arithmetic and copies ran while one was open for 0% of the time, Pallas kernels for 26%

profile of v10, /device:TPU:0, one launch (start us, length us, event | category | flops | bytes accessed | tf_op | source)
XLA Modules:
  0.0 51.3 jit_solution(532488755736057823)
XLA Ops:
  0.0 4.2 %shard_map.154 = (bf16[2048,512]{1,0:T(8,128)(2,1)S(1)}, bf16[256,512]{1,0:T(8,128)(2,1)S(1)}, bf16[256,512]{1,0:T(8,128)(2,1)S(1)}, s32[1,2048]{1,0:T(1,128)S(1)}) custom-call(s32[1,2048]{1,0:T(1,128)} %bitcast.7, s32[1,2048]{1,0:T(1,128)} %bitcast.8, bf16[2048,512]{1,0:T(8,128)(2,1)} %grid.3, bf16[512,512]{1,0:T(8,128)(2,1)} %w1.1, f32[1,512]{1,0:T(1,128)} %bitcast.9), custom_call_target="tpu_custom_call" | custom-call | flops 2147483648 | bytes 2639872 | tf_op jit(solution)/shard_map/pallas_call | solution.py:305
  4.2 0.5 %collective-permute-start = (bf16[256,512]{1,0:T(8,128)(2,1)S(1)}, bf16[256,512]{1,0:T(8,128)(2,1)S(1)}, u32[]{:S(2)}, u32[]{:S(2)}) collective-permute-start(bf16[256,512]{1,0:T(8,128)(2,1)S(1)} %get-tuple-element.38), channel_id=1, source_target_pairs={{0,1},{1,0},{2,3},{3,2},{4,5},{5,4},{6,7},{7,6},{8,9},{9,8},{10,11... | collective-permute-start | bytes 786440 | tf_op jit(solution)/shard_map/ppermute | solution.py:345
  4.8 5.6 %collective-permute-start.1 = (bf16[256,512]{1,0:T(8,128)(2,1)S(1)}, bf16[256,512]{1,0:T(8,128)(2,1)S(1)}, u32[]{:S(2)}, u32[]{:S(2)}) collective-permute-start(bf16[256,512]{1,0:T(8,128)(2,1)S(1)} %get-tuple-element.40), channel_id=1, source_target_pairs={{0,14},{1,3},{2,0},{3,5},{4,2},{5,7},{6,4},{7,9},{8,6},{9,11},{10,... | collective-permute-start | bytes 786440 | tf_op jit(solution)/shard_map/ppermute | solution.py:351
  10.4 0.7 %shard_map.155.after = bf16[256,512]{1,0:T(8,128)(2,1)S(1)} custom-call(s32[1,2048]{1,0:T(1,128)S(1)} %get-tuple-element.36.code, bf16[2048,512]{1,0:T(8,128)(2,1)S(1)} %get-tuple-element.37.hidden, bf16[256,512]{1,0:T(8,128)(2,1)S(1)} %collective-permute-done.crossed), custom_call_target="tpu_custom_call" | custom-call | flops 1 | bytes 1 | tf_op jit(solution)/shard_map/pallas_call | solution.py:305
  11.2 3.1 %shard_map.156 = (f32[256,512]{1,0:T(8,128)S(1)}, bf16[256,512]{1,0:T(8,128)(2,1)S(1)}, bf16[256,64]{1,0:T(8,128)(2,1)S(1)}, bf16[3,512,512]{2,1,0:T(8,128)(2,1)...) custom-call(bf16[256,512]{1,0:T(8,128)(2,1)S(1)} %shard_map.155.after, ...), custom_call_target="tpu_custom_call" | custom-call | flops 1073741824 | bytes 5775616 | tf_op jit(solution)/shard_map/pallas_call | solution.py:305
  14.3 1.4 %collective-permute-start.2 = (bf16[256,512]{1,0:T(8,128)(2,1)S(1)}, bf16[256,512]{1,0:T(8,128)(2,1)S(1)}, u32[]{:S(2)}, u32[]{:S(2)}) collective-permute-start(bf16[256,512]{1,0:T(8,128)(2,1)S(1)} %get-tuple-element.44), channel_id=1, source_target_pairs={{0,1},{1,0},{2,3},{3,2},{4,5},{5,4},{6,7},{7,6},{8,9},{9,8},{10,11... | collective-permute-start | bytes 786440 | tf_op jit(solution)/shard_map/ppermute | solution.py:345
  15.7 0.6 %shard_map.157 = (bf16[1536,256]{1,0:T(8,128)(2,1)S(1)}, bf16[1536,128]{1,0:T(8,128)(2,1)S(1)}, bf16[384,256]{1,0:T(8,128)(2,1)S(1)}, bf16[384,128]{1,0:T(8,128)(2,1)S(1)}) custom-call(bf16[256,512]{1,0:T(8,128)(2,1)S(1)} %collective-permute-done.1.after.near, s32[6,256]{1,0:T(8,128)S(1)} %bitcast.6, bf16[256,64]{1,0:T(8,128)(2,1)S(1)} %get-tuple-element.41.pick.refs_0_), custom_call_target="tpu_custom_call" | custom-call | flops 40000000000 | bytes 301056 | tf_op jit(solution)/shard_map/pallas_call | solution.py:305
  16.4 3.8 %collective-permute-done.3.far = bf16[256,512]{1,0:T(8,128)(2,1)S(1)} collective-permute-done((bf16[256,512]{1,0:T(8,128)(2,1)S(1)}, bf16[256,512]{1,0:T(8,128)(2,1)S(1)}, u32[]{:S(2)}, u32[]{:S(2)}) %collective-permute-start.3) | collective-permute-done | bytes 262176 | tf_op jit(solution)/shard_map/ppermute | solution.py:354
  20.2 0.4 shard_map.158
  20.6 2.8 %collective-permute-start.4 = (bf16[64,512]{1,0:T(8,128)(2,1)S(1)}, bf16[64,512]{1,0:T(8,128)(2,1)S(1)}, u32[]{:S(2)}, u32[]{:S(2)}) collective-permute-start(bf16[64,512]{1,0:T(8,128)(2,1)S(1)} %get-tuple-element.49.halo), channel_id=1, source_target_pairs={{0,15},{1,2},{2,1},{3,4},{4,3},{5,6},{6,5},{7,8},{8,7},{9,10},{10,... | collective-permute-start | bytes 196616 | tf_op jit(solution)/shard_map/ppermute | solution.py:348
  23.4 0.3 shard_map.159.latent
  23.7 1.5 %shard_map.160 = (f32[1536,512]{1,0:T(8,128)S(1)}, bf16[64,512]{1,0:T(8,128)(2,1)S(1)}, f32[64,512]{1,0:T(8,128)S(1)}, f32[384,512]{1,0:T(8,128)S(1)}) custom-call(bf16[256,512]{1,0:T(8,128)(2,1)S(1)} %shard_map.159.latent, bf16[2,512,512]{2,1,0:T(8,128)(2,1)S(1)} %copy-done, bf16[2,512,512]{2,1,0:T(8,128)(2,1)S(1)} %copy-done.1, f32[2,512]{1,0:T(2,128)S(1)} %copy-done.9, ...), custom_call_target="tpu_custom_call" | custom-call | flops 1 | bytes 1 | tf_op jit(solution)/shard_map/pallas_call | solution.py:305
  25.3 1.8 %collective-permute-done.4.table = bf16[64,512]{1,0:T(8,128)(2,1)S(1)} collective-permute-done((bf16[64,512]{1,0:T(8,128)(2,1)S(1)}, bf16[64,512]{1,0:T(8,128)(2,1)S(1)}, u32[]{:S(2)}, u32[]{:S(2)}) %collective-permute-start.4) | collective-permute-done | bytes 65568 | tf_op jit(solution)/shard_map/ppermute | solution.py:348
  27.1 0.5 shard_map.163.halo
  27.6 2.8 %collective-permute-start.6 = (bf16[64,512]{1,0:T(8,128)(2,1)S(1)}, bf16[64,512]{1,0:T(8,128)(2,1)S(1)}, u32[]{:S(2)}, u32[]{:S(2)}) collective-permute-start(bf16[64,512]{1,0:T(8,128)(2,1)S(1)} %shard_map.163.halo), channel_id=1, source_target_pairs={{0,15},{1,2},{2,1},{3,4},{4,3},{5,6},{6,5},{7,8},{8,7},{9,10},{10,... | collective-permute-start | bytes 196616 | tf_op jit(solution)/shard_map/ppermute | solution.py:348
  30.4 0.9 %shard_map.162.latent = bf16[256,512]{1,0:T(8,128)(2,1)S(1)} custom-call(bf16[256,512]{1,0:T(8,128)(2,1)S(1)} %shard_map.159.latent, f32[1536,512]{1,0:T(8,128)S(1)} %get-tuple-element.51.before, bf16[64,512]{1,0:T(8,128)(2,1)S(1)} %shard_map.161.across, bf16[64,512]{1,0:T(8,128)(2,1)S(1)} %collective-permute-done.5.beside, ...), custom_call_target="tpu_custom_call" | custom-call | flops 1 | bytes 1 | tf_op jit(solution)/shard_map/pallas_call | solution.py:305
  31.3 1.0 %shard_map.164 = (f32[1536,512]{1,0:T(8,128)S(1)}, bf16[64,512]{1,0:T(8,128)(2,1)S(1)}, f32[256,512]{1,0:T(8,128)S(1)}) custom-call(bf16[256,512]{1,0:T(8,128)(2,1)S(1)} %shard_map.162.latent, bf16[2,512,512]{2,1,0:T(8,128)(2,1)S(1)} %copy-done, bf16[2,512,512]{2,1,0:T(8,128)(2,1)S(1)} %copy-done.1, f32[2,512]{1,0:T(2,128)S(1)} %copy-done.9, ...), custom_call_target="tpu_custom_call" | custom-call | flops 1 | bytes 1 | tf_op jit(solution)/shard_map/pallas_call | solution.py:305
  32.4 1.7 %collective-permute-done.6.table = bf16[64,512]{1,0:T(8,128)(2,1)S(1)} collective-permute-done((bf16[64,512]{1,0:T(8,128)(2,1)S(1)}, bf16[64,512]{1,0:T(8,128)(2,1)S(1)}, u32[]{:S(2)}, u32[]{:S(2)}) %collective-permute-start.6) | collective-permute-done | bytes 65568 | tf_op jit(solution)/shard_map/ppermute | solution.py:348
  34.1 0.9 %shard_map.166.own = bf16[256,512]{1,0:T(8,128)(2,1)S(1)} custom-call(f32[1536,512]{1,0:T(8,128)S(1)} %get-tuple-element.56.before, bf16[64,512]{1,0:T(8,128)(2,1)S(1)} %shard_map.165.across, bf16[64,512]{1,0:T(8,128)(2,1)S(1)} %collective-permute-done.7.beside, bf16[1536,128]{1,0:T(8,128)(2,1)S(1)} %get-tuple-element.53.gather_halo, ...), custom_call_target="tpu_custom_call" | custom-call | flops 469762048 | bytes 5767168 | tf_op jit(solution)/shard_map/pallas_call | solution.py:305
  35.0 1.5 %collective-permute-start.10 = (bf16[256,512]{1,0:T(8,128)(2,1)S(1)}, bf16[256,512]{1,0:T(8,128)(2,1)S(1)}, u32[]{:S(2)}, u32[]{:S(2)}) collective-permute-start(bf16[256,512]{1,0:T(8,128)(2,1)S(1)} %shard_map.166.own), channel_id=1, source_target_pairs={{0,14},{1,3},{2,0},{3,5},{4,2},{5,7},{6,4},{7,9},{8,6},{9,11},{10,... | collective-permute-start | bytes 786440 | tf_op jit(solution)/shard_map/ppermute | solution.py:351
  36.6 1.8 %shard_map.167 = (f32[2048,512]{1,0:T(8,128)S(1)}, bf16[128,512]{1,0:T(8,128)(2,1)S(1)}, bf16[128,512]{1,0:T(8,128)(2,1)S(1)}) custom-call(bf16[2048,512]{1,0:T(8,128)(2,1)S(1)} %copy-done.6, bf16[512,512]{1,0:T(8,128)(2,1)S(1)} %copy-done.8, bf16[2048,1280]{1,0:T(8,128)(2,1)S(1)} %get-tuple-element.39.fetch, bf16[256,512]{1,0:T(8,128)(2,1)S(1)} %shard_map.166.own), custom_call_target="tpu_custom_call" | custom-call | flops 1 | bytes 1 | tf_op jit(solution)/shard_map/pallas_call | solution.py:305
  38.4 0.5 collective-permute-start.9
  38.9 0.8 %collective-permute-done.8.refs_0_.first_after = bf16[128,512]{1,0:T(8,128)(2,1)S(1)} collective-permute-done((bf16[128,512]{1,0:T(8,128)(2,1)S(1)}, bf16[128,512]{1,0:T(8,128)(2,1)S(1)}, u32[]{:S(2)}, u32[]{:S(2)}) %collective-permute-start.8) | collective-permute-done | bytes 131104 | tf_op jit(solution)/shard_map/ppermute | solution.py:345
  40.0 0.8 %collective-permute-start.15 = (bf16[256,256]{1,0:T(8,128)(2,1)S(1)}, bf16[256,256]{1,0:T(8,128)(2,1)S(1)}, u32[]{:S(2)}, u32[]{:S(2)}) collective-permute-start(bf16[256,256]{1,0:T(8,128)(2,1)S(1)} %get-tuple-element.66), channel_id=1, source_target_pairs={{0,2},{1,15},{2,4},{3,1},{4,6},{5,3},{6,8},{7,5},{8,10},{9,7},{10,... | collective-permute-start | bytes 393224 | tf_op jit(solution)/shard_map/ppermute | solution.py:354
  40.8 0.7 %shard_map.168.base.after = f32[2048,512]{1,0:T(8,128)S(1)} custom-call(bf16[2048,1280]{1,0:T(8,128)(2,1)S(1)} %get-tuple-element.39.fetch, f32[2048,512]{1,0:T(8,128)S(1)} %get-tuple-element.59.base, bf16[128,512]{1,0:T(8,128)(2,1)S(1)} %collective-permute-done.8.refs_0_.first_after, bf16[128,512]{1,0:T(8,128)(2,1)S(1)} %collective-permute-done.9.refs_1_.after), custom_call_target="tpu_custom_call" | custom-call | flops 1 | bytes 1 | tf_op jit(solution)/shard_map/pallas_call | solution.py:305
  41.5 4.1 %collective-permute-done.10.far.table = bf16[256,512]{1,0:T(8,128)(2,1)S(1)} collective-permute-done((bf16[256,512]{1,0:T(8,128)(2,1)S(1)}, bf16[256,512]{1,0:T(8,128)(2,1)S(1)}, u32[]{:S(2)}, u32[]{:S(2)}) %collective-permute-start.10) | collective-permute-done | bytes 262176 | tf_op jit(solution)/shard_map/ppermute | solution.py:351
  45.7 0.5 collective-permute-start.12
  46.3 0.7 %shard_map.169.base = f32[2048,512]{1,0:T(8,128)S(1)} custom-call(bf16[2048,1280]{1,0:T(8,128)(2,1)S(1)} %get-tuple-element.39.fetch, f32[2048,512]{1,0:T(8,128)S(1)} %shard_map.168.base.after, bf16[256,512]{1,0:T(8,128)(2,1)S(1)} %collective-permute-done.10.far.table), custom_call_target="tpu_custom_call" | custom-call | flops 1 | bytes 1 | tf_op jit(solution)/shard_map/pallas_call | solution.py:305
  47.0 0.4 collective-permute-done.13.refs_2_
  47.5 0.7 %shard_map.171.base = f32[2048,512]{1,0:T(8,128)S(1)} custom-call(bf16[2048,1280]{1,0:T(8,128)(2,1)S(1)} %get-tuple-element.39.fetch, f32[2048,512]{1,0:T(8,128)S(1)} %shard_map.169.base, bf16[112,512]{1,0:T(8,128)(2,1)S(1)} %collective-permute-done.11.refs_0_, bf16[80,512]{1,0:T(8,128)(2,1)S(1)} %collective-permute-done.12.refs_1_, ...), custom_call_target="tpu_custom_call" | custom-call | flops 1 | bytes 1 | tf_op jit(solution)/shard_map/pallas_call | solution.py:305
  48.2 1.0 %shard_map.173.partial = f32[2048,512]{1,0:T(8,128)S(1)} custom-call(bf16[2048,1280]{1,0:T(8,128)(2,1)S(1)} %get-tuple-element.39.fetch, f32[2048,512]{1,0:T(8,128)S(1)} %shard_map.171.base, bf16[256,256]{1,0:T(8,128)(2,1)S(1)} %collective-permute-done.15.near, bf16[512,512]{1,0:T(8,128)(2,1)S(1)} %copy-done.3), custom_call_target="tpu_custom_call" | custom-call | flops 1 | bytes 1 | tf_op jit(solution)/shard_map/pallas_call | solution.py:305
  49.2 1.9 %shard_map.174 = bf16[2048,512]{1,0:T(8,128)(2,1)} custom-call(bf16[2048,1280]{1,0:T(8,128)(2,1)S(1)} %get-tuple-element.39.fetch, f32[2048,512]{1,0:T(8,128)S(1)} %shard_map.171.base, bf16[256,256]{1,0:T(8,128)(2,1)S(1)} %collective-permute-done.14.near, bf16[512,512]{1,0:T(8,128)(2,1)S(1)} %copy-done.3, f32[2048,512]{1,0:T(8,128)S(1)} %shard_map.173.partial), custom_call_target="tpu_custom_call" | custom-call | flops 1610612736 | bytes 14286848 | tf_op jit(solution)/shard_map/pallas_call | solution.py:305
  (45 shorter events, 0.8 us)
Async XLA Ops:
  0.0 11.2 %copy-start.10 = (s32[64]{0:T(128)S(1)}, s32[64]{0:T(128)}, u32[]{:S(2)}) copy-start(s32[64]{0:T(128)} %param.20) | copy-start | bytes 772
  4.2 6.1 %collective-permute-start = (bf16[256,512]{1,0:T(8,128)(2,1)S(1)}, bf16[256,512]{1,0:T(8,128)(2,1)S(1)}, u32[]{:S(2)}, u32[]{:S(2)}) collective-permute-start(bf16[256,512]{1,0:T(8,128)(2,1)S(1)} %get-tuple-element.38), channel_id=1, source_target_pairs={{0,1},{1,0},{2,3},{3,2},{4,5},{5,4},{6,7},{7,6},{8,9},{9,8},{10,11... | collective-permute-start | bytes 786440 | tf_op jit(solution)/shard_map/ppermute | solution.py:345
  4.8 10.9 %collective-permute-start.1 = (bf16[256,512]{1,0:T(8,128)(2,1)S(1)}, bf16[256,512]{1,0:T(8,128)(2,1)S(1)}, u32[]{:S(2)}, u32[]{:S(2)}) collective-permute-start(bf16[256,512]{1,0:T(8,128)(2,1)S(1)} %get-tuple-element.40), channel_id=1, source_target_pairs={{0,14},{1,3},{2,0},{3,5},{4,2},{5,7},{6,4},{7,9},{8,6},{9,11},{10,... | collective-permute-start | bytes 786440 | tf_op jit(solution)/shard_map/ppermute | solution.py:351
  10.4 5.3 %copy-start.11 = (s32[256,6]{0,1:T(8,128)S(1)}, s32[256,6]{0,1:T(8,128)}, u32[]{:S(2)}) copy-start(s32[256,6]{0,1:T(8,128)} %param.21) | copy-start | bytes 18436
  11.1 9.1 %collective-permute-start.3 = (bf16[256,512]{1,0:T(8,128)(2,1)S(1)}, bf16[256,512]{1,0:T(8,128)(2,1)S(1)}, u32[]{:S(2)}, u32[]{:S(2)}) collective-permute-start(bf16[256,512]{1,0:T(8,128)(2,1)S(1)} %shard_map.155.after), channel_id=1, source_target_pairs={{0,2},{1,15},{2,4},{3,1},{4,6},{5,3},{6,8},{7,5},{8,10},{9,7},{10,... | collective-permute-start | bytes 786440 | tf_op jit(solution)/shard_map/ppermute | solution.py:354
  14.3 5.9 %collective-permute-start.2 = (bf16[256,512]{1,0:T(8,128)(2,1)S(1)}, bf16[256,512]{1,0:T(8,128)(2,1)S(1)}, u32[]{:S(2)}, u32[]{:S(2)}) collective-permute-start(bf16[256,512]{1,0:T(8,128)(2,1)S(1)} %get-tuple-element.44), channel_id=1, source_target_pairs={{0,1},{1,0},{2,3},{3,2},{4,5},{5,4},{6,7},{7,6},{8,9},{9,8},{10,11... | collective-permute-start | bytes 786440 | tf_op jit(solution)/shard_map/ppermute | solution.py:345
  15.7 7.7 %copy-start.4 = (bf16[512,512]{1,0:T(8,128)(2,1)S(1)}, bf16[512,512]{1,0:T(8,128)(2,1)}, u32[]{:S(2)}) copy-start(bf16[512,512]{1,0:T(8,128)(2,1)} %w2.1) | copy-start | bytes 1572868
  15.7 7.7 %copy-start.7 = (bf16[256,512]{1,0:T(8,128)(2,1)S(1)}, bf16[256,512]{1,0:T(8,128)(2,1)}, u32[]{:S(2)}) copy-start(bf16[256,512]{1,0:T(8,128)(2,1)} %mesh.1) | copy-start | bytes 786436
  16.3 7.4 %copy-start = (bf16[2,512,512]{2,1,0:T(8,128)(2,1)S(1)}, bf16[2,512,512]{2,1,0:T(8,128)(2,1)}, u32[]{:S(2)}) copy-start(bf16[2,512,512]{2,1,0:T(8,128)(2,1)} %w_src.3) | copy-start | bytes 3145732
  16.3 7.4 %copy-start.1 = (bf16[2,512,512]{2,1,0:T(8,128)(2,1)S(1)}, bf16[2,512,512]{2,1,0:T(8,128)(2,1)}, u32[]{:S(2)}) copy-start(bf16[2,512,512]{2,1,0:T(8,128)(2,1)} %w_dst.3) | copy-start | bytes 3145732
  16.4 7.4 %copy-start.9 = (f32[2,512]{1,0:T(2,128)S(1)}, f32[2,512]{1,0:T(2,128)}, u32[]{:S(2)}) copy-start(f32[2,512]{1,0:T(2,128)} %bias.3) | copy-start | bytes 12292
  20.6 6.5 %collective-permute-start.4 = (bf16[64,512]{1,0:T(8,128)(2,1)S(1)}, bf16[64,512]{1,0:T(8,128)(2,1)S(1)}, u32[]{:S(2)}, u32[]{:S(2)}) collective-permute-start(bf16[64,512]{1,0:T(8,128)(2,1)S(1)} %get-tuple-element.49.halo), channel_id=1, source_target_pairs={{0,15},{1,2},{2,1},{3,4},{4,3},{5,6},{6,5},{7,8},{8,7},{9,10},{10,... | collective-permute-start | bytes 196616 | tf_op jit(solution)/shard_map/ppermute | solution.py:348
  25.2 5.1 %copy-start.2 = (bf16[2,512,512]{2,1,0:T(8,128)(2,1)S(1)}, bf16[2,512,512]{2,1,0:T(8,128)(2,1)}, u32[]{:S(2)}) copy-start(bf16[2,512,512]{2,1,0:T(8,128)(2,1)} %w_out.3) | copy-start | bytes 3145732
  25.2 1.9 %collective-permute-start.5 = (bf16[64,512]{1,0:T(8,128)(2,1)S(1)}, bf16[64,512]{1,0:T(8,128)(2,1)S(1)}, u32[]{:S(2)}, u32[]{:S(2)}) collective-permute-start(bf16[64,512]{1,0:T(8,128)(2,1)S(1)} %get-tuple-element.52), channel_id=1, source_target_pairs={{0,1},{1,0},{2,3},{3,2},{4,5},{5,4},{6,7},{7,6},{8,9},{9,8},{10,11... | collective-permute-start | bytes 196616 | tf_op jit(solution)/shard_map/ppermute | solution.py:345
  27.1 4.2 %copy-start.5 = (bf16[512,512]{1,0:T(8,128)(2,1)S(1)}, bf16[512,512]{1,0:T(8,128)(2,1)}, u32[]{:S(2)}) copy-start(bf16[512,512]{1,0:T(8,128)(2,1)} %w_next.3) | copy-start | bytes 1572868
  27.6 6.5 %collective-permute-start.6 = (bf16[64,512]{1,0:T(8,128)(2,1)S(1)}, bf16[64,512]{1,0:T(8,128)(2,1)S(1)}, u32[]{:S(2)}, u32[]{:S(2)}) collective-permute-start(bf16[64,512]{1,0:T(8,128)(2,1)S(1)} %shard_map.163.halo), channel_id=1, source_target_pairs={{0,15},{1,2},{2,1},{3,4},{4,3},{5,6},{6,5},{7,8},{8,7},{9,10},{10,... | collective-permute-start | bytes 196616 | tf_op jit(solution)/shard_map/ppermute | solution.py:348
  32.3 1.8 %collective-permute-start.7 = (bf16[64,512]{1,0:T(8,128)(2,1)S(1)}, bf16[64,512]{1,0:T(8,128)(2,1)S(1)}, u32[]{:S(2)}, u32[]{:S(2)}) collective-permute-start(bf16[64,512]{1,0:T(8,128)(2,1)S(1)} %get-tuple-element.57), channel_id=1, source_target_pairs={{0,1},{1,0},{2,3},{3,2},{4,5},{5,4},{6,7},{7,6},{8,9},{9,8},{10,11... | collective-permute-start | bytes 196616 | tf_op jit(solution)/shard_map/ppermute | solution.py:345
  34.0 2.5 %copy-start.6 = (bf16[2048,512]{1,0:T(8,128)(2,1)S(1)}, bf16[2048,512]{1,0:T(8,128)(2,1)}, u32[]{:S(2)}) copy-start(bf16[2048,512]{1,0:T(8,128)(2,1)} %grid.3) | copy-start | bytes 6291460
  34.0 2.5 %copy-start.8 = (bf16[512,512]{1,0:T(8,128)(2,1)S(1)}, bf16[512,512]{1,0:T(8,128)(2,1)}, u32[]{:S(2)}) copy-start(bf16[512,512]{1,0:T(8,128)(2,1)} %w_grid.1) | copy-start | bytes 1572868
  35.0 10.6 %collective-permute-start.10 = (bf16[256,512]{1,0:T(8,128)(2,1)S(1)}, bf16[256,512]{1,0:T(8,128)(2,1)S(1)}, u32[]{:S(2)}, u32[]{:S(2)}) collective-permute-start(bf16[256,512]{1,0:T(8,128)(2,1)S(1)} %shard_map.166.own), channel_id=1, source_target_pairs={{0,14},{1,3},{2,0},{3,5},{4,2},{5,7},{6,4},{7,9},{8,6},{9,11},{10,... | collective-permute-start | bytes 786440 | tf_op jit(solution)/shard_map/ppermute | solution.py:351
  38.4 1.4 %collective-permute-start.8 = (bf16[128,512]{1,0:T(8,128)(2,1)S(1)}, bf16[128,512]{1,0:T(8,128)(2,1)S(1)}, u32[]{:S(2)}, u32[]{:S(2)}) collective-permute-start(bf16[128,512]{1,0:T(8,128)(2,1)S(1)} %get-tuple-element.60), channel_id=1, source_target_pairs={{0,1},{1,0},{2,3},{3,2},{4,5},{5,4},{6,7},{7,6},{8,9},{9,8},{10,11... | collective-permute-start | bytes 393224 | tf_op jit(solution)/shard_map/ppermute | solution.py:345
  38.4 1.5 %collective-permute-start.9 = (bf16[128,512]{1,0:T(8,128)(2,1)S(1)}, bf16[128,512]{1,0:T(8,128)(2,1)S(1)}, u32[]{:S(2)}, u32[]{:S(2)}) collective-permute-start(bf16[128,512]{1,0:T(8,128)(2,1)S(1)} %get-tuple-element.61), channel_id=1, source_target_pairs={{0,1},{1,0},{2,3},{3,2},{4,5},{5,4},{6,7},{7,6},{8,9},{9,8},{10,11... | collective-permute-start | bytes 393224 | tf_op jit(solution)/shard_map/ppermute | solution.py:345
  40.0 8.2 %collective-permute-start.15 = (bf16[256,256]{1,0:T(8,128)(2,1)S(1)}, bf16[256,256]{1,0:T(8,128)(2,1)S(1)}, u32[]{:S(2)}, u32[]{:S(2)}) collective-permute-start(bf16[256,256]{1,0:T(8,128)(2,1)S(1)} %get-tuple-element.66), channel_id=1, source_target_pairs={{0,2},{1,15},{2,4},{3,1},{4,6},{5,3},{6,8},{7,5},{8,10},{9,7},{10,... | collective-permute-start | bytes 393224 | tf_op jit(solution)/shard_map/ppermute | solution.py:354
  40.8 8.5 %collective-permute-start.14 = (bf16[256,256]{1,0:T(8,128)(2,1)S(1)}, bf16[256,256]{1,0:T(8,128)(2,1)S(1)}, u32[]{:S(2)}, u32[]{:S(2)}) collective-permute-start(bf16[256,256]{1,0:T(8,128)(2,1)S(1)} %get-tuple-element.65), channel_id=1, source_target_pairs={{0,2},{1,15},{2,4},{3,1},{4,6},{5,3},{6,8},{7,5},{8,10},{9,7},{10,... | collective-permute-start | bytes 393224 | tf_op jit(solution)/shard_map/ppermute | solution.py:354
  45.7 1.8 %collective-permute-start.11 = (bf16[112,512]{1,0:T(8,128)(2,1)S(1)}, bf16[112,512]{1,0:T(8,128)(2,1)S(1)}, u32[]{:S(2)}, u32[]{:S(2)}) collective-permute-start(bf16[112,512]{1,0:T(8,128)(2,1)S(1)} %get-tuple-element.62), channel_id=1, source_target_pairs={{0,1},{1,0},{2,3},{3,2},{4,5},{5,4},{6,7},{7,6},{8,9},{9,8},{10,11... | collective-permute-start | bytes 344072 | tf_op jit(solution)/shard_map/ppermute | solution.py:345
  45.7 1.8 %collective-permute-start.12 = (bf16[80,512]{1,0:T(8,128)(2,1)S(1)}, bf16[80,512]{1,0:T(8,128)(2,1)S(1)}, u32[]{:S(2)}, u32[]{:S(2)}) collective-permute-start(bf16[80,512]{1,0:T(8,128)(2,1)S(1)} %get-tuple-element.63), channel_id=1, source_target_pairs={{0,1},{1,0},{2,3},{3,2},{4,5},{5,4},{6,7},{7,6},{8,9},{9,8},{10,11... | collective-permute-start | bytes 245768 | tf_op jit(solution)/shard_map/ppermute | solution.py:345
  46.2 1.3 %collective-permute-start.13 = (bf16[64,512]{1,0:T(8,128)(2,1)S(1)}, bf16[64,512]{1,0:T(8,128)(2,1)S(1)}, u32[]{:S(2)}, u32[]{:S(2)}) collective-permute-start(bf16[64,512]{1,0:T(8,128)(2,1)S(1)} %get-tuple-element.64), channel_id=1, source_target_pairs={{0,1},{1,0},{2,3},{3,2},{4,5},{5,4},{6,7},{7,6},{8,9},{9,8},{10,11... | collective-permute-start | bytes 196616 | tf_op jit(solution)/shard_map/ppermute | solution.py:345
  47.0 1.2 %copy-start.3 = (bf16[512,512]{1,0:T(8,128)(2,1)S(1)}, bf16[512,512]{1,0:T(8,128)(2,1)}, u32[]{:S(2)}) copy-start(bf16[512,512]{1,0:T(8,128)(2,1)} %w_out.5) | copy-start | bytes 1572868
